TPU v7x, 32 devices: a whole 2x2x4 slice. The times are simulated.
32 devices in a mesh: groups: 2 (over y), tp: 4 (over z), batch: 4 (over x, core).
Axes of the slice: x: 2, y: 2, z: 4, core: 2. Of those that a mesh axis runs over, the one named last changes fastest.
Arguments:
- gate_input: bfloat16 [1024, 53248], P(('groups', 'batch'), 'tp'), parts along dimension 0, may hold values from -6 to 6
- up_input: bfloat16 [1024, 53248], P(('groups', 'batch'), 'tp'), parts along dimension 0, may hold values from -6 to 6
- down_weight: bfloat16 [53248, 8192], P('tp', 'batch'), may hold values from -0.02734375 to 0.02734375
Outputs:
- mixed_codes: bfloat16 [1024, 8192], P(('groups', 'batch')), parts along dimension 0
- mixed_scales: bfloat16 [1024, 64], P(('groups', 'batch')), parts along dimension 0
There are 2 independent parts, one for each index of `groups`. A program takes and returns all parts, laid end to end along the dimension named above; an argument that names none is the same for every part. Nothing has to cross between parts.
All inputs are finite; a program needn't handle non-finite values.
Results may differ from a plain program's by a relative error of at most 0.011.
Values may be sent and summed in bfloat16 or wider, within the bound.
No kernel may reach another device: no remote copies, remote signals or barrier semaphores. Data moves between devices by JAX's collectives and lax.ppermute only.
A program may use at most 192 MiB of HBM per device.

v0:
```python
import jax
import jax.numpy as jnp
from jax import lax
from jax.sharding import PartitionSpec as P

BLOCK = 128


EPSILON = 1e-06


def encode(values):
    leading = values.shape[:-1]
    blocks = values.reshape(leading + (values.shape[-1] // BLOCK, BLOCK))
    scales = (jnp.max(jnp.abs(blocks), axis=-1) + EPSILON).astype(jnp.bfloat16)
    widened = lax.optimization_barrier(scales).astype(jnp.float32)
    encoded = (blocks / widened[..., None]).astype(jnp.bfloat16)
    return (encoded.reshape(values.shape), scales)


def decode(encoded, scales):
    blocks = encoded.reshape(scales.shape + (BLOCK,)).astype(jnp.float32)
    return (blocks * scales.astype(jnp.float32)[..., None]).reshape(encoded.shape)


def shards(gate_input, up_input, down_weight):
    hidden = (jax.nn.silu(gate_input.astype(jnp.float32)) * up_input.astype(jnp.float32)).astype(
        jnp.bfloat16
    )
    partial_value = jnp.dot(
        lax.all_gather(hidden, "batch", axis=0, tiled=True),
        down_weight,
        preferred_element_type=jnp.float32,
    )
    part_codes, part_scales = encode(partial_value)
    tp_count = lax.axis_size("tp")
    batch_count = lax.axis_size("batch")
    row_count = hidden.shape[0]
    local_cols = partial_value.shape[1]
    local_blocks = part_scales.shape[1]
    row_share = row_count // tp_count
    got_codes, got_scales = (
        lax.all_to_all(
            part_codes.reshape(batch_count, tp_count, row_share, local_cols),
            "tp",
            split_axis=1,
            concat_axis=1,
            tiled=True,
        ),
        lax.all_to_all(
            part_scales.reshape(batch_count, tp_count, row_share, local_blocks),
            "tp",
            split_axis=1,
            concat_axis=1,
            tiled=True,
        ),
    )
    summed = jnp.sum(decode(got_codes, got_scales), axis=1)
    new_codes, new_scales = encode(summed)
    home_codes, home_scales = (
        lax.all_to_all(new_codes, "batch", split_axis=0, concat_axis=2, tiled=True),
        lax.all_to_all(new_scales, "batch", split_axis=0, concat_axis=2, tiled=True),
    )
    out_codes, out_scales = (
        lax.all_gather(home_codes, "tp", axis=1, tiled=True),
        lax.all_gather(home_scales, "tp", axis=1, tiled=True),
    )
    return (out_codes.reshape(row_count, -1), out_scales.reshape(row_count, -1))


def solution(mesh):
    in_specs = (P(("groups", "batch"), "tp"), P(("groups", "batch"), "tp"), P("tp", "batch"))
    out_specs = (P(("groups", "batch"), None), P(("groups", "batch"), None))
    return jax.shard_map(shards, mesh=mesh, in_specs=in_specs, out_specs=out_specs, check_vma=False)
```

profile of v0, /device:TPU:0, one launch (start us, length us, event | category | flops | bytes accessed | tf_op | source)
XLA Modules:
  0.0 289.6 jit_solution(947298916343925255)
XLA Ops:
  7.2 0.0 all-gather.3.cloned.1.call-start
  7.2 5.2 %fusion.4 = bf16[128,13312]{1,0:T(8,128)(2,1)} fusion(bf16[128,13312]{1,0:T(8,128)(2,1)} %param.4, bf16[128,13312]{1,0:T(8,128)(2,1)} %param.3), kind=kLoop, calls=%fused_computation.6 | loop fusion | flops 13631488 | bytes 10223616 | tf_op jit(solution)/shard_map/convert_element_type | solution.py:27
  12.4 0.0 all-gather.3.cloned.1.call-update
  12.4 90.9 %all-gather.3.cloned.1.call-done = bf16[512,13312]{1,0:T(8,128)(2,1)} async-done(((bf16[128,13312]{1,0:T(8,128)(2,1)}), bf16[512,13312]{1,0:T(8,128)(2,1)}) %all-gather.3.cloned.1.call-update) | async-done | bytes 13631504 | tf_op jit(solution)/shard_map/all_gather | solution.py:31
  103.3 34.8 %fusion.5 = f32[512,2048]{1,0:T(8,128)S(1)} fusion(bf16[512,13312]{1,0:T(8,128)(2,1)} %all-gather.3.cloned.1.call-done, bf16[13312,2048]{1,0:T(8,128)(2,1)} %param.5), kind=kOutput, calls=%fused_computation.15 | convolution fusion | flops 27917287424 | bytes 72351744 | tf_op jit(solution)/shard_map/dot_general | solution.py:30
  138.1 0.0 copy-start
  138.1 0.7 abs_bitcast_fusion
  138.9 1.2 copy-done
  140.0 2.9 copy.50
  142.9 3.4 %reduce_max.18 = f32[512,16]{1,0:T(8,128)S(1)} reduce(f32[512,16,128]{2,1,0:T(8,128)} %bitcast.40, f32[]{:T(128)} %constant.1.clone.1), dimensions={2}, to_apply=%region_0.1 | reduce | flops 1040384 | bytes 4227076 | tf_op jit(solution)/shard_map/reduce_max | solution.py:15
  146.3 0.1 copy.34
  146.4 0.1 convert_element_type.47
  146.5 0.7 reshape.34
  147.3 4.6 %all-to-all-start.1 = ((bf16[4,2,1024]{2,1,0:T(2,128)(2,1)}), bf16[4,2,1024]{2,1,0:T(2,128)(2,1)S(1)}, u32[]{:S(2)}, u32[]{:S(2)}) async-start(bf16[4,2,1024]{2,1,0:T(2,128)(2,1)} %reshape.34), calls=%async_computation.1 | async-start | bytes 32768 | tf_op jit(solution)/shard_map/all_to_all | solution.py:50
  151.9 0.1 copy.35
  152.0 2.6 div.27
  154.5 4.9 %div.28 = f32[4,4,32,2048]{3,2,1,0:T(8,128)} reshape(f32[512,16,128]{2,1,0:T(8,128)} %div.27) | data formatting | bytes 8388608 | tf_op jit(solution)/shard_map/div | solution.py:17
  159.5 4.3 %divide_convert_fusion = bf16[4,4,32,2048]{3,2,1,0:T(8,128)(2,1)S(1)} fusion(f32[4,4,32,2048]{3,2,1,0:T(8,128)} %bitcast.39, f32[4,4,32,2048]{3,2,1,0:T(8,128)} %div.28), kind=kLoop, calls=%fused_computation.8 | loop fusion | flops 2097152 | bytes 10485760 | tf_op jit(solution)/shard_map/convert_element_type | solution.py:17
  163.7 1.5 copy.36
  165.2 0.0 all-to-all-done.1
  165.2 5.1 %all-to-all-start = ((bf16[4,4,32,2048]{3,2,0,1:T(8,128)(2,1)}), bf16[4,4,32,2048]{3,2,0,1:T(8,128)(2,1)S(1)}, u32[]{:S(2)}, u32[]{:S(2)}) async-start(bf16[4,4,32,2048]{3,2,0,1:T(8,128)(2,1)} %copy.36), calls=%async_computation | async-start | bytes 4194304 | tf_op jit(solution)/shard_map/all_to_all | solution.py:43
  170.3 0.0 all-gather.5.cloned.1.call-start
  170.3 0.1 reshape.35
  170.4 0.1 copy.38
  170.5 2.6 mul.20
  173.1 4.9 %mul.21 = f32[4,4,32,2048]{3,2,0,1:T(8,128)} reshape(f32[4,4,32,16,128]{4,3,2,0,1:T(8,128)} %mul.20) | data formatting | bytes 8388608 | tf_op jit(solution)/shard_map/mul | solution.py:23
  178.0 40.4 %all-to-all-done = bf16[4,4,32,2048]{3,2,0,1:T(8,128)(2,1)S(1)} async-done(((bf16[4,4,32,2048]{3,2,0,1:T(8,128)(2,1)}), bf16[4,4,32,2048]{3,2,0,1:T(8,128)(2,1)S(1)}, u32[]{:S(2)}, u32[]{:S(2)}) %all-to-all-start) | async-done | bytes 2097184 | tf_op jit(solution)/shard_map/all_to_all | solution.py:43
  218.3 2.9 %multiply_reduce_fusion = f32[4,32,2048]{2,1,0:T(8,128)S(1)} fusion(f32[4,4,32,2048]{3,2,0,1:T(8,128)} %mul.21, bf16[4,4,32,2048]{3,2,0,1:T(8,128)(2,1)S(1)} %all-to-all-done), kind=kLoop, calls=%fused_computation.7 | loop fusion | flops 2883584 | bytes 7340032 | tf_op jit(solution)/shard_map/reduce_sum | solution.py:58
  221.2 0.1 abs.14
  221.3 0.2 copy.51
  221.5 0.3 bitcast_reduce_fusion
  221.9 0.1 copy.41
  222.0 0.1 copy.42
  222.1 0.3 div.30
  222.4 0.2 div.31
  222.6 0.2 divide_convert_fusion.1
  222.7 11.2 %all_to_all.46 = bf16[4,32,2048]{2,1,0:T(8,128)(2,1)S(1)} all-to-all(bf16[4,32,2048]{2,1,0:T(8,128)(2,1)S(1)} %divide_convert_fusion.1), channel_id=1, replica_groups=mesh['groups'=2,'tp'=4,'batch'=4] {'batch'}, dimensions={0} | all-to-all | bytes 1048576 | tf_op jit(solution)/shard_map/all_to_all | solution.py:61
  234.0 0.8 copy.49
  234.8 0.0 all-gather.5.cloned.1.call-update
  234.8 0.1 reshape.36
  234.9 6.1 %all_to_all.47 = bf16[4,2,256]{2,1,0:T(2,128)(2,1)S(1)} all-to-all(bf16[4,2,256]{2,1,0:T(2,128)(2,1)S(1)} %reshape.36), channel_id=1, replica_groups=mesh['groups'=2,'tp'=4,'batch'=4] {'batch'}, dimensions={0} | all-to-all | bytes 8192 | tf_op jit(solution)/shard_map/all_to_all | solution.py:62
  241.0 0.1 reshape.37
  241.1 0.1 copy.44
  241.2 13.3 %all_gather.11 = bf16[1,128,64]{2,1,0:T(8,128)(2,1)S(1)} all-gather(bf16[1,32,64]{2,1,0:T(8,128)(2,1)S(1)} %copy.44), channel_id=1, replica_groups=mesh['groups'=2,'tp'=4,'batch'=4] {'tp'}, dimensions={1}, use_global_device_ids=true | all-gather | bytes 20480 | tf_op jit(solution)/shard_map/all_gather | solution.py:66
  254.6 0.7 copy.45
  255.2 24.4 %all-gather.5.cloned.1.call-done = bf16[1,128,8192]{2,1,0:T(8,128)(2,1)} async-done(((bf16[1,32,8192]{2,1,0:T(8,128)(2,1)}), bf16[1,128,8192]{2,1,0:T(8,128)(2,1)}) %all-gather.5.cloned.1.call-update) | async-done | bytes 2097168 | tf_op jit(solution)/shard_map/all_gather | solution.py:65
  279.7 3.1 %copy.55 = bf16[128,8192]{1,0:T(8,128)(2,1)} copy(bf16[128,8192]{1,0:T(8,128)(2,1)} %bitcast.43) | data formatting | bytes 4194304
  (4 shorter events, 0.0 us)
Async XLA Ops:
  7.2 96.2 %all-gather.3.cloned.1.call-start = ((), (), s32[]{:S(2)}) async-start(), calls=%async_computation.4 | async-start | bytes 17039360 | tf_op jit(solution)/shard_map/all_gather | solution.py:31
  138.1 1.9 copy-start
  147.3 17.9 %all-to-all-start.1 = ((bf16[4,2,1024]{2,1,0:T(2,128)(2,1)}), bf16[4,2,1024]{2,1,0:T(2,128)(2,1)S(1)}, u32[]{:S(2)}, u32[]{:S(2)}) async-start(bf16[4,2,1024]{2,1,0:T(2,128)(2,1)} %reshape.34), calls=%async_computation.1 | async-start | bytes 32768 | tf_op jit(solution)/shard_map/all_to_all | solution.py:50
  165.2 53.2 %all-to-all-start = ((bf16[4,4,32,2048]{3,2,0,1:T(8,128)(2,1)}), bf16[4,4,32,2048]{3,2,0,1:T(8,128)(2,1)S(1)}, u32[]{:S(2)}, u32[]{:S(2)}) async-start(bf16[4,4,32,2048]{3,2,0,1:T(8,128)(2,1)} %copy.36), calls=%async_computation | async-start | bytes 4194304 | tf_op jit(solution)/shard_map/all_to_all | solution.py:43
  170.3 109.4 %all-gather.5.cloned.1.call-start = ((), (), s32[]{:S(2)}) async-start(), calls=%async_computation.5 | async-start | bytes 2621440 | tf_op jit(solution)/shard_map/all_gather | solution.py:65
Sparse Core Ops, SparseCore 0:
  12.5 90.7 all-gather.2
  235.0 44.6 all-gather.4
where the time goes:
time: 290 us
  waiting for transfers between devices  156 us (54%)
  matrix products  34.8 us (12%)
  blocking collectives  30.7 us (11%)
  local copies, waits for them, and re-layouts  27.5 us (9%)
  other arithmetic  17 us (6%)
  between operations  14.2 us (5%)
  starting transfers between devices  9.73 us (3%)
    all_gather x1, waiting for transfers between devices, shards(): lax.all_gather(hidden, 'batch', axis=0, tiled=True)  90.9 us
    all_to_all x1, waiting for transfers between devices, shards(): lax.all_to_all(part_codes.reshape(batch_count, tp_count, row_share, local...  40.4 us
    dot_general x1, matrix products, shards(): jnp.dot(lax.all_gather(hidden, 'batch', axis=0, tiled=True), down_weight,...  34.8 us
    all_gather x1, waiting for transfers between devices, shards(): lax.all_gather(home_codes, 'tp', axis=1, tiled=True)  24.4 us
    all_gather x1, blocking collectives, shards(): lax.all_gather(home_scales, 'tp', axis=1, tiled=True)  13.3 us
    all_to_all x1, blocking collectives, shards(): lax.all_to_all(new_codes, 'batch', split_axis=0, concat_axis=2, tiled=True)  11.2 us
    unnamed x10, local copies, waits for them, and re-layouts  9.05 us
    div x4, local copies, waits for them, and re-layouts, encode(): encoded = (blocks / widened[..., None]).astype(jnp.bfloat16)  8 us
  transfers between devices with their start and end apart: 4, of which 3 were waited for; matrix products, arithmetic and copies ran while one was open for 8% of the time, Pallas kernels for 0%

commit v1 on v0

--- a/solution.py
+++ b/solution.py
@@ -1,12 +1,18 @@
+import functools
+
 import jax
 import jax.numpy as jnp
 from jax import lax
+from jax.experimental import pallas as pl
+from jax.experimental.pallas import tpu as pltpu
 from jax.sharding import PartitionSpec as P
 
 BLOCK = 128
-
-
 EPSILON = 1e-06
+
+STEP = 512
+CHUNKS = (7, 7, 6, 6)
+VMEM = 40 * 2**20
 
 
 def encode(values):
@@ -23,7 +29,7 @@
     return (blocks * scales.astype(jnp.float32)[..., None]).reshape(encoded.shape)
 
 
-def shards(gate_input, up_input, down_weight):
+def general_shards(gate_input, up_input, down_weight):
     hidden = (jax.nn.silu(gate_input.astype(jnp.float32)) * up_input.astype(jnp.float32)).astype(
         jnp.bfloat16
     )
@@ -68,7 +74,250 @@
     return (out_codes.reshape(row_count, -1), out_scales.reshape(row_count, -1))
 
 
+def params(limit=VMEM):
+    return pltpu.CompilerParams(vmem_limit_bytes=limit)
+
+
+ANY = pl.BlockSpec(memory_space=pl.ANY)
+
+
+def after(value, *earlier):
+    def body(*refs):
+        pass
+
+    return pl.pallas_call(
+        body,
+        out_shape=jax.ShapeDtypeStruct(value.shape, value.dtype),
+        in_specs=[ANY] * (1 + len(earlier)),
+        out_specs=ANY,
+        input_output_aliases={0: 0},
+        name="after",
+    )(value, *earlier)
+
+
+def activate(gate, up, first, steps, cut):
+    rows = gate.shape[0]
+
+    def body(gate_ref, up_ref, all_ref, low_ref, high_ref):
+        value = gate_ref[...].astype(jnp.float32)
+        value = value / (1.0 + jnp.exp(-value)) * up_ref[...].astype(jnp.float32)
+        value = value.astype(jnp.bfloat16)
+        all_ref[...] = value
+        low_ref[...] = value[:cut]
+        high_ref[...] = value[cut:]
+
+    width = steps * STEP
+    return pl.pallas_call(
+        body,
+        grid=(steps,),
+        in_specs=[pl.BlockSpec((rows, STEP), lambda k: (0, first + k))] * 2,
+        out_specs=[pl.BlockSpec((n, STEP), lambda k: (0, k)) for n in (rows, cut, rows - cut)],
+        out_shape=[jax.ShapeDtypeStruct((n, width), jnp.bfloat16) for n in (rows, cut, rows - cut)],
+        compiler_params=params(),
+        cost_estimate=pl.CostEstimate(
+            flops=8 * rows * width, bytes_accessed=8 * rows * width, transcendentals=rows * width
+        ),
+        name="activate",
+    )(gate, up)
+
+
+def multiply(pieces, weight, first, total, split, final, earlier=()):
+    steps = pieces[0].shape[1] // STEP
+    counts = [piece.shape[0] for piece in pieces]
+    rows, cols = sum(counts), weight.shape[1]
+    tile = min(512, cols)
+    part = cols // split
+    n_pieces, has_total, n_earlier = len(pieces), total is not None, len(earlier)
+
+    def body(*refs):
+        piece_refs = refs[:n_pieces]
+        weight_ref = refs[n_pieces]
+        total_ref = refs[n_pieces + 1] if has_total else None
+        out_ref, sums = refs[-2:]
+        k = pl.program_id(0)
+        left = jnp.concatenate([ref[...] for ref in piece_refs], axis=0)
+        for n in range(cols // tile):
+            at = pl.ds(n * tile, tile)
+            value = jnp.dot(left, weight_ref[:, at], preferred_element_type=jnp.float32)
+
+            @pl.when(k == 0)
+            def _():
+                sums[:, at] = value + total_ref[:, at] if has_total else value
+
+            @pl.when(k > 0)
+            def _():
+                sums[:, at] += value
+
+        @pl.when(k == steps - 1)
+        def _():
+            if not final:
+                out_ref[...] = sums[...]
+            elif split == 1:
+                out_ref[...] = sums[...].astype(jnp.bfloat16)
+            else:
+                for s in range(split):
+                    out_ref[s] = sums[:, s * part : (s + 1) * part].astype(jnp.bfloat16)
+
+    if not final:
+        out = jax.ShapeDtypeStruct((rows, cols), jnp.float32)
+    elif split == 1:
+        out = jax.ShapeDtypeStruct((rows, cols), jnp.bfloat16)
+    else:
+        out = jax.ShapeDtypeStruct((split, rows, part), jnp.bfloat16)
+    whole = pl.BlockSpec((rows, cols), lambda k: (0, 0))
+    return pl.pallas_call(
+        body,
+        grid=(steps,),
+        in_specs=[pl.BlockSpec((n, STEP), lambda k: (0, k)) for n in counts]
+        + [pl.BlockSpec((STEP, cols), lambda k: (first + k, 0))]
+        + ([whole] if has_total else [])
+        + [ANY] * n_earlier,
+        out_specs=pl.BlockSpec(out.shape, lambda k: (0,) * len(out.shape)),
+        out_shape=out,
+        scratch_shapes=[pltpu.VMEM((rows, cols), jnp.float32)],
+        compiler_params=params(),
+        cost_estimate=pl.CostEstimate(
+            flops=2 * rows * cols * steps * STEP,
+            bytes_accessed=2 * cols * steps * STEP,
+            transcendentals=0,
+        ),
+        name="multiply",
+    )(*pieces, weight, *([total] if has_total else []), *earlier)
+
+
+def encode_blocks(value, code_ref, scale_ref):
+    for n in range(value.shape[1] // BLOCK):
+        block = value[:, n * BLOCK : (n + 1) * BLOCK]
+        scale = (jnp.max(jnp.abs(block), axis=1, keepdims=True) + EPSILON).astype(jnp.bfloat16)
+        code_ref[:, n * BLOCK : (n + 1) * BLOCK] = (block / scale.astype(jnp.float32)).astype(
+            jnp.bfloat16
+        )
+        scale_ref[:, n : n + 1] = scale
+
+
+def encode_near(own, beside, place, width):
+    rows, cols = beside.shape
+    blocks = cols // BLOCK
+
+    def body(place_ref, own_ref, beside_ref, code_ref, scale_ref):
+        @pl.when(pl.program_id(0) == 0)
+        def _():
+            encode_blocks(own_ref[...].astype(jnp.float32), code_ref, scale_ref)
+
+        @pl.when(pl.program_id(0) == 1)
+        def _():
+            encode_blocks(beside_ref[...].astype(jnp.float32), code_ref, scale_ref)
+
+    return pl.pallas_call(
+        body,
+        grid_spec=pltpu.PrefetchScalarGridSpec(
+            num_scalar_prefetch=1,
+            grid=(2,),
+            in_specs=[pl.BlockSpec((rows, cols), lambda j, place: (0, 0))] * 2,
+            out_specs=[
+                pl.BlockSpec((rows, cols), lambda j, place: (0, place[0] ^ j)),
+                pl.BlockSpec((None, rows, blocks), lambda j, place: (j, 0, 0)),
+            ],
+        ),
+        out_shape=[
+            jax.ShapeDtypeStruct((rows, width), jnp.bfloat16),
+            jax.ShapeDtypeStruct((2, rows, blocks), jnp.bfloat16),
+        ],
+        compiler_params=params(),
+        name="encode_near",
+    )(place, own, beside)
+
+
+def encode_far(codes, shares, place, start):
+    tp, _, rows, part = shares.shape
+    blocks = part // BLOCK
+
+    def body(place_ref, codes_ref, share_ref, code_ref, scale_ref):
+        encode_blocks(share_ref[...].astype(jnp.float32), code_ref, scale_ref)
+
+    return pl.pallas_call(
+        body,
+        grid_spec=pltpu.PrefetchScalarGridSpec(
+            num_scalar_prefetch=1,
+            grid=(2, tp),
+            in_specs=[
+                ANY,
+                pl.BlockSpec((None, None, rows, part), lambda j, t, place: (t, j, 0, 0)),
+            ],
+            out_specs=[
+                pl.BlockSpec(
+                    (rows, part),
+                    lambda j, t, place: (start // rows, (place[0] ^ (j + 2)) * tp + t),
+                ),
+                pl.BlockSpec((None, None, rows, blocks), lambda j, t, place: (j, t, 0, 0)),
+            ],
+        ),
+        out_shape=[
+            jax.ShapeDtypeStruct(codes.shape, codes.dtype),
+            jax.ShapeDtypeStruct((2, tp, rows, blocks), jnp.bfloat16),
+        ],
+        input_output_aliases={1: 0},
+        compiler_params=params(),
+        name="encode_far",
+    )(place, codes, shares)
+
+
+def swap(value, flip, count):
+    return lax.ppermute(value, "batch", [(b, b ^ flip) for b in range(count)])
+
+
+def paired_shards(gate_input, up_input, down_weight):
+    rows, width = gate_input.shape
+    cols = down_weight.shape[1]
+    tp, batch = lax.axis_size("tp"), lax.axis_size("batch")
+    cut = rows * 3 // 4
+    place = lax.axis_index("batch").astype(jnp.int32).reshape(1)
+
+    firsts = [sum(CHUNKS[:c]) for c in range(len(CHUNKS))]
+    hidden, low, high = zip(
+        *[activate(gate_input, up_input, f, n, cut) for f, n in zip(firsts, CHUNKS)]
+    )
+
+    got = []
+    for piece in low + high:
+        if len(got) >= 2:
+            piece = after(piece, got[-2])
+        got.append(swap(piece, 2, batch))
+    beside = [swap(h, 1, batch) for h in hidden]
+    got_beside = [swap(g, 1, batch) for g in got]
+
+    near = None
+    for c, f in enumerate(firsts):
+        last = c == len(firsts) - 1
+        near = multiply([hidden[c], beside[c]], down_weight, f, near, 1, last)
+    near = lax.psum(near, "tp")
+    codes, near_scales = encode_near(near[:rows], swap(near[rows:], 1, batch), place, cols * batch)
+
+    far_scales = []
+    for group, start in ((0, 0), (1, cut)):
+        far = None
+        for c, f in enumerate(firsts):
+            last = c == len(firsts) - 1
+            i = group * len(firsts) + c
+            far = multiply([got[i], got_beside[i]], down_weight, f, far, tp, last)
+        share = lax.psum_scatter(far, "tp", scatter_dimension=0)
+        n = share.shape[0] // 2
+        home = jnp.stack([swap(share[:n], 2, batch), swap(share[n:], 3, batch)])
+        shares = lax.all_gather(home, "tp")
+        codes, scales = encode_far(codes, shares, place, start)
+        far_scales.append(scales.transpose(0, 2, 1, 3).reshape(2, n, -1))
+    scales = jnp.concatenate([near_scales, jnp.concatenate(far_scales, axis=1)], axis=0)
+    scales = jnp.take(scales, jnp.arange(batch) ^ place, axis=0)
+    return codes, scales.transpose(1, 0, 2).reshape(rows, -1)
+
+
 def solution(mesh):
+    def shards(gate_input, up_input, down_weight):
+        tp, batch = mesh.shape["tp"], mesh.shape["batch"]
+        width, cols = down_weight.shape
+        paired = batch == 4 and cols % (tp * BLOCK) == 0 and width == sum(CHUNKS) * STEP
+        return (paired_shards if paired else general_shards)(gate_input, up_input, down_weight)
+
     in_specs = (P(("groups", "batch"), "tp"), P(("groups", "batch"), "tp"), P("tp", "batch"))
     out_specs = (P(("groups", "batch"), None), P(("groups", "batch"), None))
     return jax.shard_map(shards, mesh=mesh, in_specs=in_specs, out_specs=out_specs, check_vma=False)

time: 290 us -> 278 us (0.959)
  Pallas kernels: 0 us -> 147 us
  waiting for transfers between devices: 156 us -> 48.6 us
  matrix products: 34.8 us -> 0 us
  other arithmetic: 17 us -> 0.81 us
  local copies, waits for them, and re-layouts: 27.5 us -> 16.8 us
  starting transfers between devices: 9.73 us -> 16.6 us
    pallas_call x0 -> x25, Pallas kernels: none -> 147 us  [the longest x12 130 us: multiply(): pl.pallas_call(body, grid=(steps,), in_specs=[pl.BlockSpec((n, STEP), lam...]
    all_gather x2 -> x0, waiting for transfers between devices: 115 us -> none  [the longest x1 90.9 us: shards(): lax.all_gather(hidden, 'batch', axis=0, tiled=True)]
    all_to_all x2 -> x0, waiting for transfers between devices: 40.4 us -> none  [the longest x1 40.4 us: shards(): lax.all_to_all(part_codes.reshape(batch_count, tp_count, row_share, local...]
    dot_general x1 -> x0, matrix products: 34.8 us -> none  [shards(): jnp.dot(lax.all_gather(hidden, 'batch', axis=0, tiled=True), down_weight,...]
    ppermute x0 -> x25, waiting for transfers between devices: none -> 30.9 us  [swap(): return lax.ppermute(value, 'batch', [(b, b ^ flip) for b in range(count)])]
    all_gather x1 -> x2, blocking collectives: 13.3 us -> 32.1 us  [paired_shards(): shares = lax.all_gather(home, 'tp')]
    reduce_scatter x0 -> x2, waiting for transfers between devices: none -> 17.6 us  [paired_shards(): share = lax.psum_scatter(far, 'tp', scatter_dimension=0)]
    all_to_all x2 -> x0, blocking collectives: 17.4 us -> none  [the longest x1 11.2 us: shards(): lax.all_to_all(new_codes, 'batch', split_axis=0, concat_axis=2, tiled=True)]
  transfers between devices with their start and end apart: 4 -> 28, of which waited for: 3 -> 8; matrix products, arithmetic and copies ran while one was open for 8% -> 1% of each run, Pallas kernels for 0% -> 51%
where the time goes in v1:
time: 278 us; the launch traced here: 276 us
  Pallas kernels  147 us (53%)
  waiting for transfers between devices  48.6 us (17%)
  blocking collectives  32.1 us (12%)
  local copies, waits for them, and re-layouts  16.8 us (6%)
  starting transfers between devices  16.6 us (6%)
  between operations  14.1 us (5%)
    pallas_call x12, Pallas kernels, multiply(): pl.pallas_call(body, grid=(steps,), in_specs=[pl.BlockSpec((n, STEP), lam...  130 us
    all_gather x2, blocking collectives, paired_shards(): shares = lax.all_gather(home, 'tp')  32.1 us
    ppermute x25, waiting for transfers between devices, swap(): return lax.ppermute(value, 'batch', [(b, b ^ flip) for b in range(count)])  30.9 us
    reduce_scatter x2, waiting for transfers between devices, paired_shards(): share = lax.psum_scatter(far, 'tp', scatter_dimension=0)  17.6 us
    ppermute x25, starting transfers between devices, swap(): return lax.ppermute(value, 'batch', [(b, b ^ flip) for b in range(count)])  16.3 us
    unnamed x46, local copies, waits for them, and re-layouts  12.9 us
    pallas_call x4, Pallas kernels, activate(): pl.pallas_call(body, grid=(steps,), in_specs=[pl.BlockSpec((rows, STEP),...  9.31 us
    pallas_call x2, Pallas kernels, encode_far(): pl.pallas_call(body, grid_spec=pltpu.PrefetchScalarGridSpec(num_scalar_pr...  6.29 us
  transfers between devices with their start and end apart: 28, of which 8 were waited for; matrix products, arithmetic and copies ran while one was open for 1% of the time, Pallas kernels for 51%

profile of v1, /device:TPU:0, one launch (start us, length us, event | category | flops | bytes accessed | tf_op | source)
XLA Modules:
  0.0 276.3 jit_solution(4000331247181686066)
XLA Ops:
  7.2 2.0 copy-done
  9.2 2.0 copy-done.1
  11.1 1.0 activate.7
  12.9 2.9 %collective-permute-start.8 = (bf16[96,3584]{1,0:T(8,128)(2,1)S(1)}, bf16[96,3584]{1,0:T(8,128)(2,1)S(1)}, u32[]{:S(2)}, u32[]{:S(2)}) collective-permute-start(bf16[96,3584]{1,0:T(8,128)(2,1)S(1)} %get-tuple-element.28), channel_id=1, source_target_pairs={{0,2},{1,3},{2,0},{3,1},{4,6},{5,7},{6,4},{7,5},{8,10},{9,11},{10,... | collective-permute-start | bytes 2064392 | tf_op jit(solution)/shard_map/ppermute | solution.py:266
  15.8 3.1 %activate.6 = (bf16[128,3584]{1,0:T(8,128)(2,1)}, bf16[96,3584]{1,0:T(8,128)(2,1)}, bf16[32,3584]{1,0:T(8,128)(2,1)S(1)}) custom-call(bf16[128,13312]{1,0:T(8,128)(2,1)S(1)} %copy-done, bf16[128,13312]{1,0:T(8,128)(2,1)S(1)} %copy-done.1), custom_call_target="tpu_custom_call" | custom-call | flops 3670016 | bytes 3670016 | tf_op jit(solution)/shard_map/activate/pallas_call | solution.py:110
  19.0 2.6 activate.5
  21.6 0.8 copy-done.18
  23.6 2.6 activate.4
  26.8 5.2 %collective-permute-done.8.refs_1_.refs_0_ = bf16[96,3584]{1,0:T(8,128)(2,1)S(1)} collective-permute-done((bf16[96,3584]{1,0:T(8,128)(2,1)S(1)}, bf16[96,3584]{1,0:T(8,128)(2,1)S(1)}, u32[]{:S(2)}, u32[]{:S(2)}) %collective-permute-start.8) | collective-permute-done | bytes 688160 | tf_op jit(solution)/shard_map/ppermute | solution.py:266
  32.1 0.9 copy-done.4
  33.0 13.1 %collective-permute-done.5.refs_1_.refs_0_ = bf16[96,3584]{1,0:T(8,128)(2,1)S(1)} collective-permute-done((bf16[96,3584]{1,0:T(8,128)(2,1)}, bf16[96,3584]{1,0:T(8,128)(2,1)S(1)}, u32[]{:S(2)}, u32[]{:S(2)}) %collective-permute-start.5) | collective-permute-done | bytes 688160 | tf_op jit(solution)/shard_map/ppermute | solution.py:266
  46.1 1.7 collective-permute-start.9
  47.8 0.9 collective-permute-start.6
  48.7 12.3 %multiply.12.refs_3_ = f32[256,2048]{1,0:T(8,128)S(1)} custom-call(bf16[128,3584]{1,0:T(8,128)(2,1)S(1)} %get-tuple-element.23.refs_0_, bf16[128,3584]{1,0:T(8,128)(2,1)} %collective-permute-done.3.refs_1_, bf16[13312,2048]{1,0:T(8,128)(2,1)} %refs_2_.23), custom_call_target="tpu_custom_call" | custom-call | flops 3758096384 | bytes 14680064 | tf_op jit(solution)/shard_map/multiply/pallas_call | solution.py:168
  61.1 12.7 %multiply.13.refs_3_ = f32[256,2048]{1,0:T(8,128)S(1)} custom-call(bf16[128,3584]{1,0:T(8,128)(2,1)} %get-tuple-element.22.refs_0_, bf16[128,3584]{1,0:T(8,128)(2,1)} %collective-permute-done.2.refs_1_, bf16[13312,2048]{1,0:T(8,128)(2,1)} %refs_2_.23, f32[256,2048]{1,0:T(8,128)S(1)} %multiply.12.refs_3_), custom_call_target="tpu_custom_call" | custom-call | flops 3758096384 | bytes 14680064 | tf_op jit(solution)/shard_map/multiply/pallas_call | solution.py:168
  73.8 11.1 %multiply.14.refs_3_ = f32[256,2048]{1,0:T(8,128)S(1)} custom-call(bf16[128,3072]{1,0:T(8,128)(2,1)} %get-tuple-element.21.refs_0_, bf16[128,3072]{1,0:T(8,128)(2,1)} %collective-permute-done.1.refs_1_, bf16[13312,2048]{1,0:T(8,128)(2,1)} %refs_2_.23, f32[256,2048]{1,0:T(8,128)S(1)} %multiply.13.refs_3_), custom_call_target="tpu_custom_call" | custom-call | flops 3221225472 | bytes 12582912 | tf_op jit(solution)/shard_map/multiply/pallas_call | solution.py:168
  84.9 12.0 %multiply.15 = bf16[256,2048]{1,0:T(8,128)(2,1)} custom-call(bf16[128,3072]{1,0:T(8,128)(2,1)} %get-tuple-element.20.refs_0_, bf16[128,3072]{1,0:T(8,128)(2,1)} %collective-permute-done.refs_1_, bf16[13312,2048]{1,0:T(8,128)(2,1)} %refs_2_.23, f32[256,2048]{1,0:T(8,128)S(1)} %multiply.14.refs_3_), custom_call_target="tpu_custom_call" | custom-call | flops 3221225472 | bytes 12582912 | tf_op jit(solution)/shard_map/multiply/pallas_call | solution.py:168
  97.0 0.8 copy-done.6
  97.8 1.2 collective-permute-start.18
  99.0 0.8 copy-done.8
  99.9 0.8 collective-permute-start.15
  100.7 5.8 %collective-permute-done.18.refs_1_.refs_0_ = bf16[32,3584]{1,0:T(8,128)(2,1)S(1)} collective-permute-done((bf16[32,3584]{1,0:T(8,128)(2,1)}, bf16[32,3584]{1,0:T(8,128)(2,1)S(1)}, u32[]{:S(2)}, u32[]{:S(2)}) %collective-permute-start.18) | collective-permute-done | bytes 229408 | tf_op jit(solution)/shard_map/ppermute | solution.py:266
  107.1 1.2 collective-permute-start.19
  108.4 3.0 %collective-permute-done.15.refs_1_.refs_0_ = bf16[32,3584]{1,0:T(8,128)(2,1)S(1)} collective-permute-done((bf16[32,3584]{1,0:T(8,128)(2,1)}, bf16[32,3584]{1,0:T(8,128)(2,1)S(1)}, u32[]{:S(2)}, u32[]{:S(2)}) %collective-permute-start.15) | collective-permute-done | bytes 229408 | tf_op jit(solution)/shard_map/ppermute | solution.py:266
  112.0 1.2 collective-permute-start.16
  113.3 0.9 copy-done.15
  114.6 1.0 collective-permute-done.19.refs_0_
  115.7 1.1 copy-done.16
  116.8 11.4 %multiply.16.refs_3_ = f32[192,2048]{1,0:T(8,128)S(1)} custom-call(bf16[96,3584]{1,0:T(8,128)(2,1)S(1)} %copy-done.5, bf16[96,3584]{1,0:T(8,128)(2,1)S(1)} %copy-done.16, bf16[13312,2048]{1,0:T(8,128)(2,1)} %refs_2_.23), custom_call_target="tpu_custom_call" | custom-call | flops 2818572288 | bytes 14680064 | tf_op jit(solution)/shard_map/multiply/pallas_call | solution.py:168
  128.9 10.1 %multiply.20.refs_3_ = f32[64,2048]{1,0:T(8,128)S(1)} custom-call(bf16[32,3584]{1,0:T(8,128)(2,1)S(1)} %copy-done.12, bf16[32,3584]{1,0:T(8,128)(2,1)S(1)} %collective-permute-done.22.refs_1_, bf16[13312,2048]{1,0:T(8,128)(2,1)} %refs_2_.23), custom_call_target="tpu_custom_call" | custom-call | flops 939524096 | bytes 14680064 | tf_op jit(solution)/shard_map/multiply/pallas_call | solution.py:168
  139.6 10.1 %multiply.21.refs_3_ = f32[64,2048]{1,0:T(8,128)S(1)} custom-call(bf16[32,3584]{1,0:T(8,128)(2,1)S(1)} %copy-done.14, bf16[32,3584]{1,0:T(8,128)(2,1)S(1)} %collective-permute-done.21.refs_1_, bf16[13312,2048]{1,0:T(8,128)(2,1)} %refs_2_.23, f32[64,2048]{1,0:T(8,128)S(1)} %multiply.20.refs_3_), custom_call_target="tpu_custom_call" | custom-call | flops 939524096 | bytes 14680064 | tf_op jit(solution)/shard_map/multiply/pallas_call | solution.py:168
  149.7 8.7 %multiply.22.refs_3_ = f32[64,2048]{1,0:T(8,128)S(1)} custom-call(bf16[32,3072]{1,0:T(8,128)(2,1)} %collective-permute-done.19.refs_0_, bf16[32,3072]{1,0:T(8,128)(2,1)S(1)} %collective-permute-done.20.refs_1_, bf16[13312,2048]{1,0:T(8,128)(2,1)} %refs_2_.23, f32[64,2048]{1,0:T(8,128)S(1)} %multiply.21.refs_3_), custom_call_target="tpu_custom_call" | custom-call | flops 805306368 | bytes 12582912 | tf_op jit(solution)/shard_map/multiply/pallas_call | solution.py:168
  158.4 8.7 %multiply.23 = bf16[4,64,512]{2,1,0:T(8,128)(2,1)S(1)} custom-call(bf16[32,3072]{1,0:T(8,128)(2,1)S(1)} %collective-permute-done.16.refs_0_, bf16[32,3072]{1,0:T(8,128)(2,1)S(1)} %collective-permute-done.17.refs_1_, bf16[13312,2048]{1,0:T(8,128)(2,1)} %refs_2_.23, f32[64,2048]{1,0:T(8,128)S(1)} %multiply.22.refs_3_), custom_call_target="tpu_custom_call" | custom-call | flops 805306368 | bytes 12582912 | tf_op jit(solution)/shard_map/multiply/pallas_call | solution.py:168
  168.1 11.7 %multiply.17.refs_3_ = f32[192,2048]{1,0:T(8,128)S(1)} custom-call(bf16[96,3584]{1,0:T(8,128)(2,1)S(1)} %copy-done.3, bf16[96,3584]{1,0:T(8,128)(2,1)} %collective-permute-done.11.refs_1_, bf16[13312,2048]{1,0:T(8,128)(2,1)} %refs_2_.23, f32[192,2048]{1,0:T(8,128)S(1)} %multiply.16.refs_3_), custom_call_target="tpu_custom_call" | custom-call | flops 2818572288 | bytes 14680064 | tf_op jit(solution)/shard_map/multiply/pallas_call | solution.py:168
  179.9 10.2 %multiply.18.refs_3_ = f32[192,2048]{1,0:T(8,128)S(1)} custom-call(bf16[96,3072]{1,0:T(8,128)(2,1)S(1)} %copy-done.7, bf16[96,3072]{1,0:T(8,128)(2,1)} %collective-permute-done.10.refs_1_, bf16[13312,2048]{1,0:T(8,128)(2,1)} %refs_2_.23, f32[192,2048]{1,0:T(8,128)S(1)} %multiply.17.refs_3_), custom_call_target="tpu_custom_call" | custom-call | flops 2415919104 | bytes 12582912 | tf_op jit(solution)/shard_map/multiply/pallas_call | solution.py:168
  190.1 11.0 %multiply.19 = bf16[4,192,512]{2,1,0:T(8,128)(2,1)} custom-call(bf16[96,3072]{1,0:T(8,128)(2,1)S(1)} %copy-done.9, bf16[96,3072]{1,0:T(8,128)(2,1)} %collective-permute-done.7.refs_1_, bf16[13312,2048]{1,0:T(8,128)(2,1)} %refs_2_.23, f32[192,2048]{1,0:T(8,128)S(1)} %multiply.18.refs_3_), custom_call_target="tpu_custom_call" | custom-call | flops 2415919104 | bytes 12582912 | tf_op jit(solution)/shard_map/multiply/pallas_call | solution.py:168
  201.2 1.3 fusion.1
  202.6 0.8 slice_bitcast_fusion.3
  203.4 1.2 collective-permute-start.23
  205.2 2.1 collective-permute-done.23
  208.0 17.5 %reduce-scatter.3.cloned.1.call-done = bf16[1,192,512]{2,1,0:T(8,128)(2,1)} async-done(((bf16[4,192,512]{2,1,0:T(8,128)(2,1)}), bf16[1,192,512]{2,1,0:T(8,128)(2,1)}) %reduce-scatter.3.cloned.1.call-update) | async-done | bytes 196624 | tf_op jit(solution)/shard_map/reduce_scatter | solution.py:303
  225.5 1.0 slice_bitcast_fusion.1
  226.5 1.5 collective-permute-start.13
  228.0 14.2 %all-gather.1 = bf16[8,32,512]{2,1,0:T(8,128)(2,1)S(1)} all-gather(bf16[2,32,512]{2,1,0:T(8,128)(2,1)S(1)} %pad_maximum_fusion.1), channel_id=3, replica_groups=mesh['groups'=2,'tp'=4,'batch'=4] {'tp'}, dimensions={0}, use_global_device_ids=true | all-gather | bytes 327680 | tf_op jit(solution)/shard_map/all_gather | solution.py:306
  242.2 1.6 encode_near.1
  243.9 17.9 %all-gather = bf16[8,96,512]{2,1,0:T(8,128)(2,1)S(1)} all-gather(bf16[2,96,512]{2,1,0:T(8,128)(2,1)S(1)} %pad_maximum_fusion), channel_id=2, replica_groups=mesh['groups'=2,'tp'=4,'batch'=4] {'tp'}, dimensions={0}, use_global_device_ids=true | all-gather | bytes 983040 | tf_op jit(solution)/shard_map/all_gather | solution.py:306
  261.9 3.3 %encode_far.2 = (bf16[128,8192]{1,0:T(8,128)(2,1)}, bf16[2,4,96,4]{3,2,1,0:T(8,128)(2,1)S(1)}) custom-call(s32[1]{0:T(128)} %bitcast.place_ref, bf16[128,8192]{1,0:T(8,128)(2,1)} %get-tuple-element.24.codes_ref, bf16[4,2,96,512]{3,2,1,0:T(8,128)(2,1)S(1)} %bitcast.24), custom_call_target="tpu_custom_call", output_to_operand_aliasing={{0}: (1, {})} | custom-call | tf_op jit(solution)/shard_map/encode_far/pallas_call | solution.py:238
  265.1 3.0 %encode_far.3 = (bf16[128,8192]{1,0:T(8,128)(2,1)}, bf16[2,4,32,4]{3,2,1,0:T(8,128)(2,1)S(1)}) custom-call(s32[1]{0:T(128)} %bitcast.place_ref, bf16[128,8192]{1,0:T(8,128)(2,1)} %get-tuple-element.29.codes_ref, bf16[4,2,32,512]{3,2,1,0:T(8,128)(2,1)S(1)} %bitcast.25), custom_call_target="tpu_custom_call", output_to_operand_aliasing={{0}: (1, {})} | custom-call | tf_op jit(solution)/shard_map/encode_far/pallas_call | solution.py:238
  (98 shorter events, 10.0 us)
Async XLA Ops:
  7.2 194.0 %all-reduce.2.cloned.1.call-start = ((), (), s32[]{:S(2)}) async-start(), calls=%async_computation.2 | async-start | bytes 2097152 | tf_op jit(solution)/shard_map/psum | solution.py:293
  7.2 2.0 copy-start
  9.2 2.0 copy-start.1
  12.2 0.7 copy-start.19
  12.2 35.6 %collective-permute-start.3 = (bf16[128,3584]{1,0:T(8,128)(2,1)S(1)}, bf16[128,3584]{1,0:T(8,128)(2,1)}, u32[]{:S(2)}, u32[]{:S(2)}) collective-permute-start(bf16[128,3584]{1,0:T(8,128)(2,1)S(1)} %get-tuple-element.23.refs_0_), channel_id=1, source_target_pairs={{0,1},{1,0},{2,3},{3,2},{4,5},{5,4},{6,7},{7,6},{8,9},{9,8},{10,11... | collective-permute-start | bytes 2752520 | tf_op jit(solution)/shard_map/ppermute | solution.py:266
  12.9 19.2 %collective-permute-start.8 = (bf16[96,3584]{1,0:T(8,128)(2,1)S(1)}, bf16[96,3584]{1,0:T(8,128)(2,1)S(1)}, u32[]{:S(2)}, u32[]{:S(2)}) collective-permute-start(bf16[96,3584]{1,0:T(8,128)(2,1)S(1)} %get-tuple-element.28), channel_id=1, source_target_pairs={{0,2},{1,3},{2,0},{3,1},{4,6},{5,7},{6,4},{7,5},{8,10},{9,11},{10,... | collective-permute-start | bytes 2064392 | tf_op jit(solution)/shard_map/ppermute | solution.py:266
  19.0 7.2 %copy-start.20 = (bf16[32,3584]{1,0:T(8,128)(2,1)}, bf16[32,3584]{1,0:T(8,128)(2,1)S(1)}, u32[]{:S(2)}) copy-start(bf16[32,3584]{1,0:T(8,128)(2,1)S(1)} %get-tuple-element.31.refs_0_) | copy-start | bytes 688132
  19.0 27.1 %collective-permute-start.5 = (bf16[96,3584]{1,0:T(8,128)(2,1)}, bf16[96,3584]{1,0:T(8,128)(2,1)S(1)}, u32[]{:S(2)}, u32[]{:S(2)}) collective-permute-start(bf16[96,3584]{1,0:T(8,128)(2,1)} %get-tuple-element.26), channel_id=1, source_target_pairs={{0,2},{1,3},{2,0},{3,1},{4,6},{5,7},{6,4},{7,5},{8,10},{9,11},{10,... | collective-permute-start | bytes 2064392 | tf_op jit(solution)/shard_map/ppermute | solution.py:266
  19.0 42.1 %collective-permute-start.2 = (bf16[128,3584]{1,0:T(8,128)(2,1)}, bf16[128,3584]{1,0:T(8,128)(2,1)}, u32[]{:S(2)}, u32[]{:S(2)}) collective-permute-start(bf16[128,3584]{1,0:T(8,128)(2,1)} %get-tuple-element.22.refs_0_), channel_id=1, source_target_pairs={{0,1},{1,0},{2,3},{3,2},{4,5},{5,4},{6,7},{7,6},{8,9},{9,8},{10,11... | collective-permute-start | bytes 2752520 | tf_op jit(solution)/shard_map/ppermute | solution.py:266
  21.6 0.8 copy-start.18
  23.1 50.7 %collective-permute-start.1 = (bf16[128,3072]{1,0:T(8,128)(2,1)}, bf16[128,3072]{1,0:T(8,128)(2,1)}, u32[]{:S(2)}, u32[]{:S(2)}) collective-permute-start(bf16[128,3072]{1,0:T(8,128)(2,1)} %get-tuple-element.21.refs_0_), channel_id=1, source_target_pairs={{0,1},{1,0},{2,3},{3,2},{4,5},{5,4},{6,7},{7,6},{8,9},{9,8},{10,11... | collective-permute-start | bytes 2359304 | tf_op jit(solution)/shard_map/ppermute | solution.py:266
  26.8 5.2 %copy-start.17 = (bf16[96,3072]{1,0:T(8,128)(2,1)}, bf16[96,3072]{1,0:T(8,128)(2,1)S(1)}, u32[]{:S(2)}) copy-start(bf16[96,3072]{1,0:T(8,128)(2,1)S(1)} %get-tuple-element.25.refs_0_) | copy-start | bytes 1769476
  32.1 0.9 copy-start.4
  32.1 52.8 %collective-permute-start = (bf16[128,3072]{1,0:T(8,128)(2,1)}, bf16[128,3072]{1,0:T(8,128)(2,1)}, u32[]{:S(2)}, u32[]{:S(2)}) collective-permute-start(bf16[128,3072]{1,0:T(8,128)(2,1)} %get-tuple-element.20.refs_0_), channel_id=1, source_target_pairs={{0,1},{1,0},{2,3},{3,2},{4,5},{5,4},{6,7},{7,6},{8,9},{9,8},{10,11... | collective-permute-start | bytes 2359304 | tf_op jit(solution)/shard_map/ppermute | solution.py:266
  46.1 1.7 copy-start.2
  46.1 50.9 %collective-permute-start.9 = (bf16[96,3072]{1,0:T(8,128)(2,1)}, bf16[96,3072]{1,0:T(8,128)(2,1)S(1)}, u32[]{:S(2)}, u32[]{:S(2)}) collective-permute-start(bf16[96,3072]{1,0:T(8,128)(2,1)} %after.7), channel_id=1, source_target_pairs={{0,2},{1,3},{2,0},{3,1},{4,6},{5,7},{6,4},{7,5},{8,10},{9,11},{10,... | collective-permute-start | bytes 1769480 | tf_op jit(solution)/shard_map/ppermute | solution.py:266
  47.8 13.2 %copy-start.5 = (bf16[96,3584]{1,0:T(8,128)(2,1)S(1)}, bf16[96,3584]{1,0:T(8,128)(2,1)}, u32[]{:S(2)}) copy-start(bf16[96,3584]{1,0:T(8,128)(2,1)} %copy-done.4) | copy-start | bytes 2064388
  47.8 51.2 %collective-permute-start.6 = (bf16[96,3072]{1,0:T(8,128)(2,1)}, bf16[96,3072]{1,0:T(8,128)(2,1)S(1)}, u32[]{:S(2)}, u32[]{:S(2)}) collective-permute-start(bf16[96,3072]{1,0:T(8,128)(2,1)} %after.6), channel_id=1, source_target_pairs={{0,2},{1,3},{2,0},{3,1},{4,6},{5,7},{6,4},{7,5},{8,10},{9,11},{10,... | collective-permute-start | bytes 1769480 | tf_op jit(solution)/shard_map/ppermute | solution.py:266
  61.0 52.2 %collective-permute-start.12 = (bf16[96,3584]{1,0:T(8,128)(2,1)S(1)}, bf16[96,3584]{1,0:T(8,128)(2,1)S(1)}, u32[]{:S(2)}, u32[]{:S(2)}) collective-permute-start(bf16[96,3584]{1,0:T(8,128)(2,1)S(1)} %copy-done.5), channel_id=1, source_target_pairs={{0,1},{1,0},{2,3},{3,2},{4,5},{5,4},{6,7},{7,6},{8,9},{9,8},{10,11... | collective-permute-start | bytes 2064392 | tf_op jit(solution)/shard_map/ppermute | solution.py:266
  96.9 11.5 %copy-start.3 = (bf16[96,3584]{1,0:T(8,128)(2,1)S(1)}, bf16[96,3584]{1,0:T(8,128)(2,1)}, u32[]{:S(2)}) copy-start(bf16[96,3584]{1,0:T(8,128)(2,1)} %copy-done.2) | copy-start | bytes 2064388
  96.9 105.7 %reduce-scatter.5.cloned.1.call-start = ((), (), s32[]{:S(2)}) async-start(), calls=%async_computation.4 | async-start | bytes 327680 | tf_op jit(solution)/shard_map/reduce_scatter | solution.py:303
  97.0 0.8 copy-start.6
  97.8 8.6 %collective-permute-start.18 = (bf16[32,3584]{1,0:T(8,128)(2,1)}, bf16[32,3584]{1,0:T(8,128)(2,1)S(1)}, u32[]{:S(2)}, u32[]{:S(2)}) collective-permute-start(bf16[32,3584]{1,0:T(8,128)(2,1)} %after.10), channel_id=1, source_target_pairs={{0,2},{1,3},{2,0},{3,1},{4,6},{5,7},{6,4},{7,5},{8,10},{9,11},{10,... | collective-permute-start | bytes 688136 | tf_op jit(solution)/shard_map/ppermute | solution.py:266
  99.0 0.8 copy-start.8
  99.9 11.5 %collective-permute-start.15 = (bf16[32,3584]{1,0:T(8,128)(2,1)}, bf16[32,3584]{1,0:T(8,128)(2,1)S(1)}, u32[]{:S(2)}, u32[]{:S(2)}) collective-permute-start(bf16[32,3584]{1,0:T(8,128)(2,1)} %after.8), channel_id=1, source_target_pairs={{0,2},{1,3},{2,0},{3,1},{4,6},{5,7},{6,4},{7,5},{8,10},{9,11},{10,... | collective-permute-start | bytes 688136 | tf_op jit(solution)/shard_map/ppermute | solution.py:266
  106.4 0.7 copy-start.11
  107.1 8.5 %collective-permute-start.19 = (bf16[32,3072]{1,0:T(8,128)(2,1)}, bf16[32,3072]{1,0:T(8,128)(2,1)}, u32[]{:S(2)}, u32[]{:S(2)}) collective-permute-start(bf16[32,3072]{1,0:T(8,128)(2,1)} %after.11), channel_id=1, source_target_pairs={{0,2},{1,3},{2,0},{3,1},{4,6},{5,7},{6,4},{7,5},{8,10},{9,11},{10,... | collective-permute-start | bytes 589832 | tf_op jit(solution)/shard_map/ppermute | solution.py:266
  108.4 59.7 %collective-permute-start.11 = (bf16[96,3584]{1,0:T(8,128)(2,1)S(1)}, bf16[96,3584]{1,0:T(8,128)(2,1)}, u32[]{:S(2)}, u32[]{:S(2)}) collective-permute-start(bf16[96,3584]{1,0:T(8,128)(2,1)S(1)} %copy-done.3), channel_id=1, source_target_pairs={{0,1},{1,0},{2,3},{3,2},{4,5},{5,4},{6,7},{7,6},{8,9},{9,8},{10,11... | collective-permute-start | bytes 2064392 | tf_op jit(solution)/shard_map/ppermute | solution.py:266
  112.0 16.2 %copy-start.7 = (bf16[96,3072]{1,0:T(8,128)(2,1)S(1)}, bf16[96,3072]{1,0:T(8,128)(2,1)}, u32[]{:S(2)}) copy-start(bf16[96,3072]{1,0:T(8,128)(2,1)} %copy-done.6) | copy-start | bytes 1769476
  112.0 16.9 %copy-start.12 = (bf16[32,3584]{1,0:T(8,128)(2,1)S(1)}, bf16[32,3584]{1,0:T(8,128)(2,1)}, u32[]{:S(2)}) copy-start(bf16[32,3584]{1,0:T(8,128)(2,1)} %copy-done.11) | copy-start | bytes 688132
  112.0 16.2 %collective-permute-start.16 = (bf16[32,3072]{1,0:T(8,128)(2,1)}, bf16[32,3072]{1,0:T(8,128)(2,1)S(1)}, u32[]{:S(2)}, u32[]{:S(2)}) collective-permute-start(bf16[32,3072]{1,0:T(8,128)(2,1)} %after.9), channel_id=1, source_target_pairs={{0,2},{1,3},{2,0},{3,1},{4,6},{5,7},{6,4},{7,5},{8,10},{9,11},{10,... | collective-permute-start | bytes 589832 | tf_op jit(solution)/shard_map/ppermute | solution.py:266
  113.2 15.6 %collective-permute-start.22 = (bf16[32,3584]{1,0:T(8,128)(2,1)}, bf16[32,3584]{1,0:T(8,128)(2,1)S(1)}, u32[]{:S(2)}, u32[]{:S(2)}) collective-permute-start(bf16[32,3584]{1,0:T(8,128)(2,1)} %copy-done.11), channel_id=1, source_target_pairs={{0,1},{1,0},{2,3},{3,2},{4,5},{5,4},{6,7},{7,6},{8,9},{9,8},{10,11... | collective-permute-start | bytes 688136 | tf_op jit(solution)/shard_map/ppermute | solution.py:266
  113.3 0.9 copy-start.15
  114.1 24.9 %collective-permute-start.21 = (bf16[32,3584]{1,0:T(8,128)(2,1)}, bf16[32,3584]{1,0:T(8,128)(2,1)S(1)}, u32[]{:S(2)}, u32[]{:S(2)}) collective-permute-start(bf16[32,3584]{1,0:T(8,128)(2,1)} %copy-done.13), channel_id=1, source_target_pairs={{0,1},{1,0},{2,3},{3,2},{4,5},{5,4},{6,7},{7,6},{8,9},{9,8},{10,11... | collective-permute-start | bytes 688136 | tf_op jit(solution)/shard_map/ppermute | solution.py:266
  115.6 34.0 %collective-permute-start.20 = (bf16[32,3072]{1,0:T(8,128)(2,1)}, bf16[32,3072]{1,0:T(8,128)(2,1)S(1)}, u32[]{:S(2)}, u32[]{:S(2)}) collective-permute-start(bf16[32,3072]{1,0:T(8,128)(2,1)} %collective-permute-done.19.refs_0_), channel_id=1, source_target_pairs={{0,1},{1,0},{2,3},{3,2},{4,5},{5,4},{6,7},{7,6},{8,9},{9,8},{10,11... | collective-permute-start | bytes 589832 | tf_op jit(solution)/shard_map/ppermute | solution.py:266
  115.6 1.1 copy-start.16
  128.2 10.9 %copy-start.9 = (bf16[96,3072]{1,0:T(8,128)(2,1)S(1)}, bf16[96,3072]{1,0:T(8,128)(2,1)}, u32[]{:S(2)}) copy-start(bf16[96,3072]{1,0:T(8,128)(2,1)} %copy-done.8) | copy-start | bytes 1769476
  128.2 11.4 %copy-start.14 = (bf16[32,3584]{1,0:T(8,128)(2,1)S(1)}, bf16[32,3584]{1,0:T(8,128)(2,1)}, u32[]{:S(2)}) copy-start(bf16[32,3584]{1,0:T(8,128)(2,1)} %copy-done.13) | copy-start | bytes 688132
  128.2 51.6 %collective-permute-start.10 = (bf16[96,3072]{1,0:T(8,128)(2,1)S(1)}, bf16[96,3072]{1,0:T(8,128)(2,1)}, u32[]{:S(2)}, u32[]{:S(2)}) collective-permute-start(bf16[96,3072]{1,0:T(8,128)(2,1)S(1)} %copy-done.7), channel_id=1, source_target_pairs={{0,1},{1,0},{2,3},{3,2},{4,5},{5,4},{6,7},{7,6},{8,9},{9,8},{10,11... | collective-permute-start | bytes 1769480 | tf_op jit(solution)/shard_map/ppermute | solution.py:266
  128.8 29.6 %collective-permute-start.17 = (bf16[32,3072]{1,0:T(8,128)(2,1)S(1)}, bf16[32,3072]{1,0:T(8,128)(2,1)S(1)}, u32[]{:S(2)}, u32[]{:S(2)}) collective-permute-start(bf16[32,3072]{1,0:T(8,128)(2,1)S(1)} %collective-permute-done.16.refs_0_), channel_id=1, source_target_pairs={{0,1},{1,0},{2,3},{3,2},{4,5},{5,4},{6,7},{7,6},{8,9},{9,8},{10,11... | collective-permute-start | bytes 589832 | tf_op jit(solution)/shard_map/ppermute | solution.py:266
  139.1 51.0 %collective-permute-start.7 = (bf16[96,3072]{1,0:T(8,128)(2,1)S(1)}, bf16[96,3072]{1,0:T(8,128)(2,1)}, u32[]{:S(2)}, u32[]{:S(2)}) collective-permute-start(bf16[96,3072]{1,0:T(8,128)(2,1)S(1)} %copy-done.9), channel_id=1, source_target_pairs={{0,1},{1,0},{2,3},{3,2},{4,5},{5,4},{6,7},{7,6},{8,9},{9,8},{10,11... | collective-permute-start | bytes 1769480 | tf_op jit(solution)/shard_map/ppermute | solution.py:266
  167.1 0.7 copy-start.10
  167.9 57.7 %reduce-scatter.3.cloned.1.call-start = ((), (), s32[]{:S(2)}) async-start(), calls=%async_computation.3 | async-start | bytes 983040 | tf_op jit(solution)/shard_map/reduce_scatter | solution.py:303
  202.5 39.7 %collective-permute-start.4 = (bf16[128,2048]{1,0:T(8,128)(2,1)S(1)}, bf16[128,2048]{1,0:T(8,128)(2,1)S(1)}, u32[]{:S(2)}, u32[]{:S(2)}) collective-permute-start(bf16[128,2048]{1,0:T(8,128)(2,1)S(1)} %get-tuple-element.38), channel_id=1, source_target_pairs={{0,1},{1,0},{2,3},{3,2},{4,5},{5,4},{6,7},{7,6},{8,9},{9,8},{10,11... | collective-permute-start | bytes 1572872 | tf_op jit(solution)/shard_map/ppermute | solution.py:266
  203.4 3.9 %collective-permute-start.23 = (bf16[32,512]{1,0:T(8,128)(2,1)S(1)}, bf16[32,512]{1,0:T(8,128)(2,1)S(1)}, u32[]{:S(2)}, u32[]{:S(2)}) collective-permute-start(bf16[32,512]{1,0:T(8,128)(2,1)S(1)} %get-tuple-element.42), channel_id=1, source_target_pairs={{0,2},{1,3},{2,0},{3,1},{4,6},{5,7},{6,4},{7,5},{8,10},{9,11},{10,... | collective-permute-start | bytes 98312 | tf_op jit(solution)/shard_map/ppermute | solution.py:266
  204.6 3.4 %collective-permute-start.24 = (bf16[32,512]{1,0:T(8,128)(2,1)S(1)}, bf16[32,512]{1,0:T(8,128)(2,1)S(1)}, u32[]{:S(2)}, u32[]{:S(2)}) collective-permute-start(bf16[32,512]{1,0:T(8,128)(2,1)S(1)} %get-tuple-element.43), channel_id=1, source_target_pairs={{0,3},{1,2},{2,1},{3,0},{4,7},{5,6},{6,5},{7,4},{8,11},{9,10},{10,... | collective-permute-start | bytes 98312 | tf_op jit(solution)/shard_map/ppermute | solution.py:266
  226.5 17.4 %collective-permute-start.13 = (bf16[96,512]{1,0:T(8,128)(2,1)S(1)}, bf16[96,512]{1,0:T(8,128)(2,1)S(1)}, u32[]{:S(2)}, u32[]{:S(2)}) collective-permute-start(bf16[96,512]{1,0:T(8,128)(2,1)S(1)} %get-tuple-element.40), channel_id=1, source_target_pairs={{0,2},{1,3},{2,0},{3,1},{4,6},{5,7},{6,4},{7,5},{8,10},{9,11},{10,... | collective-permute-start | bytes 294920 | tf_op jit(solution)/shard_map/ppermute | solution.py:266
  228.0 15.9 %collective-permute-start.14 = (bf16[96,512]{1,0:T(8,128)(2,1)S(1)}, bf16[96,512]{1,0:T(8,128)(2,1)S(1)}, u32[]{:S(2)}, u32[]{:S(2)}) collective-permute-start(bf16[96,512]{1,0:T(8,128)(2,1)S(1)} %get-tuple-element.41), channel_id=1, source_target_pairs={{0,3},{1,2},{2,1},{3,0},{4,7},{5,6},{6,5},{7,4},{8,11},{9,10},{10,... | collective-permute-start | bytes 294920 | tf_op jit(solution)/shard_map/ppermute | solution.py:266
  (3 other events, 2.0 us)
Sparse Core Ops, SparseCore 0:
  97.0 52.9 all-reduce.1
  168.0 20.6 reduce-scatter.4
  201.2 24.2 reduce-scatter.2

commit v2 on v0

--- a/solution.py
+++ b/solution.py
@@ -1,12 +1,20 @@
+import functools
+
 import jax
 import jax.numpy as jnp
 from jax import lax
+from jax.experimental import pallas as pl
+from jax.experimental.pallas import tpu as pltpu
 from jax.sharding import PartitionSpec as P
 
 BLOCK = 128
-
-
 EPSILON = 1e-06
+
+STEP = 1024
+CHUNKS = (4, 3, 3, 3)
+GROUPS = (3, 1)
+TILE = 512
+VMEM = 24 * 2**20
 
 
 def encode(values):
@@ -23,7 +31,7 @@
     return (blocks * scales.astype(jnp.float32)[..., None]).reshape(encoded.shape)
 
 
-def shards(gate_input, up_input, down_weight):
+def general_shards(gate_input, up_input, down_weight):
     hidden = (jax.nn.silu(gate_input.astype(jnp.float32)) * up_input.astype(jnp.float32)).astype(
         jnp.bfloat16
     )
@@ -68,7 +76,373 @@
     return (out_codes.reshape(row_count, -1), out_scales.reshape(row_count, -1))
 
 
+ANY = pl.BlockSpec(memory_space=pl.ANY)
+SMALL = pl.CostEstimate(flops=1024, bytes_accessed=1024, transcendentals=0)
+
+
+TOKEN = (8, 128)
+
+
+def large(value):
+    return value.size * value.dtype.itemsize > 3 * 2**20
+
+
+class Chain:
+    def __init__(self):
+        self.tokens = []
+
+    def call(self, body, operands, in_specs, out_specs, out_shape, name, grid=(), scratch=(), aliases=None):
+        count, n_tokens, n_outs = len(operands), len(self.tokens), len(out_shape)
+
+        def with_tokens(*refs):
+            outs = count + n_tokens
+            body(*refs[:count], *refs[outs : outs + n_outs], *refs[outs + n_outs + 1 :])
+
+        operands = [
+            pltpu.with_memory_space_constraint(value, pltpu.HBM) if large(value) else value
+            for value in operands
+        ]
+        outs = pl.pallas_call(
+            with_tokens,
+            grid=grid,
+            in_specs=list(in_specs) + [ANY] * n_tokens,
+            out_specs=list(out_specs) + [ANY],
+            out_shape=list(out_shape) + [jax.ShapeDtypeStruct(TOKEN, jnp.float32)],
+            scratch_shapes=scratch,
+            input_output_aliases=aliases or {},
+            compiler_params=pltpu.CompilerParams(vmem_limit_bytes=VMEM),
+            cost_estimate=SMALL,
+            name=name,
+        )(*operands, *self.tokens)
+        self.tokens = [outs[-1]]
+        return outs[:-1]
+
+    def pin(self, value):
+        pinned = self.call(
+            lambda *refs: None,
+            [value],
+            [ANY],
+            [ANY],
+            [jax.ShapeDtypeStruct(value.shape, value.dtype)],
+            "pin",
+            aliases={0: 0},
+        )
+        return pinned[0]
+
+
+def activate(chain, gate, up, first, steps, cuts):
+    rows = gate.shape[0]
+    counts = [rows] + [b - a for a, b in zip(cuts, cuts[1:])]
+
+    def body(gate_ref, up_ref, all_ref, *group_refs):
+        value = gate_ref[...].astype(jnp.float32)
+        value = value / (1.0 + jnp.exp(-value)) * up_ref[...].astype(jnp.float32)
+        value = value.astype(jnp.bfloat16)
+        all_ref[...] = value
+        for ref, a, b in zip(group_refs, cuts, cuts[1:]):
+            ref[...] = value[a:b]
+
+    return chain.call(
+        body,
+        [gate, up],
+        [pl.BlockSpec((rows, STEP), lambda k: (0, first + k))] * 2,
+        [pl.BlockSpec((n, STEP), lambda k: (0, k)) for n in counts],
+        [jax.ShapeDtypeStruct((n, steps * STEP), jnp.bfloat16) for n in counts],
+        "activate",
+        grid=(steps,),
+    )
+
+
+def multiply(chain, chunks, weight, first, total, place, split):
+    steps = [pieces[0].shape[1] // STEP for pieces in chunks]
+    starts = [sum(steps[:c]) for c in range(len(steps))]
+    counts = [piece.shape[0] for piece in chunks[0]]
+    rows, cols = sum(counts), weight.shape[1]
+    tiles, part = cols // TILE, cols // max(split, 1)
+    flat = [piece for pieces in chunks for piece in pieces]
+    n_total = 0 if total is None else 1
+
+    def body(place_ref, *refs):
+        piece_refs, refs = refs[: len(flat)], refs[len(flat) :]
+        weight_refs, refs = refs[:tiles], refs[tiles:]
+        total_refs, refs = refs[:n_total], refs[n_total:]
+        outs, (left, *sums) = refs[: max(split, 1)], refs[max(split, 1) :]
+        sums = sums[0] if sums else outs[0]
+        k = pl.program_id(0)
+
+        @pl.when(k == 0)
+        def _():
+            sums[...] = total_refs[0][...] if n_total else jnp.zeros(sums.shape, sums.dtype)
+
+        for c, n in enumerate(steps):
+
+            @pl.when((k >= starts[c]) & (k < starts[c] + n))
+            def _():
+                at = 0
+                for ref in piece_refs[c * len(counts) : (c + 1) * len(counts)]:
+                    left[at : at + ref.shape[0]] = ref[...]
+                    at += ref.shape[0]
+
+        for n in range(tiles):
+            sums[:, n * TILE : (n + 1) * TILE] += jnp.dot(
+                left[...], weight_refs[n][...], preferred_element_type=jnp.float32
+            )
+
+        if split:
+
+            @pl.when(k == sum(steps) - 1)
+            def _():
+                for o in range(split):
+                    at = lax.rem(place_ref[0] + o, split) * part
+                    outs[o][...] = sums[:, pl.ds(pl.multiple_of(at, part), part)].astype(jnp.bfloat16)
+
+    def piece_spec(c, n):
+        return pl.BlockSpec((n, STEP), lambda k: (0, jnp.clip(k - starts[c], 0, steps[c] - 1)))
+
+    def weight_spec(n):
+        return pl.BlockSpec((STEP, TILE), lambda k: (first + k, n))
+
+    whole = pl.BlockSpec((rows, cols), lambda k: (0, 0))
+    return chain.call(
+        body,
+        [place] + flat + [weight] * tiles + ([total] if n_total else []),
+        [pl.BlockSpec(memory_space=pltpu.SMEM)]
+        + [piece_spec(c, n) for c in range(len(chunks)) for n in counts]
+        + [weight_spec(n) for n in range(tiles)]
+        + [whole] * n_total,
+        [pl.BlockSpec((rows, part), lambda k: (0, 0))] * max(split, 1),
+        [jax.ShapeDtypeStruct((rows, part), jnp.bfloat16 if split else jnp.float32)] * max(split, 1),
+        "multiply",
+        grid=(sum(steps),),
+        scratch=[pltpu.VMEM((rows, STEP), jnp.bfloat16)]
+        + ([pltpu.VMEM((rows, cols), jnp.float32)] if split else []),
+    )
+
+
+def add_parts(chain, parts):
+    rows, cols = parts[0].shape
+    half = rows // 2
+
+    def body(*refs):
+        value = sum(ref[...].astype(jnp.float32) for ref in refs[:-2]).astype(jnp.bfloat16)
+        refs[-2][...] = value[:half]
+        refs[-1][...] = value[half:]
+
+    return chain.call(
+        body,
+        parts,
+        [pl.BlockSpec((rows, cols), lambda k: (0, 0))] * len(parts),
+        [pl.BlockSpec((half, cols), lambda k: (0, 0))] * 2,
+        [jax.ShapeDtypeStruct((half, cols), jnp.bfloat16)] * 2,
+        "add_parts",
+        grid=(1,),
+    )
+
+
+def encode_blocks(value, store, scales, first):
+    lanes = lax.broadcasted_iota(jnp.int32, scales.shape, 1)
+    for n in range(value.shape[1] // BLOCK):
+        block = value[:, n * BLOCK : (n + 1) * BLOCK].astype(jnp.float32)
+        scale = (jnp.max(jnp.abs(block), axis=1, keepdims=True) + EPSILON).astype(jnp.bfloat16)
+        scale = scale.astype(jnp.float32)
+        store(n, (block / scale).astype(jnp.bfloat16))
+        scales = jnp.where(lanes == first + n, scale, scales)
+    return scales
+
+
+def encode_near(chain, own, beside, place, rows, batch):
+    cols = own.shape[1]
+    blocks = cols // BLOCK
+
+    def body(place_ref, own_ref, beside_ref, code_ref, scale_ref):
+        j = pl.program_id(0)
+
+        def store(n, codes):
+            code_ref[:, n * BLOCK : (n + 1) * BLOCK] = codes
+
+        first = (place_ref[0] ^ j) * blocks
+
+        @pl.when(j == 0)
+        def _():
+            scales = jnp.zeros(scale_ref.shape, jnp.float32)
+            scale_ref[...] = encode_blocks(own_ref[...], store, scales, first).astype(jnp.bfloat16)
+
+        @pl.when(j == 1)
+        def _():
+            scales = scale_ref[...].astype(jnp.float32)
+            scale_ref[...] = encode_blocks(beside_ref[...], store, scales, first).astype(jnp.bfloat16)
+
+    return chain.call(
+        body,
+        [place, own, beside],
+        [
+            pl.BlockSpec(memory_space=pltpu.SMEM),
+            pl.BlockSpec((rows, cols), lambda j: (0, 0)),
+            pl.BlockSpec((rows, cols), lambda j: (1, 0)),
+        ],
+        [
+            pl.BlockSpec((rows, cols), lambda j: (0, lax.axis_index("batch") ^ j)),
+            pl.BlockSpec((rows, batch * blocks), lambda j: (0, 0)),
+        ],
+        [
+            jax.ShapeDtypeStruct((rows, batch * cols), jnp.bfloat16),
+            jax.ShapeDtypeStruct((rows, batch * blocks), jnp.bfloat16),
+        ],
+        "encode_near",
+        grid=(2,),
+    )
+
+
+def encode_far(chain, codes, scales, shares, place, spot, start):
+    _, rows, part = shares[0].shape
+    tp = len(shares)
+    blocks = part // BLOCK
+    width = scales.shape[1]
+
+    def body(place_ref, spot_ref, codes_in, scales_in, *refs):
+        share_refs, (code_ref, scale_ref) = refs[:tp], refs[tp:]
+        j = pl.program_id(0)
+
+        @pl.when(j == 0)
+        def _():
+            scale_ref[...] = scales_in[...]
+
+        total = scale_ref[...].astype(jnp.float32)
+        for o in range(tp):
+            t = lax.rem(spot_ref[0] + tp - o, tp)
+
+            def store(n, value, t=t):
+                code_ref[:, pl.ds(pl.multiple_of((t * blocks + n) * BLOCK, BLOCK), BLOCK)] = value
+
+            first = ((place_ref[0] ^ (j + 2)) * tp + t) * blocks
+            total = encode_blocks(share_refs[o][...], store, total, first)
+        scale_ref[...] = total.astype(jnp.bfloat16)
+
+    smem = pl.BlockSpec(memory_space=pltpu.SMEM)
+    group = pl.BlockSpec((rows, width), lambda j: (start // rows, 0))
+    return chain.call(
+        body,
+        [place, spot, codes, scales, *shares],
+        [smem, smem, ANY, group] + [pl.BlockSpec((None, rows, part), lambda j: (j, 0, 0))] * tp,
+        [
+            pl.BlockSpec((rows, tp * part), lambda j: (start // rows, lax.axis_index("batch") ^ (j + 2))),
+            group,
+        ],
+        [
+            jax.ShapeDtypeStruct(codes.shape, codes.dtype),
+            jax.ShapeDtypeStruct(scales.shape, scales.dtype),
+        ],
+        "encode_far",
+        grid=(2,),
+        aliases={2: 0, 3: 1},
+    )
+
+
+def paired_shards(gate_input, up_input, down_weight):
+    rows = gate_input.shape[0]
+    tp, batch = lax.axis_size("tp"), lax.axis_size("batch")
+    place = lax.axis_index("batch").astype(jnp.int32).reshape(1)
+    spot = lax.axis_index("tp").astype(jnp.int32).reshape(1)
+    zero = jnp.zeros(1, jnp.int32)
+    quarter = rows // sum(GROUPS)
+    cuts = [sum(GROUPS[:g]) * quarter for g in range(len(GROUPS) + 1)]
+    firsts = [sum(CHUNKS[:c]) for c in range(len(CHUNKS))]
+    n_chunks = len(CHUNKS)
+    chain = Chain()
+
+    def swap(value, flip):
+        return lax.ppermute(value, "batch", [(b, b ^ flip) for b in range(batch)])
+
+    def shift(value, o):
+        return lax.ppermute(value, "tp", [(t, (t + o) % tp) for t in range(tp)])
+
+    hidden, beside, pieces, got = [], [], [[] for _ in GROUPS], []
+    for first, steps in zip(firsts, CHUNKS):
+        whole, *parts = activate(chain, gate_input, up_input, first, steps, cuts)
+        for group, part in zip(pieces, parts):
+            group.append(part)
+        hidden.append(whole)
+        beside.append(swap(whole, 1))
+    queue = [piece for group in pieces for piece in group]
+    for _ in range(3):
+        got.append(swap(queue.pop(0), 2))
+
+    def arrive(i):
+        got[i] = chain.pin(got[i])
+        if queue:
+            got.append(swap(chain.pin(queue.pop(0)), 2))
+        got[i] = [got[i], swap(got[i], 1)]
+
+    def spread(parts):
+        parts = [parts[0]] + [shift(parts[o], o) for o in range(1, tp)]
+
+        def home():
+            ahead, behind = add_parts(chain, parts)
+            ahead, behind = swap(ahead, 2), swap(behind, 3)
+
+            def everywhere():
+                both = chain.pin(jnp.stack([ahead, behind]))
+                return [both] + [shift(both, o) for o in range(1, tp)]
+
+            return everywhere
+
+        return home
+
+    near = None
+    for c in range(0, n_chunks, 2):
+        last = c + 2 >= n_chunks
+        near = multiply(
+            chain,
+            [[hidden[i], beside[i]] for i in (c, c + 1)],
+            down_weight,
+            firsts[c],
+            near,
+            zero,
+            1 if last else 0,
+        )[0]
+        arrive(c // 2)
+    near = lax.psum(near, "tp")
+
+    def far_product(group, c, total):
+        last = c == n_chunks - 1
+        pieces = got[group * n_chunks + c]
+        outs = multiply(
+            chain, [pieces], down_weight, firsts[c], total, spot, tp if last else 0
+        )
+        return outs if last else outs[0]
+
+    total = None
+    for c in range(n_chunks):
+        total = far_product(0, c, total)
+        if c + 2 < len(got):
+            arrive(c + 2)
+    home_0 = spread(total)
+    total = far_product(1, 0, None)
+    arrive(n_chunks + 2)
+    total = far_product(1, 1, total)
+    all_0 = home_0()
+    arrive(n_chunks + 3)
+    total = far_product(1, 2, total)
+    shares_0 = all_0()
+    near = chain.pin(near)
+    near_beside = swap(near, 1)
+    total = far_product(1, 3, total)
+    home_1 = spread(total)
+    codes, scales = encode_near(chain, near, near_beside, place, rows, batch)
+    all_1 = home_1()
+    codes, scales = encode_far(chain, codes, scales, shares_0, place, spot, cuts[0])
+    shares_1 = all_1()
+    codes, scales = encode_far(chain, codes, scales, shares_1, place, spot, cuts[1])
+    return codes, scales
+
+
 def solution(mesh):
+    def shards(gate_input, up_input, down_weight):
+        tp, batch = mesh.shape["tp"], mesh.shape["batch"]
+        width, cols = down_weight.shape
+        paired = batch == 4 and cols % (tp * TILE) == 0 and width == sum(CHUNKS) * STEP
+        return (paired_shards if paired else general_shards)(gate_input, up_input, down_weight)
+
     in_specs = (P(("groups", "batch"), "tp"), P(("groups", "batch"), "tp"), P("tp", "batch"))
     out_specs = (P(("groups", "batch"), None), P(("groups", "batch"), None))
     return jax.shard_map(shards, mesh=mesh, in_specs=in_specs, out_specs=out_specs, check_vma=False)

time: 290 us -> 194 us (0.67)
  waiting for transfers between devices: 156 us -> 24 us
  Pallas kernels: 0 us -> 99.6 us
  starting transfers between devices: 9.73 us -> 46.5 us
  matrix products: 34.8 us -> 0 us
  blocking collectives: 30.7 us -> 0 us
  local copies, waits for them, and re-layouts: 27.5 us -> 8.86 us
  other arithmetic: 17 us -> 0.03 us
    all_gather x2 -> x0, waiting for transfers between devices: 115 us -> none  [the longest x1 90.9 us: shards(): lax.all_gather(hidden, 'batch', axis=0, tiled=True)]
    pallas_call x0 -> x35, Pallas kernels: none -> 99.6 us  [call(): pl.pallas_call(with_tokens, grid=grid, in_specs=list(in_specs) + [ANY] *...]
    ppermute x0 -> x37, starting transfers between devices: none -> 46.4 us  [the longest x12 30.2 us: shift(): return lax.ppermute(value, 'tp', [(t, (t + o) % tp) for t in range(tp)])]
    all_to_all x2 -> x0, waiting for transfers between devices: 40.4 us -> none  [the longest x1 40.4 us: shards(): lax.all_to_all(part_codes.reshape(batch_count, tp_count, row_share, local...]
    dot_general x1 -> x0, matrix products: 34.8 us -> none  [shards(): jnp.dot(lax.all_gather(hidden, 'batch', axis=0, tiled=True), down_weight,...]
    ppermute x0 -> x37, waiting for transfers between devices: none -> 24 us  [the longest x12 18.7 us: shift(): return lax.ppermute(value, 'tp', [(t, (t + o) % tp) for t in range(tp)])]
    all_to_all x2 -> x0, blocking collectives: 17.4 us -> none  [the longest x1 11.2 us: shards(): lax.all_to_all(new_codes, 'batch', split_axis=0, concat_axis=2, tiled=True)]
    all_gather x1 -> x0, blocking collectives: 13.3 us -> none  [shards(): lax.all_gather(home_scales, 'tp', axis=1, tiled=True)]
  transfers between devices with their start and end apart: 4 -> 38, of which waited for: 3 -> 9; matrix products, arithmetic and copies ran while one was open for 8% -> 0% of each run, Pallas kernels for 0% -> 50%
where the time goes in v2:
time: 194 us; the launch traced here: 193 us
  Pallas kernels  99.6 us (51%)
  starting transfers between devices  46.5 us (24%)
  waiting for transfers between devices  24 us (12%)
  between operations  14.4 us (7%)
  local copies, waits for them, and re-layouts  8.86 us (5%)
    pallas_call x35, Pallas kernels, call(): pl.pallas_call(with_tokens, grid=grid, in_specs=list(in_specs) + [ANY] *...  99.6 us
    ppermute x12, starting transfers between devices, shift(): return lax.ppermute(value, 'tp', [(t, (t + o) % tp) for t in range(tp)])  30.2 us
    ppermute x12, waiting for transfers between devices, shift(): return lax.ppermute(value, 'tp', [(t, (t + o) % tp) for t in range(tp)])  18.7 us
    ppermute x25, starting transfers between devices, swap(): return lax.ppermute(value, 'batch', [(b, b ^ flip) for b in range(batch)])  16.2 us
    unnamed x27, local copies, waits for them, and re-layouts  8.86 us
    ppermute x25, waiting for transfers between devices, swap(): return lax.ppermute(value, 'batch', [(b, b ^ flip) for b in range(batch)])  5.29 us
  transfers between devices with their start and end apart: 38, of which 9 were waited for; matrix products, arithmetic and copies ran while one was open for 0% of the time, Pallas kernels for 50%

profile of v2, /device:TPU:0, one launch (start us, length us, event | category | flops | bytes accessed | tf_op | source)
XLA Modules:
  0.0 193.4 jit_solution(14125827225472712460)
XLA Ops:
  7.2 2.8 %activate.4 = (bf16[128,4096]{1,0:T(8,128)(2,1)S(1)}, bf16[96,4096]{1,0:T(8,128)(2,1)S(1)}, bf16[32,4096]{1,0:T(8,128)(2,1)S(1)}, f32[8,128]{1,0:T(8,128)S(1)}) custom-call(bf16[128,13312]{1,0:T(8,128)(2,1)} %refs_0_.7, bf16[128,13312]{1,0:T(8,128)(2,1)} %refs_1_.7), custom_call_target="tpu_custom_call" | custom-call | flops 1024 | bytes 1024 | tf_op jit(solution)/shard_map/activate/pallas_call | solution.py:105
  10.0 0.7 copy-done.3
  11.1 2.5 %activate.5 = (bf16[128,3072]{1,0:T(8,128)(2,1)S(1)}, bf16[96,3072]{1,0:T(8,128)(2,1)S(1)}, bf16[32,3072]{1,0:T(8,128)(2,1)S(1)}, f32[8,128]{1,0:T(8,128)S(1)}) custom-call(bf16[128,13312]{1,0:T(8,128)(2,1)} %refs_0_.7, bf16[128,13312]{1,0:T(8,128)(2,1)} %refs_1_.7, f32[8,128]{1,0:T(8,128)S(1)} %get-tuple-element.90.refs_2_), custom_call_target="tpu_custom_call" | custom-call | flops 1024 | bytes 1024 | tf_op jit(solution)/shard_map/activate/pallas_call | solution.py:105
  13.6 0.7 copy-done.9
  14.4 2.9 %collective-permute-start.4 = (bf16[96,4096]{1,0:T(8,128)(2,1)S(1)}, bf16[96,4096]{1,0:T(8,128)(2,1)S(1)}, u32[]{:S(2)}, u32[]{:S(2)}) collective-permute-start(bf16[96,4096]{1,0:T(8,128)(2,1)S(1)} %get-tuple-element.100), channel_id=1, source_target_pairs={{0,2},{1,3},{2,0},{3,1},{4,6},{5,7},{6,4},{7,5},{8,10},{9,11},{10,... | collective-permute-start | bytes 2359304 | tf_op jit(solution)/shard_map/ppermute | solution.py:354
  17.3 3.3 %activate.6 = (bf16[128,3072]{1,0:T(8,128)(2,1)S(1)}, bf16[96,3072]{1,0:T(8,128)(2,1)}, bf16[32,3072]{1,0:T(8,128)(2,1)S(1)}, f32[8,128]{1,0:T(8,128)S(1)}) custom-call(bf16[128,13312]{1,0:T(8,128)(2,1)} %refs_0_.7, bf16[128,13312]{1,0:T(8,128)(2,1)} %refs_1_.7, f32[8,128]{1,0:T(8,128)S(1)} %get-tuple-element.91.refs_2_), custom_call_target="tpu_custom_call" | custom-call | flops 1024 | bytes 1024 | tf_op jit(solution)/shard_map/activate/pallas_call | solution.py:105
  20.6 3.3 %activate.7 = (bf16[128,3072]{1,0:T(8,128)(2,1)S(1)}, bf16[96,3072]{1,0:T(8,128)(2,1)}, bf16[32,3072]{1,0:T(8,128)(2,1)S(1)}, f32[8,128]{1,0:T(8,128)S(1)}) custom-call(bf16[128,13312]{1,0:T(8,128)(2,1)} %refs_0_.7, bf16[128,13312]{1,0:T(8,128)(2,1)} %refs_1_.7, f32[8,128]{1,0:T(8,128)S(1)} %get-tuple-element.93.refs_2_), custom_call_target="tpu_custom_call" | custom-call | flops 1024 | bytes 1024 | tf_op jit(solution)/shard_map/activate/pallas_call | solution.py:105
  24.5 14.5 %multiply.10 = (f32[256,2048]{1,0:T(8,128)S(1)}, f32[8,128]{1,0:T(8,128)S(1)}) custom-call(s32[1]{0:T(128)} %constant.8.clone.1.refs_0_, bf16[128,4096]{1,0:T(8,128)(2,1)S(1)} %get-tuple-element.95.refs_1_, bf16[128,4096]{1,0:T(8,128)(2,1)S(1)} %collective-permute-done.2.refs_2_, bf16[128,3072]{1,0:T(8,128)(2,1)S(1)} %get-tuple-element.96.refs_3_, ...), custom_call_target="tpu_custom_call" | custom-call | flops 1024 | bytes 1024 | tf_op jit(solution)/shard_map/multiply/pallas_call | solution.py:105
  39.2 2.0 %collective-permute-start.9 = (bf16[96,3072]{1,0:T(8,128)(2,1)}, bf16[96,3072]{1,0:T(8,128)(2,1)S(1)}, u32[]{:S(2)}, u32[]{:S(2)}) collective-permute-start(bf16[96,3072]{1,0:T(8,128)(2,1)} %get-tuple-element.115), channel_id=1, source_target_pairs={{0,2},{1,3},{2,0},{3,1},{4,6},{5,7},{6,4},{7,5},{8,10},{9,11},{10,... | collective-permute-start | bytes 1769480 | tf_op jit(solution)/shard_map/ppermute | solution.py:354
  41.2 12.7 %multiply.11 = (bf16[256,2048]{1,0:T(8,128)(2,1)S(1)}, f32[8,128]{1,0:T(8,128)S(1)}) custom-call(s32[1]{0:T(128)} %constant.8.clone.1.refs_0_, bf16[128,3072]{1,0:T(8,128)(2,1)S(1)} %get-tuple-element.92.refs_1_, bf16[128,3072]{1,0:T(8,128)(2,1)S(1)} %collective-permute-done.refs_2_, bf16[128,3072]{1,0:T(8,128)(2,1)S(1)} %get-tuple-element.94.refs_3_, ...), custom_call_target="tpu_custom_call" | custom-call | flops 1024 | bytes 1024 | tf_op jit(solution)/shard_map/multiply/pallas_call | solution.py:105
  53.9 1.0 copy-done.2
  55.3 0.9 copy-done.4
  56.2 0.7 copy-done.5
  56.9 8.1 %multiply.12 = (f32[192,2048]{1,0:T(8,128)S(1)}, f32[8,128]{1,0:T(8,128)S(1)}) custom-call(s32[1]{0:T(128)} %bitcast.1.refs_0_.refs_1_, bf16[96,4096]{1,0:T(8,128)(2,1)S(1)} %get-tuple-element.109.refs_1_, bf16[96,4096]{1,0:T(8,128)(2,1)S(1)} %collective-permute-done.8.refs_2_, bf16[13312,2048]{1,0:T(8,128)(2,1)} %refs_6_.19, bf16[13312,2048]{1,0:T(8,128)(2,1)} %refs_6_.19, ...), custom_call_target="tpu_custom_call" | custom-call | flops 1024 | bytes 1024 | tf_op jit(solution)/shard_map/multiply/pallas_call | solution.py:105
  65.1 1.1 copy-done
  66.3 0.9 copy-done.10
  67.2 0.7 copy-done.11
  67.9 1.4 copy-done.1
  69.3 6.9 %multiply.13 = (f32[192,2048]{1,0:T(8,128)S(1)}, f32[8,128]{1,0:T(8,128)S(1)}) custom-call(s32[1]{0:T(128)} %bitcast.1.refs_0_.refs_1_, bf16[96,3072]{1,0:T(8,128)(2,1)S(1)} %get-tuple-element.108.refs_1_, bf16[96,3072]{1,0:T(8,128)(2,1)} %collective-permute-done.7.refs_2_, bf16[13312,2048]{1,0:T(8,128)(2,1)} %refs_6_.19, bf16[13312,2048]{1,0:T(8,128)(2,1)} %refs_6_.19, ...), custom_call_target="tpu_custom_call" | custom-call | flops 1024 | bytes 1024 | tf_op jit(solution)/shard_map/multiply/pallas_call | solution.py:105
  76.8 1.7 collective-permute-start.12
  78.8 1.7 collective-permute-start.19
  80.5 6.7 %multiply.14 = (f32[192,2048]{1,0:T(8,128)S(1)}, f32[8,128]{1,0:T(8,128)S(1)}) custom-call(s32[1]{0:T(128)} %bitcast.1.refs_0_.refs_1_, bf16[96,3072]{1,0:T(8,128)(2,1)S(1)} %get-tuple-element.121.refs_1_, bf16[96,3072]{1,0:T(8,128)(2,1)S(1)} %collective-permute-done.11.refs_2_, bf16[13312,2048]{1,0:T(8,128)(2,1)} %refs_6_.19, bf16[13312,2048]{1,0:T(8,128)(2,1)} %refs_6_.19, ...), custom_call_target="tpu_custom_call" | custom-call | flops 1024 | bytes 1024 | tf_op jit(solution)/shard_map/multiply/pallas_call | solution.py:105
  87.4 6.8 %multiply.15 = (bf16[192,512]{1,0:T(8,128)(2,1)S(1)}, bf16[192,512]{1,0:T(8,128)(2,1)S(1)}, bf16[192,512]{1,0:T(8,128)(2,1)S(1)}, bf16[192,512]{1,0:T(8,128)(2,1)S(1)}, f32[8,128]{1,0:T(8,128)S(1)}) custom-call(s32[1]{0:T(128)} %bitcast.1.refs_0_.refs_1_, bf16[96,3072]{1,0:T(8,128)(2,1)S(1)} %get-tuple-element.120.refs_1_, ...), custom_call_target="tpu_custom_call" | custom-call | flops 1024 | bytes 1024 | tf_op jit(solution)/shard_map/multiply/pallas_call | solution.py:105
  94.8 1.6 collective-permute-start.13
  96.4 2.5 %collective-permute-start.14 = (bf16[192,512]{1,0:T(8,128)(2,1)S(1)}, bf16[192,512]{1,0:T(8,128)(2,1)S(1)}, u32[]{:S(2)}, u32[]{:S(2)}) collective-permute-start(bf16[192,512]{1,0:T(8,128)(2,1)S(1)} %get-tuple-element.134), channel_id=1, source_target_pairs={{0,8},{4,12},{8,0},{12,4},{1,9},{5,13},{9,1},{13,5},{2,10},{6,14},... | collective-permute-start | bytes 589832 | tf_op jit(solution)/shard_map/ppermute | solution.py:357
  98.9 1.4 collective-permute-start.15
  100.8 7.7 %multiply.16 = (f32[64,2048]{1,0:T(8,128)S(1)}, f32[8,128]{1,0:T(8,128)S(1)}) custom-call(s32[1]{0:T(128)} %bitcast.1.refs_0_.refs_1_, bf16[32,4096]{1,0:T(8,128)(2,1)S(1)} %get-tuple-element.139.refs_1_, bf16[32,4096]{1,0:T(8,128)(2,1)S(1)} %collective-permute-done.18.refs_2_, bf16[13312,2048]{1,0:T(8,128)(2,1)} %refs_6_.19, bf16[13312,2048]{1,0:T(8,128)(2,1)} %refs_6_.19, ...), custom_call_target="tpu_custom_call" | custom-call | flops 1024 | bytes 1024 | tf_op jit(solution)/shard_map/multiply/pallas_call | solution.py:105
  108.6 6.3 %multiply.17 = (f32[64,2048]{1,0:T(8,128)S(1)}, f32[8,128]{1,0:T(8,128)S(1)}) custom-call(s32[1]{0:T(128)} %bitcast.1.refs_0_.refs_1_, bf16[32,3072]{1,0:T(8,128)(2,1)S(1)} %get-tuple-element.138.refs_1_, bf16[32,3072]{1,0:T(8,128)(2,1)S(1)} %collective-permute-done.17.refs_2_, bf16[13312,2048]{1,0:T(8,128)(2,1)} %refs_6_.19, bf16[13312,2048]{1,0:T(8,128)(2,1)} %refs_6_.19, ...), custom_call_target="tpu_custom_call" | custom-call | flops 1024 | bytes 1024 | tf_op jit(solution)/shard_map/multiply/pallas_call | solution.py:105
  114.9 6.2 %collective-permute-done.14.refs_2_ = bf16[192,512]{1,0:T(8,128)(2,1)S(1)} collective-permute-done((bf16[192,512]{1,0:T(8,128)(2,1)S(1)}, bf16[192,512]{1,0:T(8,128)(2,1)S(1)}, u32[]{:S(2)}, u32[]{:S(2)}) %collective-permute-start.14) | collective-permute-done | bytes 196640 | tf_op jit(solution)/shard_map/ppermute | solution.py:357
  121.8 1.7 collective-permute-start.22
  123.5 3.0 %collective-permute-done.20 = bf16[96,512]{1,0:T(8,128)(2,1)S(1)} collective-permute-done((bf16[96,512]{1,0:T(8,128)(2,1)S(1)}, bf16[96,512]{1,0:T(8,128)(2,1)S(1)}, u32[]{:S(2)}, u32[]{:S(2)}) %collective-permute-start.20) | collective-permute-done | bytes 98336 | tf_op jit(solution)/shard_map/ppermute | solution.py:354
  126.5 6.3 %multiply.18 = (f32[64,2048]{1,0:T(8,128)S(1)}, f32[8,128]{1,0:T(8,128)S(1)}) custom-call(s32[1]{0:T(128)} %bitcast.1.refs_0_.refs_1_, bf16[32,3072]{1,0:T(8,128)(2,1)S(1)} %get-tuple-element.148.refs_1_, bf16[32,3072]{1,0:T(8,128)(2,1)S(1)} %collective-permute-done.22.refs_2_, bf16[13312,2048]{1,0:T(8,128)(2,1)} %refs_6_.19, bf16[13312,2048]{1,0:T(8,128)(2,1)} %refs_6_.19, ...), custom_call_target="tpu_custom_call" | custom-call | flops 1024 | bytes 1024 | tf_op jit(solution)/shard_map/multiply/pallas_call | solution.py:105
  132.9 1.3 collective-permute-start.24
  134.3 11.8 %collective-permute-start.26 = (bf16[2,96,512]{2,1,0:T(8,128)(2,1)S(1)}, bf16[2,96,512]{2,1,0:T(8,128)(2,1)S(1)}, u32[]{:S(2)}, u32[]{:S(2)}) collective-permute-start(bf16[2,96,512]{2,1,0:T(8,128)(2,1)S(1)} %get-tuple-element.162.refs_4_), channel_id=1, source_target_pairs={{0,4},{4,8},{8,12},{12,0},{1,5},{5,9},{9,13},{13,1},{2,6},{6,10},{... | collective-permute-start | bytes 589832 | tf_op jit(solution)/shard_map/ppermute | solution.py:357
  146.1 2.4 %collective-permute-start.28 = (bf16[2,96,512]{2,1,0:T(8,128)(2,1)S(1)}, bf16[2,96,512]{2,1,0:T(8,128)(2,1)S(1)}, u32[]{:S(2)}, u32[]{:S(2)}) collective-permute-start(bf16[2,96,512]{2,1,0:T(8,128)(2,1)S(1)} %get-tuple-element.162.refs_4_), channel_id=1, source_target_pairs={{0,12},{4,0},{8,4},{12,8},{1,13},{5,1},{9,5},{13,9},{2,14},{6,2},{... | collective-permute-start | bytes 589832 | tf_op jit(solution)/shard_map/ppermute | solution.py:357
  148.5 6.3 %multiply.19 = (bf16[64,512]{1,0:T(8,128)(2,1)S(1)}, bf16[64,512]{1,0:T(8,128)(2,1)S(1)}, bf16[64,512]{1,0:T(8,128)(2,1)S(1)}, bf16[64,512]{1,0:T(8,128)(2,1)S(1)}, f32[8,128]{1,0:T(8,128)S(1)}) custom-call(s32[1]{0:T(128)} %bitcast.1.refs_0_.refs_1_, bf16[32,3072]{1,0:T(8,128)(2,1)S(1)} %get-tuple-element.156.refs_1_, ...), custom_call_target="tpu_custom_call" | custom-call | flops 1024 | bytes 1024 | tf_op jit(solution)/shard_map/multiply/pallas_call | solution.py:105
  154.9 6.1 %collective-permute-done.29.refs_1_ = bf16[64,512]{1,0:T(8,128)(2,1)S(1)} collective-permute-done((bf16[64,512]{1,0:T(8,128)(2,1)S(1)}, bf16[64,512]{1,0:T(8,128)(2,1)S(1)}, u32[]{:S(2)}, u32[]{:S(2)}) %collective-permute-start.29) | collective-permute-done | bytes 65568 | tf_op jit(solution)/shard_map/ppermute | solution.py:357
  161.0 6.2 %collective-permute-start.30 = (bf16[64,512]{1,0:T(8,128)(2,1)S(1)}, bf16[64,512]{1,0:T(8,128)(2,1)S(1)}, u32[]{:S(2)}, u32[]{:S(2)}) collective-permute-start(bf16[64,512]{1,0:T(8,128)(2,1)S(1)} %get-tuple-element.165), channel_id=1, source_target_pairs={{0,8},{4,12},{8,0},{12,4},{1,9},{5,13},{9,1},{13,5},{2,10},{6,14},... | collective-permute-start | bytes 196616 | tf_op jit(solution)/shard_map/ppermute | solution.py:357
  167.6 2.7 %encode_near.1 = (bf16[128,8192]{1,0:T(8,128)(2,1)}, bf16[128,64]{1,0:T(8,128)(2,1)S(1)}, f32[8,128]{1,0:T(8,128)S(1)}) custom-call(s32[1]{0:T(128)} %bitcast.refs_0_, bf16[256,2048]{1,0:T(8,128)(2,1)} %get-tuple-element.155.refs_1_, bf16[256,2048]{1,0:T(8,128)(2,1)S(1)} %collective-permute-done.24.refs_2_, f32[8,128]{1,0:T(8,128)S(1)} %get-tuple-element.159.refs_3_), custom_call_target="tpu_custom_call" | custom-call | flops 1024 | bytes 1024 | tf_op jit(solution)/shard_map/encode_near/pallas_call | solution.py:105
  170.2 0.7 collective-permute-done.30.refs_2_
  172.2 1.4 encode_far.2
  173.6 2.2 %collective-permute-done.32 = bf16[32,512]{1,0:T(8,128)(2,1)S(1)} collective-permute-done((bf16[32,512]{1,0:T(8,128)(2,1)S(1)}, bf16[32,512]{1,0:T(8,128)(2,1)S(1)}, u32[]{:S(2)}, u32[]{:S(2)}) %collective-permute-start.32) | collective-permute-done | bytes 32800 | tf_op jit(solution)/shard_map/ppermute | solution.py:354
  175.8 0.9 collective-permute-start.34
  176.7 2.8 %collective-permute-start.35 = (bf16[2,32,512]{2,1,0:T(8,128)(2,1)S(1)}, bf16[2,32,512]{2,1,0:T(8,128)(2,1)S(1)}, u32[]{:S(2)}, u32[]{:S(2)}) collective-permute-start(bf16[2,32,512]{2,1,0:T(8,128)(2,1)S(1)} %get-tuple-element.174.refs_4_), channel_id=1, source_target_pairs={{0,8},{4,12},{8,0},{12,4},{1,9},{5,13},{9,1},{13,5},{2,10},{6,14},... | collective-permute-start | bytes 196616 | tf_op jit(solution)/shard_map/ppermute | solution.py:357
  179.7 3.0 %collective-permute-done.34.refs_5_ = bf16[2,32,512]{2,1,0:T(8,128)(2,1)S(1)} collective-permute-done((bf16[2,32,512]{2,1,0:T(8,128)(2,1)S(1)}, bf16[2,32,512]{2,1,0:T(8,128)(2,1)S(1)}, u32[]{:S(2)}, u32[]{:S(2)}) %collective-permute-start.34) | collective-permute-done | bytes 65568 | tf_op jit(solution)/shard_map/ppermute | solution.py:357
  182.8 2.0 %collective-permute-done.35.refs_6_ = bf16[2,32,512]{2,1,0:T(8,128)(2,1)S(1)} collective-permute-done((bf16[2,32,512]{2,1,0:T(8,128)(2,1)S(1)}, bf16[2,32,512]{2,1,0:T(8,128)(2,1)S(1)}, u32[]{:S(2)}, u32[]{:S(2)}) %collective-permute-start.35) | collective-permute-done | bytes 65568 | tf_op jit(solution)/shard_map/ppermute | solution.py:357
  184.9 1.0 encode_far.3
  185.8 0.7 copy.25
  (93 shorter events, 6.5 us)
Async XLA Ops:
  7.2 125.7 %all-reduce.2.cloned.1.call-start = ((), (), s32[]{:S(2)}) async-start(), calls=%async_computation | async-start | bytes 2097152 | tf_op jit(solution)/shard_map/psum | solution.py:404
  10.0 0.7 copy-start.3
  10.7 13.8 %collective-permute-start.2 = (bf16[128,4096]{1,0:T(8,128)(2,1)S(1)}, bf16[128,4096]{1,0:T(8,128)(2,1)S(1)}, u32[]{:S(2)}, u32[]{:S(2)}) collective-permute-start(bf16[128,4096]{1,0:T(8,128)(2,1)S(1)} %get-tuple-element.95.refs_1_), channel_id=1, source_target_pairs={{0,1},{1,0},{2,3},{3,2},{4,5},{5,4},{6,7},{7,6},{8,9},{9,8},{10,11... | collective-permute-start | bytes 3145736 | tf_op jit(solution)/shard_map/ppermute | solution.py:354
  14.3 10.1 %collective-permute-start.3 = (bf16[128,3072]{1,0:T(8,128)(2,1)S(1)}, bf16[128,3072]{1,0:T(8,128)(2,1)S(1)}, u32[]{:S(2)}, u32[]{:S(2)}) collective-permute-start(bf16[128,3072]{1,0:T(8,128)(2,1)S(1)} %get-tuple-element.96.refs_3_), channel_id=1, source_target_pairs={{0,1},{1,0},{2,3},{3,2},{4,5},{5,4},{6,7},{7,6},{8,9},{9,8},{10,11... | collective-permute-start | bytes 2359304 | tf_op jit(solution)/shard_map/ppermute | solution.py:354
  14.4 24.6 %collective-permute-start.4 = (bf16[96,4096]{1,0:T(8,128)(2,1)S(1)}, bf16[96,4096]{1,0:T(8,128)(2,1)S(1)}, u32[]{:S(2)}, u32[]{:S(2)}) collective-permute-start(bf16[96,4096]{1,0:T(8,128)(2,1)S(1)} %get-tuple-element.100), channel_id=1, source_target_pairs={{0,2},{1,3},{2,0},{3,1},{4,6},{5,7},{6,4},{7,5},{8,10},{9,11},{10,... | collective-permute-start | bytes 2359304 | tf_op jit(solution)/shard_map/ppermute | solution.py:354
  20.6 3.3 %copy-start.7 = (bf16[32,3072]{1,0:T(8,128)(2,1)}, bf16[32,3072]{1,0:T(8,128)(2,1)S(1)}, u32[]{:S(2)}) copy-start(bf16[32,3072]{1,0:T(8,128)(2,1)S(1)} %get-tuple-element.123.refs_0_) | copy-start | bytes 589828
  23.9 17.2 %collective-permute-start.1 = (bf16[128,3072]{1,0:T(8,128)(2,1)S(1)}, bf16[128,3072]{1,0:T(8,128)(2,1)S(1)}, u32[]{:S(2)}, u32[]{:S(2)}) collective-permute-start(bf16[128,3072]{1,0:T(8,128)(2,1)S(1)} %get-tuple-element.94.refs_3_), channel_id=1, source_target_pairs={{0,1},{1,0},{2,3},{3,2},{4,5},{5,4},{6,7},{7,6},{8,9},{9,8},{10,11... | collective-permute-start | bytes 2359304 | tf_op jit(solution)/shard_map/ppermute | solution.py:354
  24.0 17.2 %collective-permute-start = (bf16[128,3072]{1,0:T(8,128)(2,1)S(1)}, bf16[128,3072]{1,0:T(8,128)(2,1)S(1)}, u32[]{:S(2)}, u32[]{:S(2)}) collective-permute-start(bf16[128,3072]{1,0:T(8,128)(2,1)S(1)} %get-tuple-element.92.refs_1_), channel_id=1, source_target_pairs={{0,1},{1,0},{2,3},{3,2},{4,5},{5,4},{6,7},{7,6},{8,9},{9,8},{10,11... | collective-permute-start | bytes 2359304 | tf_op jit(solution)/shard_map/ppermute | solution.py:354
  24.5 30.4 %collective-permute-start.6 = (bf16[96,3072]{1,0:T(8,128)(2,1)S(1)}, bf16[96,3072]{1,0:T(8,128)(2,1)S(1)}, u32[]{:S(2)}, u32[]{:S(2)}) collective-permute-start(bf16[96,3072]{1,0:T(8,128)(2,1)S(1)} %get-tuple-element.106), channel_id=1, source_target_pairs={{0,2},{1,3},{2,0},{3,1},{4,6},{5,7},{6,4},{7,5},{8,10},{9,11},{10,... | collective-permute-start | bytes 1769480 | tf_op jit(solution)/shard_map/ppermute | solution.py:354
  39.0 17.9 %collective-permute-start.8 = (bf16[96,4096]{1,0:T(8,128)(2,1)S(1)}, bf16[96,4096]{1,0:T(8,128)(2,1)S(1)}, u32[]{:S(2)}, u32[]{:S(2)}) collective-permute-start(bf16[96,4096]{1,0:T(8,128)(2,1)S(1)} %get-tuple-element.109.refs_1_), channel_id=1, source_target_pairs={{0,1},{1,0},{2,3},{3,2},{4,5},{5,4},{6,7},{7,6},{8,9},{9,8},{10,11... | collective-permute-start | bytes 2359304 | tf_op jit(solution)/shard_map/ppermute | solution.py:354
  39.2 27.0 %collective-permute-start.9 = (bf16[96,3072]{1,0:T(8,128)(2,1)}, bf16[96,3072]{1,0:T(8,128)(2,1)S(1)}, u32[]{:S(2)}, u32[]{:S(2)}) collective-permute-start(bf16[96,3072]{1,0:T(8,128)(2,1)} %get-tuple-element.115), channel_id=1, source_target_pairs={{0,2},{1,3},{2,0},{3,1},{4,6},{5,7},{6,4},{7,5},{8,10},{9,11},{10,... | collective-permute-start | bytes 1769480 | tf_op jit(solution)/shard_map/ppermute | solution.py:354
  53.8 1.0 copy-start.2
  54.8 13.1 %collective-permute-start.7 = (bf16[96,3072]{1,0:T(8,128)(2,1)S(1)}, bf16[96,3072]{1,0:T(8,128)(2,1)}, u32[]{:S(2)}, u32[]{:S(2)}) collective-permute-start(bf16[96,3072]{1,0:T(8,128)(2,1)S(1)} %get-tuple-element.108.refs_1_), channel_id=1, source_target_pairs={{0,1},{1,0},{2,3},{3,2},{4,5},{5,4},{6,7},{7,6},{8,9},{9,8},{10,11... | collective-permute-start | bytes 1769480 | tf_op jit(solution)/shard_map/ppermute | solution.py:354
  55.0 21.3 %collective-permute-start.5 = (bf16[96,3072]{1,0:T(8,128)(2,1)}, bf16[96,3072]{1,0:T(8,128)(2,1)S(1)}, u32[]{:S(2)}, u32[]{:S(2)}) collective-permute-start(bf16[96,3072]{1,0:T(8,128)(2,1)} %get-tuple-element.105), channel_id=1, source_target_pairs={{0,2},{1,3},{2,0},{3,1},{4,6},{5,7},{6,4},{7,5},{8,10},{9,11},{10,... | collective-permute-start | bytes 1769480 | tf_op jit(solution)/shard_map/ppermute | solution.py:354
  55.3 0.9 copy-start.4
  65.1 1.1 copy-start
  66.2 14.3 %collective-permute-start.11 = (bf16[96,3072]{1,0:T(8,128)(2,1)S(1)}, bf16[96,3072]{1,0:T(8,128)(2,1)S(1)}, u32[]{:S(2)}, u32[]{:S(2)}) collective-permute-start(bf16[96,3072]{1,0:T(8,128)(2,1)S(1)} %get-tuple-element.121.refs_1_), channel_id=1, source_target_pairs={{0,1},{1,0},{2,3},{3,2},{4,5},{5,4},{6,7},{7,6},{8,9},{9,8},{10,11... | collective-permute-start | bytes 1769480 | tf_op jit(solution)/shard_map/ppermute | solution.py:354
  66.3 0.9 copy-start.10
  67.9 1.4 copy-start.1
  69.3 7.5 %copy-start.6 = (bf16[32,4096]{1,0:T(8,128)(2,1)S(1)}, bf16[32,4096]{1,0:T(8,128)(2,1)}, u32[]{:S(2)}) copy-start(bf16[32,4096]{1,0:T(8,128)(2,1)} %copy-done.5) | copy-start | bytes 786436
  69.3 9.2 %copy-start.12 = (bf16[32,3072]{1,0:T(8,128)(2,1)S(1)}, bf16[32,3072]{1,0:T(8,128)(2,1)}, u32[]{:S(2)}) copy-start(bf16[32,3072]{1,0:T(8,128)(2,1)} %copy-done.11) | copy-start | bytes 589828
  69.3 9.5 %copy-start.8 = (bf16[32,3072]{1,0:T(8,128)(2,1)S(1)}, bf16[32,3072]{1,0:T(8,128)(2,1)}, u32[]{:S(2)}) copy-start(bf16[32,3072]{1,0:T(8,128)(2,1)} %copy-done.7) | copy-start | bytes 589828
  76.3 11.1 %collective-permute-start.10 = (bf16[96,3072]{1,0:T(8,128)(2,1)S(1)}, bf16[96,3072]{1,0:T(8,128)(2,1)S(1)}, u32[]{:S(2)}, u32[]{:S(2)}) collective-permute-start(bf16[96,3072]{1,0:T(8,128)(2,1)S(1)} %get-tuple-element.120.refs_1_), channel_id=1, source_target_pairs={{0,1},{1,0},{2,3},{3,2},{4,5},{5,4},{6,7},{7,6},{8,9},{9,8},{10,11... | collective-permute-start | bytes 1769480 | tf_op jit(solution)/shard_map/ppermute | solution.py:354
  76.8 10.5 %collective-permute-start.12 = (bf16[32,4096]{1,0:T(8,128)(2,1)S(1)}, bf16[32,4096]{1,0:T(8,128)(2,1)S(1)}, u32[]{:S(2)}, u32[]{:S(2)}) collective-permute-start(bf16[32,4096]{1,0:T(8,128)(2,1)S(1)} %copy-done.6), channel_id=1, source_target_pairs={{0,2},{1,3},{2,0},{3,1},{4,6},{5,7},{6,4},{7,5},{8,10},{9,11},{10,... | collective-permute-start | bytes 786440 | tf_op jit(solution)/shard_map/ppermute | solution.py:354
  78.5 15.7 %collective-permute-start.16 = (bf16[32,3072]{1,0:T(8,128)(2,1)S(1)}, bf16[32,3072]{1,0:T(8,128)(2,1)S(1)}, u32[]{:S(2)}, u32[]{:S(2)}) collective-permute-start(bf16[32,3072]{1,0:T(8,128)(2,1)S(1)} %copy-done.12), channel_id=1, source_target_pairs={{0,2},{1,3},{2,0},{3,1},{4,6},{5,7},{6,4},{7,5},{8,10},{9,11},{10,... | collective-permute-start | bytes 589832 | tf_op jit(solution)/shard_map/ppermute | solution.py:354
  78.8 20.1 %collective-permute-start.19 = (bf16[32,3072]{1,0:T(8,128)(2,1)S(1)}, bf16[32,3072]{1,0:T(8,128)(2,1)S(1)}, u32[]{:S(2)}, u32[]{:S(2)}) collective-permute-start(bf16[32,3072]{1,0:T(8,128)(2,1)S(1)} %get-tuple-element.142), channel_id=1, source_target_pairs={{0,2},{1,3},{2,0},{3,1},{4,6},{5,7},{6,4},{7,5},{8,10},{9,11},{10,... | collective-permute-start | bytes 589832 | tf_op jit(solution)/shard_map/ppermute | solution.py:354
  87.3 13.0 %collective-permute-start.18 = (bf16[32,4096]{1,0:T(8,128)(2,1)S(1)}, bf16[32,4096]{1,0:T(8,128)(2,1)S(1)}, u32[]{:S(2)}, u32[]{:S(2)}) collective-permute-start(bf16[32,4096]{1,0:T(8,128)(2,1)S(1)} %get-tuple-element.139.refs_1_), channel_id=1, source_target_pairs={{0,1},{1,0},{2,3},{3,2},{4,5},{5,4},{6,7},{7,6},{8,9},{9,8},{10,11... | collective-permute-start | bytes 786440 | tf_op jit(solution)/shard_map/ppermute | solution.py:354
  94.2 14.3 %collective-permute-start.17 = (bf16[32,3072]{1,0:T(8,128)(2,1)S(1)}, bf16[32,3072]{1,0:T(8,128)(2,1)S(1)}, u32[]{:S(2)}, u32[]{:S(2)}) collective-permute-start(bf16[32,3072]{1,0:T(8,128)(2,1)S(1)} %get-tuple-element.138.refs_1_), channel_id=1, source_target_pairs={{0,1},{1,0},{2,3},{3,2},{4,5},{5,4},{6,7},{7,6},{8,9},{9,8},{10,11... | collective-permute-start | bytes 589832 | tf_op jit(solution)/shard_map/ppermute | solution.py:354
  94.8 20.1 %collective-permute-start.13 = (bf16[192,512]{1,0:T(8,128)(2,1)S(1)}, bf16[192,512]{1,0:T(8,128)(2,1)S(1)}, u32[]{:S(2)}, u32[]{:S(2)}) collective-permute-start(bf16[192,512]{1,0:T(8,128)(2,1)S(1)} %get-tuple-element.133), channel_id=1, source_target_pairs={{0,4},{4,8},{8,12},{12,0},{1,5},{5,9},{9,13},{13,1},{2,6},{6,10},{... | collective-permute-start | bytes 589832 | tf_op jit(solution)/shard_map/ppermute | solution.py:357
  96.4 24.8 %collective-permute-start.14 = (bf16[192,512]{1,0:T(8,128)(2,1)S(1)}, bf16[192,512]{1,0:T(8,128)(2,1)S(1)}, u32[]{:S(2)}, u32[]{:S(2)}) collective-permute-start(bf16[192,512]{1,0:T(8,128)(2,1)S(1)} %get-tuple-element.134), channel_id=1, source_target_pairs={{0,8},{4,12},{8,0},{12,4},{1,9},{5,13},{9,1},{13,5},{2,10},{6,14},... | collective-permute-start | bytes 589832 | tf_op jit(solution)/shard_map/ppermute | solution.py:357
  98.9 22.2 %collective-permute-start.15 = (bf16[192,512]{1,0:T(8,128)(2,1)S(1)}, bf16[192,512]{1,0:T(8,128)(2,1)S(1)}, u32[]{:S(2)}, u32[]{:S(2)}) collective-permute-start(bf16[192,512]{1,0:T(8,128)(2,1)S(1)} %get-tuple-element.135), channel_id=1, source_target_pairs={{0,12},{4,0},{8,4},{12,8},{1,13},{5,1},{9,5},{13,9},{2,14},{6,2},{... | collective-permute-start | bytes 589832 | tf_op jit(solution)/shard_map/ppermute | solution.py:357
  100.3 23.2 %collective-permute-start.23 = (bf16[32,3072]{1,0:T(8,128)(2,1)S(1)}, bf16[32,3072]{1,0:T(8,128)(2,1)S(1)}, u32[]{:S(2)}, u32[]{:S(2)}) collective-permute-start(bf16[32,3072]{1,0:T(8,128)(2,1)S(1)} %get-tuple-element.150), channel_id=1, source_target_pairs={{0,2},{1,3},{2,0},{3,1},{4,6},{5,7},{6,4},{7,5},{8,10},{9,11},{10,... | collective-permute-start | bytes 589832 | tf_op jit(solution)/shard_map/ppermute | solution.py:354
  121.3 5.2 %collective-permute-start.20 = (bf16[96,512]{1,0:T(8,128)(2,1)S(1)}, bf16[96,512]{1,0:T(8,128)(2,1)S(1)}, u32[]{:S(2)}, u32[]{:S(2)}) collective-permute-start(bf16[96,512]{1,0:T(8,128)(2,1)S(1)} %get-tuple-element.146), channel_id=1, source_target_pairs={{0,2},{1,3},{2,0},{3,1},{4,6},{5,7},{6,4},{7,5},{8,10},{9,11},{10,... | collective-permute-start | bytes 294920 | tf_op jit(solution)/shard_map/ppermute | solution.py:354
  121.3 5.2 %collective-permute-start.21 = (bf16[96,512]{1,0:T(8,128)(2,1)S(1)}, bf16[96,512]{1,0:T(8,128)(2,1)S(1)}, u32[]{:S(2)}, u32[]{:S(2)}) collective-permute-start(bf16[96,512]{1,0:T(8,128)(2,1)S(1)} %get-tuple-element.147), channel_id=1, source_target_pairs={{0,3},{1,2},{2,1},{3,0},{4,7},{5,6},{6,5},{7,4},{8,11},{9,10},{10,... | collective-permute-start | bytes 294920 | tf_op jit(solution)/shard_map/ppermute | solution.py:354
  121.8 4.7 %collective-permute-start.22 = (bf16[32,3072]{1,0:T(8,128)(2,1)S(1)}, bf16[32,3072]{1,0:T(8,128)(2,1)S(1)}, u32[]{:S(2)}, u32[]{:S(2)}) collective-permute-start(bf16[32,3072]{1,0:T(8,128)(2,1)S(1)} %get-tuple-element.148.refs_1_), channel_id=1, source_target_pairs={{0,1},{1,0},{2,3},{3,2},{4,5},{5,4},{6,7},{7,6},{8,9},{9,8},{10,11... | collective-permute-start | bytes 589832 | tf_op jit(solution)/shard_map/ppermute | solution.py:354
  132.9 34.2 %collective-permute-start.24 = (bf16[256,2048]{1,0:T(8,128)(2,1)}, bf16[256,2048]{1,0:T(8,128)(2,1)S(1)}, u32[]{:S(2)}, u32[]{:S(2)}) collective-permute-start(bf16[256,2048]{1,0:T(8,128)(2,1)} %get-tuple-element.155.refs_1_), channel_id=1, source_target_pairs={{0,1},{1,0},{2,3},{3,2},{4,5},{5,4},{6,7},{7,6},{8,9},{9,8},{10,11... | collective-permute-start | bytes 3145736 | tf_op jit(solution)/shard_map/ppermute | solution.py:354
  134.3 14.2 %collective-permute-start.25 = (bf16[32,3072]{1,0:T(8,128)(2,1)S(1)}, bf16[32,3072]{1,0:T(8,128)(2,1)S(1)}, u32[]{:S(2)}, u32[]{:S(2)}) collective-permute-start(bf16[32,3072]{1,0:T(8,128)(2,1)S(1)} %get-tuple-element.156.refs_1_), channel_id=1, source_target_pairs={{0,1},{1,0},{2,3},{3,2},{4,5},{5,4},{6,7},{7,6},{8,9},{9,8},{10,11... | collective-permute-start | bytes 589832 | tf_op jit(solution)/shard_map/ppermute | solution.py:354
  134.3 37.8 %collective-permute-start.26 = (bf16[2,96,512]{2,1,0:T(8,128)(2,1)S(1)}, bf16[2,96,512]{2,1,0:T(8,128)(2,1)S(1)}, u32[]{:S(2)}, u32[]{:S(2)}) collective-permute-start(bf16[2,96,512]{2,1,0:T(8,128)(2,1)S(1)} %get-tuple-element.162.refs_4_), channel_id=1, source_target_pairs={{0,4},{4,8},{8,12},{12,0},{1,5},{5,9},{9,13},{13,1},{2,6},{6,10},{... | collective-permute-start | bytes 589832 | tf_op jit(solution)/shard_map/ppermute | solution.py:357
  146.1 26.1 %collective-permute-start.27 = (bf16[2,96,512]{2,1,0:T(8,128)(2,1)S(1)}, bf16[2,96,512]{2,1,0:T(8,128)(2,1)S(1)}, u32[]{:S(2)}, u32[]{:S(2)}) collective-permute-start(bf16[2,96,512]{2,1,0:T(8,128)(2,1)S(1)} %get-tuple-element.162.refs_4_), channel_id=1, source_target_pairs={{0,8},{4,12},{8,0},{12,4},{1,9},{5,13},{9,1},{13,5},{2,10},{6,14},... | collective-permute-start | bytes 589832 | tf_op jit(solution)/shard_map/ppermute | solution.py:357
  146.1 26.1 %collective-permute-start.28 = (bf16[2,96,512]{2,1,0:T(8,128)(2,1)S(1)}, bf16[2,96,512]{2,1,0:T(8,128)(2,1)S(1)}, u32[]{:S(2)}, u32[]{:S(2)}) collective-permute-start(bf16[2,96,512]{2,1,0:T(8,128)(2,1)S(1)} %get-tuple-element.162.refs_4_), channel_id=1, source_target_pairs={{0,12},{4,0},{8,4},{12,8},{1,13},{5,1},{9,5},{13,9},{2,14},{6,2},{... | collective-permute-start | bytes 589832 | tf_op jit(solution)/shard_map/ppermute | solution.py:357
  154.8 6.2 %collective-permute-start.29 = (bf16[64,512]{1,0:T(8,128)(2,1)S(1)}, bf16[64,512]{1,0:T(8,128)(2,1)S(1)}, u32[]{:S(2)}, u32[]{:S(2)}) collective-permute-start(bf16[64,512]{1,0:T(8,128)(2,1)S(1)} %get-tuple-element.164), channel_id=1, source_target_pairs={{0,4},{4,8},{8,12},{12,0},{1,5},{5,9},{9,13},{13,1},{2,6},{6,10},{... | collective-permute-start | bytes 196616 | tf_op jit(solution)/shard_map/ppermute | solution.py:357
  161.0 10.0 %collective-permute-start.30 = (bf16[64,512]{1,0:T(8,128)(2,1)S(1)}, bf16[64,512]{1,0:T(8,128)(2,1)S(1)}, u32[]{:S(2)}, u32[]{:S(2)}) collective-permute-start(bf16[64,512]{1,0:T(8,128)(2,1)S(1)} %get-tuple-element.165), channel_id=1, source_target_pairs={{0,8},{4,12},{8,0},{12,4},{1,9},{5,13},{9,1},{13,5},{2,10},{6,14},... | collective-permute-start | bytes 196616 | tf_op jit(solution)/shard_map/ppermute | solution.py:357
  167.1 4.4 %collective-permute-start.31 = (bf16[64,512]{1,0:T(8,128)(2,1)S(1)}, bf16[64,512]{1,0:T(8,128)(2,1)S(1)}, u32[]{:S(2)}, u32[]{:S(2)}) collective-permute-start(bf16[64,512]{1,0:T(8,128)(2,1)S(1)} %get-tuple-element.166), channel_id=1, source_target_pairs={{0,12},{4,0},{8,4},{12,8},{1,13},{5,1},{9,5},{13,9},{2,14},{6,2},{... | collective-permute-start | bytes 196616 | tf_op jit(solution)/shard_map/ppermute | solution.py:357
  171.6 4.2 %collective-permute-start.32 = (bf16[32,512]{1,0:T(8,128)(2,1)S(1)}, bf16[32,512]{1,0:T(8,128)(2,1)S(1)}, u32[]{:S(2)}, u32[]{:S(2)}) collective-permute-start(bf16[32,512]{1,0:T(8,128)(2,1)S(1)} %get-tuple-element.171), channel_id=1, source_target_pairs={{0,2},{1,3},{2,0},{3,1},{4,6},{5,7},{6,4},{7,5},{8,10},{9,11},{10,... | collective-permute-start | bytes 98312 | tf_op jit(solution)/shard_map/ppermute | solution.py:354
  172.1 3.7 %collective-permute-start.33 = (bf16[32,512]{1,0:T(8,128)(2,1)S(1)}, bf16[32,512]{1,0:T(8,128)(2,1)S(1)}, u32[]{:S(2)}, u32[]{:S(2)}) collective-permute-start(bf16[32,512]{1,0:T(8,128)(2,1)S(1)} %get-tuple-element.172), channel_id=1, source_target_pairs={{0,3},{1,2},{2,1},{3,0},{4,7},{5,6},{6,5},{7,4},{8,11},{9,10},{10,... | collective-permute-start | bytes 98312 | tf_op jit(solution)/shard_map/ppermute | solution.py:354
  175.8 6.9 %collective-permute-start.34 = (bf16[2,32,512]{2,1,0:T(8,128)(2,1)S(1)}, bf16[2,32,512]{2,1,0:T(8,128)(2,1)S(1)}, u32[]{:S(2)}, u32[]{:S(2)}) collective-permute-start(bf16[2,32,512]{2,1,0:T(8,128)(2,1)S(1)} %get-tuple-element.174.refs_4_), channel_id=1, source_target_pairs={{0,4},{4,8},{8,12},{12,0},{1,5},{5,9},{9,13},{13,1},{2,6},{6,10},{... | collective-permute-start | bytes 196616 | tf_op jit(solution)/shard_map/ppermute | solution.py:357
  176.7 8.0 %collective-permute-start.35 = (bf16[2,32,512]{2,1,0:T(8,128)(2,1)S(1)}, bf16[2,32,512]{2,1,0:T(8,128)(2,1)S(1)}, u32[]{:S(2)}, u32[]{:S(2)}) collective-permute-start(bf16[2,32,512]{2,1,0:T(8,128)(2,1)S(1)} %get-tuple-element.174.refs_4_), channel_id=1, source_target_pairs={{0,8},{4,12},{8,0},{12,4},{1,9},{5,13},{9,1},{13,5},{2,10},{6,14},... | collective-permute-start | bytes 196616 | tf_op jit(solution)/shard_map/ppermute | solution.py:357
  179.6 5.3 %collective-permute-start.36 = (bf16[2,32,512]{2,1,0:T(8,128)(2,1)S(1)}, bf16[2,32,512]{2,1,0:T(8,128)(2,1)S(1)}, u32[]{:S(2)}, u32[]{:S(2)}) collective-permute-start(bf16[2,32,512]{2,1,0:T(8,128)(2,1)S(1)} %get-tuple-element.174.refs_4_), channel_id=1, source_target_pairs={{0,12},{4,0},{8,4},{12,8},{1,13},{5,1},{9,5},{13,9},{2,14},{6,2},{... | collective-permute-start | bytes 196616 | tf_op jit(solution)/shard_map/ppermute | solution.py:357
  (3 other events, 2.1 us)
Sparse Core Ops, SparseCore 0:
  66.4 66.2 all-reduce.1

commit v3 on v0

--- a/solution.py
+++ b/solution.py
@@ -1,12 +1,23 @@
+import functools
+
 import jax
 import jax.numpy as jnp
 from jax import lax
+from jax.experimental import pallas as pl
+from jax.experimental.pallas import tpu as pltpu
 from jax.sharding import PartitionSpec as P
 
 BLOCK = 128
-
-
 EPSILON = 1e-06
+
+STEP = 1024
+FIRST = 1
+PIECE = 4
+DEPTH = 512
+SLOTS = 6
+TILE = 512
+EARLY = 5
+VMEM = 32 * 2**20
 
 
 def encode(values):
@@ -23,7 +34,7 @@
     return (blocks * scales.astype(jnp.float32)[..., None]).reshape(encoded.shape)
 
 
-def shards(gate_input, up_input, down_weight):
+def general_shards(gate_input, up_input, down_weight):
     hidden = (jax.nn.silu(gate_input.astype(jnp.float32)) * up_input.astype(jnp.float32)).astype(
         jnp.bfloat16
     )
@@ -68,7 +79,380 @@
     return (out_codes.reshape(row_count, -1), out_scales.reshape(row_count, -1))
 
 
+ANY = pl.BlockSpec(memory_space=pl.ANY)
+COST = pl.CostEstimate(flops=10**10, bytes_accessed=10**7, transcendentals=0)
+
+
+TOKEN = (8, 128)
+
+
+def large(value):
+    return value.size * value.dtype.itemsize > 3 * 2**20
+
+
+class Chain:
+    def __init__(self):
+        self.tokens = []
+
+    def call(self, body, operands, in_specs, out_specs, out_shape, name, grid=(), scratch=(), aliases=None):
+        count, n_tokens, n_outs = len(operands), len(self.tokens), len(out_shape)
+
+        def with_tokens(*refs):
+            outs = count + n_tokens
+            body(*refs[:count], *refs[outs : outs + n_outs], *refs[outs + n_outs + 1 :])
+
+        operands = [
+            pltpu.with_memory_space_constraint(value, pltpu.HBM) if large(value) else value
+            for value in operands
+        ]
+        outs = pl.pallas_call(
+            with_tokens,
+            grid=grid,
+            in_specs=list(in_specs) + [ANY] * n_tokens,
+            out_specs=list(out_specs) + [ANY],
+            out_shape=list(out_shape) + [jax.ShapeDtypeStruct(TOKEN, jnp.float32)],
+            scratch_shapes=scratch,
+            input_output_aliases=aliases or {},
+            compiler_params=pltpu.CompilerParams(vmem_limit_bytes=VMEM),
+            cost_estimate=COST,
+            name=name,
+        )(*operands, *self.tokens)
+        self.tokens = [outs[-1]]
+        return list(outs[:-1])
+
+    def pin(self, value):
+        pinned = self.call(
+            lambda *refs: None,
+            [value],
+            [ANY],
+            [ANY],
+            [jax.ShapeDtypeStruct(value.shape, value.dtype)],
+            "pin",
+            aliases={0: 0},
+        )
+        return pinned[0]
+
+
+def activate(chain, gate, up, first, steps, parts):
+    rows = gate.shape[0]
+
+    def body(gate_ref, up_ref, *refs):
+        outs, (gates, ups, hidden, in_sems, out_sems) = refs[: len(parts)], refs[len(parts) :]
+
+        def fetch(k, source, target, side):
+            at = pl.ds((first + k) * STEP, STEP)
+            return pltpu.make_async_copy(source.at[:, at], target.at[k], in_sems.at[side, k])
+
+        for k in range(steps):
+            fetch(k, gate_ref, gates, 0).start()
+            fetch(k, up_ref, ups, 1).start()
+        sent = []
+        for k in range(steps):
+            fetch(k, gate_ref, gates, 0).wait()
+            fetch(k, up_ref, ups, 1).wait()
+            value = gates[k].astype(jnp.float32)
+            value = value / (1.0 + jnp.exp(-value)) * ups[k].astype(jnp.float32)
+            hidden[k] = value.astype(jnp.bfloat16)
+            for p, (a, b, s, e) in enumerate(parts):
+                if s <= first + k < e:
+                    copy = pltpu.make_async_copy(
+                        hidden.at[k, pl.ds(a, b - a)],
+                        outs[p].at[:, pl.ds((first + k - s) * STEP, STEP)],
+                        out_sems.at[p, k],
+                    )
+                    copy.start()
+                    sent.append(copy)
+        for copy in sent:
+            copy.wait()
+
+    buffer = pltpu.VMEM((steps, rows, STEP), jnp.bfloat16)
+    return chain.call(
+        body,
+        [gate, up],
+        [ANY] * 2,
+        [ANY] * len(parts),
+        [jax.ShapeDtypeStruct((b - a, (e - s) * STEP), jnp.bfloat16) for a, b, s, e in parts],
+        "activate",
+        scratch=[buffer] * 3
+        + [pltpu.SemaphoreType.DMA((2, steps)), pltpu.SemaphoreType.DMA((len(parts), steps))],
+    )
+
+
+def multiply(chain, chunks, weight, first, total, split):
+    counts = [piece.shape[0] for piece in chunks[0]]
+    rows, cols = sum(counts), weight.shape[1]
+    width = sum(pieces[0].shape[1] for pieces in chunks)
+    steps, part = width // DEPTH, cols // sum(map(len, split or [(0,)]))
+    flat, col = [], 0
+    for pieces in chunks:
+        row = 0
+        for piece in pieces:
+            flat.append((piece, row, col))
+            row += piece.shape[0]
+        col += pieces[0].shape[1]
+    n_total = 0 if total is None else 1
+    n_in = len(flat) + 1 + n_total
+    shapes = [jax.ShapeDtypeStruct((len(flips), rows, part), jnp.bfloat16) for flips in split]
+    if not split:
+        shapes = [jax.ShapeDtypeStruct((rows, cols), jnp.float32)]
+
+    def body(*refs):
+        piece_refs, weight_ref = refs[: len(flat)], refs[len(flat)]
+        total_refs, refs = refs[len(flat) + 1 : n_in], refs[n_in:]
+        outs, (left, slots, *sums, sems, piece_sems) = refs[: len(shapes)], refs[len(shapes) :]
+        sums = sums[0] if sums else outs[0]
+
+        def fetch(k, slot):
+            return pltpu.make_async_copy(
+                weight_ref.at[pl.ds(first * STEP + k * DEPTH, DEPTH)], slots.at[slot], sems.at[slot]
+            )
+
+        for k in range(min(SLOTS, steps)):
+            fetch(k, k).start()
+        copies = [
+            pltpu.make_async_copy(
+                ref,
+                left.at[pl.ds(row, piece.shape[0]), pl.ds(col, piece.shape[1])],
+                piece_sems.at[n],
+            )
+            for n, (ref, (piece, row, col)) in enumerate(zip(piece_refs, flat))
+        ]
+        if n_total:
+            copies.append(pltpu.make_async_copy(total_refs[0], sums, piece_sems.at[len(flat)]))
+        for copy in copies:
+            copy.start()
+        if not n_total:
+            sums[...] = jnp.zeros(sums.shape, sums.dtype)
+        for copy in copies:
+            copy.wait()
+
+        def step(k, carry):
+            slot = lax.rem(k, SLOTS)
+            fetch(k, slot).wait()
+            piece = left[:, pl.ds(pl.multiple_of(k * DEPTH, DEPTH), DEPTH)]
+            for n in range(cols // TILE):
+                at = pl.ds(n * TILE, TILE)
+                sums[:, at] += jnp.dot(piece, slots[slot, :, at], preferred_element_type=jnp.float32)
+
+            @pl.when(k + SLOTS < steps)
+            def _():
+                fetch(k + SLOTS, slot).start()
+
+            return carry
+
+        lax.fori_loop(0, steps, step, 0)
+        for out, flips in zip(outs, split):
+            for n, flip in enumerate(flips):
+                at = pl.ds(pl.multiple_of((lax.axis_index("tp") ^ flip) * part, part), part)
+                out[n] = sums[:, at].astype(jnp.bfloat16)
+
+    return chain.call(
+        body,
+        [piece for piece, _, _ in flat] + [weight] + ([total] if n_total else []),
+        [ANY] * n_in,
+        [pl.BlockSpec(memory_space=pltpu.VMEM)] * len(shapes),
+        shapes,
+        "multiply",
+        scratch=[pltpu.VMEM((rows, width), jnp.bfloat16), pltpu.VMEM((SLOTS, DEPTH, cols), jnp.bfloat16)]
+        + ([pltpu.VMEM((rows, cols), jnp.float32)] if split else [])
+        + [pltpu.SemaphoreType.DMA((SLOTS,)), pltpu.SemaphoreType.DMA((len(flat) + 1,))],
+    )
+
+
+def add(chain, parts, outs):
+    count = len(parts)
+
+    def body(*refs):
+        value = sum(ref[...].astype(jnp.float32) for ref in refs[:count]).astype(jnp.bfloat16)
+        for ref, (n, a, b) in zip(refs[count:], outs):
+            ref[0] = value[n, a:b]
+
+    vmem = pl.BlockSpec(memory_space=pltpu.VMEM)
+    shapes = [jax.ShapeDtypeStruct((1, b - a, parts[0].shape[2]), jnp.bfloat16) for _, a, b in outs]
+    return chain.call(body, parts, [vmem] * count, [vmem] * len(outs), shapes, "add")
+
+
+def join(chain, first, second):
+    n = first.shape[0]
+
+    def body(first_ref, second_ref, out_ref):
+        out_ref[:n] = first_ref[...]
+        out_ref[n:] = second_ref[...]
+
+    vmem = pl.BlockSpec(memory_space=pltpu.VMEM)
+    shape = jax.ShapeDtypeStruct((n + second.shape[0],) + first.shape[1:], first.dtype)
+    return chain.call(body, [first, second], [vmem] * 2, [vmem], [shape], "join")[0]
+
+
+def encode_blocks(value, store, scales, first):
+    lanes = lax.broadcasted_iota(jnp.int32, scales.shape, 1)
+    for n in range(value.shape[1] // BLOCK):
+        block = value[:, n * BLOCK : (n + 1) * BLOCK].astype(jnp.float32)
+        scale = (jnp.max(jnp.abs(block), axis=1, keepdims=True) + EPSILON).astype(jnp.bfloat16)
+        scale = scale.astype(jnp.float32)
+        store(n, (block / scale).astype(jnp.bfloat16))
+        scales = jnp.where(lanes == first + n, scale, scales)
+    return scales
+
+
+def encode_columns(chain, codes, scales, shares, away, start, width):
+    rows, part = shares[0][0].shape[1:]
+    tp = len(shares)
+    blocks = part // BLOCK
+    at = slice(start, start + rows)
+    height = start + rows if codes is None else codes.shape[0]
+    given = [] if codes is None else [codes, scales]
+
+    def body(*refs):
+        share_refs = refs[len(given) : len(given) + tp]
+        code_ref, scale_ref = refs[len(given) + tp :]
+        j = pl.program_id(0)
+
+        @pl.when(j == 0)
+        def _():
+            scale_ref[...] = refs[1][...] if given else jnp.zeros(scale_ref.shape, scale_ref.dtype)
+
+        if given:
+            code_ref[...] = refs[0][...]
+        total = scale_ref[at].astype(jnp.float32)
+        for flip in range(tp):
+            t = lax.axis_index("tp") ^ flip
+
+            def store(n, value, t=t):
+                code_ref[at, pl.ds(pl.multiple_of((t * blocks + n) * BLOCK, BLOCK), BLOCK)] = value
+
+            first = ((lax.axis_index("batch") ^ (j + away)) * tp + t) * blocks
+            total = encode_blocks(share_refs[flip][...], store, total, first)
+        scale_ref[at] = total.astype(jnp.bfloat16)
+
+    whole = pl.BlockSpec((height, width // BLOCK), lambda j: (0, 0))
+    columns = pl.BlockSpec((height, tp * part), lambda j: (0, lax.axis_index("batch") ^ (j + away)))
+
+    def share_spec(n):
+        return pl.BlockSpec((None, rows, part), lambda j: (n + j, 0, 0))
+
+    return chain.call(
+        body,
+        given + [array for array, _ in shares],
+        [columns, whole][: len(given)] + [share_spec(n) for _, n in shares],
+        [columns, whole],
+        [
+            jax.ShapeDtypeStruct((height, width), jnp.bfloat16),
+            jax.ShapeDtypeStruct((height, width // BLOCK), jnp.bfloat16),
+        ],
+        "encode",
+        grid=(2,),
+        aliases={0: 0, 1: 1} if given else {},
+    )
+
+
+DIRECT = [(0,), (1,), (2,), (3,)]
+HALVES = [(0, 2), (1, 3)]
+
+
+def paired_shards(gate_input, up_input, down_weight):
+    rows, width = gate_input.shape
+    tp, batch = lax.axis_size("tp"), lax.axis_size("batch")
+    out_width = down_weight.shape[1] * batch
+    cut = rows * EARLY // 8
+    ends = [FIRST, FIRST + PIECE, FIRST + 2 * PIECE, FIRST + 3 * PIECE]
+    spans = list(zip([0] + ends, ends))
+    chain = Chain()
+
+    def swap(value, flip):
+        return lax.ppermute(value, "batch", [(b, b ^ flip) for b in range(batch)]) if flip else value
+
+    def shift(value, flip):
+        return lax.ppermute(value, "tp", [(t, t ^ flip) for t in range(tp)])
+
+    def both_cores(piece):
+        piece = chain.pin(piece)
+        return [piece, swap(piece, 1)]
+
+    def product(chunks, first, total, split=()):
+        outs = multiply(chain, chunks, down_weight, first, total, split)
+        return outs if split else outs[0]
+
+    def sum_home(parts, away):
+        half = parts[0].shape[1] // 2
+        ahead, behind = add(chain, parts, [(0, 0, half), (0, half, 2 * half)])
+        return swap(ahead, away), swap(behind, away + 1)
+
+    def sum_pair(parts):
+        keep, got = parts
+        total = add(chain, [keep, got], [(0, 0, keep.shape[1]), (1, 0, keep.shape[1])])
+        return [total[0], shift(total[1], 2)]
+
+    near_0, send_0 = activate(
+        chain, gate_input, up_input, 0, FIRST, [(0, rows, 0, FIRST), (0, cut, 0, FIRST)]
+    )
+    far_0 = swap(send_0, 2)
+    pieces = activate(
+        chain,
+        gate_input,
+        up_input,
+        0,
+        width // STEP,
+        [(0, rows, a, b) for a, b in spans[1:]]
+        + [(0, cut, a, b) for a, b in spans[1:]]
+        + [(cut, rows, a, b) for a, b in [(0, ends[1])] + spans[2:]],
+    )
+    near, early, late = [near_0] + pieces[:3], pieces[3:6], pieces[6:]
+    near = [[h, swap(h, 1)] for h in near]
+    far_0 = both_cores(far_0)
+    far_1, far_2 = swap(early[0], 2), swap(early[1], 2)
+
+    total = product(near[:2], 0, None)
+    near = product(near[2:], ends[1], total, HALVES)
+    near = [near[0], shift(near[1], 1)]
+
+    far_1 = both_cores(far_1)
+    far_3 = swap(chain.pin(early[2]), 2)
+    total = product([far_0, far_1], 0, None)
+    far_2 = both_cores(far_2)
+    late_0 = swap(chain.pin(late[0]), 2)
+    near = sum_pair(near)
+    total = product([far_2], ends[1], total)
+    far_3 = both_cores(far_3)
+    late_1 = swap(chain.pin(late[1]), 2)
+    far = product([far_3], ends[2], total, HALVES)
+    far = [far[0], shift(far[1], 1)]
+    near = sum_home(near, 0)
+
+    late_0 = both_cores(late_0)
+    late_2 = swap(chain.pin(late[2]), 2)
+    near = join(chain, *near)
+    near = [near, shift(near, 2)]
+    total = product([late_0], 0, None)
+    far = sum_pair(far)
+    late_1 = both_cores(late_1)
+    total = product([late_1], ends[1], total)
+    near.append(join(chain, *near))
+    near[2] = shift(near[2], 1)
+    far = sum_home(far, 2)
+    late_2 = both_cores(late_2)
+    parts = product([late_2], ends[2], total, DIRECT)
+    parts = [parts[0]] + [shift(parts[flip], flip) for flip in range(1, tp)]
+    far = join(chain, *far)
+    far = [far] + [shift(far, flip) for flip in range(1, tp)]
+    near = [(near[0], 0), (near[2], 0), (near[1], 0), (near[2], 2)]
+    codes, scales = encode_columns(chain, None, None, near, 0, 0, out_width)
+    last = sum_home(parts, 2)
+    last = join(chain, *last)
+    last = [last] + [shift(last, flip) for flip in range(1, tp)]
+    far, last = [(array, 0) for array in far], [(array, 0) for array in last]
+    codes, scales = encode_columns(chain, codes, scales, far, 2, 0, out_width)
+    codes, scales = encode_columns(chain, codes, scales, last, 2, cut, out_width)
+    return codes, scales
+
+
 def solution(mesh):
+    def shards(gate_input, up_input, down_weight):
+        tp, batch = mesh.shape["tp"], mesh.shape["batch"]
+        width, cols = down_weight.shape
+        paired = batch == tp == 4 and cols % (tp * TILE) == 0 and width == (FIRST + 3 * PIECE) * STEP
+        return (paired_shards if paired else general_shards)(gate_input, up_input, down_weight)
+
     in_specs = (P(("groups", "batch"), "tp"), P(("groups", "batch"), "tp"), P("tp", "batch"))
     out_specs = (P(("groups", "batch"), None), P(("groups", "batch"), None))
     return jax.shard_map(shards, mesh=mesh, in_specs=in_specs, out_specs=out_specs, check_vma=False)

time: 290 us -> 157 us (0.54)
  waiting for transfers between devices: 156 us -> 40 us
  Pallas kernels: 0 us -> 78.5 us
  matrix products: 34.8 us -> 0 us
  blocking collectives: 30.7 us -> 0 us
  starting transfers between devices: 9.73 us -> 36.6 us
  local copies, waits for them, and re-layouts: 27.5 us -> 0.7 us
  other arithmetic: 17 us -> 0 us
  between operations: 14.2 us -> 0.95 us
    all_gather x2 -> x0, waiting for transfers between devices: 115 us -> none  [the longest x1 90.9 us: shards(): lax.all_gather(hidden, 'batch', axis=0, tiled=True)]
    pallas_call x0 -> x33, Pallas kernels: none -> 78.5 us  [call(): pl.pallas_call(with_tokens, grid=grid, in_specs=list(in_specs) + [ANY] *...]
    all_to_all x2 -> x0, waiting for transfers between devices: 40.4 us -> none  [the longest x1 40.4 us: shards(): lax.all_to_all(part_codes.reshape(batch_count, tp_count, row_share, local...]
    ppermute x0 -> x38, waiting for transfers between devices: none -> 40 us  [the longest x15 36.5 us: shift(): return lax.ppermute(value, 'tp', [(t, t ^ flip) for t in range(tp)])]
    ppermute x0 -> x38, starting transfers between devices: none -> 36.6 us  [the longest x15 23.4 us: shift(): return lax.ppermute(value, 'tp', [(t, t ^ flip) for t in range(tp)])]
    dot_general x1 -> x0, matrix products: 34.8 us -> none  [shards(): jnp.dot(lax.all_gather(hidden, 'batch', axis=0, tiled=True), down_weight,...]
    all_to_all x2 -> x0, blocking collectives: 17.4 us -> none  [the longest x1 11.2 us: shards(): lax.all_to_all(new_codes, 'batch', split_axis=0, concat_axis=2, tiled=True)]
    all_gather x1 -> x0, blocking collectives: 13.3 us -> none  [shards(): lax.all_gather(home_scales, 'tp', axis=1, tiled=True)]
  transfers between devices with their start and end apart: 4 -> 38, of which waited for: 3 -> 11; matrix products, arithmetic and copies ran while one was open for 8% -> 0% of each run, Pallas kernels for 0% -> 48%
where the time goes in v3:
time: 157 us
  Pallas kernels  78.5 us (50%)
  waiting for transfers between devices  40 us (25%)
  starting transfers between devices  36.6 us (23%)
    pallas_call x33, Pallas kernels, call(): pl.pallas_call(with_tokens, grid=grid, in_specs=list(in_specs) + [ANY] *...  78.5 us
    ppermute x15, waiting for transfers between devices, shift(): return lax.ppermute(value, 'tp', [(t, t ^ flip) for t in range(tp)])  36.5 us
    ppermute x15, starting transfers between devices, shift(): return lax.ppermute(value, 'tp', [(t, t ^ flip) for t in range(tp)])  23.4 us
    ppermute x23, starting transfers between devices, swap(): lax.ppermute(value, 'batch', [(b, b ^ flip) for b in range(batch)])  13.2 us
    ppermute x23, waiting for transfers between devices, swap(): lax.ppermute(value, 'batch', [(b, b ^ flip) for b in range(batch)])  3.51 us
  transfers between devices with their start and end apart: 38, of which 11 were waited for; matrix products, arithmetic and copies ran while one was open for 0% of the time, Pallas kernels for 48%

profile of v3, /device:TPU:0, one launch (start us, length us, event | category | flops | bytes accessed | tf_op | source)
XLA Modules:
  0.0 156.7 jit_solution(2127080241932701787)
XLA Ops:
  0.6 1.5 activate.2
  2.1 3.0 %collective-permute-start.4 = (bf16[80,1024]{1,0:T(8,128)(2,1)S(1)}, bf16[80,1024]{1,0:T(8,128)(2,1)S(1)}, u32[]{:S(2)}, u32[]{:S(2)}) collective-permute-start(bf16[80,1024]{1,0:T(8,128)(2,1)S(1)} %get-tuple-element.94), channel_id=1, source_target_pairs={{0,2},{1,3},{2,0},{3,1},{4,6},{5,7},{6,4},{7,5},{8,10},{9,11},{10,... | collective-permute-start | bytes 491528 | tf_op jit(solution)/shard_map/ppermute | solution.py:363
  5.1 5.5 %activate.3 = (bf16[128,4096]{1,0:T(8,128)(2,1)S(1)}, bf16[128,4096]{1,0:T(8,128)(2,1)S(1)}, bf16[128,4096]{1,0:T(8,128)(2,1)S(1)}, bf16[80,4096]{1,0:T(8,128)(2...) custom-call(bf16[128,13312]{1,0:T(8,128)(2,1)} %refs_0_.3, ...), custom_call_target="tpu_custom_call" | custom-call | flops 10000000000 | bytes 10000000 | tf_op jit(solution)/shard_map/activate/pallas_call | solution.py:108
  10.7 0.5 collective-permute-start.2
  11.2 0.4 collective-permute-start.1
  11.7 2.0 %collective-permute-done.2.refs_1_ = bf16[128,1024]{1,0:T(8,128)(2,1)S(1)} collective-permute-done((bf16[128,1024]{1,0:T(8,128)(2,1)S(1)}, bf16[128,1024]{1,0:T(8,128)(2,1)S(1)}, u32[]{:S(2)}, u32[]{:S(2)}) %collective-permute-start.2) | collective-permute-done | bytes 262176 | tf_op jit(solution)/shard_map/ppermute | solution.py:363
  13.8 9.0 %multiply.8 = (f32[256,2048]{1,0:T(8,128)S(1)}, f32[8,128]{1,0:T(8,128)S(1)}) custom-call(bf16[128,1024]{1,0:T(8,128)(2,1)S(1)} %get-tuple-element.92.refs_0_, bf16[128,1024]{1,0:T(8,128)(2,1)S(1)} %collective-permute-done.2.refs_1_, bf16[128,4096]{1,0:T(8,128)(2,1)S(1)} %get-tuple-element.93.refs_2_, bf16[128,4096]{1,0:T(8,128)(2,1)S(1)} %collective-permute-done.3.refs_3_, ...), custom_call_target="tpu_custom_call" | custom-call | flops 10000000000 | bytes 10000000 | tf_op jit(solution)/shard_map/multiply/pallas_call | solution.py:108
  22.9 13.3 %multiply.9 = (bf16[2,256,512]{2,1,0:T(8,128)(2,1)S(1)}, bf16[2,256,512]{2,1,0:T(8,128)(2,1)S(1)}, f32[8,128]{1,0:T(8,128)S(1)}) custom-call(bf16[128,4096]{1,0:T(8,128)(2,1)S(1)} %get-tuple-element.90.refs_0_, bf16[128,4096]{1,0:T(8,128)(2,1)S(1)} %collective-permute-done.refs_1_, bf16[128,4096]{1,0:T(8,128)(2,1)S(1)} %get-tuple-element.91.refs_2_, ...), custom_call_target="tpu_custom_call" | custom-call | flops 10000000000 | bytes 10000000 | tf_op jit(solution)/shard_map/multiply/pallas_call | solution.py:108
  36.2 0.4 collective-permute-start.9
  36.7 2.1 %collective-permute-start.5 = (bf16[2,256,512]{2,1,0:T(8,128)(2,1)S(1)}, bf16[2,256,512]{2,1,0:T(8,128)(2,1)S(1)}, u32[]{:S(2)}, u32[]{:S(2)}) collective-permute-start(bf16[2,256,512]{2,1,0:T(8,128)(2,1)S(1)} %get-tuple-element.100), channel_id=1, source_target_pairs={{0,4},{4,0},{8,12},{12,8},{1,5},{5,1},{9,13},{13,9},{2,6},{6,2},{1... | collective-permute-start | bytes 1572872 | tf_op jit(solution)/shard_map/ppermute | solution.py:366
  38.8 1.5 collective-permute-start.11
  40.3 7.9 %multiply.10 = (f32[160,2048]{1,0:T(8,128)S(1)}, f32[8,128]{1,0:T(8,128)S(1)}) custom-call(bf16[80,1024]{1,0:T(8,128)(2,1)S(1)} %get-tuple-element.103.refs_0_, bf16[80,1024]{1,0:T(8,128)(2,1)S(1)} %collective-permute-done.7.refs_1_, bf16[80,4096]{1,0:T(8,128)(2,1)S(1)} %get-tuple-element.106.refs_2_, bf16[80,4096]{1,0:T(8,128)(2,1)S(1)} %collective-permute-done.9.refs_3_, ...), custom_call_target="tpu_custom_call" | custom-call | flops 10000000000 | bytes 10000000 | tf_op jit(solution)/shard_map/multiply/pallas_call | solution.py:108
  48.3 2.6 %collective-permute-done.5.refs_1_ = bf16[2,256,512]{2,1,0:T(8,128)(2,1)S(1)} collective-permute-done((bf16[2,256,512]{2,1,0:T(8,128)(2,1)S(1)}, bf16[2,256,512]{2,1,0:T(8,128)(2,1)S(1)}, u32[]{:S(2)}, u32[]{:S(2)}) %collective-permute-start.5) | collective-permute-done | bytes 524320 | tf_op jit(solution)/shard_map/ppermute | solution.py:366
  51.1 2.8 %collective-permute-start.10 = (bf16[1,256,512]{2,1,0:T(8,128)(2,1)S(1)}, bf16[1,256,512]{2,1,0:T(8,128)(2,1)S(1)}, u32[]{:S(2)}, u32[]{:S(2)}) collective-permute-start(bf16[1,256,512]{2,1,0:T(8,128)(2,1)S(1)} %get-tuple-element.114), channel_id=1, source_target_pairs={{0,8},{4,12},{8,0},{12,4},{1,9},{5,13},{9,1},{13,5},{2,10},{6,14},... | collective-permute-start | bytes 786440 | tf_op jit(solution)/shard_map/ppermute | solution.py:366
  53.9 1.5 collective-permute-start.15
  55.4 6.7 %multiply.11 = (f32[160,2048]{1,0:T(8,128)S(1)}, f32[8,128]{1,0:T(8,128)S(1)}) custom-call(bf16[80,4096]{1,0:T(8,128)(2,1)S(1)} %get-tuple-element.116.refs_0_, bf16[80,4096]{1,0:T(8,128)(2,1)S(1)} %collective-permute-done.12.refs_1_, bf16[13312,2048]{1,0:T(8,128)(2,1)} %refs_2_.9, f32[160,2048]{1,0:T(8,128)S(1)} %get-tuple-element.117.refs_3_, ...), custom_call_target="tpu_custom_call" | custom-call | flops 10000000000 | bytes 10000000 | tf_op jit(solution)/shard_map/multiply/pallas_call | solution.py:108
  62.2 0.6 collective-permute-start.17
  62.8 1.5 collective-permute-done.13.refs_1_
  64.3 6.8 %multiply.12 = (bf16[2,160,512]{2,1,0:T(8,128)(2,1)S(1)}, bf16[2,160,512]{2,1,0:T(8,128)(2,1)S(1)}, f32[8,128]{1,0:T(8,128)S(1)}) custom-call(bf16[80,4096]{1,0:T(8,128)(2,1)S(1)} %get-tuple-element.120.refs_0_, bf16[80,4096]{1,0:T(8,128)(2,1)S(1)} %collective-permute-done.13.refs_1_, bf16[13312,2048]{1,0:T(8,128)(2,1)} %refs_2_.9, ...), custom_call_target="tpu_custom_call" | custom-call | flops 10000000000 | bytes 10000000 | tf_op jit(solution)/shard_map/multiply/pallas_call | solution.py:108
  71.3 0.4 collective-permute-start.19
  71.7 1.6 %collective-permute-start.18 = (bf16[2,160,512]{2,1,0:T(8,128)(2,1)S(1)}, bf16[2,160,512]{2,1,0:T(8,128)(2,1)S(1)}, u32[]{:S(2)}, u32[]{:S(2)}) collective-permute-start(bf16[2,160,512]{2,1,0:T(8,128)(2,1)S(1)} %get-tuple-element.136), channel_id=1, source_target_pairs={{0,4},{4,0},{8,12},{12,8},{1,5},{5,1},{9,13},{13,9},{2,6},{6,2},{1... | collective-permute-start | bytes 983048 | tf_op jit(solution)/shard_map/ppermute | solution.py:366
  73.3 7.8 %multiply.13 = (f32[96,2048]{1,0:T(8,128)S(1)}, f32[8,128]{1,0:T(8,128)S(1)}) custom-call(bf16[48,5120]{1,0:T(8,128)(2,1)S(1)} %get-tuple-element.137.refs_0_, bf16[48,5120]{1,0:T(8,128)(2,1)S(1)} %collective-permute-done.19.refs_1_, bf16[13312,2048]{1,0:T(8,128)(2,1)} %refs_2_.9, f32[8,128]{1,0:T(8,128)S(1)} %get-tuple-element.138.refs_3_), custom_call_target="tpu_custom_call" | custom-call | flops 10000000000 | bytes 10000000 | tf_op jit(solution)/shard_map/multiply/pallas_call | solution.py:108
  81.1 0.3 collective-permute-done.18.refs_1_
  81.6 0.6 collective-permute-start.25
  82.4 2.8 %collective-permute-start.22 = (bf16[1,160,512]{2,1,0:T(8,128)(2,1)S(1)}, bf16[1,160,512]{2,1,0:T(8,128)(2,1)S(1)}, u32[]{:S(2)}, u32[]{:S(2)}) collective-permute-start(bf16[1,160,512]{2,1,0:T(8,128)(2,1)S(1)} %get-tuple-element.147), channel_id=1, source_target_pairs={{0,8},{4,12},{8,0},{12,4},{1,9},{5,13},{9,1},{13,5},{2,10},{6,14},... | collective-permute-start | bytes 491528 | tf_op jit(solution)/shard_map/ppermute | solution.py:366
  85.2 6.6 %multiply.14 = (f32[96,2048]{1,0:T(8,128)S(1)}, f32[8,128]{1,0:T(8,128)S(1)}) custom-call(bf16[48,4096]{1,0:T(8,128)(2,1)S(1)} %get-tuple-element.141.refs_0_, bf16[48,4096]{1,0:T(8,128)(2,1)S(1)} %collective-permute-done.20.refs_1_, bf16[13312,2048]{1,0:T(8,128)(2,1)} %refs_2_.9, f32[96,2048]{1,0:T(8,128)S(1)} %get-tuple-element.142.refs_3_, ...), custom_call_target="tpu_custom_call" | custom-call | flops 10000000000 | bytes 10000000 | tf_op jit(solution)/shard_map/multiply/pallas_call | solution.py:108
  91.8 9.6 %collective-permute-done.16.refs_1_.refs_2_ = bf16[2,128,512]{2,1,0:T(8,128)(2,1)S(1)} collective-permute-done((bf16[2,128,512]{2,1,0:T(8,128)(2,1)S(1)}, bf16[2,128,512]{2,1,0:T(8,128)(2,1)S(1)}, u32[]{:S(2)}, u32[]{:S(2)}) %collective-permute-start.16) | collective-permute-done | bytes 262176 | tf_op jit(solution)/shard_map/ppermute | solution.py:366
  101.4 2.7 %collective-permute-done.22.refs_1_ = bf16[1,160,512]{2,1,0:T(8,128)(2,1)S(1)} collective-permute-done((bf16[1,160,512]{2,1,0:T(8,128)(2,1)S(1)}, bf16[1,160,512]{2,1,0:T(8,128)(2,1)S(1)}, u32[]{:S(2)}, u32[]{:S(2)}) %collective-permute-start.22) | collective-permute-done | bytes 163872 | tf_op jit(solution)/shard_map/ppermute | solution.py:366
  104.3 1.6 collective-permute-start.23
  105.8 0.3 collective-permute-start.24
  106.2 6.7 %multiply.15 = (bf16[1,96,512]{2,1,0:T(8,128)(2,1)S(1)}, bf16[1,96,512]{2,1,0:T(8,128)(2,1)S(1)}, bf16[1,96,512]{2,1,0:T(8,128)(2,1)S(1)}, bf16[1,96,512]{2,1,0:T(8,128)(2,1)S(1)}, f32[8,128]{1,0:T(8,128)S(1)}) custom-call(bf16[48,4096]{1,0:T(8,128)(2,1)S(1)} %get-tuple-element.153.refs_0_, bf16[48,4096]{1,0:T(8,128)(2,1)S(1)} %collective-permute-done.26.refs_1_, ...), custom_call_target="tpu_custom_call" | custom-call | flops 10000000000 | bytes 10000000 | tf_op jit(solution)/shard_map/multiply/pallas_call | solution.py:108
  112.8 2.1 %collective-permute-start.30 = (bf16[1,96,512]{2,1,0:T(8,128)(2,1)S(1)}, bf16[1,96,512]{2,1,0:T(8,128)(2,1)S(1)}, u32[]{:S(2)}, u32[]{:S(2)}) collective-permute-start(bf16[1,96,512]{2,1,0:T(8,128)(2,1)S(1)} %get-tuple-element.162), channel_id=1, source_target_pairs={{0,4},{4,0},{8,12},{12,8},{1,5},{5,1},{9,13},{13,9},{2,6},{6,2},{1... | collective-permute-start | bytes 294920 | tf_op jit(solution)/shard_map/ppermute | solution.py:366
  114.9 2.4 %collective-permute-start.32 = (bf16[1,96,512]{2,1,0:T(8,128)(2,1)S(1)}, bf16[1,96,512]{2,1,0:T(8,128)(2,1)S(1)}, u32[]{:S(2)}, u32[]{:S(2)}) collective-permute-start(bf16[1,96,512]{2,1,0:T(8,128)(2,1)S(1)} %get-tuple-element.164), channel_id=1, source_target_pairs={{0,12},{4,8},{8,4},{12,0},{1,13},{5,9},{9,5},{13,1},{2,14},{6,10},... | collective-permute-start | bytes 294920 | tf_op jit(solution)/shard_map/ppermute | solution.py:366
  117.4 5.6 %collective-permute-done.21.refs_1_.refs_3_ = bf16[4,128,512]{2,1,0:T(8,128)(2,1)S(1)} collective-permute-done((bf16[4,128,512]{2,1,0:T(8,128)(2,1)S(1)}, bf16[4,128,512]{2,1,0:T(8,128)(2,1)S(1)}, u32[]{:S(2)}, u32[]{:S(2)}) %collective-permute-start.21) | collective-permute-done | bytes 524320 | tf_op jit(solution)/shard_map/ppermute | solution.py:366
  123.0 1.6 %encode.3 = (bf16[128,8192]{1,0:T(8,128)(2,1)}, bf16[128,64]{1,0:T(8,128)(2,1)S(1)}, f32[8,128]{1,0:T(8,128)S(1)}) custom-call(bf16[2,128,512]{2,1,0:T(8,128)(2,1)S(1)} %get-tuple-element.133.refs_0_, bf16[4,128,512]{2,1,0:T(8,128)(2,1)S(1)} %collective-permute-done.21.refs_1_.refs_3_, bf16[2,128,512]{2,1,0:T(8,128)(2,1)S(1)} %collective-permute-done.16.refs_1_.refs_2_, ...), custom_call_target="tpu_custom_call" | custom-call | flops 10000000000 | bytes 10000000 | tf_op jit(solution)/shard_map/encode/pallas_call | solution.py:108
  124.6 2.0 %collective-permute-done.30.refs_1_ = bf16[1,96,512]{2,1,0:T(8,128)(2,1)S(1)} collective-permute-done((bf16[1,96,512]{2,1,0:T(8,128)(2,1)S(1)}, bf16[1,96,512]{2,1,0:T(8,128)(2,1)S(1)}, u32[]{:S(2)}, u32[]{:S(2)}) %collective-permute-start.30) | collective-permute-done | bytes 98336 | tf_op jit(solution)/shard_map/ppermute | solution.py:366
  126.7 1.6 collective-permute-start.33
  128.3 0.6 collective-permute-start.27
  128.9 2.1 %collective-permute-start.28 = (bf16[2,80,512]{2,1,0:T(8,128)(2,1)S(1)}, bf16[2,80,512]{2,1,0:T(8,128)(2,1)S(1)}, u32[]{:S(2)}, u32[]{:S(2)}) collective-permute-start(bf16[2,80,512]{2,1,0:T(8,128)(2,1)S(1)} %get-tuple-element.160.refs_2_), channel_id=1, source_target_pairs={{0,8},{4,12},{8,0},{12,4},{1,9},{5,13},{9,1},{13,5},{2,10},{6,14},... | collective-permute-start | bytes 491528 | tf_op jit(solution)/shard_map/ppermute | solution.py:366
  130.9 1.8 %collective-permute-start.29 = (bf16[2,80,512]{2,1,0:T(8,128)(2,1)S(1)}, bf16[2,80,512]{2,1,0:T(8,128)(2,1)S(1)}, u32[]{:S(2)}, u32[]{:S(2)}) collective-permute-start(bf16[2,80,512]{2,1,0:T(8,128)(2,1)S(1)} %get-tuple-element.160.refs_2_), channel_id=1, source_target_pairs={{0,12},{4,8},{8,4},{12,0},{1,13},{5,9},{9,5},{13,1},{2,14},{6,10},... | collective-permute-start | bytes 491528 | tf_op jit(solution)/shard_map/ppermute | solution.py:366
  132.8 2.6 %collective-permute-start.36 = (bf16[2,48,512]{2,1,0:T(8,128)(2,1)S(1)}, bf16[2,48,512]{2,1,0:T(8,128)(2,1)S(1)}, u32[]{:S(2)}, u32[]{:S(2)}) collective-permute-start(bf16[2,48,512]{2,1,0:T(8,128)(2,1)S(1)} %get-tuple-element.172.refs_2_), channel_id=1, source_target_pairs={{0,8},{4,12},{8,0},{12,4},{1,9},{5,13},{9,1},{13,5},{2,10},{6,14},... | collective-permute-start | bytes 294920 | tf_op jit(solution)/shard_map/ppermute | solution.py:366
  135.4 2.6 %collective-permute-done.27.refs_3_ = bf16[2,80,512]{2,1,0:T(8,128)(2,1)S(1)} collective-permute-done((bf16[2,80,512]{2,1,0:T(8,128)(2,1)S(1)}, bf16[2,80,512]{2,1,0:T(8,128)(2,1)S(1)}, u32[]{:S(2)}, u32[]{:S(2)}) %collective-permute-start.27) | collective-permute-done | bytes 163872 | tf_op jit(solution)/shard_map/ppermute | solution.py:366
  138.0 2.4 %collective-permute-start.37 = (bf16[2,48,512]{2,1,0:T(8,128)(2,1)S(1)}, bf16[2,48,512]{2,1,0:T(8,128)(2,1)S(1)}, u32[]{:S(2)}, u32[]{:S(2)}) collective-permute-start(bf16[2,48,512]{2,1,0:T(8,128)(2,1)S(1)} %get-tuple-element.172.refs_2_), channel_id=1, source_target_pairs={{0,12},{4,8},{8,4},{12,0},{1,13},{5,9},{9,5},{13,1},{2,14},{6,10},... | collective-permute-start | bytes 294920 | tf_op jit(solution)/shard_map/ppermute | solution.py:366
  140.4 3.5 %collective-permute-done.28.refs_4_ = bf16[2,80,512]{2,1,0:T(8,128)(2,1)S(1)} collective-permute-done((bf16[2,80,512]{2,1,0:T(8,128)(2,1)S(1)}, bf16[2,80,512]{2,1,0:T(8,128)(2,1)S(1)}, u32[]{:S(2)}, u32[]{:S(2)}) %collective-permute-start.28) | collective-permute-done | bytes 163872 | tf_op jit(solution)/shard_map/ppermute | solution.py:366
  143.9 2.4 %encode.4 = (bf16[128,8192]{1,0:T(8,128)(2,1)}, bf16[128,64]{1,0:T(8,128)(2,1)S(1)}, f32[8,128]{1,0:T(8,128)S(1)}) custom-call(bf16[128,8192]{1,0:T(8,128)(2,1)} %get-tuple-element.158.refs_0_, bf16[128,64]{1,0:T(8,128)(2,1)S(1)} %get-tuple-element.159.refs_1_, ...), custom_call_target="tpu_custom_call", output_to_operand_aliasing={{0}: (0, {}), {1}: (1, {})} | custom-call | flops 10000000000 | bytes 10000000 | tf_op jit(solution)/shard_map/encode/pallas_call | solution.py:108
  146.3 7.4 %collective-permute-done.36.refs_4_ = bf16[2,48,512]{2,1,0:T(8,128)(2,1)S(1)} collective-permute-done((bf16[2,48,512]{2,1,0:T(8,128)(2,1)S(1)}, bf16[2,48,512]{2,1,0:T(8,128)(2,1)S(1)}, u32[]{:S(2)}, u32[]{:S(2)}) %collective-permute-start.36) | collective-permute-done | bytes 98336 | tf_op jit(solution)/shard_map/ppermute | solution.py:366
  153.7 2.3 %encode.5 = (bf16[128,8192]{1,0:T(8,128)(2,1)}, bf16[128,64]{1,0:T(8,128)(2,1)S(1)}, f32[8,128]{1,0:T(8,128)}) custom-call(bf16[128,8192]{1,0:T(8,128)(2,1)} %get-tuple-element.170.refs_0_, bf16[128,64]{1,0:T(8,128)(2,1)S(1)} %get-tuple-element.171.refs_1_, ...), custom_call_target="tpu_custom_call", output_to_operand_aliasing={{0}: (0, {}), {1}: (1, {})} | custom-call | flops 10000000000 | bytes 10000000 | tf_op jit(solution)/shard_map/encode/pallas_call | solution.py:108
  156.0 0.7 copy.20
  (62 shorter events, 1.6 us)
Async XLA Ops:
  2.1 9.6 %collective-permute-start.4 = (bf16[80,1024]{1,0:T(8,128)(2,1)S(1)}, bf16[80,1024]{1,0:T(8,128)(2,1)S(1)}, u32[]{:S(2)}, u32[]{:S(2)}) collective-permute-start(bf16[80,1024]{1,0:T(8,128)(2,1)S(1)} %get-tuple-element.94), channel_id=1, source_target_pairs={{0,2},{1,3},{2,0},{3,1},{4,6},{5,7},{6,4},{7,5},{8,10},{9,11},{10,... | collective-permute-start | bytes 491528 | tf_op jit(solution)/shard_map/ppermute | solution.py:363
  10.6 3.1 %collective-permute-start.3 = (bf16[128,4096]{1,0:T(8,128)(2,1)S(1)}, bf16[128,4096]{1,0:T(8,128)(2,1)S(1)}, u32[]{:S(2)}, u32[]{:S(2)}) collective-permute-start(bf16[128,4096]{1,0:T(8,128)(2,1)S(1)} %get-tuple-element.93.refs_2_), channel_id=1, source_target_pairs={{0,1},{1,0},{2,3},{3,2},{4,5},{5,4},{6,7},{7,6},{8,9},{9,8},{10,11... | collective-permute-start | bytes 3145736 | tf_op jit(solution)/shard_map/ppermute | solution.py:363
  10.7 3.0 %collective-permute-start.2 = (bf16[128,1024]{1,0:T(8,128)(2,1)S(1)}, bf16[128,1024]{1,0:T(8,128)(2,1)S(1)}, u32[]{:S(2)}, u32[]{:S(2)}) collective-permute-start(bf16[128,1024]{1,0:T(8,128)(2,1)S(1)} %get-tuple-element.92.refs_0_), channel_id=1, source_target_pairs={{0,1},{1,0},{2,3},{3,2},{4,5},{5,4},{6,7},{7,6},{8,9},{9,8},{10,11... | collective-permute-start | bytes 786440 | tf_op jit(solution)/shard_map/ppermute | solution.py:363
  11.2 11.7 %collective-permute-start = (bf16[128,4096]{1,0:T(8,128)(2,1)S(1)}, bf16[128,4096]{1,0:T(8,128)(2,1)S(1)}, u32[]{:S(2)}, u32[]{:S(2)}) collective-permute-start(bf16[128,4096]{1,0:T(8,128)(2,1)S(1)} %get-tuple-element.90.refs_0_), channel_id=1, source_target_pairs={{0,1},{1,0},{2,3},{3,2},{4,5},{5,4},{6,7},{7,6},{8,9},{9,8},{10,11... | collective-permute-start | bytes 3145736 | tf_op jit(solution)/shard_map/ppermute | solution.py:363
  11.2 11.6 %collective-permute-start.1 = (bf16[128,4096]{1,0:T(8,128)(2,1)S(1)}, bf16[128,4096]{1,0:T(8,128)(2,1)S(1)}, u32[]{:S(2)}, u32[]{:S(2)}) collective-permute-start(bf16[128,4096]{1,0:T(8,128)(2,1)S(1)} %get-tuple-element.91.refs_2_), channel_id=1, source_target_pairs={{0,1},{1,0},{2,3},{3,2},{4,5},{5,4},{6,7},{7,6},{8,9},{9,8},{10,11... | collective-permute-start | bytes 3145736 | tf_op jit(solution)/shard_map/ppermute | solution.py:363
  11.7 24.6 %collective-permute-start.8 = (bf16[80,4096]{1,0:T(8,128)(2,1)S(1)}, bf16[80,4096]{1,0:T(8,128)(2,1)S(1)}, u32[]{:S(2)}, u32[]{:S(2)}) collective-permute-start(bf16[80,4096]{1,0:T(8,128)(2,1)S(1)} %get-tuple-element.104), channel_id=1, source_target_pairs={{0,2},{1,3},{2,0},{3,1},{4,6},{5,7},{6,4},{7,5},{8,10},{9,11},{10,... | collective-permute-start | bytes 1966088 | tf_op jit(solution)/shard_map/ppermute | solution.py:363
  13.7 34.5 %collective-permute-start.6 = (bf16[80,4096]{1,0:T(8,128)(2,1)S(1)}, bf16[80,4096]{1,0:T(8,128)(2,1)S(1)}, u32[]{:S(2)}, u32[]{:S(2)}) collective-permute-start(bf16[80,4096]{1,0:T(8,128)(2,1)S(1)} %get-tuple-element.102), channel_id=1, source_target_pairs={{0,2},{1,3},{2,0},{3,1},{4,6},{5,7},{6,4},{7,5},{8,10},{9,11},{10,... | collective-permute-start | bytes 1966088 | tf_op jit(solution)/shard_map/ppermute | solution.py:363
  13.7 26.6 %collective-permute-start.7 = (bf16[80,1024]{1,0:T(8,128)(2,1)S(1)}, bf16[80,1024]{1,0:T(8,128)(2,1)S(1)}, u32[]{:S(2)}, u32[]{:S(2)}) collective-permute-start(bf16[80,1024]{1,0:T(8,128)(2,1)S(1)} %get-tuple-element.103.refs_0_), channel_id=1, source_target_pairs={{0,1},{1,0},{2,3},{3,2},{4,5},{5,4},{6,7},{7,6},{8,9},{9,8},{10,11... | collective-permute-start | bytes 491528 | tf_op jit(solution)/shard_map/ppermute | solution.py:363
  36.2 4.0 %collective-permute-start.9 = (bf16[80,4096]{1,0:T(8,128)(2,1)S(1)}, bf16[80,4096]{1,0:T(8,128)(2,1)S(1)}, u32[]{:S(2)}, u32[]{:S(2)}) collective-permute-start(bf16[80,4096]{1,0:T(8,128)(2,1)S(1)} %get-tuple-element.106.refs_2_), channel_id=1, source_target_pairs={{0,1},{1,0},{2,3},{3,2},{4,5},{5,4},{6,7},{7,6},{8,9},{9,8},{10,11... | collective-permute-start | bytes 1966088 | tf_op jit(solution)/shard_map/ppermute | solution.py:363
  36.7 14.3 %collective-permute-start.5 = (bf16[2,256,512]{2,1,0:T(8,128)(2,1)S(1)}, bf16[2,256,512]{2,1,0:T(8,128)(2,1)S(1)}, u32[]{:S(2)}, u32[]{:S(2)}) collective-permute-start(bf16[2,256,512]{2,1,0:T(8,128)(2,1)S(1)} %get-tuple-element.100), channel_id=1, source_target_pairs={{0,4},{4,0},{8,12},{12,8},{1,5},{5,1},{9,13},{13,9},{2,6},{6,2},{1... | collective-permute-start | bytes 1572872 | tf_op jit(solution)/shard_map/ppermute | solution.py:366
  38.8 23.3 %collective-permute-start.11 = (bf16[80,4096]{1,0:T(8,128)(2,1)S(1)}, bf16[80,4096]{1,0:T(8,128)(2,1)S(1)}, u32[]{:S(2)}, u32[]{:S(2)}) collective-permute-start(bf16[80,4096]{1,0:T(8,128)(2,1)S(1)} %get-tuple-element.115), channel_id=1, source_target_pairs={{0,2},{1,3},{2,0},{3,1},{4,6},{5,7},{6,4},{7,5},{8,10},{9,11},{10,... | collective-permute-start | bytes 1966088 | tf_op jit(solution)/shard_map/ppermute | solution.py:363
  48.2 7.2 %collective-permute-start.12 = (bf16[80,4096]{1,0:T(8,128)(2,1)S(1)}, bf16[80,4096]{1,0:T(8,128)(2,1)S(1)}, u32[]{:S(2)}, u32[]{:S(2)}) collective-permute-start(bf16[80,4096]{1,0:T(8,128)(2,1)S(1)} %get-tuple-element.116.refs_0_), channel_id=1, source_target_pairs={{0,1},{1,0},{2,3},{3,2},{4,5},{5,4},{6,7},{7,6},{8,9},{9,8},{10,11... | collective-permute-start | bytes 1966088 | tf_op jit(solution)/shard_map/ppermute | solution.py:363
  51.1 20.0 %collective-permute-start.10 = (bf16[1,256,512]{2,1,0:T(8,128)(2,1)S(1)}, bf16[1,256,512]{2,1,0:T(8,128)(2,1)S(1)}, u32[]{:S(2)}, u32[]{:S(2)}) collective-permute-start(bf16[1,256,512]{2,1,0:T(8,128)(2,1)S(1)} %get-tuple-element.114), channel_id=1, source_target_pairs={{0,8},{4,12},{8,0},{12,4},{1,9},{5,13},{9,1},{13,5},{2,10},{6,14},... | collective-permute-start | bytes 786440 | tf_op jit(solution)/shard_map/ppermute | solution.py:366
  53.9 17.4 %collective-permute-start.15 = (bf16[48,5120]{1,0:T(8,128)(2,1)S(1)}, bf16[48,5120]{1,0:T(8,128)(2,1)S(1)}, u32[]{:S(2)}, u32[]{:S(2)}) collective-permute-start(bf16[48,5120]{1,0:T(8,128)(2,1)S(1)} %get-tuple-element.129), channel_id=1, source_target_pairs={{0,2},{1,3},{2,0},{3,1},{4,6},{5,7},{6,4},{7,5},{8,10},{9,11},{10,... | collective-permute-start | bytes 1474568 | tf_op jit(solution)/shard_map/ppermute | solution.py:363
  62.1 2.2 %collective-permute-start.13 = (bf16[80,4096]{1,0:T(8,128)(2,1)S(1)}, bf16[80,4096]{1,0:T(8,128)(2,1)S(1)}, u32[]{:S(2)}, u32[]{:S(2)}) collective-permute-start(bf16[80,4096]{1,0:T(8,128)(2,1)S(1)} %get-tuple-element.120.refs_0_), channel_id=1, source_target_pairs={{0,1},{1,0},{2,3},{3,2},{4,5},{5,4},{6,7},{7,6},{8,9},{9,8},{10,11... | collective-permute-start | bytes 1966088 | tf_op jit(solution)/shard_map/ppermute | solution.py:363
  62.2 19.3 %collective-permute-start.17 = (bf16[48,4096]{1,0:T(8,128)(2,1)S(1)}, bf16[48,4096]{1,0:T(8,128)(2,1)S(1)}, u32[]{:S(2)}, u32[]{:S(2)}) collective-permute-start(bf16[48,4096]{1,0:T(8,128)(2,1)S(1)} %get-tuple-element.134), channel_id=1, source_target_pairs={{0,2},{1,3},{2,0},{3,1},{4,6},{5,7},{6,4},{7,5},{8,10},{9,11},{10,... | collective-permute-start | bytes 1179656 | tf_op jit(solution)/shard_map/ppermute | solution.py:363
  71.1 2.2 %collective-permute-start.14 = (bf16[1,128,512]{2,1,0:T(8,128)(2,1)S(1)}, bf16[1,128,512]{2,1,0:T(8,128)(2,1)S(1)}, u32[]{:S(2)}, u32[]{:S(2)}) collective-permute-start(bf16[1,128,512]{2,1,0:T(8,128)(2,1)S(1)} %get-tuple-element.127), channel_id=1, source_target_pairs={{0,1},{1,0},{2,3},{3,2},{4,5},{5,4},{6,7},{7,6},{8,9},{9,8},{10,11... | collective-permute-start | bytes 393224 | tf_op jit(solution)/shard_map/ppermute | solution.py:363
  71.3 2.0 %collective-permute-start.19 = (bf16[48,5120]{1,0:T(8,128)(2,1)S(1)}, bf16[48,5120]{1,0:T(8,128)(2,1)S(1)}, u32[]{:S(2)}, u32[]{:S(2)}) collective-permute-start(bf16[48,5120]{1,0:T(8,128)(2,1)S(1)} %get-tuple-element.137.refs_0_), channel_id=1, source_target_pairs={{0,1},{1,0},{2,3},{3,2},{4,5},{5,4},{6,7},{7,6},{8,9},{9,8},{10,11... | collective-permute-start | bytes 1474568 | tf_op jit(solution)/shard_map/ppermute | solution.py:363
  71.7 9.8 %collective-permute-start.18 = (bf16[2,160,512]{2,1,0:T(8,128)(2,1)S(1)}, bf16[2,160,512]{2,1,0:T(8,128)(2,1)S(1)}, u32[]{:S(2)}, u32[]{:S(2)}) collective-permute-start(bf16[2,160,512]{2,1,0:T(8,128)(2,1)S(1)} %get-tuple-element.136), channel_id=1, source_target_pairs={{0,4},{4,0},{8,12},{12,8},{1,5},{5,1},{9,13},{13,9},{2,6},{6,2},{1... | collective-permute-start | bytes 983048 | tf_op jit(solution)/shard_map/ppermute | solution.py:366
  81.5 3.6 %collective-permute-start.20 = (bf16[48,4096]{1,0:T(8,128)(2,1)S(1)}, bf16[48,4096]{1,0:T(8,128)(2,1)S(1)}, u32[]{:S(2)}, u32[]{:S(2)}) collective-permute-start(bf16[48,4096]{1,0:T(8,128)(2,1)S(1)} %get-tuple-element.141.refs_0_), channel_id=1, source_target_pairs={{0,1},{1,0},{2,3},{3,2},{4,5},{5,4},{6,7},{7,6},{8,9},{9,8},{10,11... | collective-permute-start | bytes 1179656 | tf_op jit(solution)/shard_map/ppermute | solution.py:363
  81.6 22.6 %collective-permute-start.25 = (bf16[48,4096]{1,0:T(8,128)(2,1)S(1)}, bf16[48,4096]{1,0:T(8,128)(2,1)S(1)}, u32[]{:S(2)}, u32[]{:S(2)}) collective-permute-start(bf16[48,4096]{1,0:T(8,128)(2,1)S(1)} %get-tuple-element.151), channel_id=1, source_target_pairs={{0,2},{1,3},{2,0},{3,1},{4,6},{5,7},{6,4},{7,5},{8,10},{9,11},{10,... | collective-permute-start | bytes 1179656 | tf_op jit(solution)/shard_map/ppermute | solution.py:363
  82.2 19.2 %collective-permute-start.16 = (bf16[2,128,512]{2,1,0:T(8,128)(2,1)S(1)}, bf16[2,128,512]{2,1,0:T(8,128)(2,1)S(1)}, u32[]{:S(2)}, u32[]{:S(2)}) collective-permute-start(bf16[2,128,512]{2,1,0:T(8,128)(2,1)S(1)} %get-tuple-element.133.refs_0_), channel_id=1, source_target_pairs={{0,8},{4,12},{8,0},{12,4},{1,9},{5,13},{9,1},{13,5},{2,10},{6,14},... | collective-permute-start | bytes 786440 | tf_op jit(solution)/shard_map/ppermute | solution.py:366
  82.4 21.8 %collective-permute-start.22 = (bf16[1,160,512]{2,1,0:T(8,128)(2,1)S(1)}, bf16[1,160,512]{2,1,0:T(8,128)(2,1)S(1)}, u32[]{:S(2)}, u32[]{:S(2)}) collective-permute-start(bf16[1,160,512]{2,1,0:T(8,128)(2,1)S(1)} %get-tuple-element.147), channel_id=1, source_target_pairs={{0,8},{4,12},{8,0},{12,4},{1,9},{5,13},{9,1},{13,5},{2,10},{6,14},... | collective-permute-start | bytes 491528 | tf_op jit(solution)/shard_map/ppermute | solution.py:366
  104.2 1.9 %collective-permute-start.26 = (bf16[48,4096]{1,0:T(8,128)(2,1)S(1)}, bf16[48,4096]{1,0:T(8,128)(2,1)S(1)}, u32[]{:S(2)}, u32[]{:S(2)}) collective-permute-start(bf16[48,4096]{1,0:T(8,128)(2,1)S(1)} %get-tuple-element.153.refs_0_), channel_id=1, source_target_pairs={{0,1},{1,0},{2,3},{3,2},{4,5},{5,4},{6,7},{7,6},{8,9},{9,8},{10,11... | collective-permute-start | bytes 1179656 | tf_op jit(solution)/shard_map/ppermute | solution.py:363
  104.3 10.6 %collective-permute-start.23 = (bf16[1,80,512]{2,1,0:T(8,128)(2,1)S(1)}, bf16[1,80,512]{2,1,0:T(8,128)(2,1)S(1)}, u32[]{:S(2)}, u32[]{:S(2)}) collective-permute-start(bf16[1,80,512]{2,1,0:T(8,128)(2,1)S(1)} %get-tuple-element.149), channel_id=1, source_target_pairs={{0,2},{1,3},{2,0},{3,1},{4,6},{5,7},{6,4},{7,5},{8,10},{9,11},{10,... | collective-permute-start | bytes 245768 | tf_op jit(solution)/shard_map/ppermute | solution.py:363
  105.8 11.5 %collective-permute-start.24 = (bf16[1,80,512]{2,1,0:T(8,128)(2,1)S(1)}, bf16[1,80,512]{2,1,0:T(8,128)(2,1)S(1)}, u32[]{:S(2)}, u32[]{:S(2)}) collective-permute-start(bf16[1,80,512]{2,1,0:T(8,128)(2,1)S(1)} %get-tuple-element.150), channel_id=1, source_target_pairs={{0,3},{1,2},{2,1},{3,0},{4,7},{5,6},{6,5},{7,4},{8,11},{9,10},{10,... | collective-permute-start | bytes 245768 | tf_op jit(solution)/shard_map/ppermute | solution.py:363
  106.1 16.8 %collective-permute-start.21 = (bf16[4,128,512]{2,1,0:T(8,128)(2,1)S(1)}, bf16[4,128,512]{2,1,0:T(8,128)(2,1)S(1)}, u32[]{:S(2)}, u32[]{:S(2)}) collective-permute-start(bf16[4,128,512]{2,1,0:T(8,128)(2,1)S(1)} %get-tuple-element.145), channel_id=1, source_target_pairs={{0,4},{4,0},{8,12},{12,8},{1,5},{5,1},{9,13},{13,9},{2,6},{6,2},{1... | collective-permute-start | bytes 1572872 | tf_op jit(solution)/shard_map/ppermute | solution.py:366
  112.8 13.8 %collective-permute-start.30 = (bf16[1,96,512]{2,1,0:T(8,128)(2,1)S(1)}, bf16[1,96,512]{2,1,0:T(8,128)(2,1)S(1)}, u32[]{:S(2)}, u32[]{:S(2)}) collective-permute-start(bf16[1,96,512]{2,1,0:T(8,128)(2,1)S(1)} %get-tuple-element.162), channel_id=1, source_target_pairs={{0,4},{4,0},{8,12},{12,8},{1,5},{5,1},{9,13},{13,9},{2,6},{6,2},{1... | collective-permute-start | bytes 294920 | tf_op jit(solution)/shard_map/ppermute | solution.py:366
  114.9 11.7 %collective-permute-start.31 = (bf16[1,96,512]{2,1,0:T(8,128)(2,1)S(1)}, bf16[1,96,512]{2,1,0:T(8,128)(2,1)S(1)}, u32[]{:S(2)}, u32[]{:S(2)}) collective-permute-start(bf16[1,96,512]{2,1,0:T(8,128)(2,1)S(1)} %get-tuple-element.163), channel_id=1, source_target_pairs={{0,8},{4,12},{8,0},{12,4},{1,9},{5,13},{9,1},{13,5},{2,10},{6,14},... | collective-permute-start | bytes 294920 | tf_op jit(solution)/shard_map/ppermute | solution.py:366
  114.9 11.7 %collective-permute-start.32 = (bf16[1,96,512]{2,1,0:T(8,128)(2,1)S(1)}, bf16[1,96,512]{2,1,0:T(8,128)(2,1)S(1)}, u32[]{:S(2)}, u32[]{:S(2)}) collective-permute-start(bf16[1,96,512]{2,1,0:T(8,128)(2,1)S(1)} %get-tuple-element.164), channel_id=1, source_target_pairs={{0,12},{4,8},{8,4},{12,0},{1,13},{5,9},{9,5},{13,1},{2,14},{6,10},... | collective-permute-start | bytes 294920 | tf_op jit(solution)/shard_map/ppermute | solution.py:366
  126.7 6.0 %collective-permute-start.33 = (bf16[1,48,512]{2,1,0:T(8,128)(2,1)S(1)}, bf16[1,48,512]{2,1,0:T(8,128)(2,1)S(1)}, u32[]{:S(2)}, u32[]{:S(2)}) collective-permute-start(bf16[1,48,512]{2,1,0:T(8,128)(2,1)S(1)} %get-tuple-element.166), channel_id=1, source_target_pairs={{0,2},{1,3},{2,0},{3,1},{4,6},{5,7},{6,4},{7,5},{8,10},{9,11},{10,... | collective-permute-start | bytes 147464 | tf_op jit(solution)/shard_map/ppermute | solution.py:363
  128.3 4.4 %collective-permute-start.34 = (bf16[1,48,512]{2,1,0:T(8,128)(2,1)S(1)}, bf16[1,48,512]{2,1,0:T(8,128)(2,1)S(1)}, u32[]{:S(2)}, u32[]{:S(2)}) collective-permute-start(bf16[1,48,512]{2,1,0:T(8,128)(2,1)S(1)} %get-tuple-element.167), channel_id=1, source_target_pairs={{0,3},{1,2},{2,1},{3,0},{4,7},{5,6},{6,5},{7,4},{8,11},{9,10},{10,... | collective-permute-start | bytes 147464 | tf_op jit(solution)/shard_map/ppermute | solution.py:363
  128.3 9.8 %collective-permute-start.27 = (bf16[2,80,512]{2,1,0:T(8,128)(2,1)S(1)}, bf16[2,80,512]{2,1,0:T(8,128)(2,1)S(1)}, u32[]{:S(2)}, u32[]{:S(2)}) collective-permute-start(bf16[2,80,512]{2,1,0:T(8,128)(2,1)S(1)} %get-tuple-element.160.refs_2_), channel_id=1, source_target_pairs={{0,4},{4,0},{8,12},{12,8},{1,5},{5,1},{9,13},{13,9},{2,6},{6,2},{1... | collective-permute-start | bytes 491528 | tf_op jit(solution)/shard_map/ppermute | solution.py:366
  128.9 15.0 %collective-permute-start.28 = (bf16[2,80,512]{2,1,0:T(8,128)(2,1)S(1)}, bf16[2,80,512]{2,1,0:T(8,128)(2,1)S(1)}, u32[]{:S(2)}, u32[]{:S(2)}) collective-permute-start(bf16[2,80,512]{2,1,0:T(8,128)(2,1)S(1)} %get-tuple-element.160.refs_2_), channel_id=1, source_target_pairs={{0,8},{4,12},{8,0},{12,4},{1,9},{5,13},{9,1},{13,5},{2,10},{6,14},... | collective-permute-start | bytes 491528 | tf_op jit(solution)/shard_map/ppermute | solution.py:366
  130.9 13.0 %collective-permute-start.29 = (bf16[2,80,512]{2,1,0:T(8,128)(2,1)S(1)}, bf16[2,80,512]{2,1,0:T(8,128)(2,1)S(1)}, u32[]{:S(2)}, u32[]{:S(2)}) collective-permute-start(bf16[2,80,512]{2,1,0:T(8,128)(2,1)S(1)} %get-tuple-element.160.refs_2_), channel_id=1, source_target_pairs={{0,12},{4,8},{8,4},{12,0},{1,13},{5,9},{9,5},{13,1},{2,14},{6,10},... | collective-permute-start | bytes 491528 | tf_op jit(solution)/shard_map/ppermute | solution.py:366
  132.7 13.7 %collective-permute-start.35 = (bf16[2,48,512]{2,1,0:T(8,128)(2,1)S(1)}, bf16[2,48,512]{2,1,0:T(8,128)(2,1)S(1)}, u32[]{:S(2)}, u32[]{:S(2)}) collective-permute-start(bf16[2,48,512]{2,1,0:T(8,128)(2,1)S(1)} %get-tuple-element.172.refs_2_), channel_id=1, source_target_pairs={{0,4},{4,0},{8,12},{12,8},{1,5},{5,1},{9,13},{13,9},{2,6},{6,2},{1... | collective-permute-start | bytes 294920 | tf_op jit(solution)/shard_map/ppermute | solution.py:366
  132.8 21.0 %collective-permute-start.36 = (bf16[2,48,512]{2,1,0:T(8,128)(2,1)S(1)}, bf16[2,48,512]{2,1,0:T(8,128)(2,1)S(1)}, u32[]{:S(2)}, u32[]{:S(2)}) collective-permute-start(bf16[2,48,512]{2,1,0:T(8,128)(2,1)S(1)} %get-tuple-element.172.refs_2_), channel_id=1, source_target_pairs={{0,8},{4,12},{8,0},{12,4},{1,9},{5,13},{9,1},{13,5},{2,10},{6,14},... | collective-permute-start | bytes 294920 | tf_op jit(solution)/shard_map/ppermute | solution.py:366
  138.0 15.7 %collective-permute-start.37 = (bf16[2,48,512]{2,1,0:T(8,128)(2,1)S(1)}, bf16[2,48,512]{2,1,0:T(8,128)(2,1)S(1)}, u32[]{:S(2)}, u32[]{:S(2)}) collective-permute-start(bf16[2,48,512]{2,1,0:T(8,128)(2,1)S(1)} %get-tuple-element.172.refs_2_), channel_id=1, source_target_pairs={{0,12},{4,8},{8,4},{12,0},{1,13},{5,9},{9,5},{13,1},{2,14},{6,10},... | collective-permute-start | bytes 294920 | tf_op jit(solution)/shard_map/ppermute | solution.py:366

commit v4 on v3

--- a/solution.py
+++ b/solution.py
@@ -80,7 +80,7 @@
 
 
 ANY = pl.BlockSpec(memory_space=pl.ANY)
-COST = pl.CostEstimate(flops=10**10, bytes_accessed=10**7, transcendentals=0)
+WEIGHTS = {"activate": 10**10, "multiply": 10**10, "pin": 10**10, "add": 0, "join": 0, "encode": 0}
 
 
 TOKEN = (8, 128)
@@ -94,7 +94,7 @@
     def __init__(self):
         self.tokens = []
 
-    def call(self, body, operands, in_specs, out_specs, out_shape, name, grid=(), scratch=(), aliases=None):
+    def call(self, body, operands, in_specs, out_specs, out_shape, name, grid=(), scratch=(), aliases=None, cost=None):
         count, n_tokens, n_outs = len(operands), len(self.tokens), len(out_shape)
 
         def with_tokens(*refs):
@@ -114,7 +114,9 @@
             scratch_shapes=scratch,
             input_output_aliases=aliases or {},
             compiler_params=pltpu.CompilerParams(vmem_limit_bytes=VMEM),
-            cost_estimate=COST,
+            cost_estimate=pl.CostEstimate(
+                flops=WEIGHTS[name] if cost is None else cost, bytes_accessed=1024, transcendentals=0
+            ),
             name=name,
         )(*operands, *self.tokens)
         self.tokens = [outs[-1]]
@@ -178,7 +180,7 @@
     )
 
 
-def multiply(chain, chunks, weight, first, total, split):
+def multiply(chain, chunks, weight, first, total, split, cost):
     counts = [piece.shape[0] for piece in chunks[0]]
     rows, cols = sum(counts), weight.shape[1]
     width = sum(pieces[0].shape[1] for pieces in chunks)
@@ -253,6 +255,7 @@
         [pl.BlockSpec(memory_space=pltpu.VMEM)] * len(shapes),
         shapes,
         "multiply",
+        cost=cost,
         scratch=[pltpu.VMEM((rows, width), jnp.bfloat16), pltpu.VMEM((SLOTS, DEPTH, cols), jnp.bfloat16)]
         + ([pltpu.VMEM((rows, cols), jnp.float32)] if split else [])
         + [pltpu.SemaphoreType.DMA((SLOTS,)), pltpu.SemaphoreType.DMA((len(flat) + 1,))],
@@ -369,8 +372,8 @@
         piece = chain.pin(piece)
         return [piece, swap(piece, 1)]
 
-    def product(chunks, first, total, split=()):
-        outs = multiply(chain, chunks, down_weight, first, total, split)
+    def product(chunks, first, total, split=(), cost=None):
+        outs = multiply(chain, chunks, down_weight, first, total, split, cost)
         return outs if split else outs[0]
 
     def sum_home(parts, away):
@@ -402,46 +405,48 @@
     far_0 = both_cores(far_0)
     far_1, far_2 = swap(early[0], 2), swap(early[1], 2)
 
-    total = product(near[:2], 0, None)
-    near = product(near[2:], ends[1], total, HALVES)
-    near = [near[0], shift(near[1], 1)]
-
+    total = product(near[:3], 0, None)
     far_1 = both_cores(far_1)
     far_3 = swap(chain.pin(early[2]), 2)
+    near = product(near[3:], ends[2], total, HALVES)
+    near = [near[0], shift(near[1], 1)]
+
     total = product([far_0, far_1], 0, None)
     far_2 = both_cores(far_2)
     late_0 = swap(chain.pin(late[0]), 2)
     near = sum_pair(near)
     total = product([far_2], ends[1], total)
     far_3 = both_cores(far_3)
-    late_1 = swap(chain.pin(late[1]), 2)
+    late_1, late_2 = swap(chain.pin(late[1]), 2), swap(chain.pin(late[2]), 2)
+    near = sum_home(near, 0)
     far = product([far_3], ends[2], total, HALVES)
     far = [far[0], shift(far[1], 1)]
-    near = sum_home(near, 0)
 
     late_0 = both_cores(late_0)
-    late_2 = swap(chain.pin(late[2]), 2)
     near = join(chain, *near)
     near = [near, shift(near, 2)]
     total = product([late_0], 0, None)
+    near.append(join(chain, *near))
+    near[2] = shift(near[2], 1)
     far = sum_pair(far)
     late_1 = both_cores(late_1)
     total = product([late_1], ends[1], total)
-    near.append(join(chain, *near))
-    near[2] = shift(near[2], 1)
+    near = [(near[0], 0), (near[2], 0), (near[1], 0), (near[2], 2)]
+    codes, scales = encode_columns(chain, None, None, near, 0, 0, out_width)
     far = sum_home(far, 2)
     late_2 = both_cores(late_2)
-    parts = product([late_2], ends[2], total, DIRECT)
-    parts = [parts[0]] + [shift(parts[flip], flip) for flip in range(1, tp)]
     far = join(chain, *far)
-    far = [far] + [shift(far, flip) for flip in range(1, tp)]
-    near = [(near[0], 0), (near[2], 0), (near[1], 0), (near[2], 2)]
-    codes, scales = encode_columns(chain, None, None, near, 0, 0, out_width)
-    last = sum_home(parts, 2)
+    far = [far, shift(far, 2)]
+    last = product([late_2], ends[2], total, HALVES)
+    last = [last[0], shift(last[1], 1)]
+    far.append(join(chain, *far))
+    far[2] = shift(far[2], 1)
+    last = sum_home(sum_pair(last), 2)
+    far = [(far[0], 0), (far[2], 0), (far[1], 0), (far[2], 2)]
+    codes, scales = encode_columns(chain, codes, scales, far, 2, 0, out_width)
     last = join(chain, *last)
     last = [last] + [shift(last, flip) for flip in range(1, tp)]
-    far, last = [(array, 0) for array in far], [(array, 0) for array in last]
-    codes, scales = encode_columns(chain, codes, scales, far, 2, 0, out_width)
+    last = [(array, 0) for array in last]
     codes, scales = encode_columns(chain, codes, scales, last, 2, cut, out_width)
     return codes, scales
 

time: 157 us -> 164 us (1.045)
  waiting for transfers between devices: 40 us -> 47.3 us
    ppermute x23, waiting for transfers between devices: 3.51 us -> 9.55 us  [swap(): lax.ppermute(value, 'batch', [(b, b ^ flip) for b in range(batch)])]
    ppermute x15 -> x13, waiting for transfers between devices: 36.5 us -> 37.8 us  [shift(): return lax.ppermute(value, 'tp', [(t, t ^ flip) for t in range(tp)])]
    ppermute x15 -> x13, starting transfers between devices: 23.4 us -> 22.2 us  [shift(): return lax.ppermute(value, 'tp', [(t, t ^ flip) for t in range(tp)])]
    pallas_call x33 -> x35, Pallas kernels: 78.5 us -> 78.7 us  [call(): pl.pallas_call(with_tokens, grid=grid, in_specs=list(in_specs) + [ANY] *...]
  transfers between devices with their start and end apart: 38 -> 36, of which waited for: 11 -> 16; matrix products, arithmetic and copies ran while one was open for 0% -> 0% of each run, Pallas kernels for 48% -> 46%
where the time goes in v4:
time: 164 us
  Pallas kernels  78.7 us (48%)
  waiting for transfers between devices  47.3 us (29%)
  starting transfers between devices  36 us (22%)
    pallas_call x35, Pallas kernels, call(): pl.pallas_call(with_tokens, grid=grid, in_specs=list(in_specs) + [ANY] *...  78.7 us
    ppermute x13, waiting for transfers between devices, shift(): return lax.ppermute(value, 'tp', [(t, t ^ flip) for t in range(tp)])  37.8 us
    ppermute x13, starting transfers between devices, shift(): return lax.ppermute(value, 'tp', [(t, t ^ flip) for t in range(tp)])  22.2 us
    ppermute x23, starting transfers between devices, swap(): lax.ppermute(value, 'batch', [(b, b ^ flip) for b in range(batch)])  13.8 us
    ppermute x23, waiting for transfers between devices, swap(): lax.ppermute(value, 'batch', [(b, b ^ flip) for b in range(batch)])  9.55 us
  transfers between devices with their start and end apart: 36, of which 16 were waited for; matrix products, arithmetic and copies ran while one was open for 0% of the time, Pallas kernels for 46%

profile of v4, /device:TPU:0, one launch (start us, length us, event | category | flops | bytes accessed | tf_op | source)
XLA Modules:
  0.0 163.7 jit_solution(21012398080913317)
XLA Ops:
  0.6 1.5 activate.2
  2.1 3.0 %collective-permute-start.4 = (bf16[80,1024]{1,0:T(8,128)(2,1)S(1)}, bf16[80,1024]{1,0:T(8,128)(2,1)S(1)}, u32[]{:S(2)}, u32[]{:S(2)}) collective-permute-start(bf16[80,1024]{1,0:T(8,128)(2,1)S(1)} %get-tuple-element.97), channel_id=1, source_target_pairs={{0,2},{1,3},{2,0},{3,1},{4,6},{5,7},{6,4},{7,5},{8,10},{9,11},{10,... | collective-permute-start | bytes 491528 | tf_op jit(solution)/shard_map/ppermute | solution.py:366
  5.1 5.5 %activate.3 = (bf16[128,4096]{1,0:T(8,128)(2,1)S(1)}, bf16[128,4096]{1,0:T(8,128)(2,1)S(1)}, bf16[128,4096]{1,0:T(8,128)(2,1)S(1)}, bf16[80,4096]{1,0:T(8,128)(2...) custom-call(bf16[128,13312]{1,0:T(8,128)(2,1)} %refs_0_.3, ...), custom_call_target="tpu_custom_call" | custom-call | flops 10000000000 | bytes 1024 | tf_op jit(solution)/shard_map/activate/pallas_call | solution.py:108
  10.7 0.5 collective-permute-start.3
  11.7 3.5 %collective-permute-done.1.refs_1_ = bf16[128,1024]{1,0:T(8,128)(2,1)S(1)} collective-permute-done((bf16[128,1024]{1,0:T(8,128)(2,1)S(1)}, bf16[128,1024]{1,0:T(8,128)(2,1)S(1)}, u32[]{:S(2)}, u32[]{:S(2)}) %collective-permute-start.1) | collective-permute-done | bytes 262176 | tf_op jit(solution)/shard_map/ppermute | solution.py:366
  15.3 14.9 %multiply.8 = (f32[256,2048]{1,0:T(8,128)S(1)}, f32[8,128]{1,0:T(8,128)S(1)}) custom-call(bf16[128,1024]{1,0:T(8,128)(2,1)S(1)} %get-tuple-element.94.refs_0_, bf16[128,1024]{1,0:T(8,128)(2,1)S(1)} %collective-permute-done.1.refs_1_, bf16[128,4096]{1,0:T(8,128)(2,1)S(1)} %get-tuple-element.95.refs_2_, bf16[128,4096]{1,0:T(8,128)(2,1)S(1)} %collective-permute-done.2.refs_3_, ...), custom_call_target="tpu_custom_call" | custom-call | flops 10000000000 | bytes 1024 | tf_op jit(solution)/shard_map/multiply/pallas_call | solution.py:108
  30.7 7.5 %multiply.9 = (bf16[2,256,512]{2,1,0:T(8,128)(2,1)S(1)}, bf16[2,256,512]{2,1,0:T(8,128)(2,1)S(1)}, f32[8,128]{1,0:T(8,128)S(1)}) custom-call(bf16[128,4096]{1,0:T(8,128)(2,1)S(1)} %get-tuple-element.93.refs_0_, bf16[128,4096]{1,0:T(8,128)(2,1)S(1)} %collective-permute-done.refs_1_, bf16[13312,2048]{1,0:T(8,128)(2,1)} %refs_2_.11, ...), custom_call_target="tpu_custom_call" | custom-call | flops 10000000000 | bytes 1024 | tf_op jit(solution)/shard_map/multiply/pallas_call | solution.py:108
  38.2 2.2 %collective-permute-start.6 = (bf16[2,256,512]{2,1,0:T(8,128)(2,1)S(1)}, bf16[2,256,512]{2,1,0:T(8,128)(2,1)S(1)}, u32[]{:S(2)}, u32[]{:S(2)}) collective-permute-start(bf16[2,256,512]{2,1,0:T(8,128)(2,1)S(1)} %get-tuple-element.107), channel_id=1, source_target_pairs={{0,4},{4,0},{8,12},{12,8},{1,5},{5,1},{9,13},{13,9},{2,6},{6,2},{1... | collective-permute-start | bytes 1572872 | tf_op jit(solution)/shard_map/ppermute | solution.py:369
  40.4 1.5 collective-permute-start.11
  41.9 7.9 %multiply.10 = (f32[160,2048]{1,0:T(8,128)S(1)}, f32[8,128]{1,0:T(8,128)S(1)}) custom-call(bf16[80,1024]{1,0:T(8,128)(2,1)S(1)} %get-tuple-element.110.refs_0_, bf16[80,1024]{1,0:T(8,128)(2,1)S(1)} %collective-permute-done.8.refs_1_, bf16[80,4096]{1,0:T(8,128)(2,1)S(1)} %get-tuple-element.111.refs_2_, bf16[80,4096]{1,0:T(8,128)(2,1)S(1)} %collective-permute-done.9.refs_3_, ...), custom_call_target="tpu_custom_call" | custom-call | flops 10000000000 | bytes 1024 | tf_op jit(solution)/shard_map/multiply/pallas_call | solution.py:108
  49.9 2.6 %collective-permute-done.6.refs_1_ = bf16[2,256,512]{2,1,0:T(8,128)(2,1)S(1)} collective-permute-done((bf16[2,256,512]{2,1,0:T(8,128)(2,1)S(1)}, bf16[2,256,512]{2,1,0:T(8,128)(2,1)S(1)}, u32[]{:S(2)}, u32[]{:S(2)}) %collective-permute-start.6) | collective-permute-done | bytes 524320 | tf_op jit(solution)/shard_map/ppermute | solution.py:369
  52.6 2.9 %collective-permute-start.10 = (bf16[1,256,512]{2,1,0:T(8,128)(2,1)S(1)}, bf16[1,256,512]{2,1,0:T(8,128)(2,1)S(1)}, u32[]{:S(2)}, u32[]{:S(2)}) collective-permute-start(bf16[1,256,512]{2,1,0:T(8,128)(2,1)S(1)} %get-tuple-element.117), channel_id=1, source_target_pairs={{0,8},{4,12},{8,0},{12,4},{1,9},{5,13},{9,1},{13,5},{2,10},{6,14},... | collective-permute-start | bytes 786440 | tf_op jit(solution)/shard_map/ppermute | solution.py:369
  55.5 1.4 collective-permute-start.14
  57.0 6.7 %multiply.11 = (f32[160,2048]{1,0:T(8,128)S(1)}, f32[8,128]{1,0:T(8,128)S(1)}) custom-call(bf16[80,4096]{1,0:T(8,128)(2,1)S(1)} %get-tuple-element.121.refs_0_, bf16[80,4096]{1,0:T(8,128)(2,1)S(1)} %collective-permute-done.12.refs_1_, bf16[13312,2048]{1,0:T(8,128)(2,1)} %refs_2_.11, f32[160,2048]{1,0:T(8,128)S(1)} %get-tuple-element.122.refs_3_, ...), custom_call_target="tpu_custom_call" | custom-call | flops 10000000000 | bytes 1024 | tf_op jit(solution)/shard_map/multiply/pallas_call | solution.py:108
  63.8 3.2 %collective-permute-done.10.refs_1_ = bf16[1,256,512]{2,1,0:T(8,128)(2,1)S(1)} collective-permute-done((bf16[1,256,512]{2,1,0:T(8,128)(2,1)S(1)}, bf16[1,256,512]{2,1,0:T(8,128)(2,1)S(1)}, u32[]{:S(2)}, u32[]{:S(2)}) %collective-permute-start.10) | collective-permute-done | bytes 262176 | tf_op jit(solution)/shard_map/ppermute | solution.py:369
  67.0 6.8 %multiply.12 = (bf16[2,160,512]{2,1,0:T(8,128)(2,1)S(1)}, bf16[2,160,512]{2,1,0:T(8,128)(2,1)S(1)}, f32[8,128]{1,0:T(8,128)S(1)}) custom-call(bf16[80,4096]{1,0:T(8,128)(2,1)S(1)} %get-tuple-element.131.refs_0_, bf16[80,4096]{1,0:T(8,128)(2,1)S(1)} %collective-permute-done.15.refs_1_, bf16[13312,2048]{1,0:T(8,128)(2,1)} %refs_2_.11, ...), custom_call_target="tpu_custom_call" | custom-call | flops 10000000000 | bytes 1024 | tf_op jit(solution)/shard_map/multiply/pallas_call | solution.py:108
  73.9 0.5 collective-permute-start.13
  74.4 1.4 collective-permute-start.19
  76.0 3.9 %collective-permute-start.20 = (bf16[2,160,512]{2,1,0:T(8,128)(2,1)S(1)}, bf16[2,160,512]{2,1,0:T(8,128)(2,1)S(1)}, u32[]{:S(2)}, u32[]{:S(2)}) collective-permute-start(bf16[2,160,512]{2,1,0:T(8,128)(2,1)S(1)} %get-tuple-element.143), channel_id=1, source_target_pairs={{0,4},{4,0},{8,12},{12,8},{1,5},{5,1},{9,13},{13,9},{2,6},{6,2},{1... | collective-permute-start | bytes 983048 | tf_op jit(solution)/shard_map/ppermute | solution.py:369
  80.0 7.8 %multiply.13 = (f32[96,2048]{1,0:T(8,128)S(1)}, f32[8,128]{1,0:T(8,128)S(1)}) custom-call(bf16[48,5120]{1,0:T(8,128)(2,1)S(1)} %get-tuple-element.137.refs_0_, bf16[48,5120]{1,0:T(8,128)(2,1)S(1)} %collective-permute-done.17.refs_1_, bf16[13312,2048]{1,0:T(8,128)(2,1)} %refs_2_.11, f32[8,128]{1,0:T(8,128)S(1)} %get-tuple-element.138.refs_3_), custom_call_target="tpu_custom_call" | custom-call | flops 10000000000 | bytes 1024 | tf_op jit(solution)/shard_map/multiply/pallas_call | solution.py:108
  87.8 3.2 %collective-permute-done.16.refs_1_.refs_2_ = bf16[2,128,512]{2,1,0:T(8,128)(2,1)S(1)} collective-permute-done((bf16[2,128,512]{2,1,0:T(8,128)(2,1)S(1)}, bf16[2,128,512]{2,1,0:T(8,128)(2,1)S(1)}, u32[]{:S(2)}, u32[]{:S(2)}) %collective-permute-start.16) | collective-permute-done | bytes 262176 | tf_op jit(solution)/shard_map/ppermute | solution.py:369
  91.0 1.4 collective-permute-done.20.refs_1_
  92.6 1.4 collective-permute-start.25
  94.1 3.0 %collective-permute-start.22 = (bf16[1,160,512]{2,1,0:T(8,128)(2,1)S(1)}, bf16[1,160,512]{2,1,0:T(8,128)(2,1)S(1)}, u32[]{:S(2)}, u32[]{:S(2)}) collective-permute-start(bf16[1,160,512]{2,1,0:T(8,128)(2,1)S(1)} %get-tuple-element.153), channel_id=1, source_target_pairs={{0,8},{4,12},{8,0},{12,4},{1,9},{5,13},{9,1},{13,5},{2,10},{6,14},... | collective-permute-start | bytes 491528 | tf_op jit(solution)/shard_map/ppermute | solution.py:369
  97.1 6.6 %multiply.14 = (f32[96,2048]{1,0:T(8,128)S(1)}, f32[8,128]{1,0:T(8,128)S(1)}) custom-call(bf16[48,4096]{1,0:T(8,128)(2,1)S(1)} %get-tuple-element.146.refs_0_, bf16[48,4096]{1,0:T(8,128)(2,1)S(1)} %collective-permute-done.21.refs_1_, bf16[13312,2048]{1,0:T(8,128)(2,1)} %refs_2_.11, f32[96,2048]{1,0:T(8,128)S(1)} %get-tuple-element.147.refs_3_, ...), custom_call_target="tpu_custom_call" | custom-call | flops 10000000000 | bytes 1024 | tf_op jit(solution)/shard_map/multiply/pallas_call | solution.py:108
  103.8 7.8 %collective-permute-done.18.refs_1_.refs_3_ = bf16[4,128,512]{2,1,0:T(8,128)(2,1)S(1)} collective-permute-done((bf16[4,128,512]{2,1,0:T(8,128)(2,1)S(1)}, bf16[4,128,512]{2,1,0:T(8,128)(2,1)S(1)}, u32[]{:S(2)}, u32[]{:S(2)}) %collective-permute-start.18) | collective-permute-done | bytes 524320 | tf_op jit(solution)/shard_map/ppermute | solution.py:369
  111.6 1.6 encode.3
  113.3 0.7 collective-permute-start.23
  114.1 1.1 collective-permute-start.24
  115.2 3.4 %collective-permute-done.23.refs_0_ = bf16[1,80,512]{2,1,0:T(8,128)(2,1)S(1)} collective-permute-done((bf16[1,80,512]{2,1,0:T(8,128)(2,1)S(1)}, bf16[1,80,512]{2,1,0:T(8,128)(2,1)S(1)}, u32[]{:S(2)}, u32[]{:S(2)}) %collective-permute-start.23) | collective-permute-done | bytes 81952 | tf_op jit(solution)/shard_map/ppermute | solution.py:366
  118.7 0.8 collective-permute-done.24.refs_1_
  119.5 0.6 collective-permute-start.26
  120.1 6.7 %multiply.15 = (bf16[2,96,512]{2,1,0:T(8,128)(2,1)S(1)}, bf16[2,96,512]{2,1,0:T(8,128)(2,1)S(1)}, f32[8,128]{1,0:T(8,128)S(1)}) custom-call(bf16[48,4096]{1,0:T(8,128)(2,1)S(1)} %get-tuple-element.161.refs_0_, bf16[48,4096]{1,0:T(8,128)(2,1)S(1)} %collective-permute-done.27.refs_1_, bf16[13312,2048]{1,0:T(8,128)(2,1)} %refs_2_.11, ...), custom_call_target="tpu_custom_call" | custom-call | flops 10000000000 | bytes 1024 | tf_op jit(solution)/shard_map/multiply/pallas_call | solution.py:108
  126.8 2.6 %collective-permute-start.29 = (bf16[2,96,512]{2,1,0:T(8,128)(2,1)S(1)}, bf16[2,96,512]{2,1,0:T(8,128)(2,1)S(1)}, u32[]{:S(2)}, u32[]{:S(2)}) collective-permute-start(bf16[2,96,512]{2,1,0:T(8,128)(2,1)S(1)} %get-tuple-element.167), channel_id=1, source_target_pairs={{0,4},{4,0},{8,12},{12,8},{1,5},{5,1},{9,13},{13,9},{2,6},{6,2},{1... | collective-permute-start | bytes 589832 | tf_op jit(solution)/shard_map/ppermute | solution.py:369
  129.4 0.8 collective-permute-done.26.refs_1_.refs_4_
  130.3 4.8 %collective-permute-done.29.refs_1_ = bf16[2,96,512]{2,1,0:T(8,128)(2,1)S(1)} collective-permute-done((bf16[2,96,512]{2,1,0:T(8,128)(2,1)S(1)}, bf16[2,96,512]{2,1,0:T(8,128)(2,1)S(1)}, u32[]{:S(2)}, u32[]{:S(2)}) %collective-permute-start.29) | collective-permute-done | bytes 196640 | tf_op jit(solution)/shard_map/ppermute | solution.py:369
  135.1 2.0 %collective-permute-start.30 = (bf16[1,96,512]{2,1,0:T(8,128)(2,1)S(1)}, bf16[1,96,512]{2,1,0:T(8,128)(2,1)S(1)}, u32[]{:S(2)}, u32[]{:S(2)}) collective-permute-start(bf16[1,96,512]{2,1,0:T(8,128)(2,1)S(1)} %get-tuple-element.170), channel_id=1, source_target_pairs={{0,8},{4,12},{8,0},{12,4},{1,9},{5,13},{9,1},{13,5},{2,10},{6,14},... | collective-permute-start | bytes 294920 | tf_op jit(solution)/shard_map/ppermute | solution.py:369
  137.2 5.6 %collective-permute-done.30.refs_1_ = bf16[1,96,512]{2,1,0:T(8,128)(2,1)S(1)} collective-permute-done((bf16[1,96,512]{2,1,0:T(8,128)(2,1)S(1)}, bf16[1,96,512]{2,1,0:T(8,128)(2,1)S(1)}, u32[]{:S(2)}, u32[]{:S(2)}) %collective-permute-start.30) | collective-permute-done | bytes 98336 | tf_op jit(solution)/shard_map/ppermute | solution.py:369
  142.8 0.6 collective-permute-start.31
  143.5 2.4 %encode.4 = (bf16[128,8192]{1,0:T(8,128)(2,1)}, bf16[128,64]{1,0:T(8,128)(2,1)S(1)}, f32[8,128]{1,0:T(8,128)S(1)}) custom-call(bf16[128,8192]{1,0:T(8,128)(2,1)} %get-tuple-element.150.refs_0_, bf16[128,64]{1,0:T(8,128)(2,1)S(1)} %get-tuple-element.151.refs_1_, ...), custom_call_target="tpu_custom_call", output_to_operand_aliasing={{0}: (0, {}), {1}: (1, {})} | custom-call | bytes 1024 | tf_op jit(solution)/shard_map/encode/pallas_call | solution.py:108
  146.0 1.5 collective-permute-done.31.refs_0_
  147.5 2.5 %collective-permute-start.33 = (bf16[2,48,512]{2,1,0:T(8,128)(2,1)S(1)}, bf16[2,48,512]{2,1,0:T(8,128)(2,1)S(1)}, u32[]{:S(2)}, u32[]{:S(2)}) collective-permute-start(bf16[2,48,512]{2,1,0:T(8,128)(2,1)S(1)} %get-tuple-element.178.refs_2_), channel_id=1, source_target_pairs={{0,4},{4,0},{8,12},{12,8},{1,5},{5,1},{9,13},{13,9},{2,6},{6,2},{1... | collective-permute-start | bytes 294920 | tf_op jit(solution)/shard_map/ppermute | solution.py:369
  150.1 1.0 collective-permute-start.34
  151.1 1.4 collective-permute-start.35
  152.5 0.8 collective-permute-done.33.refs_3_
  153.3 7.4 %collective-permute-done.34.refs_4_ = bf16[2,48,512]{2,1,0:T(8,128)(2,1)S(1)} collective-permute-done((bf16[2,48,512]{2,1,0:T(8,128)(2,1)S(1)}, bf16[2,48,512]{2,1,0:T(8,128)(2,1)S(1)}, u32[]{:S(2)}, u32[]{:S(2)}) %collective-permute-start.34) | collective-permute-done | bytes 98336 | tf_op jit(solution)/shard_map/ppermute | solution.py:369
  160.7 2.3 %encode.5 = (bf16[128,8192]{1,0:T(8,128)(2,1)}, bf16[128,64]{1,0:T(8,128)(2,1)S(1)}, f32[8,128]{1,0:T(8,128)}) custom-call(bf16[128,8192]{1,0:T(8,128)(2,1)} %get-tuple-element.173.refs_0_, bf16[128,64]{1,0:T(8,128)(2,1)S(1)} %get-tuple-element.174.refs_1_, ...), custom_call_target="tpu_custom_call", output_to_operand_aliasing={{0}: (0, {}), {1}: (1, {})} | custom-call | bytes 1024 | tf_op jit(solution)/shard_map/encode/pallas_call | solution.py:108
  163.0 0.7 copy.20
  (60 shorter events, 2.5 us)
Async XLA Ops:
  2.1 9.2 %collective-permute-start.4 = (bf16[80,1024]{1,0:T(8,128)(2,1)S(1)}, bf16[80,1024]{1,0:T(8,128)(2,1)S(1)}, u32[]{:S(2)}, u32[]{:S(2)}) collective-permute-start(bf16[80,1024]{1,0:T(8,128)(2,1)S(1)} %get-tuple-element.97), channel_id=1, source_target_pairs={{0,2},{1,3},{2,0},{3,1},{4,6},{5,7},{6,4},{7,5},{8,10},{9,11},{10,... | collective-permute-start | bytes 491528 | tf_op jit(solution)/shard_map/ppermute | solution.py:366
  10.6 4.6 %collective-permute-start.2 = (bf16[128,4096]{1,0:T(8,128)(2,1)S(1)}, bf16[128,4096]{1,0:T(8,128)(2,1)S(1)}, u32[]{:S(2)}, u32[]{:S(2)}) collective-permute-start(bf16[128,4096]{1,0:T(8,128)(2,1)S(1)} %get-tuple-element.95.refs_2_), channel_id=1, source_target_pairs={{0,1},{1,0},{2,3},{3,2},{4,5},{5,4},{6,7},{7,6},{8,9},{9,8},{10,11... | collective-permute-start | bytes 3145736 | tf_op jit(solution)/shard_map/ppermute | solution.py:366
  10.7 4.7 %collective-permute-start.3 = (bf16[128,4096]{1,0:T(8,128)(2,1)S(1)}, bf16[128,4096]{1,0:T(8,128)(2,1)S(1)}, u32[]{:S(2)}, u32[]{:S(2)}) collective-permute-start(bf16[128,4096]{1,0:T(8,128)(2,1)S(1)} %get-tuple-element.96.refs_4_), channel_id=1, source_target_pairs={{0,1},{1,0},{2,3},{3,2},{4,5},{5,4},{6,7},{7,6},{8,9},{9,8},{10,11... | collective-permute-start | bytes 3145736 | tf_op jit(solution)/shard_map/ppermute | solution.py:366
  11.2 4.0 %collective-permute-start.1 = (bf16[128,1024]{1,0:T(8,128)(2,1)S(1)}, bf16[128,1024]{1,0:T(8,128)(2,1)S(1)}, u32[]{:S(2)}, u32[]{:S(2)}) collective-permute-start(bf16[128,1024]{1,0:T(8,128)(2,1)S(1)} %get-tuple-element.94.refs_0_), channel_id=1, source_target_pairs={{0,1},{1,0},{2,3},{3,2},{4,5},{5,4},{6,7},{7,6},{8,9},{9,8},{10,11... | collective-permute-start | bytes 786440 | tf_op jit(solution)/shard_map/ppermute | solution.py:366
  11.2 19.0 %collective-permute-start.5 = (bf16[80,4096]{1,0:T(8,128)(2,1)S(1)}, bf16[80,4096]{1,0:T(8,128)(2,1)S(1)}, u32[]{:S(2)}, u32[]{:S(2)}) collective-permute-start(bf16[80,4096]{1,0:T(8,128)(2,1)S(1)} %get-tuple-element.102), channel_id=1, source_target_pairs={{0,2},{1,3},{2,0},{3,1},{4,6},{5,7},{6,4},{7,5},{8,10},{9,11},{10,... | collective-permute-start | bytes 1966088 | tf_op jit(solution)/shard_map/ppermute | solution.py:366
  11.3 19.4 %collective-permute-start = (bf16[128,4096]{1,0:T(8,128)(2,1)S(1)}, bf16[128,4096]{1,0:T(8,128)(2,1)S(1)}, u32[]{:S(2)}, u32[]{:S(2)}) collective-permute-start(bf16[128,4096]{1,0:T(8,128)(2,1)S(1)} %get-tuple-element.93.refs_0_), channel_id=1, source_target_pairs={{0,1},{1,0},{2,3},{3,2},{4,5},{5,4},{6,7},{7,6},{8,9},{9,8},{10,11... | collective-permute-start | bytes 3145736 | tf_op jit(solution)/shard_map/ppermute | solution.py:366
  15.2 34.6 %collective-permute-start.7 = (bf16[80,4096]{1,0:T(8,128)(2,1)S(1)}, bf16[80,4096]{1,0:T(8,128)(2,1)S(1)}, u32[]{:S(2)}, u32[]{:S(2)}) collective-permute-start(bf16[80,4096]{1,0:T(8,128)(2,1)S(1)} %get-tuple-element.109), channel_id=1, source_target_pairs={{0,2},{1,3},{2,0},{3,1},{4,6},{5,7},{6,4},{7,5},{8,10},{9,11},{10,... | collective-permute-start | bytes 1966088 | tf_op jit(solution)/shard_map/ppermute | solution.py:366
  15.2 26.7 %collective-permute-start.8 = (bf16[80,1024]{1,0:T(8,128)(2,1)S(1)}, bf16[80,1024]{1,0:T(8,128)(2,1)S(1)}, u32[]{:S(2)}, u32[]{:S(2)}) collective-permute-start(bf16[80,1024]{1,0:T(8,128)(2,1)S(1)} %get-tuple-element.110.refs_0_), channel_id=1, source_target_pairs={{0,1},{1,0},{2,3},{3,2},{4,5},{5,4},{6,7},{7,6},{8,9},{9,8},{10,11... | collective-permute-start | bytes 491528 | tf_op jit(solution)/shard_map/ppermute | solution.py:366
  30.3 11.6 %collective-permute-start.9 = (bf16[80,4096]{1,0:T(8,128)(2,1)S(1)}, bf16[80,4096]{1,0:T(8,128)(2,1)S(1)}, u32[]{:S(2)}, u32[]{:S(2)}) collective-permute-start(bf16[80,4096]{1,0:T(8,128)(2,1)S(1)} %get-tuple-element.111.refs_2_), channel_id=1, source_target_pairs={{0,1},{1,0},{2,3},{3,2},{4,5},{5,4},{6,7},{7,6},{8,9},{9,8},{10,11... | collective-permute-start | bytes 1966088 | tf_op jit(solution)/shard_map/ppermute | solution.py:366
  38.2 14.3 %collective-permute-start.6 = (bf16[2,256,512]{2,1,0:T(8,128)(2,1)S(1)}, bf16[2,256,512]{2,1,0:T(8,128)(2,1)S(1)}, u32[]{:S(2)}, u32[]{:S(2)}) collective-permute-start(bf16[2,256,512]{2,1,0:T(8,128)(2,1)S(1)} %get-tuple-element.107), channel_id=1, source_target_pairs={{0,4},{4,0},{8,12},{12,8},{1,5},{5,1},{9,13},{13,9},{2,6},{6,2},{1... | collective-permute-start | bytes 1572872 | tf_op jit(solution)/shard_map/ppermute | solution.py:369
  40.4 23.3 %collective-permute-start.11 = (bf16[80,4096]{1,0:T(8,128)(2,1)S(1)}, bf16[80,4096]{1,0:T(8,128)(2,1)S(1)}, u32[]{:S(2)}, u32[]{:S(2)}) collective-permute-start(bf16[80,4096]{1,0:T(8,128)(2,1)S(1)} %get-tuple-element.120), channel_id=1, source_target_pairs={{0,2},{1,3},{2,0},{3,1},{4,6},{5,7},{6,4},{7,5},{8,10},{9,11},{10,... | collective-permute-start | bytes 1966088 | tf_op jit(solution)/shard_map/ppermute | solution.py:366
  49.8 7.1 %collective-permute-start.12 = (bf16[80,4096]{1,0:T(8,128)(2,1)S(1)}, bf16[80,4096]{1,0:T(8,128)(2,1)S(1)}, u32[]{:S(2)}, u32[]{:S(2)}) collective-permute-start(bf16[80,4096]{1,0:T(8,128)(2,1)S(1)} %get-tuple-element.121.refs_0_), channel_id=1, source_target_pairs={{0,1},{1,0},{2,3},{3,2},{4,5},{5,4},{6,7},{7,6},{8,9},{9,8},{10,11... | collective-permute-start | bytes 1966088 | tf_op jit(solution)/shard_map/ppermute | solution.py:366
  52.6 14.3 %collective-permute-start.10 = (bf16[1,256,512]{2,1,0:T(8,128)(2,1)S(1)}, bf16[1,256,512]{2,1,0:T(8,128)(2,1)S(1)}, u32[]{:S(2)}, u32[]{:S(2)}) collective-permute-start(bf16[1,256,512]{2,1,0:T(8,128)(2,1)S(1)} %get-tuple-element.117), channel_id=1, source_target_pairs={{0,8},{4,12},{8,0},{12,4},{1,9},{5,13},{9,1},{13,5},{2,10},{6,14},... | collective-permute-start | bytes 786440 | tf_op jit(solution)/shard_map/ppermute | solution.py:369
  55.5 18.3 %collective-permute-start.14 = (bf16[48,5120]{1,0:T(8,128)(2,1)S(1)}, bf16[48,5120]{1,0:T(8,128)(2,1)S(1)}, u32[]{:S(2)}, u32[]{:S(2)}) collective-permute-start(bf16[48,5120]{1,0:T(8,128)(2,1)S(1)} %get-tuple-element.130), channel_id=1, source_target_pairs={{0,2},{1,3},{2,0},{3,1},{4,6},{5,7},{6,4},{7,5},{8,10},{9,11},{10,... | collective-permute-start | bytes 1474568 | tf_op jit(solution)/shard_map/ppermute | solution.py:366
  63.7 3.3 %collective-permute-start.15 = (bf16[80,4096]{1,0:T(8,128)(2,1)S(1)}, bf16[80,4096]{1,0:T(8,128)(2,1)S(1)}, u32[]{:S(2)}, u32[]{:S(2)}) collective-permute-start(bf16[80,4096]{1,0:T(8,128)(2,1)S(1)} %get-tuple-element.131.refs_0_), channel_id=1, source_target_pairs={{0,1},{1,0},{2,3},{3,2},{4,5},{5,4},{6,7},{7,6},{8,9},{9,8},{10,11... | collective-permute-start | bytes 1966088 | tf_op jit(solution)/shard_map/ppermute | solution.py:366
  73.8 6.1 %collective-permute-start.17 = (bf16[48,5120]{1,0:T(8,128)(2,1)S(1)}, bf16[48,5120]{1,0:T(8,128)(2,1)S(1)}, u32[]{:S(2)}, u32[]{:S(2)}) collective-permute-start(bf16[48,5120]{1,0:T(8,128)(2,1)S(1)} %get-tuple-element.137.refs_0_), channel_id=1, source_target_pairs={{0,1},{1,0},{2,3},{3,2},{4,5},{5,4},{6,7},{7,6},{8,9},{9,8},{10,11... | collective-permute-start | bytes 1474568 | tf_op jit(solution)/shard_map/ppermute | solution.py:366
  73.9 2.0 %collective-permute-start.13 = (bf16[1,128,512]{2,1,0:T(8,128)(2,1)S(1)}, bf16[1,128,512]{2,1,0:T(8,128)(2,1)S(1)}, u32[]{:S(2)}, u32[]{:S(2)}) collective-permute-start(bf16[1,128,512]{2,1,0:T(8,128)(2,1)S(1)} %get-tuple-element.129), channel_id=1, source_target_pairs={{0,1},{1,0},{2,3},{3,2},{4,5},{5,4},{6,7},{7,6},{8,9},{9,8},{10,11... | collective-permute-start | bytes 393224 | tf_op jit(solution)/shard_map/ppermute | solution.py:366
  74.4 18.2 %collective-permute-start.19 = (bf16[48,4096]{1,0:T(8,128)(2,1)S(1)}, bf16[48,4096]{1,0:T(8,128)(2,1)S(1)}, u32[]{:S(2)}, u32[]{:S(2)}) collective-permute-start(bf16[48,4096]{1,0:T(8,128)(2,1)S(1)} %get-tuple-element.141), channel_id=1, source_target_pairs={{0,2},{1,3},{2,0},{3,1},{4,6},{5,7},{6,4},{7,5},{8,10},{9,11},{10,... | collective-permute-start | bytes 1179656 | tf_op jit(solution)/shard_map/ppermute | solution.py:366
  76.0 15.0 %collective-permute-start.16 = (bf16[2,128,512]{2,1,0:T(8,128)(2,1)S(1)}, bf16[2,128,512]{2,1,0:T(8,128)(2,1)S(1)}, u32[]{:S(2)}, u32[]{:S(2)}) collective-permute-start(bf16[2,128,512]{2,1,0:T(8,128)(2,1)S(1)} %get-tuple-element.136.refs_0_), channel_id=1, source_target_pairs={{0,8},{4,12},{8,0},{12,4},{1,9},{5,13},{9,1},{13,5},{2,10},{6,14},... | collective-permute-start | bytes 786440 | tf_op jit(solution)/shard_map/ppermute | solution.py:369
  76.0 16.4 %collective-permute-start.20 = (bf16[2,160,512]{2,1,0:T(8,128)(2,1)S(1)}, bf16[2,160,512]{2,1,0:T(8,128)(2,1)S(1)}, u32[]{:S(2)}, u32[]{:S(2)}) collective-permute-start(bf16[2,160,512]{2,1,0:T(8,128)(2,1)S(1)} %get-tuple-element.143), channel_id=1, source_target_pairs={{0,4},{4,0},{8,12},{12,8},{1,5},{5,1},{9,13},{13,9},{2,6},{6,2},{1... | collective-permute-start | bytes 983048 | tf_op jit(solution)/shard_map/ppermute | solution.py:369
  92.6 4.5 %collective-permute-start.21 = (bf16[48,4096]{1,0:T(8,128)(2,1)S(1)}, bf16[48,4096]{1,0:T(8,128)(2,1)S(1)}, u32[]{:S(2)}, u32[]{:S(2)}) collective-permute-start(bf16[48,4096]{1,0:T(8,128)(2,1)S(1)} %get-tuple-element.146.refs_0_), channel_id=1, source_target_pairs={{0,1},{1,0},{2,3},{3,2},{4,5},{5,4},{6,7},{7,6},{8,9},{9,8},{10,11... | collective-permute-start | bytes 1179656 | tf_op jit(solution)/shard_map/ppermute | solution.py:366
  92.6 20.6 %collective-permute-start.25 = (bf16[48,4096]{1,0:T(8,128)(2,1)S(1)}, bf16[48,4096]{1,0:T(8,128)(2,1)S(1)}, u32[]{:S(2)}, u32[]{:S(2)}) collective-permute-start(bf16[48,4096]{1,0:T(8,128)(2,1)S(1)} %get-tuple-element.157), channel_id=1, source_target_pairs={{0,2},{1,3},{2,0},{3,1},{4,6},{5,7},{6,4},{7,5},{8,10},{9,11},{10,... | collective-permute-start | bytes 1179656 | tf_op jit(solution)/shard_map/ppermute | solution.py:366
  94.1 17.5 %collective-permute-start.18 = (bf16[4,128,512]{2,1,0:T(8,128)(2,1)S(1)}, bf16[4,128,512]{2,1,0:T(8,128)(2,1)S(1)}, u32[]{:S(2)}, u32[]{:S(2)}) collective-permute-start(bf16[4,128,512]{2,1,0:T(8,128)(2,1)S(1)} %get-tuple-element.140), channel_id=1, source_target_pairs={{0,4},{4,0},{8,12},{12,8},{1,5},{5,1},{9,13},{13,9},{2,6},{6,2},{1... | collective-permute-start | bytes 1572872 | tf_op jit(solution)/shard_map/ppermute | solution.py:369
  94.1 19.1 %collective-permute-start.22 = (bf16[1,160,512]{2,1,0:T(8,128)(2,1)S(1)}, bf16[1,160,512]{2,1,0:T(8,128)(2,1)S(1)}, u32[]{:S(2)}, u32[]{:S(2)}) collective-permute-start(bf16[1,160,512]{2,1,0:T(8,128)(2,1)S(1)} %get-tuple-element.153), channel_id=1, source_target_pairs={{0,8},{4,12},{8,0},{12,4},{1,9},{5,13},{9,1},{13,5},{2,10},{6,14},... | collective-permute-start | bytes 491528 | tf_op jit(solution)/shard_map/ppermute | solution.py:369
  113.3 6.8 %collective-permute-start.27 = (bf16[48,4096]{1,0:T(8,128)(2,1)S(1)}, bf16[48,4096]{1,0:T(8,128)(2,1)S(1)}, u32[]{:S(2)}, u32[]{:S(2)}) collective-permute-start(bf16[48,4096]{1,0:T(8,128)(2,1)S(1)} %get-tuple-element.161.refs_0_), channel_id=1, source_target_pairs={{0,1},{1,0},{2,3},{3,2},{4,5},{5,4},{6,7},{7,6},{8,9},{9,8},{10,11... | collective-permute-start | bytes 1179656 | tf_op jit(solution)/shard_map/ppermute | solution.py:366
  113.3 5.3 %collective-permute-start.23 = (bf16[1,80,512]{2,1,0:T(8,128)(2,1)S(1)}, bf16[1,80,512]{2,1,0:T(8,128)(2,1)S(1)}, u32[]{:S(2)}, u32[]{:S(2)}) collective-permute-start(bf16[1,80,512]{2,1,0:T(8,128)(2,1)S(1)} %get-tuple-element.155), channel_id=1, source_target_pairs={{0,2},{1,3},{2,0},{3,1},{4,6},{5,7},{6,4},{7,5},{8,10},{9,11},{10,... | collective-permute-start | bytes 245768 | tf_op jit(solution)/shard_map/ppermute | solution.py:366
  114.1 5.4 %collective-permute-start.24 = (bf16[1,80,512]{2,1,0:T(8,128)(2,1)S(1)}, bf16[1,80,512]{2,1,0:T(8,128)(2,1)S(1)}, u32[]{:S(2)}, u32[]{:S(2)}) collective-permute-start(bf16[1,80,512]{2,1,0:T(8,128)(2,1)S(1)} %get-tuple-element.156), channel_id=1, source_target_pairs={{0,3},{1,2},{2,1},{3,0},{4,7},{5,6},{6,5},{7,4},{8,11},{9,10},{10,... | collective-permute-start | bytes 245768 | tf_op jit(solution)/shard_map/ppermute | solution.py:366
  119.5 10.7 %collective-permute-start.26 = (bf16[2,80,512]{2,1,0:T(8,128)(2,1)S(1)}, bf16[2,80,512]{2,1,0:T(8,128)(2,1)S(1)}, u32[]{:S(2)}, u32[]{:S(2)}) collective-permute-start(bf16[2,80,512]{2,1,0:T(8,128)(2,1)S(1)} %get-tuple-element.160.refs_0_.refs_2_), channel_id=1, source_target_pairs={{0,8},{4,12},{8,0},{12,4},{1,9},{5,13},{9,1},{13,5},{2,10},{6,14},... | collective-permute-start | bytes 491528 | tf_op jit(solution)/shard_map/ppermute | solution.py:369
  126.8 8.3 %collective-permute-start.29 = (bf16[2,96,512]{2,1,0:T(8,128)(2,1)S(1)}, bf16[2,96,512]{2,1,0:T(8,128)(2,1)S(1)}, u32[]{:S(2)}, u32[]{:S(2)}) collective-permute-start(bf16[2,96,512]{2,1,0:T(8,128)(2,1)S(1)} %get-tuple-element.167), channel_id=1, source_target_pairs={{0,4},{4,0},{8,12},{12,8},{1,5},{5,1},{9,13},{13,9},{2,6},{6,2},{1... | collective-permute-start | bytes 589832 | tf_op jit(solution)/shard_map/ppermute | solution.py:369
  130.2 13.3 %collective-permute-start.28 = (bf16[4,80,512]{2,1,0:T(8,128)(2,1)S(1)}, bf16[4,80,512]{2,1,0:T(8,128)(2,1)S(1)}, u32[]{:S(2)}, u32[]{:S(2)}) collective-permute-start(bf16[4,80,512]{2,1,0:T(8,128)(2,1)S(1)} %get-tuple-element.165), channel_id=1, source_target_pairs={{0,4},{4,0},{8,12},{12,8},{1,5},{5,1},{9,13},{13,9},{2,6},{6,2},{1... | collective-permute-start | bytes 983048 | tf_op jit(solution)/shard_map/ppermute | solution.py:369
  135.1 7.7 %collective-permute-start.30 = (bf16[1,96,512]{2,1,0:T(8,128)(2,1)S(1)}, bf16[1,96,512]{2,1,0:T(8,128)(2,1)S(1)}, u32[]{:S(2)}, u32[]{:S(2)}) collective-permute-start(bf16[1,96,512]{2,1,0:T(8,128)(2,1)S(1)} %get-tuple-element.170), channel_id=1, source_target_pairs={{0,8},{4,12},{8,0},{12,4},{1,9},{5,13},{9,1},{13,5},{2,10},{6,14},... | collective-permute-start | bytes 294920 | tf_op jit(solution)/shard_map/ppermute | solution.py:369
  142.8 4.7 %collective-permute-start.31 = (bf16[1,48,512]{2,1,0:T(8,128)(2,1)S(1)}, bf16[1,48,512]{2,1,0:T(8,128)(2,1)S(1)}, u32[]{:S(2)}, u32[]{:S(2)}) collective-permute-start(bf16[1,48,512]{2,1,0:T(8,128)(2,1)S(1)} %get-tuple-element.175), channel_id=1, source_target_pairs={{0,2},{1,3},{2,0},{3,1},{4,6},{5,7},{6,4},{7,5},{8,10},{9,11},{10,... | collective-permute-start | bytes 147464 | tf_op jit(solution)/shard_map/ppermute | solution.py:366
  143.5 4.0 %collective-permute-start.32 = (bf16[1,48,512]{2,1,0:T(8,128)(2,1)S(1)}, bf16[1,48,512]{2,1,0:T(8,128)(2,1)S(1)}, u32[]{:S(2)}, u32[]{:S(2)}) collective-permute-start(bf16[1,48,512]{2,1,0:T(8,128)(2,1)S(1)} %get-tuple-element.176), channel_id=1, source_target_pairs={{0,3},{1,2},{2,1},{3,0},{4,7},{5,6},{6,5},{7,4},{8,11},{9,10},{10,... | collective-permute-start | bytes 147464 | tf_op jit(solution)/shard_map/ppermute | solution.py:366
  147.5 5.8 %collective-permute-start.33 = (bf16[2,48,512]{2,1,0:T(8,128)(2,1)S(1)}, bf16[2,48,512]{2,1,0:T(8,128)(2,1)S(1)}, u32[]{:S(2)}, u32[]{:S(2)}) collective-permute-start(bf16[2,48,512]{2,1,0:T(8,128)(2,1)S(1)} %get-tuple-element.178.refs_2_), channel_id=1, source_target_pairs={{0,4},{4,0},{8,12},{12,8},{1,5},{5,1},{9,13},{13,9},{2,6},{6,2},{1... | collective-permute-start | bytes 294920 | tf_op jit(solution)/shard_map/ppermute | solution.py:369
  150.1 10.6 %collective-permute-start.34 = (bf16[2,48,512]{2,1,0:T(8,128)(2,1)S(1)}, bf16[2,48,512]{2,1,0:T(8,128)(2,1)S(1)}, u32[]{:S(2)}, u32[]{:S(2)}) collective-permute-start(bf16[2,48,512]{2,1,0:T(8,128)(2,1)S(1)} %get-tuple-element.178.refs_2_), channel_id=1, source_target_pairs={{0,8},{4,12},{8,0},{12,4},{1,9},{5,13},{9,1},{13,5},{2,10},{6,14},... | collective-permute-start | bytes 294920 | tf_op jit(solution)/shard_map/ppermute | solution.py:369
  151.1 9.7 %collective-permute-start.35 = (bf16[2,48,512]{2,1,0:T(8,128)(2,1)S(1)}, bf16[2,48,512]{2,1,0:T(8,128)(2,1)S(1)}, u32[]{:S(2)}, u32[]{:S(2)}) collective-permute-start(bf16[2,48,512]{2,1,0:T(8,128)(2,1)S(1)} %get-tuple-element.178.refs_2_), channel_id=1, source_target_pairs={{0,12},{4,8},{8,4},{12,0},{1,13},{5,9},{9,5},{13,1},{2,14},{6,10},... | collective-permute-start | bytes 294920 | tf_op jit(solution)/shard_map/ppermute | solution.py:369

commit v5 on v4

--- a/solution.py
+++ b/solution.py
@@ -80,7 +80,7 @@
 
 
 ANY = pl.BlockSpec(memory_space=pl.ANY)
-WEIGHTS = {"activate": 10**10, "multiply": 10**10, "pin": 10**10, "add": 0, "join": 0, "encode": 0}
+WEIGHTS = {"activate": 10**10, "multiply": 10**10, "pin": 10**10, "add": 0, "join": 0, "encode": 0, "encode_near": 0}
 
 
 TOKEN = (8, 128)
@@ -180,11 +180,11 @@
     )
 
 
-def multiply(chain, chunks, weight, first, total, split, cost):
+def multiply(chain, chunks, weight, first, total, last, split):
     counts = [piece.shape[0] for piece in chunks[0]]
     rows, cols = sum(counts), weight.shape[1]
     width = sum(pieces[0].shape[1] for pieces in chunks)
-    steps, part = width // DEPTH, cols // sum(map(len, split or [(0,)]))
+    steps, part = width // DEPTH, cols // max(1, sum(map(len, split)))
     flat, col = [], 0
     for pieces in chunks:
         row = 0
@@ -197,6 +197,9 @@
     shapes = [jax.ShapeDtypeStruct((len(flips), rows, part), jnp.bfloat16) for flips in split]
     if not split:
         shapes = [jax.ShapeDtypeStruct((rows, cols), jnp.float32)]
+    if last and not split:
+        part = cols // lax.axis_size("tp")
+        shapes = [jax.ShapeDtypeStruct((cols // part, rows, part), jnp.bfloat16)]
 
     def body(*refs):
         piece_refs, weight_ref = refs[: len(flat)], refs[len(flat)]
@@ -243,6 +246,9 @@
             return carry
 
         lax.fori_loop(0, steps, step, 0)
+        if last and not split:
+            for t in range(cols // part):
+                outs[0][t] = sums[:, t * part : (t + 1) * part].astype(jnp.bfloat16)
         for out, flips in zip(outs, split):
             for n, flip in enumerate(flips):
                 at = pl.ds(pl.multiple_of((lax.axis_index("tp") ^ flip) * part, part), part)
@@ -255,14 +261,13 @@
         [pl.BlockSpec(memory_space=pltpu.VMEM)] * len(shapes),
         shapes,
         "multiply",
-        cost=cost,
         scratch=[pltpu.VMEM((rows, width), jnp.bfloat16), pltpu.VMEM((SLOTS, DEPTH, cols), jnp.bfloat16)]
-        + ([pltpu.VMEM((rows, cols), jnp.float32)] if split else [])
+        + ([pltpu.VMEM((rows, cols), jnp.float32)] if last else [])
         + [pltpu.SemaphoreType.DMA((SLOTS,)), pltpu.SemaphoreType.DMA((len(flat) + 1,))],
     )
 
 
-def add(chain, parts, outs):
+def add(chain, parts, outs, spec=None):
     count = len(parts)
 
     def body(*refs):
@@ -272,7 +277,8 @@
 
     vmem = pl.BlockSpec(memory_space=pltpu.VMEM)
     shapes = [jax.ShapeDtypeStruct((1, b - a, parts[0].shape[2]), jnp.bfloat16) for _, a, b in outs]
-    return chain.call(body, parts, [vmem] * count, [vmem] * len(outs), shapes, "add")
+    specs = [spec or vmem] * count
+    return chain.call(body, parts, specs, [vmem] * len(outs), shapes, "add", grid=(1,) if spec else ())
 
 
 def join(chain, first, second):
@@ -372,8 +378,8 @@
         piece = chain.pin(piece)
         return [piece, swap(piece, 1)]
 
-    def product(chunks, first, total, split=(), cost=None):
-        outs = multiply(chain, chunks, down_weight, first, total, split, cost)
+    def product(chunks, first, total, last=False, split=()):
+        outs = multiply(chain, chunks, down_weight, first, total, last, split)
         return outs if split else outs[0]
 
     def sum_home(parts, away):
@@ -390,58 +396,64 @@
         chain, gate_input, up_input, 0, FIRST, [(0, rows, 0, FIRST), (0, cut, 0, FIRST)]
     )
     far_0 = swap(send_0, 2)
-    pieces = activate(
+    near_1, early_1, late_0 = activate(
+        chain, gate_input, up_input, 0, ends[1], [(0, rows, *spans[1]), (0, cut, *spans[1]), (cut, rows, 0, ends[1])]
+    )
+    far_1 = swap(early_1, 2)
+    near = [[h, swap(h, 1)] for h in (near_0, near_1)]
+    far_0 = both_cores(far_0)
+    near_2, near_3, early_2, early_3, late_1, late_2 = activate(
         chain,
         gate_input,
         up_input,
-        0,
-        width // STEP,
-        [(0, rows, a, b) for a, b in spans[1:]]
-        + [(0, cut, a, b) for a, b in spans[1:]]
-        + [(cut, rows, a, b) for a, b in [(0, ends[1])] + spans[2:]],
-    )
-    near, early, late = [near_0] + pieces[:3], pieces[3:6], pieces[6:]
-    near = [[h, swap(h, 1)] for h in near]
-    far_0 = both_cores(far_0)
-    far_1, far_2 = swap(early[0], 2), swap(early[1], 2)
+        ends[1],
+        ends[3] - ends[1],
+        [(a, b, *span) for a, b in ((0, rows), (0, cut), (cut, rows)) for span in spans[2:]],
+    )
+    far_2 = swap(early_2, 2)
+    near = near + [[h, swap(h, 1)] for h in (near_2, near_3)]
 
     total = product(near[:3], 0, None)
     far_1 = both_cores(far_1)
-    far_3 = swap(chain.pin(early[2]), 2)
-    near = product(near[3:], ends[2], total, HALVES)
-    near = [near[0], shift(near[1], 1)]
+    far_3 = swap(chain.pin(early_3), 2)
+    near = product(near[3:], ends[2], total, True)
+    near = lax.psum_scatter(near, "tp", scatter_dimension=0, tiled=True)
 
     total = product([far_0, far_1], 0, None)
     far_2 = both_cores(far_2)
-    late_0 = swap(chain.pin(late[0]), 2)
-    near = sum_pair(near)
+    late_0 = swap(chain.pin(late_0), 2)
     total = product([far_2], ends[1], total)
     far_3 = both_cores(far_3)
-    late_1, late_2 = swap(chain.pin(late[1]), 2), swap(chain.pin(late[2]), 2)
-    near = sum_home(near, 0)
-    far = product([far_3], ends[2], total, HALVES)
+    late_1 = swap(chain.pin(late_1), 2)
+    far = product([far_3], ends[2], total, True, HALVES)
     far = [far[0], shift(far[1], 1)]
 
+    block = pl.BlockSpec(near.shape, lambda k: (0, 0, 0))
+    near, beside = add(chain, [near], [(0, 0, rows), (0, rows, 2 * rows)], block)
+    beside = swap(beside, 1)
+
     late_0 = both_cores(late_0)
-    near = join(chain, *near)
+    late_2 = swap(chain.pin(late_2), 2)
+    total = product([late_0], 0, None)
+    near = join(chain, near, beside)
     near = [near, shift(near, 2)]
-    total = product([late_0], 0, None)
-    near.append(join(chain, *near))
-    near[2] = shift(near[2], 1)
     far = sum_pair(far)
     late_1 = both_cores(late_1)
     total = product([late_1], ends[1], total)
-    near = [(near[0], 0), (near[2], 0), (near[1], 0), (near[2], 2)]
-    codes, scales = encode_columns(chain, None, None, near, 0, 0, out_width)
+    near.append(join(chain, *near))
+    near[2] = shift(near[2], 1)
     far = sum_home(far, 2)
     late_2 = both_cores(late_2)
     far = join(chain, *far)
     far = [far, shift(far, 2)]
-    last = product([late_2], ends[2], total, HALVES)
+    last = product([late_2], ends[2], total, True, HALVES)
     last = [last[0], shift(last[1], 1)]
     far.append(join(chain, *far))
     far[2] = shift(far[2], 1)
-    last = sum_home(sum_pair(last), 2)
+    near = [(near[0], 0), (near[2], 0), (near[1], 0), (near[2], 2)]
+    codes, scales = encode_columns(chain, None, None, near, 0, 0, out_width)
+    last = sum_pair(last)
+    last = sum_home(last, 2)
     far = [(far[0], 0), (far[2], 0), (far[1], 0), (far[2], 2)]
     codes, scales = encode_columns(chain, codes, scales, far, 2, 0, out_width)
     last = join(chain, *last)

time: 164 us -> 171 us (1.043)
  between operations: 0.96 us -> 14.4 us
  waiting for transfers between devices: 47.3 us -> 37.2 us
  local copies, waits for them, and re-layouts: 0.7 us -> 3.05 us
  Pallas kernels: 78.7 us -> 80.6 us
    ppermute x13 -> x11, waiting for transfers between devices: 37.8 us -> 28.2 us  [shift(): return lax.ppermute(value, 'tp', [(t, t ^ flip) for t in range(tp)])]
    ppermute x13 -> x11, starting transfers between devices: 22.2 us -> 19 us  [shift(): return lax.ppermute(value, 'tp', [(t, t ^ flip) for t in range(tp)])]
    ppermute x23, starting transfers between devices: 13.8 us -> 16.7 us  [swap(): lax.ppermute(value, 'batch', [(b, b ^ flip) for b in range(batch)])]
    unnamed x1 -> x11, local copies, waits for them, and re-layouts: 0.7 us -> 3.05 us
    pallas_call x35, Pallas kernels: 78.7 us -> 80.6 us  [call(): pl.pallas_call(with_tokens, grid=grid, in_specs=list(in_specs) + [ANY] *...]
  transfers between devices with their start and end apart: 36 -> 35, of which waited for: 16 -> 17; matrix products, arithmetic and copies ran while one was open for 0% -> 0% of each run, Pallas kernels for 46% -> 45%
where the time goes in v5:
time: 171 us
  Pallas kernels  80.6 us (47%)
  waiting for transfers between devices  37.2 us (22%)
  starting transfers between devices  35.7 us (21%)
  between operations  14.4 us (8%)
  local copies, waits for them, and re-layouts  3.05 us (2%)
    pallas_call x35, Pallas kernels, call(): pl.pallas_call(with_tokens, grid=grid, in_specs=list(in_specs) + [ANY] *...  80.6 us
    ppermute x11, waiting for transfers between devices, shift(): return lax.ppermute(value, 'tp', [(t, t ^ flip) for t in range(tp)])  28.2 us
    ppermute x11, starting transfers between devices, shift(): return lax.ppermute(value, 'tp', [(t, t ^ flip) for t in range(tp)])  19 us
    ppermute x23, starting transfers between devices, swap(): lax.ppermute(value, 'batch', [(b, b ^ flip) for b in range(batch)])  16.7 us
    ppermute x23, waiting for transfers between devices, swap(): lax.ppermute(value, 'batch', [(b, b ^ flip) for b in range(batch)])  8.73 us
  transfers between devices with their start and end apart: 35, of which 17 were waited for; matrix products, arithmetic and copies ran while one was open for 0% of the time, Pallas kernels for 45%

profile of v5, /device:TPU:0, one launch (start us, length us, event | category | flops | bytes accessed | tf_op | source)
XLA Modules:
  0.0 170.8 jit_solution(3672520727915231208)
XLA Ops:
  7.2 1.5 activate.3
  8.7 3.0 %collective-permute-start = (bf16[80,1024]{1,0:T(8,128)(2,1)S(1)}, bf16[80,1024]{1,0:T(8,128)(2,1)S(1)}, u32[]{:S(2)}, u32[]{:S(2)}) collective-permute-start(bf16[80,1024]{1,0:T(8,128)(2,1)S(1)} %get-tuple-element.89), channel_id=1, source_target_pairs={{0,2},{1,3},{2,0},{3,1},{4,6},{5,7},{6,4},{7,5},{8,10},{9,11},{10,... | collective-permute-start | bytes 491528 | tf_op jit(solution)/shard_map/ppermute | solution.py:372
  11.7 2.4 %activate.4 = (bf16[128,4096]{1,0:T(8,128)(2,1)S(1)}, bf16[80,4096]{1,0:T(8,128)(2,1)S(1)}, bf16[48,5120]{1,0:T(8,128)(2,1)S(1)}, f32[8,128]{1,0:T(8,128)S(1)}) custom-call(bf16[128,13312]{1,0:T(8,128)(2,1)} %refs_0_.5, bf16[128,13312]{1,0:T(8,128)(2,1)} %refs_1_.5, f32[8,128]{1,0:T(8,128)S(1)} %get-tuple-element.90.refs_2_), custom_call_target="tpu_custom_call" | custom-call | flops 10000000000 | bytes 1024 | tf_op jit(solution)/shard_map/activate/pallas_call | solution.py:108
  14.2 1.7 collective-permute-done.refs_0_
  15.9 4.0 %activate.5 = (bf16[128,4096]{1,0:T(8,128)(2,1)S(1)}, bf16[128,4096]{1,0:T(8,128)(2,1)S(1)}, bf16[80,4096]{1,0:T(8,128)(2,1)}, bf16[80,4096]{1,0:T(8,128)(2,1)},...) custom-call(bf16[128,13312]{1,0:T(8,128)(2,1)} %refs_0_.5, ...), custom_call_target="tpu_custom_call" | custom-call | flops 10000000000 | bytes 1024 | tf_op jit(solution)/shard_map/activate/pallas_call | solution.py:108
  20.0 0.5 collective-permute-start.2
  20.5 1.7 %collective-permute-start.5 = (bf16[80,4096]{1,0:T(8,128)(2,1)S(1)}, bf16[80,4096]{1,0:T(8,128)(2,1)S(1)}, u32[]{:S(2)}, u32[]{:S(2)}) collective-permute-start(bf16[80,4096]{1,0:T(8,128)(2,1)S(1)} %get-tuple-element.100), channel_id=1, source_target_pairs={{0,2},{1,3},{2,0},{3,1},{4,6},{5,7},{6,4},{7,5},{8,10},{9,11},{10,... | collective-permute-start | bytes 1966088 | tf_op jit(solution)/shard_map/ppermute | solution.py:372
  22.2 0.8 collective-permute-done.2.refs_1_
  23.1 1.8 %collective-permute-start.7 = (bf16[80,4096]{1,0:T(8,128)(2,1)}, bf16[80,4096]{1,0:T(8,128)(2,1)S(1)}, u32[]{:S(2)}, u32[]{:S(2)}) collective-permute-start(bf16[80,4096]{1,0:T(8,128)(2,1)} %get-tuple-element.106), channel_id=1, source_target_pairs={{0,2},{1,3},{2,0},{3,1},{4,6},{5,7},{6,4},{7,5},{8,10},{9,11},{10,... | collective-permute-start | bytes 1966088 | tf_op jit(solution)/shard_map/ppermute | solution.py:372
  24.9 14.9 %multiply.8 = (f32[256,2048]{1,0:T(8,128)S(1)}, f32[8,128]{1,0:T(8,128)S(1)}) custom-call(bf16[128,1024]{1,0:T(8,128)(2,1)S(1)} %get-tuple-element.94.refs_0_, bf16[128,1024]{1,0:T(8,128)(2,1)S(1)} %collective-permute-done.2.refs_1_, bf16[128,4096]{1,0:T(8,128)(2,1)S(1)} %get-tuple-element.95.refs_2_, bf16[128,4096]{1,0:T(8,128)(2,1)S(1)} %collective-permute-done.3.refs_3_, ...), custom_call_target="tpu_custom_call" | custom-call | flops 10000000000 | bytes 1024 | tf_op jit(solution)/shard_map/multiply/pallas_call | solution.py:108
  40.3 8.5 %multiply.9 = (bf16[4,256,512]{2,1,0:T(8,128)(2,1)}, f32[8,128]{1,0:T(8,128)S(1)}) custom-call(bf16[128,4096]{1,0:T(8,128)(2,1)S(1)} %get-tuple-element.93.refs_0_, bf16[128,4096]{1,0:T(8,128)(2,1)S(1)} %collective-permute-done.1.refs_1_, bf16[13312,2048]{1,0:T(8,128)(2,1)} %refs_2_.11, f32[256,2048]{1,0:T(8,128)S(1)} %get-tuple-element.98.refs_3_, ...), custom_call_target="tpu_custom_call" | custom-call | flops 10000000000 | bytes 1024 | tf_op jit(solution)/shard_map/multiply/pallas_call | solution.py:108
  48.9 7.9 %multiply.10 = (f32[160,2048]{1,0:T(8,128)S(1)}, f32[8,128]{1,0:T(8,128)S(1)}) custom-call(bf16[80,1024]{1,0:T(8,128)(2,1)S(1)} %get-tuple-element.107.refs_0_, bf16[80,1024]{1,0:T(8,128)(2,1)S(1)} %collective-permute-done.8.refs_1_, bf16[80,4096]{1,0:T(8,128)(2,1)S(1)} %get-tuple-element.108.refs_2_, bf16[80,4096]{1,0:T(8,128)(2,1)S(1)} %collective-permute-done.9.refs_3_, ...), custom_call_target="tpu_custom_call" | custom-call | flops 10000000000 | bytes 1024 | tf_op jit(solution)/shard_map/multiply/pallas_call | solution.py:108
  57.0 1.8 %collective-permute-start.13 = (bf16[48,5120]{1,0:T(8,128)(2,1)S(1)}, bf16[48,5120]{1,0:T(8,128)(2,1)S(1)}, u32[]{:S(2)}, u32[]{:S(2)}) collective-permute-start(bf16[48,5120]{1,0:T(8,128)(2,1)S(1)} %get-tuple-element.125), channel_id=1, source_target_pairs={{0,2},{1,3},{2,0},{3,1},{4,6},{5,7},{6,4},{7,5},{8,10},{9,11},{10,... | collective-permute-start | bytes 1474568 | tf_op jit(solution)/shard_map/ppermute | solution.py:372
  58.9 6.7 %multiply.11 = (f32[160,2048]{1,0:T(8,128)S(1)}, f32[8,128]{1,0:T(8,128)S(1)}) custom-call(bf16[80,4096]{1,0:T(8,128)(2,1)S(1)} %get-tuple-element.111.refs_0_, bf16[80,4096]{1,0:T(8,128)(2,1)S(1)} %collective-permute-done.10.refs_1_, bf16[13312,2048]{1,0:T(8,128)(2,1)} %refs_2_.11, f32[160,2048]{1,0:T(8,128)S(1)} %get-tuple-element.112.refs_3_, ...), custom_call_target="tpu_custom_call" | custom-call | flops 10000000000 | bytes 1024 | tf_op jit(solution)/shard_map/multiply/pallas_call | solution.py:108
  66.2 1.0 copy-done.4
  67.2 1.7 %collective-permute-start.16 = (bf16[48,4096]{1,0:T(8,128)(2,1)S(1)}, bf16[48,4096]{1,0:T(8,128)(2,1)S(1)}, u32[]{:S(2)}, u32[]{:S(2)}) collective-permute-start(bf16[48,4096]{1,0:T(8,128)(2,1)S(1)} %get-tuple-element.133), channel_id=1, source_target_pairs={{0,2},{1,3},{2,0},{3,1},{4,6},{5,7},{6,4},{7,5},{8,10},{9,11},{10,... | collective-permute-start | bytes 1179656 | tf_op jit(solution)/shard_map/ppermute | solution.py:372
  68.9 6.8 %multiply.12 = (bf16[2,160,512]{2,1,0:T(8,128)(2,1)S(1)}, bf16[2,160,512]{2,1,0:T(8,128)(2,1)S(1)}, f32[8,128]{1,0:T(8,128)S(1)}) custom-call(bf16[80,4096]{1,0:T(8,128)(2,1)S(1)} %get-tuple-element.117.refs_0_, bf16[80,4096]{1,0:T(8,128)(2,1)S(1)} %collective-permute-done.11.refs_1_, bf16[13312,2048]{1,0:T(8,128)(2,1)} %refs_2_.11, ...), custom_call_target="tpu_custom_call" | custom-call | flops 10000000000 | bytes 1024 | tf_op jit(solution)/shard_map/multiply/pallas_call | solution.py:108
  75.8 1.6 collective-permute-start.17
  77.6 0.9 copy-done
  79.6 1.0 collective-permute-done.14.refs_1_
  80.6 7.8 %multiply.13 = (f32[96,2048]{1,0:T(8,128)S(1)}, f32[8,128]{1,0:T(8,128)S(1)}) custom-call(bf16[48,5120]{1,0:T(8,128)(2,1)S(1)} %get-tuple-element.127.refs_0_, bf16[48,5120]{1,0:T(8,128)(2,1)S(1)} %collective-permute-done.14.refs_1_, bf16[13312,2048]{1,0:T(8,128)(2,1)} %refs_2_.11, f32[8,128]{1,0:T(8,128)S(1)} %get-tuple-element.130.refs_3_), custom_call_target="tpu_custom_call" | custom-call | flops 10000000000 | bytes 1024 | tf_op jit(solution)/shard_map/multiply/pallas_call | solution.py:108
  88.7 1.5 collective-permute-start.23
  90.3 1.9 %collective-permute-start.15 = (bf16[2,128,512]{2,1,0:T(8,128)(2,1)S(1)}, bf16[2,128,512]{2,1,0:T(8,128)(2,1)S(1)}, u32[]{:S(2)}, u32[]{:S(2)}) collective-permute-start(bf16[2,128,512]{2,1,0:T(8,128)(2,1)S(1)} %get-tuple-element.132.refs_0_), channel_id=1, source_target_pairs={{0,8},{4,12},{8,0},{12,4},{1,9},{5,13},{9,1},{13,5},{2,10},{6,14},... | collective-permute-start | bytes 786440 | tf_op jit(solution)/shard_map/ppermute | solution.py:375
  92.2 1.0 collective-permute-start.20
  93.2 6.6 %multiply.14 = (f32[96,2048]{1,0:T(8,128)S(1)}, f32[8,128]{1,0:T(8,128)S(1)}) custom-call(bf16[48,4096]{1,0:T(8,128)(2,1)S(1)} %get-tuple-element.138.refs_0_, bf16[48,4096]{1,0:T(8,128)(2,1)S(1)} %collective-permute-done.18.refs_1_, bf16[13312,2048]{1,0:T(8,128)(2,1)} %refs_2_.11, f32[96,2048]{1,0:T(8,128)S(1)} %get-tuple-element.139.refs_3_, ...), custom_call_target="tpu_custom_call" | custom-call | flops 10000000000 | bytes 1024 | tf_op jit(solution)/shard_map/multiply/pallas_call | solution.py:108
  99.9 8.0 %collective-permute-done.15.refs_1_.refs_2_ = bf16[2,128,512]{2,1,0:T(8,128)(2,1)S(1)} collective-permute-done((bf16[2,128,512]{2,1,0:T(8,128)(2,1)S(1)}, bf16[2,128,512]{2,1,0:T(8,128)(2,1)S(1)}, u32[]{:S(2)}, u32[]{:S(2)}) %collective-permute-start.15) | collective-permute-done | bytes 262176 | tf_op jit(solution)/shard_map/ppermute | solution.py:375
  107.9 3.4 %collective-permute-done.20.refs_1_ = bf16[1,160,512]{2,1,0:T(8,128)(2,1)S(1)} collective-permute-done((bf16[1,160,512]{2,1,0:T(8,128)(2,1)S(1)}, bf16[1,160,512]{2,1,0:T(8,128)(2,1)S(1)}, u32[]{:S(2)}, u32[]{:S(2)}) %collective-permute-start.20) | collective-permute-done | bytes 163872 | tf_op jit(solution)/shard_map/ppermute | solution.py:375
  111.5 1.0 collective-permute-start.21
  112.5 0.9 collective-permute-start.22
  113.3 3.4 %collective-permute-done.21.refs_0_ = bf16[1,80,512]{2,1,0:T(8,128)(2,1)S(1)} collective-permute-done((bf16[1,80,512]{2,1,0:T(8,128)(2,1)S(1)}, bf16[1,80,512]{2,1,0:T(8,128)(2,1)S(1)}, u32[]{:S(2)}, u32[]{:S(2)}) %collective-permute-start.21) | collective-permute-done | bytes 81952 | tf_op jit(solution)/shard_map/ppermute | solution.py:372
  116.8 0.8 collective-permute-done.22.refs_1_
  117.7 6.7 %multiply.15 = (bf16[2,96,512]{2,1,0:T(8,128)(2,1)S(1)}, bf16[2,96,512]{2,1,0:T(8,128)(2,1)S(1)}, f32[8,128]{1,0:T(8,128)S(1)}) custom-call(bf16[48,4096]{1,0:T(8,128)(2,1)S(1)} %get-tuple-element.152.refs_0_, bf16[48,4096]{1,0:T(8,128)(2,1)S(1)} %collective-permute-done.25.refs_1_, bf16[13312,2048]{1,0:T(8,128)(2,1)} %refs_2_.11, ...), custom_call_target="tpu_custom_call" | custom-call | flops 10000000000 | bytes 1024 | tf_op jit(solution)/shard_map/multiply/pallas_call | solution.py:108
  124.4 3.2 %collective-permute-start.27 = (bf16[2,96,512]{2,1,0:T(8,128)(2,1)S(1)}, bf16[2,96,512]{2,1,0:T(8,128)(2,1)S(1)}, u32[]{:S(2)}, u32[]{:S(2)}) collective-permute-start(bf16[2,96,512]{2,1,0:T(8,128)(2,1)S(1)} %get-tuple-element.161), channel_id=1, source_target_pairs={{0,4},{4,0},{8,12},{12,8},{1,5},{5,1},{9,13},{13,9},{2,6},{6,2},{1... | collective-permute-start | bytes 589832 | tf_op jit(solution)/shard_map/ppermute | solution.py:375
  127.6 1.5 collective-permute-done.24.refs_1_.refs_4_
  129.2 3.7 %collective-permute-start.26 = (bf16[4,80,512]{2,1,0:T(8,128)(2,1)S(1)}, bf16[4,80,512]{2,1,0:T(8,128)(2,1)S(1)}, u32[]{:S(2)}, u32[]{:S(2)}) collective-permute-start(bf16[4,80,512]{2,1,0:T(8,128)(2,1)S(1)} %get-tuple-element.159), channel_id=1, source_target_pairs={{0,4},{4,0},{8,12},{12,8},{1,5},{5,1},{9,13},{13,9},{2,6},{6,2},{1... | collective-permute-start | bytes 983048 | tf_op jit(solution)/shard_map/ppermute | solution.py:375
  132.9 1.6 encode.3
  134.5 1.3 collective-permute-done.27.refs_1_
  135.8 1.3 collective-permute-start.28
  137.1 5.0 %collective-permute-done.28.refs_1_ = bf16[1,96,512]{2,1,0:T(8,128)(2,1)S(1)} collective-permute-done((bf16[1,96,512]{2,1,0:T(8,128)(2,1)S(1)}, bf16[1,96,512]{2,1,0:T(8,128)(2,1)S(1)}, u32[]{:S(2)}, u32[]{:S(2)}) %collective-permute-start.28) | collective-permute-done | bytes 98336 | tf_op jit(solution)/shard_map/ppermute | solution.py:375
  142.2 1.0 collective-permute-start.29
  143.2 1.2 collective-permute-done.26.refs_3_.refs_5_
  144.4 2.4 %encode.4 = (bf16[128,8192]{1,0:T(8,128)(2,1)}, bf16[128,64]{1,0:T(8,128)(2,1)S(1)}, f32[8,128]{1,0:T(8,128)S(1)}) custom-call(bf16[128,8192]{1,0:T(8,128)(2,1)} %get-tuple-element.157.refs_0_, bf16[128,64]{1,0:T(8,128)(2,1)S(1)} %get-tuple-element.158.refs_1_, ...), custom_call_target="tpu_custom_call", output_to_operand_aliasing={{0}: (0, {}), {1}: (1, {})} | custom-call | bytes 1024 | tf_op jit(solution)/shard_map/encode/pallas_call | solution.py:108
  147.1 3.8 %collective-permute-start.31 = (bf16[2,48,512]{2,1,0:T(8,128)(2,1)S(1)}, bf16[2,48,512]{2,1,0:T(8,128)(2,1)S(1)}, u32[]{:S(2)}, u32[]{:S(2)}) collective-permute-start(bf16[2,48,512]{2,1,0:T(8,128)(2,1)S(1)} %get-tuple-element.172.refs_2_), channel_id=1, source_target_pairs={{0,4},{4,0},{8,12},{12,8},{1,5},{5,1},{9,13},{13,9},{2,6},{6,2},{1... | collective-permute-start | bytes 294920 | tf_op jit(solution)/shard_map/ppermute | solution.py:375
  150.9 2.4 %collective-permute-start.33 = (bf16[2,48,512]{2,1,0:T(8,128)(2,1)S(1)}, bf16[2,48,512]{2,1,0:T(8,128)(2,1)S(1)}, u32[]{:S(2)}, u32[]{:S(2)}) collective-permute-start(bf16[2,48,512]{2,1,0:T(8,128)(2,1)S(1)} %get-tuple-element.172.refs_2_), channel_id=1, source_target_pairs={{0,12},{4,8},{8,4},{12,0},{1,13},{5,9},{9,5},{13,1},{2,14},{6,10},... | collective-permute-start | bytes 294920 | tf_op jit(solution)/shard_map/ppermute | solution.py:375
  153.3 0.7 collective-permute-done.31.refs_3_
  154.1 7.0 %collective-permute-done.32.refs_4_ = bf16[2,48,512]{2,1,0:T(8,128)(2,1)S(1)} collective-permute-done((bf16[2,48,512]{2,1,0:T(8,128)(2,1)S(1)}, bf16[2,48,512]{2,1,0:T(8,128)(2,1)S(1)}, u32[]{:S(2)}, u32[]{:S(2)}) %collective-permute-start.32) | collective-permute-done | bytes 98336 | tf_op jit(solution)/shard_map/ppermute | solution.py:375
  161.0 2.3 %encode.5 = (bf16[128,8192]{1,0:T(8,128)(2,1)}, bf16[128,64]{1,0:T(8,128)(2,1)S(1)}, f32[8,128]{1,0:T(8,128)}) custom-call(bf16[128,8192]{1,0:T(8,128)(2,1)} %get-tuple-element.167.refs_0_, bf16[128,64]{1,0:T(8,128)(2,1)S(1)} %get-tuple-element.168.refs_1_, ...), custom_call_target="tpu_custom_call", output_to_operand_aliasing={{0}: (0, {}), {1}: (1, {})} | custom-call | bytes 1024 | tf_op jit(solution)/shard_map/encode/pallas_call | solution.py:108
  163.3 0.7 copy.20
  (69 shorter events, 3.9 us)
Async XLA Ops:
  7.2 70.5 %reduce-scatter.2.cloned.1.call-start = ((), (), s32[]{:S(2)}) async-start(), calls=%async_computation.1 | async-start | bytes 1310720 | tf_op jit(solution)/shard_map/reduce_scatter | solution.py:420
  8.7 7.2 %collective-permute-start = (bf16[80,1024]{1,0:T(8,128)(2,1)S(1)}, bf16[80,1024]{1,0:T(8,128)(2,1)S(1)}, u32[]{:S(2)}, u32[]{:S(2)}) collective-permute-start(bf16[80,1024]{1,0:T(8,128)(2,1)S(1)} %get-tuple-element.89), channel_id=1, source_target_pairs={{0,2},{1,3},{2,0},{3,1},{4,6},{5,7},{6,4},{7,5},{8,10},{9,11},{10,... | collective-permute-start | bytes 491528 | tf_op jit(solution)/shard_map/ppermute | solution.py:372
  14.1 9.0 %collective-permute-start.3 = (bf16[128,4096]{1,0:T(8,128)(2,1)S(1)}, bf16[128,4096]{1,0:T(8,128)(2,1)S(1)}, u32[]{:S(2)}, u32[]{:S(2)}) collective-permute-start(bf16[128,4096]{1,0:T(8,128)(2,1)S(1)} %get-tuple-element.95.refs_2_), channel_id=1, source_target_pairs={{0,1},{1,0},{2,3},{3,2},{4,5},{5,4},{6,7},{7,6},{8,9},{9,8},{10,11... | collective-permute-start | bytes 3145736 | tf_op jit(solution)/shard_map/ppermute | solution.py:372
  19.9 20.0 %copy-start.1 = (bf16[48,4096]{1,0:T(8,128)(2,1)}, bf16[48,4096]{1,0:T(8,128)(2,1)S(1)}, u32[]{:S(2)}) copy-start(bf16[48,4096]{1,0:T(8,128)(2,1)S(1)} %get-tuple-element.128.refs_0_) | copy-start | bytes 1179652
  19.9 20.0 %copy-start.3 = (bf16[48,4096]{1,0:T(8,128)(2,1)}, bf16[48,4096]{1,0:T(8,128)(2,1)S(1)}, u32[]{:S(2)}) copy-start(bf16[48,4096]{1,0:T(8,128)(2,1)S(1)} %get-tuple-element.119.refs_0_) | copy-start | bytes 1179652
  19.9 5.0 %collective-permute-start.4 = (bf16[128,4096]{1,0:T(8,128)(2,1)S(1)}, bf16[128,4096]{1,0:T(8,128)(2,1)S(1)}, u32[]{:S(2)}, u32[]{:S(2)}) collective-permute-start(bf16[128,4096]{1,0:T(8,128)(2,1)S(1)} %get-tuple-element.96.refs_4_), channel_id=1, source_target_pairs={{0,1},{1,0},{2,3},{3,2},{4,5},{5,4},{6,7},{7,6},{8,9},{9,8},{10,11... | collective-permute-start | bytes 3145736 | tf_op jit(solution)/shard_map/ppermute | solution.py:372
  20.0 3.0 %collective-permute-start.2 = (bf16[128,1024]{1,0:T(8,128)(2,1)S(1)}, bf16[128,1024]{1,0:T(8,128)(2,1)S(1)}, u32[]{:S(2)}, u32[]{:S(2)}) collective-permute-start(bf16[128,1024]{1,0:T(8,128)(2,1)S(1)} %get-tuple-element.94.refs_0_), channel_id=1, source_target_pairs={{0,1},{1,0},{2,3},{3,2},{4,5},{5,4},{6,7},{7,6},{8,9},{9,8},{10,11... | collective-permute-start | bytes 786440 | tf_op jit(solution)/shard_map/ppermute | solution.py:372
  20.5 19.4 %collective-permute-start.5 = (bf16[80,4096]{1,0:T(8,128)(2,1)S(1)}, bf16[80,4096]{1,0:T(8,128)(2,1)S(1)}, u32[]{:S(2)}, u32[]{:S(2)}) collective-permute-start(bf16[80,4096]{1,0:T(8,128)(2,1)S(1)} %get-tuple-element.100), channel_id=1, source_target_pairs={{0,2},{1,3},{2,0},{3,1},{4,6},{5,7},{6,4},{7,5},{8,10},{9,11},{10,... | collective-permute-start | bytes 1966088 | tf_op jit(solution)/shard_map/ppermute | solution.py:372
  22.2 18.1 %collective-permute-start.1 = (bf16[128,4096]{1,0:T(8,128)(2,1)S(1)}, bf16[128,4096]{1,0:T(8,128)(2,1)S(1)}, u32[]{:S(2)}, u32[]{:S(2)}) collective-permute-start(bf16[128,4096]{1,0:T(8,128)(2,1)S(1)} %get-tuple-element.93.refs_0_), channel_id=1, source_target_pairs={{0,1},{1,0},{2,3},{3,2},{4,5},{5,4},{6,7},{7,6},{8,9},{9,8},{10,11... | collective-permute-start | bytes 3145736 | tf_op jit(solution)/shard_map/ppermute | solution.py:372
  23.0 25.8 %collective-permute-start.8 = (bf16[80,1024]{1,0:T(8,128)(2,1)S(1)}, bf16[80,1024]{1,0:T(8,128)(2,1)S(1)}, u32[]{:S(2)}, u32[]{:S(2)}) collective-permute-start(bf16[80,1024]{1,0:T(8,128)(2,1)S(1)} %get-tuple-element.107.refs_0_), channel_id=1, source_target_pairs={{0,1},{1,0},{2,3},{3,2},{4,5},{5,4},{6,7},{7,6},{8,9},{9,8},{10,11... | collective-permute-start | bytes 491528 | tf_op jit(solution)/shard_map/ppermute | solution.py:372
  23.1 33.6 %collective-permute-start.7 = (bf16[80,4096]{1,0:T(8,128)(2,1)}, bf16[80,4096]{1,0:T(8,128)(2,1)S(1)}, u32[]{:S(2)}, u32[]{:S(2)}) collective-permute-start(bf16[80,4096]{1,0:T(8,128)(2,1)} %get-tuple-element.106), channel_id=1, source_target_pairs={{0,2},{1,3},{2,0},{3,1},{4,6},{5,7},{6,4},{7,5},{8,10},{9,11},{10,... | collective-permute-start | bytes 1966088 | tf_op jit(solution)/shard_map/ppermute | solution.py:372
  39.9 9.0 %collective-permute-start.9 = (bf16[80,4096]{1,0:T(8,128)(2,1)S(1)}, bf16[80,4096]{1,0:T(8,128)(2,1)S(1)}, u32[]{:S(2)}, u32[]{:S(2)}) collective-permute-start(bf16[80,4096]{1,0:T(8,128)(2,1)S(1)} %get-tuple-element.108.refs_2_), channel_id=1, source_target_pairs={{0,1},{1,0},{2,3},{3,2},{4,5},{5,4},{6,7},{7,6},{8,9},{9,8},{10,11... | collective-permute-start | bytes 1966088 | tf_op jit(solution)/shard_map/ppermute | solution.py:372
  40.0 26.1 %collective-permute-start.6 = (bf16[80,4096]{1,0:T(8,128)(2,1)}, bf16[80,4096]{1,0:T(8,128)(2,1)S(1)}, u32[]{:S(2)}, u32[]{:S(2)}) collective-permute-start(bf16[80,4096]{1,0:T(8,128)(2,1)} %get-tuple-element.105), channel_id=1, source_target_pairs={{0,2},{1,3},{2,0},{3,1},{4,6},{5,7},{6,4},{7,5},{8,10},{9,11},{10,... | collective-permute-start | bytes 1966088 | tf_op jit(solution)/shard_map/ppermute | solution.py:372
  56.8 2.2 %collective-permute-start.10 = (bf16[80,4096]{1,0:T(8,128)(2,1)S(1)}, bf16[80,4096]{1,0:T(8,128)(2,1)S(1)}, u32[]{:S(2)}, u32[]{:S(2)}) collective-permute-start(bf16[80,4096]{1,0:T(8,128)(2,1)S(1)} %get-tuple-element.111.refs_0_), channel_id=1, source_target_pairs={{0,1},{1,0},{2,3},{3,2},{4,5},{5,4},{6,7},{7,6},{8,9},{9,8},{10,11... | collective-permute-start | bytes 1966088 | tf_op jit(solution)/shard_map/ppermute | solution.py:372
  57.0 21.6 %collective-permute-start.13 = (bf16[48,5120]{1,0:T(8,128)(2,1)S(1)}, bf16[48,5120]{1,0:T(8,128)(2,1)S(1)}, u32[]{:S(2)}, u32[]{:S(2)}) collective-permute-start(bf16[48,5120]{1,0:T(8,128)(2,1)S(1)} %get-tuple-element.125), channel_id=1, source_target_pairs={{0,2},{1,3},{2,0},{3,1},{4,6},{5,7},{6,4},{7,5},{8,10},{9,11},{10,... | collective-permute-start | bytes 1474568 | tf_op jit(solution)/shard_map/ppermute | solution.py:372
  66.2 1.0 copy-start.4
  66.2 2.7 %collective-permute-start.11 = (bf16[80,4096]{1,0:T(8,128)(2,1)S(1)}, bf16[80,4096]{1,0:T(8,128)(2,1)S(1)}, u32[]{:S(2)}, u32[]{:S(2)}) collective-permute-start(bf16[80,4096]{1,0:T(8,128)(2,1)S(1)} %get-tuple-element.117.refs_0_), channel_id=1, source_target_pairs={{0,1},{1,0},{2,3},{3,2},{4,5},{5,4},{6,7},{7,6},{8,9},{9,8},{10,11... | collective-permute-start | bytes 1966088 | tf_op jit(solution)/shard_map/ppermute | solution.py:372
  67.2 21.4 %collective-permute-start.16 = (bf16[48,4096]{1,0:T(8,128)(2,1)S(1)}, bf16[48,4096]{1,0:T(8,128)(2,1)S(1)}, u32[]{:S(2)}, u32[]{:S(2)}) collective-permute-start(bf16[48,4096]{1,0:T(8,128)(2,1)S(1)} %get-tuple-element.133), channel_id=1, source_target_pairs={{0,2},{1,3},{2,0},{3,1},{4,6},{5,7},{6,4},{7,5},{8,10},{9,11},{10,... | collective-permute-start | bytes 1179656 | tf_op jit(solution)/shard_map/ppermute | solution.py:372
  75.8 12.7 %collective-permute-start.17 = (bf16[2,160,512]{2,1,0:T(8,128)(2,1)S(1)}, bf16[2,160,512]{2,1,0:T(8,128)(2,1)S(1)}, u32[]{:S(2)}, u32[]{:S(2)}) collective-permute-start(bf16[2,160,512]{2,1,0:T(8,128)(2,1)S(1)} %get-tuple-element.135), channel_id=1, source_target_pairs={{0,4},{4,0},{8,12},{12,8},{1,5},{5,1},{9,13},{13,9},{2,6},{6,2},{1... | collective-permute-start | bytes 983048 | tf_op jit(solution)/shard_map/ppermute | solution.py:375
  77.6 0.9 copy-start
  78.6 1.0 copy-start.2
  78.6 1.9 %collective-permute-start.14 = (bf16[48,5120]{1,0:T(8,128)(2,1)S(1)}, bf16[48,5120]{1,0:T(8,128)(2,1)S(1)}, u32[]{:S(2)}, u32[]{:S(2)}) collective-permute-start(bf16[48,5120]{1,0:T(8,128)(2,1)S(1)} %get-tuple-element.127.refs_0_), channel_id=1, source_target_pairs={{0,1},{1,0},{2,3},{3,2},{4,5},{5,4},{6,7},{7,6},{8,9},{9,8},{10,11... | collective-permute-start | bytes 1474568 | tf_op jit(solution)/shard_map/ppermute | solution.py:372
  78.7 9.7 %collective-permute-start.12 = (bf16[1,128,512]{2,1,0:T(8,128)(2,1)S(1)}, bf16[1,128,512]{2,1,0:T(8,128)(2,1)S(1)}, u32[]{:S(2)}, u32[]{:S(2)}) collective-permute-start(bf16[1,128,512]{2,1,0:T(8,128)(2,1)S(1)} %get-tuple-element.124), channel_id=1, source_target_pairs={{0,1},{1,0},{2,3},{3,2},{4,5},{5,4},{6,7},{7,6},{8,9},{9,8},{10,11... | collective-permute-start | bytes 393224 | tf_op jit(solution)/shard_map/ppermute | solution.py:372
  88.5 4.7 %collective-permute-start.18 = (bf16[48,4096]{1,0:T(8,128)(2,1)S(1)}, bf16[48,4096]{1,0:T(8,128)(2,1)S(1)}, u32[]{:S(2)}, u32[]{:S(2)}) collective-permute-start(bf16[48,4096]{1,0:T(8,128)(2,1)S(1)} %get-tuple-element.138.refs_0_), channel_id=1, source_target_pairs={{0,1},{1,0},{2,3},{3,2},{4,5},{5,4},{6,7},{7,6},{8,9},{9,8},{10,11... | collective-permute-start | bytes 1179656 | tf_op jit(solution)/shard_map/ppermute | solution.py:372
  88.7 22.6 %collective-permute-start.23 = (bf16[48,4096]{1,0:T(8,128)(2,1)S(1)}, bf16[48,4096]{1,0:T(8,128)(2,1)S(1)}, u32[]{:S(2)}, u32[]{:S(2)}) collective-permute-start(bf16[48,4096]{1,0:T(8,128)(2,1)S(1)} %get-tuple-element.148), channel_id=1, source_target_pairs={{0,2},{1,3},{2,0},{3,1},{4,6},{5,7},{6,4},{7,5},{8,10},{9,11},{10,... | collective-permute-start | bytes 1179656 | tf_op jit(solution)/shard_map/ppermute | solution.py:372
  90.3 17.6 %collective-permute-start.15 = (bf16[2,128,512]{2,1,0:T(8,128)(2,1)S(1)}, bf16[2,128,512]{2,1,0:T(8,128)(2,1)S(1)}, u32[]{:S(2)}, u32[]{:S(2)}) collective-permute-start(bf16[2,128,512]{2,1,0:T(8,128)(2,1)S(1)} %get-tuple-element.132.refs_0_), channel_id=1, source_target_pairs={{0,8},{4,12},{8,0},{12,4},{1,9},{5,13},{9,1},{13,5},{2,10},{6,14},... | collective-permute-start | bytes 786440 | tf_op jit(solution)/shard_map/ppermute | solution.py:375
  92.2 19.1 %collective-permute-start.20 = (bf16[1,160,512]{2,1,0:T(8,128)(2,1)S(1)}, bf16[1,160,512]{2,1,0:T(8,128)(2,1)S(1)}, u32[]{:S(2)}, u32[]{:S(2)}) collective-permute-start(bf16[1,160,512]{2,1,0:T(8,128)(2,1)S(1)} %get-tuple-element.144), channel_id=1, source_target_pairs={{0,8},{4,12},{8,0},{12,4},{1,9},{5,13},{9,1},{13,5},{2,10},{6,14},... | collective-permute-start | bytes 491528 | tf_op jit(solution)/shard_map/ppermute | solution.py:375
  111.4 6.3 %collective-permute-start.25 = (bf16[48,4096]{1,0:T(8,128)(2,1)S(1)}, bf16[48,4096]{1,0:T(8,128)(2,1)S(1)}, u32[]{:S(2)}, u32[]{:S(2)}) collective-permute-start(bf16[48,4096]{1,0:T(8,128)(2,1)S(1)} %get-tuple-element.152.refs_0_), channel_id=1, source_target_pairs={{0,1},{1,0},{2,3},{3,2},{4,5},{5,4},{6,7},{7,6},{8,9},{9,8},{10,11... | collective-permute-start | bytes 1179656 | tf_op jit(solution)/shard_map/ppermute | solution.py:372
  111.5 5.3 %collective-permute-start.21 = (bf16[1,80,512]{2,1,0:T(8,128)(2,1)S(1)}, bf16[1,80,512]{2,1,0:T(8,128)(2,1)S(1)}, u32[]{:S(2)}, u32[]{:S(2)}) collective-permute-start(bf16[1,80,512]{2,1,0:T(8,128)(2,1)S(1)} %get-tuple-element.146), channel_id=1, source_target_pairs={{0,2},{1,3},{2,0},{3,1},{4,6},{5,7},{6,4},{7,5},{8,10},{9,11},{10,... | collective-permute-start | bytes 245768 | tf_op jit(solution)/shard_map/ppermute | solution.py:372
  112.5 5.2 %collective-permute-start.22 = (bf16[1,80,512]{2,1,0:T(8,128)(2,1)S(1)}, bf16[1,80,512]{2,1,0:T(8,128)(2,1)S(1)}, u32[]{:S(2)}, u32[]{:S(2)}) collective-permute-start(bf16[1,80,512]{2,1,0:T(8,128)(2,1)S(1)} %get-tuple-element.147), channel_id=1, source_target_pairs={{0,3},{1,2},{2,1},{3,0},{4,7},{5,6},{6,5},{7,4},{8,11},{9,10},{10,... | collective-permute-start | bytes 245768 | tf_op jit(solution)/shard_map/ppermute | solution.py:372
  113.3 19.5 %collective-permute-start.19 = (bf16[4,128,512]{2,1,0:T(8,128)(2,1)S(1)}, bf16[4,128,512]{2,1,0:T(8,128)(2,1)S(1)}, u32[]{:S(2)}, u32[]{:S(2)}) collective-permute-start(bf16[4,128,512]{2,1,0:T(8,128)(2,1)S(1)} %get-tuple-element.142), channel_id=1, source_target_pairs={{0,4},{4,0},{8,12},{12,8},{1,5},{5,1},{9,13},{13,9},{2,6},{6,2},{1... | collective-permute-start | bytes 1572872 | tf_op jit(solution)/shard_map/ppermute | solution.py:375
  117.6 11.5 %collective-permute-start.24 = (bf16[2,80,512]{2,1,0:T(8,128)(2,1)S(1)}, bf16[2,80,512]{2,1,0:T(8,128)(2,1)S(1)}, u32[]{:S(2)}, u32[]{:S(2)}) collective-permute-start(bf16[2,80,512]{2,1,0:T(8,128)(2,1)S(1)} %get-tuple-element.151.refs_0_.refs_2_), channel_id=1, source_target_pairs={{0,8},{4,12},{8,0},{12,4},{1,9},{5,13},{9,1},{13,5},{2,10},{6,14},... | collective-permute-start | bytes 491528 | tf_op jit(solution)/shard_map/ppermute | solution.py:375
  124.4 11.4 %collective-permute-start.27 = (bf16[2,96,512]{2,1,0:T(8,128)(2,1)S(1)}, bf16[2,96,512]{2,1,0:T(8,128)(2,1)S(1)}, u32[]{:S(2)}, u32[]{:S(2)}) collective-permute-start(bf16[2,96,512]{2,1,0:T(8,128)(2,1)S(1)} %get-tuple-element.161), channel_id=1, source_target_pairs={{0,4},{4,0},{8,12},{12,8},{1,5},{5,1},{9,13},{13,9},{2,6},{6,2},{1... | collective-permute-start | bytes 589832 | tf_op jit(solution)/shard_map/ppermute | solution.py:375
  129.2 15.2 %collective-permute-start.26 = (bf16[4,80,512]{2,1,0:T(8,128)(2,1)S(1)}, bf16[4,80,512]{2,1,0:T(8,128)(2,1)S(1)}, u32[]{:S(2)}, u32[]{:S(2)}) collective-permute-start(bf16[4,80,512]{2,1,0:T(8,128)(2,1)S(1)} %get-tuple-element.159), channel_id=1, source_target_pairs={{0,4},{4,0},{8,12},{12,8},{1,5},{5,1},{9,13},{13,9},{2,6},{6,2},{1... | collective-permute-start | bytes 983048 | tf_op jit(solution)/shard_map/ppermute | solution.py:375
  135.8 6.3 %collective-permute-start.28 = (bf16[1,96,512]{2,1,0:T(8,128)(2,1)S(1)}, bf16[1,96,512]{2,1,0:T(8,128)(2,1)S(1)}, u32[]{:S(2)}, u32[]{:S(2)}) collective-permute-start(bf16[1,96,512]{2,1,0:T(8,128)(2,1)S(1)} %get-tuple-element.164), channel_id=1, source_target_pairs={{0,8},{4,12},{8,0},{12,4},{1,9},{5,13},{9,1},{13,5},{2,10},{6,14},... | collective-permute-start | bytes 294920 | tf_op jit(solution)/shard_map/ppermute | solution.py:375
  142.2 4.6 %collective-permute-start.29 = (bf16[1,48,512]{2,1,0:T(8,128)(2,1)S(1)}, bf16[1,48,512]{2,1,0:T(8,128)(2,1)S(1)}, u32[]{:S(2)}, u32[]{:S(2)}) collective-permute-start(bf16[1,48,512]{2,1,0:T(8,128)(2,1)S(1)} %get-tuple-element.169), channel_id=1, source_target_pairs={{0,2},{1,3},{2,0},{3,1},{4,6},{5,7},{6,4},{7,5},{8,10},{9,11},{10,... | collective-permute-start | bytes 147464 | tf_op jit(solution)/shard_map/ppermute | solution.py:372
  143.2 3.9 %collective-permute-start.30 = (bf16[1,48,512]{2,1,0:T(8,128)(2,1)S(1)}, bf16[1,48,512]{2,1,0:T(8,128)(2,1)S(1)}, u32[]{:S(2)}, u32[]{:S(2)}) collective-permute-start(bf16[1,48,512]{2,1,0:T(8,128)(2,1)S(1)} %get-tuple-element.170), channel_id=1, source_target_pairs={{0,3},{1,2},{2,1},{3,0},{4,7},{5,6},{6,5},{7,4},{8,11},{9,10},{10,... | collective-permute-start | bytes 147464 | tf_op jit(solution)/shard_map/ppermute | solution.py:372
  147.1 6.9 %collective-permute-start.31 = (bf16[2,48,512]{2,1,0:T(8,128)(2,1)S(1)}, bf16[2,48,512]{2,1,0:T(8,128)(2,1)S(1)}, u32[]{:S(2)}, u32[]{:S(2)}) collective-permute-start(bf16[2,48,512]{2,1,0:T(8,128)(2,1)S(1)} %get-tuple-element.172.refs_2_), channel_id=1, source_target_pairs={{0,4},{4,0},{8,12},{12,8},{1,5},{5,1},{9,13},{13,9},{2,6},{6,2},{1... | collective-permute-start | bytes 294920 | tf_op jit(solution)/shard_map/ppermute | solution.py:375
  150.9 10.1 %collective-permute-start.32 = (bf16[2,48,512]{2,1,0:T(8,128)(2,1)S(1)}, bf16[2,48,512]{2,1,0:T(8,128)(2,1)S(1)}, u32[]{:S(2)}, u32[]{:S(2)}) collective-permute-start(bf16[2,48,512]{2,1,0:T(8,128)(2,1)S(1)} %get-tuple-element.172.refs_2_), channel_id=1, source_target_pairs={{0,8},{4,12},{8,0},{12,4},{1,9},{5,13},{9,1},{13,5},{2,10},{6,14},... | collective-permute-start | bytes 294920 | tf_op jit(solution)/shard_map/ppermute | solution.py:375
  150.9 10.1 %collective-permute-start.33 = (bf16[2,48,512]{2,1,0:T(8,128)(2,1)S(1)}, bf16[2,48,512]{2,1,0:T(8,128)(2,1)S(1)}, u32[]{:S(2)}, u32[]{:S(2)}) collective-permute-start(bf16[2,48,512]{2,1,0:T(8,128)(2,1)S(1)} %get-tuple-element.172.refs_2_), channel_id=1, source_target_pairs={{0,12},{4,8},{8,4},{12,0},{1,13},{5,9},{9,5},{13,1},{2,14},{6,10},... | collective-permute-start | bytes 294920 | tf_op jit(solution)/shard_map/ppermute | solution.py:375
Sparse Core Ops, SparseCore 0:
  49.0 28.6 reduce-scatter.1

commit v6 on v4

--- a/solution.py
+++ b/solution.py
@@ -17,6 +17,7 @@
 SLOTS = 6
 TILE = 512
 EARLY = 5
+LANES = 128
 VMEM = 32 * 2**20
 
 
@@ -122,7 +123,7 @@
         self.tokens = [outs[-1]]
         return list(outs[:-1])
 
-    def pin(self, value):
+    def pin(self, value, cost=None):
         pinned = self.call(
             lambda *refs: None,
             [value],
@@ -131,6 +132,7 @@
             [jax.ShapeDtypeStruct(value.shape, value.dtype)],
             "pin",
             aliases={0: 0},
+            cost=cost,
         )
         return pinned[0]
 
@@ -298,54 +300,60 @@
     return scales
 
 
-def encode_columns(chain, codes, scales, shares, away, start, width):
+def encode_columns(chain, codes, scales, shares, away, start, height, width, last=False):
     rows, part = shares[0][0].shape[1:]
     tp = len(shares)
-    blocks = part // BLOCK
-    at = slice(start, start + rows)
-    height = start + rows if codes is None else codes.shape[0]
+    blocks, spread = part // BLOCK, tp * part
     given = [] if codes is None else [codes, scales]
 
     def body(*refs):
         share_refs = refs[len(given) : len(given) + tp]
-        code_ref, scale_ref = refs[len(given) + tp :]
-        j = pl.program_id(0)
-
-        @pl.when(j == 0)
-        def _():
-            scale_ref[...] = refs[1][...] if given else jnp.zeros(scale_ref.shape, scale_ref.dtype)
-
-        if given:
-            code_ref[...] = refs[0][...]
-        total = scale_ref[at].astype(jnp.float32)
-        for flip in range(tp):
-            t = lax.axis_index("tp") ^ flip
-
-            def store(n, value, t=t):
-                code_ref[at, pl.ds(pl.multiple_of((t * blocks + n) * BLOCK, BLOCK), BLOCK)] = value
-
-            first = ((lax.axis_index("batch") ^ (j + away)) * tp + t) * blocks
-            total = encode_blocks(share_refs[flip][...], store, total, first)
-        scale_ref[at] = total.astype(jnp.bfloat16)
-
-    whole = pl.BlockSpec((height, width // BLOCK), lambda j: (0, 0))
-    columns = pl.BlockSpec((height, tp * part), lambda j: (0, lax.axis_index("batch") ^ (j + away)))
-
-    def share_spec(n):
-        return pl.BlockSpec((None, rows, part), lambda j: (n + j, 0, 0))
-
+        code_ref, scale_ref, buffer, table, sems = refs[len(given) + tp :]
+        table[...] = refs[1][...] if given else jnp.zeros(table.shape, table.dtype)
+        total = table[start : start + rows]
+        copies = []
+        for j in range(2):
+            place = lax.axis_index("batch") ^ (j + away)
+            for flip, (ref, (_, n)) in enumerate(zip(share_refs, shares)):
+                t = lax.axis_index("tp") ^ flip
+
+                def store(m, value):
+                    at = pl.ds(pl.multiple_of((t * blocks + m) * BLOCK, BLOCK), BLOCK)
+                    buffer[j, :, at] = value
+
+                total = encode_blocks(ref[n + j], store, total, (place * tp + t) * blocks)
+            columns = pl.ds(pl.multiple_of(place * spread, spread), spread)
+            copy = pltpu.make_async_copy(
+                buffer.at[j], code_ref.at[pl.ds(start, rows), columns], sems.at[j]
+            )
+            copy.start()
+            copies.append(copy)
+        table[start : start + rows] = total
+        if last:
+            scale_ref[...] = table[...].T[: width // BLOCK].astype(jnp.bfloat16)
+        else:
+            scale_ref[...] = table[...]
+        for copy in copies:
+            copy.wait()
+
+    vmem = pl.BlockSpec(memory_space=pltpu.VMEM)
+    kept = jax.ShapeDtypeStruct((height, LANES), jnp.float32)
     return chain.call(
         body,
         given + [array for array, _ in shares],
-        [columns, whole][: len(given)] + [share_spec(n) for _, n in shares],
-        [columns, whole],
+        [ANY, vmem][: len(given)] + [vmem] * tp,
+        [ANY, vmem],
         [
             jax.ShapeDtypeStruct((height, width), jnp.bfloat16),
-            jax.ShapeDtypeStruct((height, width // BLOCK), jnp.bfloat16),
+            jax.ShapeDtypeStruct((width // BLOCK, height), jnp.bfloat16) if last else kept,
         ],
         "encode",
-        grid=(2,),
-        aliases={0: 0, 1: 1} if given else {},
+        scratch=[
+            pltpu.VMEM((2, rows, spread), jnp.bfloat16),
+            pltpu.VMEM((height, LANES), jnp.float32),
+            pltpu.SemaphoreType.DMA((2,)),
+        ],
+        aliases={0: 0} if given else {},
     )
 
 
@@ -368,8 +376,8 @@
     def shift(value, flip):
         return lax.ppermute(value, "tp", [(t, t ^ flip) for t in range(tp)])
 
-    def both_cores(piece):
-        piece = chain.pin(piece)
+    def both_cores(piece, cost=None):
+        piece = chain.pin(piece, cost)
         return [piece, swap(piece, 1)]
 
     def product(chunks, first, total, split=(), cost=None):
@@ -405,12 +413,12 @@
     far_0 = both_cores(far_0)
     far_1, far_2 = swap(early[0], 2), swap(early[1], 2)
 
-    total = product(near[:3], 0, None)
+    total = product(near[:2], 0, None)
+    near = product(near[2:], ends[1], total, HALVES)
+    near = [near[0], shift(near[1], 1)]
+
     far_1 = both_cores(far_1)
     far_3 = swap(chain.pin(early[2]), 2)
-    near = product(near[3:], ends[2], total, HALVES)
-    near = [near[0], shift(near[1], 1)]
-
     total = product([far_0, far_1], 0, None)
     far_2 = both_cores(far_2)
     late_0 = swap(chain.pin(late[0]), 2)
@@ -418,9 +426,9 @@
     total = product([far_2], ends[1], total)
     far_3 = both_cores(far_3)
     late_1, late_2 = swap(chain.pin(late[1]), 2), swap(chain.pin(late[2]), 2)
-    near = sum_home(near, 0)
     far = product([far_3], ends[2], total, HALVES)
     far = [far[0], shift(far[1], 1)]
+    near = sum_home(near, 0)
 
     late_0 = both_cores(late_0)
     near = join(chain, *near)
@@ -431,31 +439,32 @@
     far = sum_pair(far)
     late_1 = both_cores(late_1)
     total = product([late_1], ends[1], total)
+    late_2 = both_cores(late_2, 0)
+    last = product([late_2], ends[2], total, HALVES, cost=0)
+    last = [last[0], shift(last[1], 1)]
+    far = sum_home(far, 2)
     near = [(near[0], 0), (near[2], 0), (near[1], 0), (near[2], 2)]
-    codes, scales = encode_columns(chain, None, None, near, 0, 0, out_width)
-    far = sum_home(far, 2)
-    late_2 = both_cores(late_2)
+    codes, scales = encode_columns(chain, None, None, near, 0, 0, rows, out_width)
+    last = sum_pair(last)
     far = join(chain, *far)
     far = [far, shift(far, 2)]
-    last = product([late_2], ends[2], total, HALVES)
-    last = [last[0], shift(last[1], 1)]
+    last = sum_home(last, 2)
     far.append(join(chain, *far))
     far[2] = shift(far[2], 1)
-    last = sum_home(sum_pair(last), 2)
-    far = [(far[0], 0), (far[2], 0), (far[1], 0), (far[2], 2)]
-    codes, scales = encode_columns(chain, codes, scales, far, 2, 0, out_width)
     last = join(chain, *last)
     last = [last] + [shift(last, flip) for flip in range(1, tp)]
+    far = [(far[0], 0), (far[2], 0), (far[1], 0), (far[2], 2)]
+    codes, scales = encode_columns(chain, codes, scales, far, 2, 0, rows, out_width)
     last = [(array, 0) for array in last]
-    codes, scales = encode_columns(chain, codes, scales, last, 2, cut, out_width)
-    return codes, scales
+    codes, scales = encode_columns(chain, codes, scales, last, 2, cut, rows, out_width, True)
+    return codes, scales.T
 
 
 def solution(mesh):
     def shards(gate_input, up_input, down_weight):
         tp, batch = mesh.shape["tp"], mesh.shape["batch"]
         width, cols = down_weight.shape
-        paired = batch == tp == 4 and cols % (tp * TILE) == 0 and width == (FIRST + 3 * PIECE) * STEP
+        paired = batch == tp == 4 and batch * cols <= LANES * BLOCK and cols % (tp * TILE) == 0 and width == (FIRST + 3 * PIECE) * STEP
         return (paired_shards if paired else general_shards)(gate_input, up_input, down_weight)
 
     in_specs = (P(("groups", "batch"), "tp"), P(("groups", "batch"), "tp"), P("tp", "batch"))

time: 164 us -> 158 us (0.963)
  starting transfers between devices: 36 us -> 32.3 us
  Pallas kernels: 78.7 us -> 76.8 us
    ppermute x13, starting transfers between devices: 22.2 us -> 19 us  [shift(): return lax.ppermute(value, 'tp', [(t, t ^ flip) for t in range(tp)])]
    ppermute x13, waiting for transfers between devices: 37.8 us -> 35.6 us  [shift(): return lax.ppermute(value, 'tp', [(t, t ^ flip) for t in range(tp)])]
    ppermute x23, waiting for transfers between devices: 9.55 us -> 11.5 us  [swap(): lax.ppermute(value, 'batch', [(b, b ^ flip) for b in range(batch)])]
    pallas_call x35, Pallas kernels: 78.7 us -> 76.8 us  [call(): pl.pallas_call(with_tokens, grid=grid, in_specs=list(in_specs) + [ANY] *...]
  transfers between devices with their start and end apart: 36 -> 36, of which waited for: 16 -> 15; matrix products, arithmetic and copies ran while one was open for 0% -> 0% of each run, Pallas kernels for 46% -> 47%
where the time goes in v6:
time: 158 us; the launch traced here: 157 us
  Pallas kernels  76.8 us (49%)
  waiting for transfers between devices  47.1 us (30%)
  starting transfers between devices  32.3 us (20%)
    pallas_call x35, Pallas kernels, call(): pl.pallas_call(with_tokens, grid=grid, in_specs=list(in_specs) + [ANY] *...  76.8 us
    ppermute x13, waiting for transfers between devices, shift(): return lax.ppermute(value, 'tp', [(t, t ^ flip) for t in range(tp)])  35.6 us
    ppermute x13, starting transfers between devices, shift(): return lax.ppermute(value, 'tp', [(t, t ^ flip) for t in range(tp)])  19 us
    ppermute x23, starting transfers between devices, swap(): lax.ppermute(value, 'batch', [(b, b ^ flip) for b in range(batch)])  13.3 us
    ppermute x23, waiting for transfers between devices, swap(): lax.ppermute(value, 'batch', [(b, b ^ flip) for b in range(batch)])  11.5 us
  transfers between devices with their start and end apart: 36, of which 15 were waited for; matrix products, arithmetic and copies ran while one was open for 0% of the time, Pallas kernels for 47%

profile of v6, /device:TPU:0, one launch (start us, length us, event | category | flops | bytes accessed | tf_op | source)
XLA Modules:
  0.0 157.4 jit_solution(5039353699432097667)
XLA Ops:
  0.6 1.5 activate.2
  2.1 3.0 %collective-permute-start.4 = (bf16[80,1024]{1,0:T(8,128)(2,1)S(1)}, bf16[80,1024]{1,0:T(8,128)(2,1)S(1)}, u32[]{:S(2)}, u32[]{:S(2)}) collective-permute-start(bf16[80,1024]{1,0:T(8,128)(2,1)S(1)} %get-tuple-element.97), channel_id=1, source_target_pairs={{0,2},{1,3},{2,0},{3,1},{4,6},{5,7},{6,4},{7,5},{8,10},{9,11},{10,... | collective-permute-start | bytes 491528 | tf_op jit(solution)/shard_map/ppermute | solution.py:374
  5.1 5.5 %activate.3 = (bf16[128,4096]{1,0:T(8,128)(2,1)S(1)}, bf16[128,4096]{1,0:T(8,128)(2,1)S(1)}, bf16[128,4096]{1,0:T(8,128)(2,1)S(1)}, bf16[80,4096]{1,0:T(8,128)(2...) custom-call(bf16[128,13312]{1,0:T(8,128)(2,1)} %refs_0_.3, ...), custom_call_target="tpu_custom_call" | custom-call | flops 10000000000 | bytes 1024 | tf_op jit(solution)/shard_map/activate/pallas_call | solution.py:109
  10.7 0.5 collective-permute-start.2
  11.2 0.4 collective-permute-start.1
  11.7 2.0 %collective-permute-done.2.refs_1_ = bf16[128,1024]{1,0:T(8,128)(2,1)S(1)} collective-permute-done((bf16[128,1024]{1,0:T(8,128)(2,1)S(1)}, bf16[128,1024]{1,0:T(8,128)(2,1)S(1)}, u32[]{:S(2)}, u32[]{:S(2)}) %collective-permute-start.2) | collective-permute-done | bytes 262176 | tf_op jit(solution)/shard_map/ppermute | solution.py:374
  13.8 9.0 %multiply.8 = (f32[256,2048]{1,0:T(8,128)S(1)}, f32[8,128]{1,0:T(8,128)S(1)}) custom-call(bf16[128,1024]{1,0:T(8,128)(2,1)S(1)} %get-tuple-element.95.refs_0_, bf16[128,1024]{1,0:T(8,128)(2,1)S(1)} %collective-permute-done.2.refs_1_, bf16[128,4096]{1,0:T(8,128)(2,1)S(1)} %get-tuple-element.96.refs_2_, bf16[128,4096]{1,0:T(8,128)(2,1)S(1)} %collective-permute-done.3.refs_3_, ...), custom_call_target="tpu_custom_call" | custom-call | flops 10000000000 | bytes 1024 | tf_op jit(solution)/shard_map/multiply/pallas_call | solution.py:109
  22.9 13.3 %multiply.9 = (bf16[2,256,512]{2,1,0:T(8,128)(2,1)S(1)}, bf16[2,256,512]{2,1,0:T(8,128)(2,1)S(1)}, f32[8,128]{1,0:T(8,128)S(1)}) custom-call(bf16[128,4096]{1,0:T(8,128)(2,1)S(1)} %get-tuple-element.93.refs_0_, bf16[128,4096]{1,0:T(8,128)(2,1)S(1)} %collective-permute-done.refs_1_, bf16[128,4096]{1,0:T(8,128)(2,1)S(1)} %get-tuple-element.94.refs_2_, ...), custom_call_target="tpu_custom_call" | custom-call | flops 10000000000 | bytes 1024 | tf_op jit(solution)/shard_map/multiply/pallas_call | solution.py:109
  36.3 0.4 collective-permute-start.9
  36.7 2.1 %collective-permute-start.5 = (bf16[2,256,512]{2,1,0:T(8,128)(2,1)S(1)}, bf16[2,256,512]{2,1,0:T(8,128)(2,1)S(1)}, u32[]{:S(2)}, u32[]{:S(2)}) collective-permute-start(bf16[2,256,512]{2,1,0:T(8,128)(2,1)S(1)} %get-tuple-element.103), channel_id=1, source_target_pairs={{0,4},{4,0},{8,12},{12,8},{1,5},{5,1},{9,13},{13,9},{2,6},{6,2},{1... | collective-permute-start | bytes 1572872 | tf_op jit(solution)/shard_map/ppermute | solution.py:377
  38.8 1.5 collective-permute-start.11
  40.3 7.9 %multiply.10 = (f32[160,2048]{1,0:T(8,128)S(1)}, f32[8,128]{1,0:T(8,128)S(1)}) custom-call(bf16[80,1024]{1,0:T(8,128)(2,1)S(1)} %get-tuple-element.106.refs_0_, bf16[80,1024]{1,0:T(8,128)(2,1)S(1)} %collective-permute-done.7.refs_1_, bf16[80,4096]{1,0:T(8,128)(2,1)S(1)} %get-tuple-element.109.refs_2_, bf16[80,4096]{1,0:T(8,128)(2,1)S(1)} %collective-permute-done.9.refs_3_, ...), custom_call_target="tpu_custom_call" | custom-call | flops 10000000000 | bytes 1024 | tf_op jit(solution)/shard_map/multiply/pallas_call | solution.py:109
  48.3 2.7 %collective-permute-done.5.refs_1_ = bf16[2,256,512]{2,1,0:T(8,128)(2,1)S(1)} collective-permute-done((bf16[2,256,512]{2,1,0:T(8,128)(2,1)S(1)}, bf16[2,256,512]{2,1,0:T(8,128)(2,1)S(1)}, u32[]{:S(2)}, u32[]{:S(2)}) %collective-permute-start.5) | collective-permute-done | bytes 524320 | tf_op jit(solution)/shard_map/ppermute | solution.py:377
  51.1 2.8 %collective-permute-start.10 = (bf16[1,256,512]{2,1,0:T(8,128)(2,1)S(1)}, bf16[1,256,512]{2,1,0:T(8,128)(2,1)S(1)}, u32[]{:S(2)}, u32[]{:S(2)}) collective-permute-start(bf16[1,256,512]{2,1,0:T(8,128)(2,1)S(1)} %get-tuple-element.117), channel_id=1, source_target_pairs={{0,8},{4,12},{8,0},{12,4},{1,9},{5,13},{9,1},{13,5},{2,10},{6,14},... | collective-permute-start | bytes 786440 | tf_op jit(solution)/shard_map/ppermute | solution.py:377
  53.9 1.5 collective-permute-start.15
  55.4 6.7 %multiply.11 = (f32[160,2048]{1,0:T(8,128)S(1)}, f32[8,128]{1,0:T(8,128)S(1)}) custom-call(bf16[80,4096]{1,0:T(8,128)(2,1)S(1)} %get-tuple-element.119.refs_0_, bf16[80,4096]{1,0:T(8,128)(2,1)S(1)} %collective-permute-done.12.refs_1_, bf16[13312,2048]{1,0:T(8,128)(2,1)} %refs_2_.9, f32[160,2048]{1,0:T(8,128)S(1)} %get-tuple-element.120.refs_3_, ...), custom_call_target="tpu_custom_call" | custom-call | flops 10000000000 | bytes 1024 | tf_op jit(solution)/shard_map/multiply/pallas_call | solution.py:109
  62.2 2.1 %collective-permute-done.13.refs_1_ = bf16[80,4096]{1,0:T(8,128)(2,1)S(1)} collective-permute-done((bf16[80,4096]{1,0:T(8,128)(2,1)S(1)}, bf16[80,4096]{1,0:T(8,128)(2,1)S(1)}, u32[]{:S(2)}, u32[]{:S(2)}) %collective-permute-start.13) | collective-permute-done | bytes 655392 | tf_op jit(solution)/shard_map/ppermute | solution.py:374
  64.3 6.8 %multiply.12 = (bf16[2,160,512]{2,1,0:T(8,128)(2,1)S(1)}, bf16[2,160,512]{2,1,0:T(8,128)(2,1)S(1)}, f32[8,128]{1,0:T(8,128)S(1)}) custom-call(bf16[80,4096]{1,0:T(8,128)(2,1)S(1)} %get-tuple-element.123.refs_0_, bf16[80,4096]{1,0:T(8,128)(2,1)S(1)} %collective-permute-done.13.refs_1_, bf16[13312,2048]{1,0:T(8,128)(2,1)} %refs_2_.9, ...), custom_call_target="tpu_custom_call" | custom-call | flops 10000000000 | bytes 1024 | tf_op jit(solution)/shard_map/multiply/pallas_call | solution.py:109
  71.2 0.2 collective-permute-start.17
  71.4 0.4 collective-permute-start.14
  71.7 0.5 collective-permute-start.22
  72.3 1.6 collective-permute-start.19
  73.8 0.4 collective-permute-start.16
  74.3 7.8 %multiply.13 = (f32[96,2048]{1,0:T(8,128)S(1)}, f32[8,128]{1,0:T(8,128)S(1)}) custom-call(bf16[48,5120]{1,0:T(8,128)(2,1)S(1)} %get-tuple-element.137.refs_0_, bf16[48,5120]{1,0:T(8,128)(2,1)S(1)} %collective-permute-done.17.refs_1_, bf16[13312,2048]{1,0:T(8,128)(2,1)} %refs_2_.9, f32[8,128]{1,0:T(8,128)S(1)} %get-tuple-element.138.refs_3_), custom_call_target="tpu_custom_call" | custom-call | flops 10000000000 | bytes 1024 | tf_op jit(solution)/shard_map/multiply/pallas_call | solution.py:109
  82.1 6.2 %collective-permute-done.16.refs_1_.refs_2_ = bf16[2,128,512]{2,1,0:T(8,128)(2,1)S(1)} collective-permute-done((bf16[2,128,512]{2,1,0:T(8,128)(2,1)S(1)}, bf16[2,128,512]{2,1,0:T(8,128)(2,1)S(1)}, u32[]{:S(2)}, u32[]{:S(2)}) %collective-permute-start.16) | collective-permute-done | bytes 262176 | tf_op jit(solution)/shard_map/ppermute | solution.py:377
  88.5 1.6 collective-permute-start.21
  90.2 6.6 %multiply.14 = (f32[96,2048]{1,0:T(8,128)S(1)}, f32[8,128]{1,0:T(8,128)S(1)}) custom-call(bf16[48,4096]{1,0:T(8,128)(2,1)S(1)} %get-tuple-element.149.refs_0_, bf16[48,4096]{1,0:T(8,128)(2,1)S(1)} %collective-permute-done.23.refs_1_, bf16[13312,2048]{1,0:T(8,128)(2,1)} %refs_2_.9, f32[96,2048]{1,0:T(8,128)S(1)} %get-tuple-element.150.refs_3_, ...), custom_call_target="tpu_custom_call" | custom-call | flops 10000000000 | bytes 1024 | tf_op jit(solution)/shard_map/multiply/pallas_call | solution.py:109
  96.9 3.2 %collective-permute-done.21.refs_0_ = bf16[48,4096]{1,0:T(8,128)(2,1)S(1)} collective-permute-done((bf16[48,4096]{1,0:T(8,128)(2,1)S(1)}, bf16[48,4096]{1,0:T(8,128)(2,1)S(1)}, u32[]{:S(2)}, u32[]{:S(2)}) %collective-permute-start.21) | collective-permute-done | bytes 393248 | tf_op jit(solution)/shard_map/ppermute | solution.py:374
  100.0 1.6 %collective-permute-start.20 = (bf16[1,160,512]{2,1,0:T(8,128)(2,1)S(1)}, bf16[1,160,512]{2,1,0:T(8,128)(2,1)S(1)}, u32[]{:S(2)}, u32[]{:S(2)}) collective-permute-start(bf16[1,160,512]{2,1,0:T(8,128)(2,1)S(1)} %get-tuple-element.145), channel_id=1, source_target_pairs={{0,8},{4,12},{8,0},{12,4},{1,9},{5,13},{9,1},{13,5},{2,10},{6,14},... | collective-permute-start | bytes 491528 | tf_op jit(solution)/shard_map/ppermute | solution.py:377
  101.8 6.9 %multiply.15 = (bf16[2,96,512]{2,1,0:T(8,128)(2,1)S(1)}, bf16[2,96,512]{2,1,0:T(8,128)(2,1)S(1)}, f32[8,128]{1,0:T(8,128)S(1)}) custom-call(bf16[48,4096]{1,0:T(8,128)(2,1)S(1)} %get-tuple-element.153.refs_0_, bf16[48,4096]{1,0:T(8,128)(2,1)S(1)} %collective-permute-done.24.refs_1_, bf16[13312,2048]{1,0:T(8,128)(2,1)} %refs_2_.9, ...), custom_call_target="tpu_custom_call" | custom-call | bytes 1024 | tf_op jit(solution)/shard_map/multiply/pallas_call | solution.py:109
  108.6 1.9 %collective-permute-start.27 = (bf16[2,96,512]{2,1,0:T(8,128)(2,1)S(1)}, bf16[2,96,512]{2,1,0:T(8,128)(2,1)S(1)}, u32[]{:S(2)}, u32[]{:S(2)}) collective-permute-start(bf16[2,96,512]{2,1,0:T(8,128)(2,1)S(1)} %get-tuple-element.163), channel_id=1, source_target_pairs={{0,4},{4,0},{8,12},{12,8},{1,5},{5,1},{9,13},{13,9},{2,6},{6,2},{1... | collective-permute-start | bytes 589832 | tf_op jit(solution)/shard_map/ppermute | solution.py:377
  110.5 5.3 %collective-permute-done.20.refs_1_ = bf16[1,160,512]{2,1,0:T(8,128)(2,1)S(1)} collective-permute-done((bf16[1,160,512]{2,1,0:T(8,128)(2,1)S(1)}, bf16[1,160,512]{2,1,0:T(8,128)(2,1)S(1)}, u32[]{:S(2)}, u32[]{:S(2)}) %collective-permute-start.20) | collective-permute-done | bytes 163872 | tf_op jit(solution)/shard_map/ppermute | solution.py:377
  115.9 1.6 collective-permute-start.25
  117.5 0.8 collective-permute-done.18.refs_1_.refs_3_
  118.3 1.5 encode.3
  119.8 2.3 %collective-permute-done.27.refs_1_ = bf16[2,96,512]{2,1,0:T(8,128)(2,1)S(1)} collective-permute-done((bf16[2,96,512]{2,1,0:T(8,128)(2,1)S(1)}, bf16[2,96,512]{2,1,0:T(8,128)(2,1)S(1)}, u32[]{:S(2)}, u32[]{:S(2)}) %collective-permute-start.27) | collective-permute-done | bytes 196640 | tf_op jit(solution)/shard_map/ppermute | solution.py:377
  122.2 3.4 %collective-permute-start.28 = (bf16[2,80,512]{2,1,0:T(8,128)(2,1)S(1)}, bf16[2,80,512]{2,1,0:T(8,128)(2,1)S(1)}, u32[]{:S(2)}, u32[]{:S(2)}) collective-permute-start(bf16[2,80,512]{2,1,0:T(8,128)(2,1)S(1)} %get-tuple-element.166.refs_0_.refs_2_), channel_id=1, source_target_pairs={{0,8},{4,12},{8,0},{12,4},{1,9},{5,13},{9,1},{13,5},{2,10},{6,14},... | collective-permute-start | bytes 491528 | tf_op jit(solution)/shard_map/ppermute | solution.py:377
  125.7 12.1 %collective-permute-done.29.refs_1_ = bf16[1,96,512]{2,1,0:T(8,128)(2,1)S(1)} collective-permute-done((bf16[1,96,512]{2,1,0:T(8,128)(2,1)S(1)}, bf16[1,96,512]{2,1,0:T(8,128)(2,1)S(1)}, u32[]{:S(2)}, u32[]{:S(2)}) %collective-permute-start.29) | collective-permute-done | bytes 98336 | tf_op jit(solution)/shard_map/ppermute | solution.py:377
  138.0 1.2 collective-permute-start.31
  139.2 2.9 %collective-permute-done.31.refs_0_ = bf16[1,48,512]{2,1,0:T(8,128)(2,1)S(1)} collective-permute-done((bf16[1,48,512]{2,1,0:T(8,128)(2,1)S(1)}, bf16[1,48,512]{2,1,0:T(8,128)(2,1)S(1)}, u32[]{:S(2)}, u32[]{:S(2)}) %collective-permute-start.31) | collective-permute-done | bytes 49184 | tf_op jit(solution)/shard_map/ppermute | solution.py:374
  142.1 1.1 collective-permute-done.32.refs_1_
  143.2 2.0 %collective-permute-start.33 = (bf16[2,48,512]{2,1,0:T(8,128)(2,1)S(1)}, bf16[2,48,512]{2,1,0:T(8,128)(2,1)S(1)}, u32[]{:S(2)}, u32[]{:S(2)}) collective-permute-start(bf16[2,48,512]{2,1,0:T(8,128)(2,1)S(1)} %get-tuple-element.178.refs_2_), channel_id=1, source_target_pairs={{0,4},{4,0},{8,12},{12,8},{1,5},{5,1},{9,13},{13,9},{2,6},{6,2},{1... | collective-permute-start | bytes 294920 | tf_op jit(solution)/shard_map/ppermute | solution.py:377
  145.2 1.6 %collective-permute-start.34 = (bf16[2,48,512]{2,1,0:T(8,128)(2,1)S(1)}, bf16[2,48,512]{2,1,0:T(8,128)(2,1)S(1)}, u32[]{:S(2)}, u32[]{:S(2)}) collective-permute-start(bf16[2,48,512]{2,1,0:T(8,128)(2,1)S(1)} %get-tuple-element.178.refs_2_), channel_id=1, source_target_pairs={{0,8},{4,12},{8,0},{12,4},{1,9},{5,13},{9,1},{13,5},{2,10},{6,14},... | collective-permute-start | bytes 294920 | tf_op jit(solution)/shard_map/ppermute | solution.py:377
  146.8 1.3 collective-permute-start.35
  148.1 1.2 encode.4
  149.3 1.5 collective-permute-done.33.refs_3_
  150.8 4.8 %collective-permute-done.34.refs_4_ = bf16[2,48,512]{2,1,0:T(8,128)(2,1)S(1)} collective-permute-done((bf16[2,48,512]{2,1,0:T(8,128)(2,1)S(1)}, bf16[2,48,512]{2,1,0:T(8,128)(2,1)S(1)}, u32[]{:S(2)}, u32[]{:S(2)}) %collective-permute-start.34) | collective-permute-done | bytes 98336 | tf_op jit(solution)/shard_map/ppermute | solution.py:377
  155.6 1.6 %encode.5 = (bf16[128,8192]{1,0:T(8,128)(2,1)}, bf16[64,128]{1,0:T(8,128)(2,1)}, f32[8,128]{1,0:T(8,128)}) custom-call(bf16[128,8192]{1,0:T(8,128)(2,1)} %get-tuple-element.176.refs_0_, f32[128,128]{1,0:T(8,128)S(1)} %get-tuple-element.177.refs_1_, bf16[2,48,512]{2,1,0:T(8,128)(2,1)S(1)} %get-tuple-element.178.refs_2_, ...), custom_call_target="tpu_custom_call", output_to_operand_aliasing={{0}: (0, {})} | custom-call | bytes 1024 | tf_op jit(solution)/shard_map/encode/pallas_call | solution.py:109
  (59 shorter events, 1.6 us)
Async XLA Ops:
  2.1 9.6 %collective-permute-start.4 = (bf16[80,1024]{1,0:T(8,128)(2,1)S(1)}, bf16[80,1024]{1,0:T(8,128)(2,1)S(1)}, u32[]{:S(2)}, u32[]{:S(2)}) collective-permute-start(bf16[80,1024]{1,0:T(8,128)(2,1)S(1)} %get-tuple-element.97), channel_id=1, source_target_pairs={{0,2},{1,3},{2,0},{3,1},{4,6},{5,7},{6,4},{7,5},{8,10},{9,11},{10,... | collective-permute-start | bytes 491528 | tf_op jit(solution)/shard_map/ppermute | solution.py:374
  10.6 3.1 %collective-permute-start.3 = (bf16[128,4096]{1,0:T(8,128)(2,1)S(1)}, bf16[128,4096]{1,0:T(8,128)(2,1)S(1)}, u32[]{:S(2)}, u32[]{:S(2)}) collective-permute-start(bf16[128,4096]{1,0:T(8,128)(2,1)S(1)} %get-tuple-element.96.refs_2_), channel_id=1, source_target_pairs={{0,1},{1,0},{2,3},{3,2},{4,5},{5,4},{6,7},{7,6},{8,9},{9,8},{10,11... | collective-permute-start | bytes 3145736 | tf_op jit(solution)/shard_map/ppermute | solution.py:374
  10.7 3.0 %collective-permute-start.2 = (bf16[128,1024]{1,0:T(8,128)(2,1)S(1)}, bf16[128,1024]{1,0:T(8,128)(2,1)S(1)}, u32[]{:S(2)}, u32[]{:S(2)}) collective-permute-start(bf16[128,1024]{1,0:T(8,128)(2,1)S(1)} %get-tuple-element.95.refs_0_), channel_id=1, source_target_pairs={{0,1},{1,0},{2,3},{3,2},{4,5},{5,4},{6,7},{7,6},{8,9},{9,8},{10,11... | collective-permute-start | bytes 786440 | tf_op jit(solution)/shard_map/ppermute | solution.py:374
  11.2 11.7 %collective-permute-start = (bf16[128,4096]{1,0:T(8,128)(2,1)S(1)}, bf16[128,4096]{1,0:T(8,128)(2,1)S(1)}, u32[]{:S(2)}, u32[]{:S(2)}) collective-permute-start(bf16[128,4096]{1,0:T(8,128)(2,1)S(1)} %get-tuple-element.93.refs_0_), channel_id=1, source_target_pairs={{0,1},{1,0},{2,3},{3,2},{4,5},{5,4},{6,7},{7,6},{8,9},{9,8},{10,11... | collective-permute-start | bytes 3145736 | tf_op jit(solution)/shard_map/ppermute | solution.py:374
  11.2 11.7 %collective-permute-start.1 = (bf16[128,4096]{1,0:T(8,128)(2,1)S(1)}, bf16[128,4096]{1,0:T(8,128)(2,1)S(1)}, u32[]{:S(2)}, u32[]{:S(2)}) collective-permute-start(bf16[128,4096]{1,0:T(8,128)(2,1)S(1)} %get-tuple-element.94.refs_2_), channel_id=1, source_target_pairs={{0,1},{1,0},{2,3},{3,2},{4,5},{5,4},{6,7},{7,6},{8,9},{9,8},{10,11... | collective-permute-start | bytes 3145736 | tf_op jit(solution)/shard_map/ppermute | solution.py:374
  11.7 24.6 %collective-permute-start.8 = (bf16[80,4096]{1,0:T(8,128)(2,1)S(1)}, bf16[80,4096]{1,0:T(8,128)(2,1)S(1)}, u32[]{:S(2)}, u32[]{:S(2)}) collective-permute-start(bf16[80,4096]{1,0:T(8,128)(2,1)S(1)} %get-tuple-element.107), channel_id=1, source_target_pairs={{0,2},{1,3},{2,0},{3,1},{4,6},{5,7},{6,4},{7,5},{8,10},{9,11},{10,... | collective-permute-start | bytes 1966088 | tf_op jit(solution)/shard_map/ppermute | solution.py:374
  13.7 34.5 %collective-permute-start.6 = (bf16[80,4096]{1,0:T(8,128)(2,1)S(1)}, bf16[80,4096]{1,0:T(8,128)(2,1)S(1)}, u32[]{:S(2)}, u32[]{:S(2)}) collective-permute-start(bf16[80,4096]{1,0:T(8,128)(2,1)S(1)} %get-tuple-element.105), channel_id=1, source_target_pairs={{0,2},{1,3},{2,0},{3,1},{4,6},{5,7},{6,4},{7,5},{8,10},{9,11},{10,... | collective-permute-start | bytes 1966088 | tf_op jit(solution)/shard_map/ppermute | solution.py:374
  13.7 26.6 %collective-permute-start.7 = (bf16[80,1024]{1,0:T(8,128)(2,1)S(1)}, bf16[80,1024]{1,0:T(8,128)(2,1)S(1)}, u32[]{:S(2)}, u32[]{:S(2)}) collective-permute-start(bf16[80,1024]{1,0:T(8,128)(2,1)S(1)} %get-tuple-element.106.refs_0_), channel_id=1, source_target_pairs={{0,1},{1,0},{2,3},{3,2},{4,5},{5,4},{6,7},{7,6},{8,9},{9,8},{10,11... | collective-permute-start | bytes 491528 | tf_op jit(solution)/shard_map/ppermute | solution.py:374
  36.3 4.0 %collective-permute-start.9 = (bf16[80,4096]{1,0:T(8,128)(2,1)S(1)}, bf16[80,4096]{1,0:T(8,128)(2,1)S(1)}, u32[]{:S(2)}, u32[]{:S(2)}) collective-permute-start(bf16[80,4096]{1,0:T(8,128)(2,1)S(1)} %get-tuple-element.109.refs_2_), channel_id=1, source_target_pairs={{0,1},{1,0},{2,3},{3,2},{4,5},{5,4},{6,7},{7,6},{8,9},{9,8},{10,11... | collective-permute-start | bytes 1966088 | tf_op jit(solution)/shard_map/ppermute | solution.py:374
  36.7 14.3 %collective-permute-start.5 = (bf16[2,256,512]{2,1,0:T(8,128)(2,1)S(1)}, bf16[2,256,512]{2,1,0:T(8,128)(2,1)S(1)}, u32[]{:S(2)}, u32[]{:S(2)}) collective-permute-start(bf16[2,256,512]{2,1,0:T(8,128)(2,1)S(1)} %get-tuple-element.103), channel_id=1, source_target_pairs={{0,4},{4,0},{8,12},{12,8},{1,5},{5,1},{9,13},{13,9},{2,6},{6,2},{1... | collective-permute-start | bytes 1572872 | tf_op jit(solution)/shard_map/ppermute | solution.py:377
  38.8 23.3 %collective-permute-start.11 = (bf16[80,4096]{1,0:T(8,128)(2,1)S(1)}, bf16[80,4096]{1,0:T(8,128)(2,1)S(1)}, u32[]{:S(2)}, u32[]{:S(2)}) collective-permute-start(bf16[80,4096]{1,0:T(8,128)(2,1)S(1)} %get-tuple-element.118), channel_id=1, source_target_pairs={{0,2},{1,3},{2,0},{3,1},{4,6},{5,7},{6,4},{7,5},{8,10},{9,11},{10,... | collective-permute-start | bytes 1966088 | tf_op jit(solution)/shard_map/ppermute | solution.py:374
  48.2 7.2 %collective-permute-start.12 = (bf16[80,4096]{1,0:T(8,128)(2,1)S(1)}, bf16[80,4096]{1,0:T(8,128)(2,1)S(1)}, u32[]{:S(2)}, u32[]{:S(2)}) collective-permute-start(bf16[80,4096]{1,0:T(8,128)(2,1)S(1)} %get-tuple-element.119.refs_0_), channel_id=1, source_target_pairs={{0,1},{1,0},{2,3},{3,2},{4,5},{5,4},{6,7},{7,6},{8,9},{9,8},{10,11... | collective-permute-start | bytes 1966088 | tf_op jit(solution)/shard_map/ppermute | solution.py:374
  51.1 20.0 %collective-permute-start.10 = (bf16[1,256,512]{2,1,0:T(8,128)(2,1)S(1)}, bf16[1,256,512]{2,1,0:T(8,128)(2,1)S(1)}, u32[]{:S(2)}, u32[]{:S(2)}) collective-permute-start(bf16[1,256,512]{2,1,0:T(8,128)(2,1)S(1)} %get-tuple-element.117), channel_id=1, source_target_pairs={{0,8},{4,12},{8,0},{12,4},{1,9},{5,13},{9,1},{13,5},{2,10},{6,14},... | collective-permute-start | bytes 786440 | tf_op jit(solution)/shard_map/ppermute | solution.py:377
  53.9 17.2 %collective-permute-start.15 = (bf16[48,5120]{1,0:T(8,128)(2,1)S(1)}, bf16[48,5120]{1,0:T(8,128)(2,1)S(1)}, u32[]{:S(2)}, u32[]{:S(2)}) collective-permute-start(bf16[48,5120]{1,0:T(8,128)(2,1)S(1)} %get-tuple-element.133), channel_id=1, source_target_pairs={{0,2},{1,3},{2,0},{3,1},{4,6},{5,7},{6,4},{7,5},{8,10},{9,11},{10,... | collective-permute-start | bytes 1474568 | tf_op jit(solution)/shard_map/ppermute | solution.py:374
  62.1 2.2 %collective-permute-start.13 = (bf16[80,4096]{1,0:T(8,128)(2,1)S(1)}, bf16[80,4096]{1,0:T(8,128)(2,1)S(1)}, u32[]{:S(2)}, u32[]{:S(2)}) collective-permute-start(bf16[80,4096]{1,0:T(8,128)(2,1)S(1)} %get-tuple-element.123.refs_0_), channel_id=1, source_target_pairs={{0,1},{1,0},{2,3},{3,2},{4,5},{5,4},{6,7},{7,6},{8,9},{9,8},{10,11... | collective-permute-start | bytes 1966088 | tf_op jit(solution)/shard_map/ppermute | solution.py:374
  71.2 3.1 %collective-permute-start.17 = (bf16[48,5120]{1,0:T(8,128)(2,1)S(1)}, bf16[48,5120]{1,0:T(8,128)(2,1)S(1)}, u32[]{:S(2)}, u32[]{:S(2)}) collective-permute-start(bf16[48,5120]{1,0:T(8,128)(2,1)S(1)} %get-tuple-element.137.refs_0_), channel_id=1, source_target_pairs={{0,1},{1,0},{2,3},{3,2},{4,5},{5,4},{6,7},{7,6},{8,9},{9,8},{10,11... | collective-permute-start | bytes 1474568 | tf_op jit(solution)/shard_map/ppermute | solution.py:374
  71.4 2.5 %collective-permute-start.14 = (bf16[1,128,512]{2,1,0:T(8,128)(2,1)S(1)}, bf16[1,128,512]{2,1,0:T(8,128)(2,1)S(1)}, u32[]{:S(2)}, u32[]{:S(2)}) collective-permute-start(bf16[1,128,512]{2,1,0:T(8,128)(2,1)S(1)} %get-tuple-element.132), channel_id=1, source_target_pairs={{0,1},{1,0},{2,3},{3,2},{4,5},{5,4},{6,7},{7,6},{8,9},{9,8},{10,11... | collective-permute-start | bytes 393224 | tf_op jit(solution)/shard_map/ppermute | solution.py:374
  71.7 16.7 %collective-permute-start.22 = (bf16[48,4096]{1,0:T(8,128)(2,1)S(1)}, bf16[48,4096]{1,0:T(8,128)(2,1)S(1)}, u32[]{:S(2)}, u32[]{:S(2)}) collective-permute-start(bf16[48,4096]{1,0:T(8,128)(2,1)S(1)} %get-tuple-element.147), channel_id=1, source_target_pairs={{0,2},{1,3},{2,0},{3,1},{4,6},{5,7},{6,4},{7,5},{8,10},{9,11},{10,... | collective-permute-start | bytes 1179656 | tf_op jit(solution)/shard_map/ppermute | solution.py:374
  72.3 16.0 %collective-permute-start.19 = (bf16[2,160,512]{2,1,0:T(8,128)(2,1)S(1)}, bf16[2,160,512]{2,1,0:T(8,128)(2,1)S(1)}, u32[]{:S(2)}, u32[]{:S(2)}) collective-permute-start(bf16[2,160,512]{2,1,0:T(8,128)(2,1)S(1)} %get-tuple-element.142), channel_id=1, source_target_pairs={{0,4},{4,0},{8,12},{12,8},{1,5},{5,1},{9,13},{13,9},{2,6},{6,2},{1... | collective-permute-start | bytes 983048 | tf_op jit(solution)/shard_map/ppermute | solution.py:377
  73.8 14.4 %collective-permute-start.16 = (bf16[2,128,512]{2,1,0:T(8,128)(2,1)S(1)}, bf16[2,128,512]{2,1,0:T(8,128)(2,1)S(1)}, u32[]{:S(2)}, u32[]{:S(2)}) collective-permute-start(bf16[2,128,512]{2,1,0:T(8,128)(2,1)S(1)} %get-tuple-element.136.refs_0_), channel_id=1, source_target_pairs={{0,8},{4,12},{8,0},{12,4},{1,9},{5,13},{9,1},{13,5},{2,10},{6,14},... | collective-permute-start | bytes 786440 | tf_op jit(solution)/shard_map/ppermute | solution.py:377
  88.4 1.8 %collective-permute-start.23 = (bf16[48,4096]{1,0:T(8,128)(2,1)S(1)}, bf16[48,4096]{1,0:T(8,128)(2,1)S(1)}, u32[]{:S(2)}, u32[]{:S(2)}) collective-permute-start(bf16[48,4096]{1,0:T(8,128)(2,1)S(1)} %get-tuple-element.149.refs_0_), channel_id=1, source_target_pairs={{0,1},{1,0},{2,3},{3,2},{4,5},{5,4},{6,7},{7,6},{8,9},{9,8},{10,11... | collective-permute-start | bytes 1179656 | tf_op jit(solution)/shard_map/ppermute | solution.py:374
  88.5 11.5 %collective-permute-start.21 = (bf16[48,4096]{1,0:T(8,128)(2,1)S(1)}, bf16[48,4096]{1,0:T(8,128)(2,1)S(1)}, u32[]{:S(2)}, u32[]{:S(2)}) collective-permute-start(bf16[48,4096]{1,0:T(8,128)(2,1)S(1)} %get-tuple-element.146), channel_id=1, source_target_pairs={{0,2},{1,3},{2,0},{3,1},{4,6},{5,7},{6,4},{7,5},{8,10},{9,11},{10,... | collective-permute-start | bytes 1179656 | tf_op jit(solution)/shard_map/ppermute | solution.py:374
  100.0 1.7 %collective-permute-start.24 = (bf16[48,4096]{1,0:T(8,128)(2,1)S(1)}, bf16[48,4096]{1,0:T(8,128)(2,1)S(1)}, u32[]{:S(2)}, u32[]{:S(2)}) collective-permute-start(bf16[48,4096]{1,0:T(8,128)(2,1)S(1)} %get-tuple-element.153.refs_0_), channel_id=1, source_target_pairs={{0,1},{1,0},{2,3},{3,2},{4,5},{5,4},{6,7},{7,6},{8,9},{9,8},{10,11... | collective-permute-start | bytes 1179656 | tf_op jit(solution)/shard_map/ppermute | solution.py:374
  100.0 18.2 %collective-permute-start.18 = (bf16[4,128,512]{2,1,0:T(8,128)(2,1)S(1)}, bf16[4,128,512]{2,1,0:T(8,128)(2,1)S(1)}, u32[]{:S(2)}, u32[]{:S(2)}) collective-permute-start(bf16[4,128,512]{2,1,0:T(8,128)(2,1)S(1)} %get-tuple-element.140), channel_id=1, source_target_pairs={{0,4},{4,0},{8,12},{12,8},{1,5},{5,1},{9,13},{13,9},{2,6},{6,2},{1... | collective-permute-start | bytes 1572872 | tf_op jit(solution)/shard_map/ppermute | solution.py:377
  100.0 15.8 %collective-permute-start.20 = (bf16[1,160,512]{2,1,0:T(8,128)(2,1)S(1)}, bf16[1,160,512]{2,1,0:T(8,128)(2,1)S(1)}, u32[]{:S(2)}, u32[]{:S(2)}) collective-permute-start(bf16[1,160,512]{2,1,0:T(8,128)(2,1)S(1)} %get-tuple-element.145), channel_id=1, source_target_pairs={{0,8},{4,12},{8,0},{12,4},{1,9},{5,13},{9,1},{13,5},{2,10},{6,14},... | collective-permute-start | bytes 491528 | tf_op jit(solution)/shard_map/ppermute | solution.py:377
  108.6 13.5 %collective-permute-start.27 = (bf16[2,96,512]{2,1,0:T(8,128)(2,1)S(1)}, bf16[2,96,512]{2,1,0:T(8,128)(2,1)S(1)}, u32[]{:S(2)}, u32[]{:S(2)}) collective-permute-start(bf16[2,96,512]{2,1,0:T(8,128)(2,1)S(1)} %get-tuple-element.163), channel_id=1, source_target_pairs={{0,4},{4,0},{8,12},{12,8},{1,5},{5,1},{9,13},{13,9},{2,6},{6,2},{1... | collective-permute-start | bytes 589832 | tf_op jit(solution)/shard_map/ppermute | solution.py:377
  115.9 6.2 %collective-permute-start.25 = (bf16[1,80,512]{2,1,0:T(8,128)(2,1)S(1)}, bf16[1,80,512]{2,1,0:T(8,128)(2,1)S(1)}, u32[]{:S(2)}, u32[]{:S(2)}) collective-permute-start(bf16[1,80,512]{2,1,0:T(8,128)(2,1)S(1)} %get-tuple-element.160), channel_id=1, source_target_pairs={{0,2},{1,3},{2,0},{3,1},{4,6},{5,7},{6,4},{7,5},{8,10},{9,11},{10,... | collective-permute-start | bytes 245768 | tf_op jit(solution)/shard_map/ppermute | solution.py:374
  117.5 4.7 %collective-permute-start.26 = (bf16[1,80,512]{2,1,0:T(8,128)(2,1)S(1)}, bf16[1,80,512]{2,1,0:T(8,128)(2,1)S(1)}, u32[]{:S(2)}, u32[]{:S(2)}) collective-permute-start(bf16[1,80,512]{2,1,0:T(8,128)(2,1)S(1)} %get-tuple-element.161), channel_id=1, source_target_pairs={{0,3},{1,2},{2,1},{3,0},{4,7},{5,6},{6,5},{7,4},{8,11},{9,10},{10,... | collective-permute-start | bytes 245768 | tf_op jit(solution)/shard_map/ppermute | solution.py:374
  122.2 15.6 %collective-permute-start.28 = (bf16[2,80,512]{2,1,0:T(8,128)(2,1)S(1)}, bf16[2,80,512]{2,1,0:T(8,128)(2,1)S(1)}, u32[]{:S(2)}, u32[]{:S(2)}) collective-permute-start(bf16[2,80,512]{2,1,0:T(8,128)(2,1)S(1)} %get-tuple-element.166.refs_0_.refs_2_), channel_id=1, source_target_pairs={{0,8},{4,12},{8,0},{12,4},{1,9},{5,13},{9,1},{13,5},{2,10},{6,14},... | collective-permute-start | bytes 491528 | tf_op jit(solution)/shard_map/ppermute | solution.py:377
  125.6 12.2 %collective-permute-start.29 = (bf16[1,96,512]{2,1,0:T(8,128)(2,1)S(1)}, bf16[1,96,512]{2,1,0:T(8,128)(2,1)S(1)}, u32[]{:S(2)}, u32[]{:S(2)}) collective-permute-start(bf16[1,96,512]{2,1,0:T(8,128)(2,1)S(1)} %get-tuple-element.168), channel_id=1, source_target_pairs={{0,8},{4,12},{8,0},{12,4},{1,9},{5,13},{9,1},{13,5},{2,10},{6,14},... | collective-permute-start | bytes 294920 | tf_op jit(solution)/shard_map/ppermute | solution.py:377
  137.9 10.2 %collective-permute-start.30 = (bf16[4,80,512]{2,1,0:T(8,128)(2,1)S(1)}, bf16[4,80,512]{2,1,0:T(8,128)(2,1)S(1)}, u32[]{:S(2)}, u32[]{:S(2)}) collective-permute-start(bf16[4,80,512]{2,1,0:T(8,128)(2,1)S(1)} %get-tuple-element.171), channel_id=1, source_target_pairs={{0,4},{4,0},{8,12},{12,8},{1,5},{5,1},{9,13},{13,9},{2,6},{6,2},{1... | collective-permute-start | bytes 983048 | tf_op jit(solution)/shard_map/ppermute | solution.py:377
  138.0 4.1 %collective-permute-start.31 = (bf16[1,48,512]{2,1,0:T(8,128)(2,1)S(1)}, bf16[1,48,512]{2,1,0:T(8,128)(2,1)S(1)}, u32[]{:S(2)}, u32[]{:S(2)}) collective-permute-start(bf16[1,48,512]{2,1,0:T(8,128)(2,1)S(1)} %get-tuple-element.172), channel_id=1, source_target_pairs={{0,2},{1,3},{2,0},{3,1},{4,6},{5,7},{6,4},{7,5},{8,10},{9,11},{10,... | collective-permute-start | bytes 147464 | tf_op jit(solution)/shard_map/ppermute | solution.py:374
  139.2 4.0 %collective-permute-start.32 = (bf16[1,48,512]{2,1,0:T(8,128)(2,1)S(1)}, bf16[1,48,512]{2,1,0:T(8,128)(2,1)S(1)}, u32[]{:S(2)}, u32[]{:S(2)}) collective-permute-start(bf16[1,48,512]{2,1,0:T(8,128)(2,1)S(1)} %get-tuple-element.173), channel_id=1, source_target_pairs={{0,3},{1,2},{2,1},{3,0},{4,7},{5,6},{6,5},{7,4},{8,11},{9,10},{10,... | collective-permute-start | bytes 147464 | tf_op jit(solution)/shard_map/ppermute | solution.py:374
  143.2 7.6 %collective-permute-start.33 = (bf16[2,48,512]{2,1,0:T(8,128)(2,1)S(1)}, bf16[2,48,512]{2,1,0:T(8,128)(2,1)S(1)}, u32[]{:S(2)}, u32[]{:S(2)}) collective-permute-start(bf16[2,48,512]{2,1,0:T(8,128)(2,1)S(1)} %get-tuple-element.178.refs_2_), channel_id=1, source_target_pairs={{0,4},{4,0},{8,12},{12,8},{1,5},{5,1},{9,13},{13,9},{2,6},{6,2},{1... | collective-permute-start | bytes 294920 | tf_op jit(solution)/shard_map/ppermute | solution.py:377
  145.2 10.4 %collective-permute-start.34 = (bf16[2,48,512]{2,1,0:T(8,128)(2,1)S(1)}, bf16[2,48,512]{2,1,0:T(8,128)(2,1)S(1)}, u32[]{:S(2)}, u32[]{:S(2)}) collective-permute-start(bf16[2,48,512]{2,1,0:T(8,128)(2,1)S(1)} %get-tuple-element.178.refs_2_), channel_id=1, source_target_pairs={{0,8},{4,12},{8,0},{12,4},{1,9},{5,13},{9,1},{13,5},{2,10},{6,14},... | collective-permute-start | bytes 294920 | tf_op jit(solution)/shard_map/ppermute | solution.py:377
  146.8 8.8 %collective-permute-start.35 = (bf16[2,48,512]{2,1,0:T(8,128)(2,1)S(1)}, bf16[2,48,512]{2,1,0:T(8,128)(2,1)S(1)}, u32[]{:S(2)}, u32[]{:S(2)}) collective-permute-start(bf16[2,48,512]{2,1,0:T(8,128)(2,1)S(1)} %get-tuple-element.178.refs_2_), channel_id=1, source_target_pairs={{0,12},{4,8},{8,4},{12,0},{1,13},{5,9},{9,5},{13,1},{2,14},{6,10},... | collective-permute-start | bytes 294920 | tf_op jit(solution)/shard_map/ppermute | solution.py:377

commit v7 on v6

--- a/solution.py
+++ b/solution.py
@@ -264,7 +264,7 @@
     )
 
 
-def add(chain, parts, outs):
+def add(chain, parts, outs, cost=None):
     count = len(parts)
 
     def body(*refs):
@@ -274,10 +274,10 @@
 
     vmem = pl.BlockSpec(memory_space=pltpu.VMEM)
     shapes = [jax.ShapeDtypeStruct((1, b - a, parts[0].shape[2]), jnp.bfloat16) for _, a, b in outs]
-    return chain.call(body, parts, [vmem] * count, [vmem] * len(outs), shapes, "add")
-
-
-def join(chain, first, second):
+    return chain.call(body, parts, [vmem] * count, [vmem] * len(outs), shapes, "add", cost=cost)
+
+
+def join(chain, first, second, cost=None):
     n = first.shape[0]
 
     def body(first_ref, second_ref, out_ref):
@@ -286,7 +286,7 @@
 
     vmem = pl.BlockSpec(memory_space=pltpu.VMEM)
     shape = jax.ShapeDtypeStruct((n + second.shape[0],) + first.shape[1:], first.dtype)
-    return chain.call(body, [first, second], [vmem] * 2, [vmem], [shape], "join")[0]
+    return chain.call(body, [first, second], [vmem] * 2, [vmem], [shape], "join", cost=cost)[0]
 
 
 def encode_blocks(value, store, scales, first):
@@ -300,7 +300,7 @@
     return scales
 
 
-def encode_columns(chain, codes, scales, shares, away, start, height, width, last=False):
+def encode_columns(chain, codes, scales, shares, away, start, height, width, last=False, cost=None):
     rows, part = shares[0][0].shape[1:]
     tp = len(shares)
     blocks, spread = part // BLOCK, tp * part
@@ -348,6 +348,7 @@
             jax.ShapeDtypeStruct((width // BLOCK, height), jnp.bfloat16) if last else kept,
         ],
         "encode",
+        cost=cost,
         scratch=[
             pltpu.VMEM((2, rows, spread), jnp.bfloat16),
             pltpu.VMEM((height, LANES), jnp.float32),
@@ -384,9 +385,9 @@
         outs = multiply(chain, chunks, down_weight, first, total, split, cost)
         return outs if split else outs[0]
 
-    def sum_home(parts, away):
+    def sum_home(parts, away, cost=None):
         half = parts[0].shape[1] // 2
-        ahead, behind = add(chain, parts, [(0, 0, half), (0, half, 2 * half)])
+        ahead, behind = add(chain, parts, [(0, 0, half), (0, half, 2 * half)], cost)
         return swap(ahead, away), swap(behind, away + 1)
 
     def sum_pair(parts):
@@ -406,7 +407,7 @@
         width // STEP,
         [(0, rows, a, b) for a, b in spans[1:]]
         + [(0, cut, a, b) for a, b in spans[1:]]
-        + [(cut, rows, a, b) for a, b in [(0, ends[1])] + spans[2:]],
+        + [(cut, rows, a, b) for a, b in [(0, ends[1]), (ends[1], ends[3])]],
     )
     near, early, late = [near_0] + pieces[:3], pieces[3:6], pieces[6:]
     near = [[h, swap(h, 1)] for h in near]
@@ -425,7 +426,7 @@
     near = sum_pair(near)
     total = product([far_2], ends[1], total)
     far_3 = both_cores(far_3)
-    late_1, late_2 = swap(chain.pin(late[1]), 2), swap(chain.pin(late[2]), 2)
+    late_1 = swap(chain.pin(late[1]), 2)
     far = product([far_3], ends[2], total, HALVES)
     far = [far[0], shift(far[1], 1)]
     near = sum_home(near, 0)
@@ -434,25 +435,23 @@
     near = join(chain, *near)
     near = [near, shift(near, 2)]
     total = product([late_0], 0, None)
+    far = sum_pair(far)
     near.append(join(chain, *near))
     near[2] = shift(near[2], 1)
-    far = sum_pair(far)
     late_1 = both_cores(late_1)
-    total = product([late_1], ends[1], total)
-    late_2 = both_cores(late_2, 0)
-    last = product([late_2], ends[2], total, HALVES, cost=0)
+    last = product([late_1], ends[1], total, HALVES)
     last = [last[0], shift(last[1], 1)]
-    far = sum_home(far, 2)
+    far = sum_home(far, 2, 10**10)
+    last = sum_pair(last)
     near = [(near[0], 0), (near[2], 0), (near[1], 0), (near[2], 2)]
-    codes, scales = encode_columns(chain, None, None, near, 0, 0, rows, out_width)
-    last = sum_pair(last)
+    codes, scales = encode_columns(chain, None, None, near, 0, 0, rows, out_width, cost=10**10)
+    last = sum_home(last, 2)
     far = join(chain, *far)
     far = [far, shift(far, 2)]
-    last = sum_home(last, 2)
+    last = join(chain, *last)
+    last = [last] + [shift(last, flip) for flip in range(1, tp)]
     far.append(join(chain, *far))
     far[2] = shift(far[2], 1)
-    last = join(chain, *last)
-    last = [last] + [shift(last, flip) for flip in range(1, tp)]
     far = [(far[0], 0), (far[2], 0), (far[1], 0), (far[2], 2)]
     codes, scales = encode_columns(chain, codes, scales, far, 2, 0, rows, out_width)
     last = [(array, 0) for array in last]

time: 158 us -> 148 us (0.937)
  waiting for transfers between devices: 47.1 us -> 43.3 us
  starting transfers between devices: 32.3 us -> 29 us
  Pallas kernels: 76.8 us -> 74.8 us
    ppermute x13, waiting for transfers between devices: 35.6 us -> 31.8 us  [shift(): return lax.ppermute(value, 'tp', [(t, t ^ flip) for t in range(tp)])]
    ppermute x23 -> x21, starting transfers between devices: 13.3 us -> 10.7 us  [swap(): lax.ppermute(value, 'batch', [(b, b ^ flip) for b in range(batch)])]
    pallas_call x35 -> x32, Pallas kernels: 76.8 us -> 74.8 us  [call(): pl.pallas_call(with_tokens, grid=grid, in_specs=list(in_specs) + [ANY] *...]
    ppermute x23 -> x21, waiting for transfers between devices: 11.5 us -> 11.5 us  [swap(): lax.ppermute(value, 'batch', [(b, b ^ flip) for b in range(batch)])]
  transfers between devices with their start and end apart: 36 -> 34, of which waited for: 15 -> 13; matrix products, arithmetic and copies ran while one was open for 0% -> 0% of each run, Pallas kernels for 47% -> 48%
where the time goes in v7:
time: 148 us
  Pallas kernels  74.8 us (51%)
  waiting for transfers between devices  43.3 us (29%)
  starting transfers between devices  29 us (20%)
    pallas_call x32, Pallas kernels, call(): pl.pallas_call(with_tokens, grid=grid, in_specs=list(in_specs) + [ANY] *...  74.8 us
    ppermute x13, waiting for transfers between devices, shift(): return lax.ppermute(value, 'tp', [(t, t ^ flip) for t in range(tp)])  31.8 us
    ppermute x13, starting transfers between devices, shift(): return lax.ppermute(value, 'tp', [(t, t ^ flip) for t in range(tp)])  18.3 us
    ppermute x21, waiting for transfers between devices, swap(): lax.ppermute(value, 'batch', [(b, b ^ flip) for b in range(batch)])  11.5 us
    ppermute x21, starting transfers between devices, swap(): lax.ppermute(value, 'batch', [(b, b ^ flip) for b in range(batch)])  10.7 us
  transfers between devices with their start and end apart: 34, of which 13 were waited for; matrix products, arithmetic and copies ran while one was open for 0% of the time, Pallas kernels for 48%

profile of v7, /device:TPU:0, one launch (start us, length us, event | category | flops | bytes accessed | tf_op | source)
XLA Modules:
  0.0 148.2 jit_solution(493166017446733935)
XLA Ops:
  0.6 1.5 activate.2
  2.1 3.0 %collective-permute-start.4 = (bf16[80,1024]{1,0:T(8,128)(2,1)S(1)}, bf16[80,1024]{1,0:T(8,128)(2,1)S(1)}, u32[]{:S(2)}, u32[]{:S(2)}) collective-permute-start(bf16[80,1024]{1,0:T(8,128)(2,1)S(1)} %get-tuple-element.90), channel_id=1, source_target_pairs={{0,2},{1,3},{2,0},{3,1},{4,6},{5,7},{6,4},{7,5},{8,10},{9,11},{10,... | collective-permute-start | bytes 491528 | tf_op jit(solution)/shard_map/ppermute | solution.py:375
  5.1 5.3 %activate.3 = (bf16[128,4096]{1,0:T(8,128)(2,1)S(1)}, bf16[128,4096]{1,0:T(8,128)(2,1)S(1)}, bf16[128,4096]{1,0:T(8,128)(2,1)S(1)}, bf16[80,4096]{1,0:T(8,128)(2...) custom-call(bf16[128,13312]{1,0:T(8,128)(2,1)} %refs_0_.3, ...), custom_call_target="tpu_custom_call" | custom-call | flops 10000000000 | bytes 1024 | tf_op jit(solution)/shard_map/activate/pallas_call | solution.py:109
  10.5 0.5 collective-permute-start.2
  11.1 0.4 collective-permute-start.1
  11.6 2.0 %collective-permute-done.2.refs_1_ = bf16[128,1024]{1,0:T(8,128)(2,1)S(1)} collective-permute-done((bf16[128,1024]{1,0:T(8,128)(2,1)S(1)}, bf16[128,1024]{1,0:T(8,128)(2,1)S(1)}, u32[]{:S(2)}, u32[]{:S(2)}) %collective-permute-start.2) | collective-permute-done | bytes 262176 | tf_op jit(solution)/shard_map/ppermute | solution.py:375
  13.7 9.0 %multiply.7 = (f32[256,2048]{1,0:T(8,128)S(1)}, f32[8,128]{1,0:T(8,128)S(1)}) custom-call(bf16[128,1024]{1,0:T(8,128)(2,1)S(1)} %get-tuple-element.88.refs_0_, bf16[128,1024]{1,0:T(8,128)(2,1)S(1)} %collective-permute-done.2.refs_1_, bf16[128,4096]{1,0:T(8,128)(2,1)S(1)} %get-tuple-element.89.refs_2_, bf16[128,4096]{1,0:T(8,128)(2,1)S(1)} %collective-permute-done.3.refs_3_, ...), custom_call_target="tpu_custom_call" | custom-call | flops 10000000000 | bytes 1024 | tf_op jit(solution)/shard_map/multiply/pallas_call | solution.py:109
  22.7 13.3 %multiply.8 = (bf16[2,256,512]{2,1,0:T(8,128)(2,1)S(1)}, bf16[2,256,512]{2,1,0:T(8,128)(2,1)S(1)}, f32[8,128]{1,0:T(8,128)S(1)}) custom-call(bf16[128,4096]{1,0:T(8,128)(2,1)S(1)} %get-tuple-element.86.refs_0_, bf16[128,4096]{1,0:T(8,128)(2,1)S(1)} %collective-permute-done.refs_1_, bf16[128,4096]{1,0:T(8,128)(2,1)S(1)} %get-tuple-element.87.refs_2_, ...), custom_call_target="tpu_custom_call" | custom-call | flops 10000000000 | bytes 1024 | tf_op jit(solution)/shard_map/multiply/pallas_call | solution.py:109
  36.1 0.5 collective-permute-start.9
  36.5 2.1 %collective-permute-start.5 = (bf16[2,256,512]{2,1,0:T(8,128)(2,1)S(1)}, bf16[2,256,512]{2,1,0:T(8,128)(2,1)S(1)}, u32[]{:S(2)}, u32[]{:S(2)}) collective-permute-start(bf16[2,256,512]{2,1,0:T(8,128)(2,1)S(1)} %get-tuple-element.96), channel_id=1, source_target_pairs={{0,4},{4,0},{8,12},{12,8},{1,5},{5,1},{9,13},{13,9},{2,6},{6,2},{1... | collective-permute-start | bytes 1572872 | tf_op jit(solution)/shard_map/ppermute | solution.py:378
  38.7 1.5 collective-permute-start.11
  40.1 7.9 %multiply.9 = (f32[160,2048]{1,0:T(8,128)S(1)}, f32[8,128]{1,0:T(8,128)S(1)}) custom-call(bf16[80,1024]{1,0:T(8,128)(2,1)S(1)} %get-tuple-element.99.refs_0_, bf16[80,1024]{1,0:T(8,128)(2,1)S(1)} %collective-permute-done.7.refs_1_, bf16[80,4096]{1,0:T(8,128)(2,1)S(1)} %get-tuple-element.102.refs_2_, bf16[80,4096]{1,0:T(8,128)(2,1)S(1)} %collective-permute-done.9.refs_3_, ...), custom_call_target="tpu_custom_call" | custom-call | flops 10000000000 | bytes 1024 | tf_op jit(solution)/shard_map/multiply/pallas_call | solution.py:109
  48.1 2.7 %collective-permute-done.5.refs_1_ = bf16[2,256,512]{2,1,0:T(8,128)(2,1)S(1)} collective-permute-done((bf16[2,256,512]{2,1,0:T(8,128)(2,1)S(1)}, bf16[2,256,512]{2,1,0:T(8,128)(2,1)S(1)}, u32[]{:S(2)}, u32[]{:S(2)}) %collective-permute-start.5) | collective-permute-done | bytes 524320 | tf_op jit(solution)/shard_map/ppermute | solution.py:378
  51.0 2.8 %collective-permute-start.10 = (bf16[1,256,512]{2,1,0:T(8,128)(2,1)S(1)}, bf16[1,256,512]{2,1,0:T(8,128)(2,1)S(1)}, u32[]{:S(2)}, u32[]{:S(2)}) collective-permute-start(bf16[1,256,512]{2,1,0:T(8,128)(2,1)S(1)} %get-tuple-element.110), channel_id=1, source_target_pairs={{0,8},{4,12},{8,0},{12,4},{1,9},{5,13},{9,1},{13,5},{2,10},{6,14},... | collective-permute-start | bytes 786440 | tf_op jit(solution)/shard_map/ppermute | solution.py:378
  53.8 1.5 collective-permute-start.15
  55.2 6.7 %multiply.10 = (f32[160,2048]{1,0:T(8,128)S(1)}, f32[8,128]{1,0:T(8,128)S(1)}) custom-call(bf16[80,4096]{1,0:T(8,128)(2,1)S(1)} %get-tuple-element.112.refs_0_, bf16[80,4096]{1,0:T(8,128)(2,1)S(1)} %collective-permute-done.12.refs_1_, bf16[13312,2048]{1,0:T(8,128)(2,1)} %refs_2_.7, f32[160,2048]{1,0:T(8,128)S(1)} %get-tuple-element.113.refs_3_, ...), custom_call_target="tpu_custom_call" | custom-call | flops 10000000000 | bytes 1024 | tf_op jit(solution)/shard_map/multiply/pallas_call | solution.py:109
  62.1 2.1 %collective-permute-done.13.refs_1_ = bf16[80,4096]{1,0:T(8,128)(2,1)S(1)} collective-permute-done((bf16[80,4096]{1,0:T(8,128)(2,1)S(1)}, bf16[80,4096]{1,0:T(8,128)(2,1)S(1)}, u32[]{:S(2)}, u32[]{:S(2)}) %collective-permute-start.13) | collective-permute-done | bytes 655392 | tf_op jit(solution)/shard_map/ppermute | solution.py:375
  64.1 6.8 %multiply.11 = (bf16[2,160,512]{2,1,0:T(8,128)(2,1)S(1)}, bf16[2,160,512]{2,1,0:T(8,128)(2,1)S(1)}, f32[8,128]{1,0:T(8,128)S(1)}) custom-call(bf16[80,4096]{1,0:T(8,128)(2,1)S(1)} %get-tuple-element.116.refs_0_, bf16[80,4096]{1,0:T(8,128)(2,1)S(1)} %collective-permute-done.13.refs_1_, bf16[13312,2048]{1,0:T(8,128)(2,1)} %refs_2_.7, ...), custom_call_target="tpu_custom_call" | custom-call | flops 10000000000 | bytes 1024 | tf_op jit(solution)/shard_map/multiply/pallas_call | solution.py:109
  71.2 0.4 collective-permute-start.14
  71.6 0.6 collective-permute-start.20
  72.1 1.6 %collective-permute-start.17 = (bf16[2,160,512]{2,1,0:T(8,128)(2,1)S(1)}, bf16[2,160,512]{2,1,0:T(8,128)(2,1)S(1)}, u32[]{:S(2)}, u32[]{:S(2)}) collective-permute-start(bf16[2,160,512]{2,1,0:T(8,128)(2,1)S(1)} %get-tuple-element.129), channel_id=1, source_target_pairs={{0,4},{4,0},{8,12},{12,8},{1,5},{5,1},{9,13},{13,9},{2,6},{6,2},{1... | collective-permute-start | bytes 983048 | tf_op jit(solution)/shard_map/ppermute | solution.py:378
  73.8 0.4 collective-permute-start.16
  74.1 7.8 %multiply.12 = (f32[96,2048]{1,0:T(8,128)S(1)}, f32[8,128]{1,0:T(8,128)S(1)}) custom-call(bf16[48,5120]{1,0:T(8,128)(2,1)S(1)} %get-tuple-element.130.refs_0_, bf16[48,5120]{1,0:T(8,128)(2,1)S(1)} %collective-permute-done.18.refs_1_, bf16[13312,2048]{1,0:T(8,128)(2,1)} %refs_2_.7, f32[8,128]{1,0:T(8,128)S(1)} %get-tuple-element.131.refs_3_), custom_call_target="tpu_custom_call" | custom-call | flops 10000000000 | bytes 1024 | tf_op jit(solution)/shard_map/multiply/pallas_call | solution.py:109
  82.0 4.0 %collective-permute-done.17.refs_1_ = bf16[2,160,512]{2,1,0:T(8,128)(2,1)S(1)} collective-permute-done((bf16[2,160,512]{2,1,0:T(8,128)(2,1)S(1)}, bf16[2,160,512]{2,1,0:T(8,128)(2,1)S(1)}, u32[]{:S(2)}, u32[]{:S(2)}) %collective-permute-start.17) | collective-permute-done | bytes 327712 | tf_op jit(solution)/shard_map/ppermute | solution.py:378
  86.1 2.1 %collective-permute-done.16.refs_1_.refs_2_ = bf16[2,128,512]{2,1,0:T(8,128)(2,1)S(1)} collective-permute-done((bf16[2,128,512]{2,1,0:T(8,128)(2,1)S(1)}, bf16[2,128,512]{2,1,0:T(8,128)(2,1)S(1)}, u32[]{:S(2)}, u32[]{:S(2)}) %collective-permute-start.16) | collective-permute-done | bytes 262176 | tf_op jit(solution)/shard_map/ppermute | solution.py:378
  88.2 3.0 %collective-permute-done.20.refs_0_ = bf16[48,8192]{1,0:T(8,128)(2,1)S(1)} collective-permute-done((bf16[48,8192]{1,0:T(8,128)(2,1)S(1)}, bf16[48,8192]{1,0:T(8,128)(2,1)S(1)}, u32[]{:S(2)}, u32[]{:S(2)}) %collective-permute-start.20) | collective-permute-done | bytes 786464 | tf_op jit(solution)/shard_map/ppermute | solution.py:375
  91.2 0.4 collective-permute-start.23
  91.5 1.5 %collective-permute-start.19 = (bf16[4,128,512]{2,1,0:T(8,128)(2,1)S(1)}, bf16[4,128,512]{2,1,0:T(8,128)(2,1)S(1)}, u32[]{:S(2)}, u32[]{:S(2)}) collective-permute-start(bf16[4,128,512]{2,1,0:T(8,128)(2,1)S(1)} %get-tuple-element.134), channel_id=1, source_target_pairs={{0,4},{4,0},{8,12},{12,8},{1,5},{5,1},{9,13},{13,9},{2,6},{6,2},{1... | collective-permute-start | bytes 1572872 | tf_op jit(solution)/shard_map/ppermute | solution.py:378
  93.1 0.4 collective-permute-done.21.refs_1_
  93.5 11.6 %multiply.13 = (bf16[2,96,512]{2,1,0:T(8,128)(2,1)S(1)}, bf16[2,96,512]{2,1,0:T(8,128)(2,1)S(1)}, f32[8,128]{1,0:T(8,128)S(1)}) custom-call(bf16[48,8192]{1,0:T(8,128)(2,1)S(1)} %get-tuple-element.137.refs_0_, bf16[48,8192]{1,0:T(8,128)(2,1)S(1)} %collective-permute-done.21.refs_1_, bf16[13312,2048]{1,0:T(8,128)(2,1)} %refs_2_.7, ...), custom_call_target="tpu_custom_call" | custom-call | flops 10000000000 | bytes 1024 | tf_op jit(solution)/shard_map/multiply/pallas_call | solution.py:109
  105.1 1.7 %collective-permute-start.22 = (bf16[2,96,512]{2,1,0:T(8,128)(2,1)S(1)}, bf16[2,96,512]{2,1,0:T(8,128)(2,1)S(1)}, u32[]{:S(2)}, u32[]{:S(2)}) collective-permute-start(bf16[2,96,512]{2,1,0:T(8,128)(2,1)S(1)} %get-tuple-element.141), channel_id=1, source_target_pairs={{0,4},{4,0},{8,12},{12,8},{1,5},{5,1},{9,13},{13,9},{2,6},{6,2},{1... | collective-permute-start | bytes 589832 | tf_op jit(solution)/shard_map/ppermute | solution.py:378
  106.8 0.6 collective-permute-start.24
  107.4 0.7 collective-permute-start.25
  108.1 5.3 %collective-permute-done.22.refs_1_ = bf16[2,96,512]{2,1,0:T(8,128)(2,1)S(1)} collective-permute-done((bf16[2,96,512]{2,1,0:T(8,128)(2,1)S(1)}, bf16[2,96,512]{2,1,0:T(8,128)(2,1)S(1)}, u32[]{:S(2)}, u32[]{:S(2)}) %collective-permute-start.22) | collective-permute-done | bytes 196640 | tf_op jit(solution)/shard_map/ppermute | solution.py:378
  113.4 2.5 %collective-permute-start.26 = (bf16[1,96,512]{2,1,0:T(8,128)(2,1)S(1)}, bf16[1,96,512]{2,1,0:T(8,128)(2,1)S(1)}, u32[]{:S(2)}, u32[]{:S(2)}) collective-permute-start(bf16[1,96,512]{2,1,0:T(8,128)(2,1)S(1)} %get-tuple-element.152), channel_id=1, source_target_pairs={{0,8},{4,12},{8,0},{12,4},{1,9},{5,13},{9,1},{13,5},{2,10},{6,14},... | collective-permute-start | bytes 294920 | tf_op jit(solution)/shard_map/ppermute | solution.py:378
  115.9 1.5 %encode.3 = (bf16[128,8192]{1,0:T(8,128)(2,1)}, f32[128,128]{1,0:T(8,128)S(1)}, f32[8,128]{1,0:T(8,128)S(1)}) custom-call(bf16[2,128,512]{2,1,0:T(8,128)(2,1)S(1)} %get-tuple-element.127.refs_0_, bf16[4,128,512]{2,1,0:T(8,128)(2,1)S(1)} %collective-permute-done.19.refs_1_.refs_3_, bf16[2,128,512]{2,1,0:T(8,128)(2,1)S(1)} %collective-permute-done.16.refs_1_.refs_2_, ...), custom_call_target="tpu_custom_call" | custom-call | flops 10000000000 | bytes 1024 | tf_op jit(solution)/shard_map/encode/pallas_call | solution.py:109
  117.4 3.3 %collective-permute-done.26.refs_1_ = bf16[1,96,512]{2,1,0:T(8,128)(2,1)S(1)} collective-permute-done((bf16[1,96,512]{2,1,0:T(8,128)(2,1)S(1)}, bf16[1,96,512]{2,1,0:T(8,128)(2,1)S(1)}, u32[]{:S(2)}, u32[]{:S(2)}) %collective-permute-start.26) | collective-permute-done | bytes 98336 | tf_op jit(solution)/shard_map/ppermute | solution.py:378
  120.7 0.8 collective-permute-start.27
  121.5 0.5 collective-permute-start.28
  122.1 4.0 %collective-permute-done.28.refs_0_ = bf16[1,48,512]{2,1,0:T(8,128)(2,1)S(1)} collective-permute-done((bf16[1,48,512]{2,1,0:T(8,128)(2,1)S(1)}, bf16[1,48,512]{2,1,0:T(8,128)(2,1)S(1)}, u32[]{:S(2)}, u32[]{:S(2)}) %collective-permute-start.28) | collective-permute-done | bytes 49184 | tf_op jit(solution)/shard_map/ppermute | solution.py:375
  126.1 4.4 %collective-permute-done.27.refs_1_.refs_4_ = bf16[2,80,512]{2,1,0:T(8,128)(2,1)S(1)} collective-permute-done((bf16[2,80,512]{2,1,0:T(8,128)(2,1)S(1)}, bf16[2,80,512]{2,1,0:T(8,128)(2,1)S(1)}, u32[]{:S(2)}, u32[]{:S(2)}) %collective-permute-start.27) | collective-permute-done | bytes 163872 | tf_op jit(solution)/shard_map/ppermute | solution.py:378
  130.7 2.0 %collective-permute-start.31 = (bf16[2,48,512]{2,1,0:T(8,128)(2,1)S(1)}, bf16[2,48,512]{2,1,0:T(8,128)(2,1)S(1)}, u32[]{:S(2)}, u32[]{:S(2)}) collective-permute-start(bf16[2,48,512]{2,1,0:T(8,128)(2,1)S(1)} %get-tuple-element.164.refs_2_), channel_id=1, source_target_pairs={{0,4},{4,0},{8,12},{12,8},{1,5},{5,1},{9,13},{13,9},{2,6},{6,2},{1... | collective-permute-start | bytes 294920 | tf_op jit(solution)/shard_map/ppermute | solution.py:378
  132.7 0.2 collective-permute-start.32
  132.9 2.2 %collective-permute-start.33 = (bf16[2,48,512]{2,1,0:T(8,128)(2,1)S(1)}, bf16[2,48,512]{2,1,0:T(8,128)(2,1)S(1)}, u32[]{:S(2)}, u32[]{:S(2)}) collective-permute-start(bf16[2,48,512]{2,1,0:T(8,128)(2,1)S(1)} %get-tuple-element.164.refs_2_), channel_id=1, source_target_pairs={{0,12},{4,8},{8,4},{12,0},{1,13},{5,9},{9,5},{13,1},{2,14},{6,10},... | collective-permute-start | bytes 294920 | tf_op jit(solution)/shard_map/ppermute | solution.py:378
  135.1 7.1 %collective-permute-done.30.refs_3_.refs_5_ = bf16[4,80,512]{2,1,0:T(8,128)(2,1)S(1)} collective-permute-done((bf16[4,80,512]{2,1,0:T(8,128)(2,1)S(1)}, bf16[4,80,512]{2,1,0:T(8,128)(2,1)S(1)}, u32[]{:S(2)}, u32[]{:S(2)}) %collective-permute-start.30) | collective-permute-done | bytes 327712 | tf_op jit(solution)/shard_map/ppermute | solution.py:378
  142.2 1.2 encode.4
  143.4 3.0 %collective-permute-done.33.refs_5_ = bf16[2,48,512]{2,1,0:T(8,128)(2,1)S(1)} collective-permute-done((bf16[2,48,512]{2,1,0:T(8,128)(2,1)S(1)}, bf16[2,48,512]{2,1,0:T(8,128)(2,1)S(1)}, u32[]{:S(2)}, u32[]{:S(2)}) %collective-permute-start.33) | collective-permute-done | bytes 98336 | tf_op jit(solution)/shard_map/ppermute | solution.py:378
  146.5 1.6 %encode.5 = (bf16[128,8192]{1,0:T(8,128)(2,1)}, bf16[64,128]{1,0:T(8,128)(2,1)}, f32[8,128]{1,0:T(8,128)}) custom-call(bf16[128,8192]{1,0:T(8,128)(2,1)} %get-tuple-element.162.refs_0_, f32[128,128]{1,0:T(8,128)S(1)} %get-tuple-element.163.refs_1_, bf16[2,48,512]{2,1,0:T(8,128)(2,1)S(1)} %get-tuple-element.164.refs_2_, ...), custom_call_target="tpu_custom_call", output_to_operand_aliasing={{0}: (0, {})} | custom-call | bytes 1024 | tf_op jit(solution)/shard_map/encode/pallas_call | solution.py:109
  (52 shorter events, 1.3 us)
Async XLA Ops:
  2.1 9.4 %collective-permute-start.4 = (bf16[80,1024]{1,0:T(8,128)(2,1)S(1)}, bf16[80,1024]{1,0:T(8,128)(2,1)S(1)}, u32[]{:S(2)}, u32[]{:S(2)}) collective-permute-start(bf16[80,1024]{1,0:T(8,128)(2,1)S(1)} %get-tuple-element.90), channel_id=1, source_target_pairs={{0,2},{1,3},{2,0},{3,1},{4,6},{5,7},{6,4},{7,5},{8,10},{9,11},{10,... | collective-permute-start | bytes 491528 | tf_op jit(solution)/shard_map/ppermute | solution.py:375
  10.5 3.1 %collective-permute-start.3 = (bf16[128,4096]{1,0:T(8,128)(2,1)S(1)}, bf16[128,4096]{1,0:T(8,128)(2,1)S(1)}, u32[]{:S(2)}, u32[]{:S(2)}) collective-permute-start(bf16[128,4096]{1,0:T(8,128)(2,1)S(1)} %get-tuple-element.89.refs_2_), channel_id=1, source_target_pairs={{0,1},{1,0},{2,3},{3,2},{4,5},{5,4},{6,7},{7,6},{8,9},{9,8},{10,11... | collective-permute-start | bytes 3145736 | tf_op jit(solution)/shard_map/ppermute | solution.py:375
  10.5 3.0 %collective-permute-start.2 = (bf16[128,1024]{1,0:T(8,128)(2,1)S(1)}, bf16[128,1024]{1,0:T(8,128)(2,1)S(1)}, u32[]{:S(2)}, u32[]{:S(2)}) collective-permute-start(bf16[128,1024]{1,0:T(8,128)(2,1)S(1)} %get-tuple-element.88.refs_0_), channel_id=1, source_target_pairs={{0,1},{1,0},{2,3},{3,2},{4,5},{5,4},{6,7},{7,6},{8,9},{9,8},{10,11... | collective-permute-start | bytes 786440 | tf_op jit(solution)/shard_map/ppermute | solution.py:375
  11.0 11.7 %collective-permute-start = (bf16[128,4096]{1,0:T(8,128)(2,1)S(1)}, bf16[128,4096]{1,0:T(8,128)(2,1)S(1)}, u32[]{:S(2)}, u32[]{:S(2)}) collective-permute-start(bf16[128,4096]{1,0:T(8,128)(2,1)S(1)} %get-tuple-element.86.refs_0_), channel_id=1, source_target_pairs={{0,1},{1,0},{2,3},{3,2},{4,5},{5,4},{6,7},{7,6},{8,9},{9,8},{10,11... | collective-permute-start | bytes 3145736 | tf_op jit(solution)/shard_map/ppermute | solution.py:375
  11.1 11.6 %collective-permute-start.1 = (bf16[128,4096]{1,0:T(8,128)(2,1)S(1)}, bf16[128,4096]{1,0:T(8,128)(2,1)S(1)}, u32[]{:S(2)}, u32[]{:S(2)}) collective-permute-start(bf16[128,4096]{1,0:T(8,128)(2,1)S(1)} %get-tuple-element.87.refs_2_), channel_id=1, source_target_pairs={{0,1},{1,0},{2,3},{3,2},{4,5},{5,4},{6,7},{7,6},{8,9},{9,8},{10,11... | collective-permute-start | bytes 3145736 | tf_op jit(solution)/shard_map/ppermute | solution.py:375
  11.6 24.5 %collective-permute-start.8 = (bf16[80,4096]{1,0:T(8,128)(2,1)S(1)}, bf16[80,4096]{1,0:T(8,128)(2,1)S(1)}, u32[]{:S(2)}, u32[]{:S(2)}) collective-permute-start(bf16[80,4096]{1,0:T(8,128)(2,1)S(1)} %get-tuple-element.100), channel_id=1, source_target_pairs={{0,2},{1,3},{2,0},{3,1},{4,6},{5,7},{6,4},{7,5},{8,10},{9,11},{10,... | collective-permute-start | bytes 1966088 | tf_op jit(solution)/shard_map/ppermute | solution.py:375
  13.6 34.5 %collective-permute-start.6 = (bf16[80,4096]{1,0:T(8,128)(2,1)S(1)}, bf16[80,4096]{1,0:T(8,128)(2,1)S(1)}, u32[]{:S(2)}, u32[]{:S(2)}) collective-permute-start(bf16[80,4096]{1,0:T(8,128)(2,1)S(1)} %get-tuple-element.98), channel_id=1, source_target_pairs={{0,2},{1,3},{2,0},{3,1},{4,6},{5,7},{6,4},{7,5},{8,10},{9,11},{10,... | collective-permute-start | bytes 1966088 | tf_op jit(solution)/shard_map/ppermute | solution.py:375
  13.6 26.5 %collective-permute-start.7 = (bf16[80,1024]{1,0:T(8,128)(2,1)S(1)}, bf16[80,1024]{1,0:T(8,128)(2,1)S(1)}, u32[]{:S(2)}, u32[]{:S(2)}) collective-permute-start(bf16[80,1024]{1,0:T(8,128)(2,1)S(1)} %get-tuple-element.99.refs_0_), channel_id=1, source_target_pairs={{0,1},{1,0},{2,3},{3,2},{4,5},{5,4},{6,7},{7,6},{8,9},{9,8},{10,11... | collective-permute-start | bytes 491528 | tf_op jit(solution)/shard_map/ppermute | solution.py:375
  36.1 4.0 %collective-permute-start.9 = (bf16[80,4096]{1,0:T(8,128)(2,1)S(1)}, bf16[80,4096]{1,0:T(8,128)(2,1)S(1)}, u32[]{:S(2)}, u32[]{:S(2)}) collective-permute-start(bf16[80,4096]{1,0:T(8,128)(2,1)S(1)} %get-tuple-element.102.refs_2_), channel_id=1, source_target_pairs={{0,1},{1,0},{2,3},{3,2},{4,5},{5,4},{6,7},{7,6},{8,9},{9,8},{10,11... | collective-permute-start | bytes 1966088 | tf_op jit(solution)/shard_map/ppermute | solution.py:375
  36.5 14.3 %collective-permute-start.5 = (bf16[2,256,512]{2,1,0:T(8,128)(2,1)S(1)}, bf16[2,256,512]{2,1,0:T(8,128)(2,1)S(1)}, u32[]{:S(2)}, u32[]{:S(2)}) collective-permute-start(bf16[2,256,512]{2,1,0:T(8,128)(2,1)S(1)} %get-tuple-element.96), channel_id=1, source_target_pairs={{0,4},{4,0},{8,12},{12,8},{1,5},{5,1},{9,13},{13,9},{2,6},{6,2},{1... | collective-permute-start | bytes 1572872 | tf_op jit(solution)/shard_map/ppermute | solution.py:378
  38.7 23.3 %collective-permute-start.11 = (bf16[80,4096]{1,0:T(8,128)(2,1)S(1)}, bf16[80,4096]{1,0:T(8,128)(2,1)S(1)}, u32[]{:S(2)}, u32[]{:S(2)}) collective-permute-start(bf16[80,4096]{1,0:T(8,128)(2,1)S(1)} %get-tuple-element.111), channel_id=1, source_target_pairs={{0,2},{1,3},{2,0},{3,1},{4,6},{5,7},{6,4},{7,5},{8,10},{9,11},{10,... | collective-permute-start | bytes 1966088 | tf_op jit(solution)/shard_map/ppermute | solution.py:375
  48.0 7.2 %collective-permute-start.12 = (bf16[80,4096]{1,0:T(8,128)(2,1)S(1)}, bf16[80,4096]{1,0:T(8,128)(2,1)S(1)}, u32[]{:S(2)}, u32[]{:S(2)}) collective-permute-start(bf16[80,4096]{1,0:T(8,128)(2,1)S(1)} %get-tuple-element.112.refs_0_), channel_id=1, source_target_pairs={{0,1},{1,0},{2,3},{3,2},{4,5},{5,4},{6,7},{7,6},{8,9},{9,8},{10,11... | collective-permute-start | bytes 1966088 | tf_op jit(solution)/shard_map/ppermute | solution.py:375
  51.0 20.0 %collective-permute-start.10 = (bf16[1,256,512]{2,1,0:T(8,128)(2,1)S(1)}, bf16[1,256,512]{2,1,0:T(8,128)(2,1)S(1)}, u32[]{:S(2)}, u32[]{:S(2)}) collective-permute-start(bf16[1,256,512]{2,1,0:T(8,128)(2,1)S(1)} %get-tuple-element.110), channel_id=1, source_target_pairs={{0,8},{4,12},{8,0},{12,4},{1,9},{5,13},{9,1},{13,5},{2,10},{6,14},... | collective-permute-start | bytes 786440 | tf_op jit(solution)/shard_map/ppermute | solution.py:378
  53.8 17.2 %collective-permute-start.15 = (bf16[48,5120]{1,0:T(8,128)(2,1)S(1)}, bf16[48,5120]{1,0:T(8,128)(2,1)S(1)}, u32[]{:S(2)}, u32[]{:S(2)}) collective-permute-start(bf16[48,5120]{1,0:T(8,128)(2,1)S(1)} %get-tuple-element.124), channel_id=1, source_target_pairs={{0,2},{1,3},{2,0},{3,1},{4,6},{5,7},{6,4},{7,5},{8,10},{9,11},{10,... | collective-permute-start | bytes 1474568 | tf_op jit(solution)/shard_map/ppermute | solution.py:375
  62.0 2.2 %collective-permute-start.13 = (bf16[80,4096]{1,0:T(8,128)(2,1)S(1)}, bf16[80,4096]{1,0:T(8,128)(2,1)S(1)}, u32[]{:S(2)}, u32[]{:S(2)}) collective-permute-start(bf16[80,4096]{1,0:T(8,128)(2,1)S(1)} %get-tuple-element.116.refs_0_), channel_id=1, source_target_pairs={{0,1},{1,0},{2,3},{3,2},{4,5},{5,4},{6,7},{7,6},{8,9},{9,8},{10,11... | collective-permute-start | bytes 1966088 | tf_op jit(solution)/shard_map/ppermute | solution.py:375
  71.0 3.1 %collective-permute-start.18 = (bf16[48,5120]{1,0:T(8,128)(2,1)S(1)}, bf16[48,5120]{1,0:T(8,128)(2,1)S(1)}, u32[]{:S(2)}, u32[]{:S(2)}) collective-permute-start(bf16[48,5120]{1,0:T(8,128)(2,1)S(1)} %get-tuple-element.130.refs_0_), channel_id=1, source_target_pairs={{0,1},{1,0},{2,3},{3,2},{4,5},{5,4},{6,7},{7,6},{8,9},{9,8},{10,11... | collective-permute-start | bytes 1474568 | tf_op jit(solution)/shard_map/ppermute | solution.py:375
  71.2 2.5 %collective-permute-start.14 = (bf16[1,128,512]{2,1,0:T(8,128)(2,1)S(1)}, bf16[1,128,512]{2,1,0:T(8,128)(2,1)S(1)}, u32[]{:S(2)}, u32[]{:S(2)}) collective-permute-start(bf16[1,128,512]{2,1,0:T(8,128)(2,1)S(1)} %get-tuple-element.123), channel_id=1, source_target_pairs={{0,1},{1,0},{2,3},{3,2},{4,5},{5,4},{6,7},{7,6},{8,9},{9,8},{10,11... | collective-permute-start | bytes 393224 | tf_op jit(solution)/shard_map/ppermute | solution.py:375
  71.6 19.6 %collective-permute-start.20 = (bf16[48,8192]{1,0:T(8,128)(2,1)S(1)}, bf16[48,8192]{1,0:T(8,128)(2,1)S(1)}, u32[]{:S(2)}, u32[]{:S(2)}) collective-permute-start(bf16[48,8192]{1,0:T(8,128)(2,1)S(1)} %get-tuple-element.135), channel_id=1, source_target_pairs={{0,2},{1,3},{2,0},{3,1},{4,6},{5,7},{6,4},{7,5},{8,10},{9,11},{10,... | collective-permute-start | bytes 2359304 | tf_op jit(solution)/shard_map/ppermute | solution.py:375
  72.1 13.9 %collective-permute-start.17 = (bf16[2,160,512]{2,1,0:T(8,128)(2,1)S(1)}, bf16[2,160,512]{2,1,0:T(8,128)(2,1)S(1)}, u32[]{:S(2)}, u32[]{:S(2)}) collective-permute-start(bf16[2,160,512]{2,1,0:T(8,128)(2,1)S(1)} %get-tuple-element.129), channel_id=1, source_target_pairs={{0,4},{4,0},{8,12},{12,8},{1,5},{5,1},{9,13},{13,9},{2,6},{6,2},{1... | collective-permute-start | bytes 983048 | tf_op jit(solution)/shard_map/ppermute | solution.py:378
  73.8 14.4 %collective-permute-start.16 = (bf16[2,128,512]{2,1,0:T(8,128)(2,1)S(1)}, bf16[2,128,512]{2,1,0:T(8,128)(2,1)S(1)}, u32[]{:S(2)}, u32[]{:S(2)}) collective-permute-start(bf16[2,128,512]{2,1,0:T(8,128)(2,1)S(1)} %get-tuple-element.127.refs_0_), channel_id=1, source_target_pairs={{0,8},{4,12},{8,0},{12,4},{1,9},{5,13},{9,1},{13,5},{2,10},{6,14},... | collective-permute-start | bytes 786440 | tf_op jit(solution)/shard_map/ppermute | solution.py:378
  91.2 2.3 %collective-permute-start.21 = (bf16[48,8192]{1,0:T(8,128)(2,1)S(1)}, bf16[48,8192]{1,0:T(8,128)(2,1)S(1)}, u32[]{:S(2)}, u32[]{:S(2)}) collective-permute-start(bf16[48,8192]{1,0:T(8,128)(2,1)S(1)} %get-tuple-element.137.refs_0_), channel_id=1, source_target_pairs={{0,1},{1,0},{2,3},{3,2},{4,5},{5,4},{6,7},{7,6},{8,9},{9,8},{10,11... | collective-permute-start | bytes 2359304 | tf_op jit(solution)/shard_map/ppermute | solution.py:375
  91.2 15.6 %collective-permute-start.23 = (bf16[1,160,512]{2,1,0:T(8,128)(2,1)S(1)}, bf16[1,160,512]{2,1,0:T(8,128)(2,1)S(1)}, u32[]{:S(2)}, u32[]{:S(2)}) collective-permute-start(bf16[1,160,512]{2,1,0:T(8,128)(2,1)S(1)} %get-tuple-element.143), channel_id=1, source_target_pairs={{0,8},{4,12},{8,0},{12,4},{1,9},{5,13},{9,1},{13,5},{2,10},{6,14},... | collective-permute-start | bytes 491528 | tf_op jit(solution)/shard_map/ppermute | solution.py:378
  91.5 24.4 %collective-permute-start.19 = (bf16[4,128,512]{2,1,0:T(8,128)(2,1)S(1)}, bf16[4,128,512]{2,1,0:T(8,128)(2,1)S(1)}, u32[]{:S(2)}, u32[]{:S(2)}) collective-permute-start(bf16[4,128,512]{2,1,0:T(8,128)(2,1)S(1)} %get-tuple-element.134), channel_id=1, source_target_pairs={{0,4},{4,0},{8,12},{12,8},{1,5},{5,1},{9,13},{13,9},{2,6},{6,2},{1... | collective-permute-start | bytes 1572872 | tf_op jit(solution)/shard_map/ppermute | solution.py:378
  105.1 8.2 %collective-permute-start.22 = (bf16[2,96,512]{2,1,0:T(8,128)(2,1)S(1)}, bf16[2,96,512]{2,1,0:T(8,128)(2,1)S(1)}, u32[]{:S(2)}, u32[]{:S(2)}) collective-permute-start(bf16[2,96,512]{2,1,0:T(8,128)(2,1)S(1)} %get-tuple-element.141), channel_id=1, source_target_pairs={{0,4},{4,0},{8,12},{12,8},{1,5},{5,1},{9,13},{13,9},{2,6},{6,2},{1... | collective-permute-start | bytes 589832 | tf_op jit(solution)/shard_map/ppermute | solution.py:378
  106.8 13.9 %collective-permute-start.24 = (bf16[1,80,512]{2,1,0:T(8,128)(2,1)S(1)}, bf16[1,80,512]{2,1,0:T(8,128)(2,1)S(1)}, u32[]{:S(2)}, u32[]{:S(2)}) collective-permute-start(bf16[1,80,512]{2,1,0:T(8,128)(2,1)S(1)} %get-tuple-element.149), channel_id=1, source_target_pairs={{0,2},{1,3},{2,0},{3,1},{4,6},{5,7},{6,4},{7,5},{8,10},{9,11},{10,... | collective-permute-start | bytes 245768 | tf_op jit(solution)/shard_map/ppermute | solution.py:375
  107.4 13.3 %collective-permute-start.25 = (bf16[1,80,512]{2,1,0:T(8,128)(2,1)S(1)}, bf16[1,80,512]{2,1,0:T(8,128)(2,1)S(1)}, u32[]{:S(2)}, u32[]{:S(2)}) collective-permute-start(bf16[1,80,512]{2,1,0:T(8,128)(2,1)S(1)} %get-tuple-element.150), channel_id=1, source_target_pairs={{0,3},{1,2},{2,1},{3,0},{4,7},{5,6},{6,5},{7,4},{8,11},{9,10},{10,... | collective-permute-start | bytes 245768 | tf_op jit(solution)/shard_map/ppermute | solution.py:375
  113.4 7.3 %collective-permute-start.26 = (bf16[1,96,512]{2,1,0:T(8,128)(2,1)S(1)}, bf16[1,96,512]{2,1,0:T(8,128)(2,1)S(1)}, u32[]{:S(2)}, u32[]{:S(2)}) collective-permute-start(bf16[1,96,512]{2,1,0:T(8,128)(2,1)S(1)} %get-tuple-element.152), channel_id=1, source_target_pairs={{0,8},{4,12},{8,0},{12,4},{1,9},{5,13},{9,1},{13,5},{2,10},{6,14},... | collective-permute-start | bytes 294920 | tf_op jit(solution)/shard_map/ppermute | solution.py:378
  120.7 9.8 %collective-permute-start.27 = (bf16[2,80,512]{2,1,0:T(8,128)(2,1)S(1)}, bf16[2,80,512]{2,1,0:T(8,128)(2,1)S(1)}, u32[]{:S(2)}, u32[]{:S(2)}) collective-permute-start(bf16[2,80,512]{2,1,0:T(8,128)(2,1)S(1)} %get-tuple-element.155.refs_0_.refs_2_), channel_id=1, source_target_pairs={{0,8},{4,12},{8,0},{12,4},{1,9},{5,13},{9,1},{13,5},{2,10},{6,14},... | collective-permute-start | bytes 491528 | tf_op jit(solution)/shard_map/ppermute | solution.py:378
  121.5 4.6 %collective-permute-start.28 = (bf16[1,48,512]{2,1,0:T(8,128)(2,1)S(1)}, bf16[1,48,512]{2,1,0:T(8,128)(2,1)S(1)}, u32[]{:S(2)}, u32[]{:S(2)}) collective-permute-start(bf16[1,48,512]{2,1,0:T(8,128)(2,1)S(1)} %get-tuple-element.156), channel_id=1, source_target_pairs={{0,2},{1,3},{2,0},{3,1},{4,6},{5,7},{6,4},{7,5},{8,10},{9,11},{10,... | collective-permute-start | bytes 147464 | tf_op jit(solution)/shard_map/ppermute | solution.py:375
  122.1 4.0 %collective-permute-start.29 = (bf16[1,48,512]{2,1,0:T(8,128)(2,1)S(1)}, bf16[1,48,512]{2,1,0:T(8,128)(2,1)S(1)}, u32[]{:S(2)}, u32[]{:S(2)}) collective-permute-start(bf16[1,48,512]{2,1,0:T(8,128)(2,1)S(1)} %get-tuple-element.157), channel_id=1, source_target_pairs={{0,3},{1,2},{2,1},{3,0},{4,7},{5,6},{6,5},{7,4},{8,11},{9,10},{10,... | collective-permute-start | bytes 147464 | tf_op jit(solution)/shard_map/ppermute | solution.py:375
  130.6 11.6 %collective-permute-start.30 = (bf16[4,80,512]{2,1,0:T(8,128)(2,1)S(1)}, bf16[4,80,512]{2,1,0:T(8,128)(2,1)S(1)}, u32[]{:S(2)}, u32[]{:S(2)}) collective-permute-start(bf16[4,80,512]{2,1,0:T(8,128)(2,1)S(1)} %get-tuple-element.160), channel_id=1, source_target_pairs={{0,4},{4,0},{8,12},{12,8},{1,5},{5,1},{9,13},{13,9},{2,6},{6,2},{1... | collective-permute-start | bytes 983048 | tf_op jit(solution)/shard_map/ppermute | solution.py:378
  130.7 12.8 %collective-permute-start.31 = (bf16[2,48,512]{2,1,0:T(8,128)(2,1)S(1)}, bf16[2,48,512]{2,1,0:T(8,128)(2,1)S(1)}, u32[]{:S(2)}, u32[]{:S(2)}) collective-permute-start(bf16[2,48,512]{2,1,0:T(8,128)(2,1)S(1)} %get-tuple-element.164.refs_2_), channel_id=1, source_target_pairs={{0,4},{4,0},{8,12},{12,8},{1,5},{5,1},{9,13},{13,9},{2,6},{6,2},{1... | collective-permute-start | bytes 294920 | tf_op jit(solution)/shard_map/ppermute | solution.py:378
  132.7 10.8 %collective-permute-start.32 = (bf16[2,48,512]{2,1,0:T(8,128)(2,1)S(1)}, bf16[2,48,512]{2,1,0:T(8,128)(2,1)S(1)}, u32[]{:S(2)}, u32[]{:S(2)}) collective-permute-start(bf16[2,48,512]{2,1,0:T(8,128)(2,1)S(1)} %get-tuple-element.164.refs_2_), channel_id=1, source_target_pairs={{0,8},{4,12},{8,0},{12,4},{1,9},{5,13},{9,1},{13,5},{2,10},{6,14},... | collective-permute-start | bytes 294920 | tf_op jit(solution)/shard_map/ppermute | solution.py:378
  132.9 13.6 %collective-permute-start.33 = (bf16[2,48,512]{2,1,0:T(8,128)(2,1)S(1)}, bf16[2,48,512]{2,1,0:T(8,128)(2,1)S(1)}, u32[]{:S(2)}, u32[]{:S(2)}) collective-permute-start(bf16[2,48,512]{2,1,0:T(8,128)(2,1)S(1)} %get-tuple-element.164.refs_2_), channel_id=1, source_target_pairs={{0,12},{4,8},{8,4},{12,0},{1,13},{5,9},{9,5},{13,1},{2,14},{6,10},... | collective-permute-start | bytes 294920 | tf_op jit(solution)/shard_map/ppermute | solution.py:378

commit v8 on v7

--- a/solution.py
+++ b/solution.py
@@ -11,7 +11,6 @@
 EPSILON = 1e-06
 
 STEP = 1024
-FIRST = 1
 PIECE = 4
 DEPTH = 512
 SLOTS = 6
@@ -367,8 +366,9 @@
     tp, batch = lax.axis_size("tp"), lax.axis_size("batch")
     out_width = down_weight.shape[1] * batch
     cut = rows * EARLY // 8
-    ends = [FIRST, FIRST + PIECE, FIRST + 2 * PIECE, FIRST + 3 * PIECE]
-    spans = list(zip([0] + ends, ends))
+    steps = width // STEP
+    first, middle = steps - 2 * PIECE, steps - PIECE
+    half = steps // 2
     chain = Chain()
 
     def swap(value, flip):
@@ -395,39 +395,34 @@
         total = add(chain, [keep, got], [(0, 0, keep.shape[1]), (1, 0, keep.shape[1])])
         return [total[0], shift(total[1], 2)]
 
-    near_0, send_0 = activate(
-        chain, gate_input, up_input, 0, FIRST, [(0, rows, 0, FIRST), (0, cut, 0, FIRST)]
-    )
-    far_0 = swap(send_0, 2)
-    pieces = activate(
+    near_0, near_1, far_0, far_1, far_2, late_0, late_1 = activate(
         chain,
         gate_input,
         up_input,
         0,
-        width // STEP,
-        [(0, rows, a, b) for a, b in spans[1:]]
-        + [(0, cut, a, b) for a, b in spans[1:]]
-        + [(cut, rows, a, b) for a, b in [(0, ends[1]), (ends[1], ends[3])]],
-    )
-    near, early, late = [near_0] + pieces[:3], pieces[3:6], pieces[6:]
-    near = [[h, swap(h, 1)] for h in near]
+        steps,
+        [(0, rows, 0, first), (0, rows, first, steps)]
+        + [(0, cut, 0, first), (0, cut, first, middle), (0, cut, middle, steps)]
+        + [(cut, rows, 0, half), (cut, rows, half, steps)],
+    )
+    far_0 = swap(far_0, 2)
+    near_0, near_1 = [near_0, swap(near_0, 1)], [near_1, swap(near_1, 1)]
+
+    total = product([near_0], 0, None)
+    far_1 = swap(chain.pin(far_1), 2)
+    near = product([near_1], first, total, HALVES)
+    near = [near[0], shift(near[1], 1)]
+
     far_0 = both_cores(far_0)
-    far_1, far_2 = swap(early[0], 2), swap(early[1], 2)
-
-    total = product(near[:2], 0, None)
-    near = product(near[2:], ends[1], total, HALVES)
-    near = [near[0], shift(near[1], 1)]
-
+    far_2 = swap(chain.pin(far_2), 2)
+    total = product([far_0], 0, None)
     far_1 = both_cores(far_1)
-    far_3 = swap(chain.pin(early[2]), 2)
-    total = product([far_0, far_1], 0, None)
+    late_0 = swap(chain.pin(late_0), 2)
+    near = sum_pair(near)
+    total = product([far_1], first, total)
     far_2 = both_cores(far_2)
-    late_0 = swap(chain.pin(late[0]), 2)
-    near = sum_pair(near)
-    total = product([far_2], ends[1], total)
-    far_3 = both_cores(far_3)
-    late_1 = swap(chain.pin(late[1]), 2)
-    far = product([far_3], ends[2], total, HALVES)
+    late_1 = swap(chain.pin(late_1), 2)
+    far = product([far_2], middle, total, HALVES)
     far = [far[0], shift(far[1], 1)]
     near = sum_home(near, 0)
 
@@ -439,19 +434,19 @@
     near.append(join(chain, *near))
     near[2] = shift(near[2], 1)
     late_1 = both_cores(late_1)
-    last = product([late_1], ends[1], total, HALVES)
+    last = product([late_1], half, total, HALVES)
     last = [last[0], shift(last[1], 1)]
     far = sum_home(far, 2, 10**10)
     last = sum_pair(last)
     near = [(near[0], 0), (near[2], 0), (near[1], 0), (near[2], 2)]
     codes, scales = encode_columns(chain, None, None, near, 0, 0, rows, out_width, cost=10**10)
-    last = sum_home(last, 2)
     far = join(chain, *far)
     far = [far, shift(far, 2)]
+    last = sum_home(last, 2)
+    far.append(join(chain, *far))
+    far[2] = shift(far[2], 1)
     last = join(chain, *last)
     last = [last] + [shift(last, flip) for flip in range(1, tp)]
-    far.append(join(chain, *far))
-    far[2] = shift(far[2], 1)
     far = [(far[0], 0), (far[2], 0), (far[1], 0), (far[2], 2)]
     codes, scales = encode_columns(chain, codes, scales, far, 2, 0, rows, out_width)
     last = [(array, 0) for array in last]
@@ -463,7 +458,7 @@
     def shards(gate_input, up_input, down_weight):
         tp, batch = mesh.shape["tp"], mesh.shape["batch"]
         width, cols = down_weight.shape
-        paired = batch == tp == 4 and batch * cols <= LANES * BLOCK and cols % (tp * TILE) == 0 and width == (FIRST + 3 * PIECE) * STEP
+        paired = batch == tp == 4 and batch * cols <= LANES * BLOCK and cols % (tp * TILE) == 0 and width % STEP == 0 and width > 2 * PIECE * STEP
         return (paired_shards if paired else general_shards)(gate_input, up_input, down_weight)
 
     in_specs = (P(("groups", "batch"), "tp"), P(("groups", "batch"), "tp"), P("tp", "batch"))

time: 148 us -> 145 us (0.980)
  waiting for transfers between devices: 43.3 us -> 37.2 us
  starting transfers between devices: 29 us -> 34.2 us
  Pallas kernels: 74.8 us -> 73.1 us
    ppermute x13, waiting for transfers between devices: 31.8 us -> 27.8 us  [shift(): return lax.ppermute(value, 'tp', [(t, t ^ flip) for t in range(tp)])]
    ppermute x13, starting transfers between devices: 18.3 us -> 21.1 us  [shift(): return lax.ppermute(value, 'tp', [(t, t ^ flip) for t in range(tp)])]
    ppermute x21 -> x17, starting transfers between devices: 10.7 us -> 13 us  [swap(): lax.ppermute(value, 'batch', [(b, b ^ flip) for b in range(batch)])]
    ppermute x21 -> x17, waiting for transfers between devices: 11.5 us -> 9.32 us  [swap(): lax.ppermute(value, 'batch', [(b, b ^ flip) for b in range(batch)])]
    pallas_call x32 -> x31, Pallas kernels: 74.8 us -> 73.1 us  [call(): pl.pallas_call(with_tokens, grid=grid, in_specs=list(in_specs) + [ANY] *...]
  transfers between devices with their start and end apart: 34 -> 30, of which waited for: 13 -> 12; matrix products, arithmetic and copies ran while one was open for 0% -> 0% of each run, Pallas kernels for 48% -> 46%
where the time goes in v8:
time: 145 us
  Pallas kernels  73.1 us (50%)
  waiting for transfers between devices  37.2 us (26%)
  starting transfers between devices  34.2 us (24%)
    pallas_call x31, Pallas kernels, call(): pl.pallas_call(with_tokens, grid=grid, in_specs=list(in_specs) + [ANY] *...  73.1 us
    ppermute x13, waiting for transfers between devices, shift(): return lax.ppermute(value, 'tp', [(t, t ^ flip) for t in range(tp)])  27.8 us
    ppermute x13, starting transfers between devices, shift(): return lax.ppermute(value, 'tp', [(t, t ^ flip) for t in range(tp)])  21.1 us
    ppermute x17, starting transfers between devices, swap(): lax.ppermute(value, 'batch', [(b, b ^ flip) for b in range(batch)])  13 us
    ppermute x17, waiting for transfers between devices, swap(): lax.ppermute(value, 'batch', [(b, b ^ flip) for b in range(batch)])  9.32 us
  transfers between devices with their start and end apart: 30, of which 12 were waited for; matrix products, arithmetic and copies ran while one was open for 0% of the time, Pallas kernels for 46%

profile of v8, /device:TPU:0, one launch (start us, length us, event | category | flops | bytes accessed | tf_op | source)
XLA Modules:
  0.0 145.3 jit_solution(5361240640144354808)
XLA Ops:
  0.6 5.3 %activate.1 = (bf16[128,5120]{1,0:T(8,128)(2,1)S(1)}, bf16[128,8192]{1,0:T(8,128)(2,1)S(1)}, bf16[80,5120]{1,0:T(8,128)(2,1)S(1)}, bf16[80,4096]{1,0:T(8,128)(2,...) custom-call(bf16[128,13312]{1,0:T(8,128)(2,1)} %refs_0_.1, ...), custom_call_target="tpu_custom_call" | custom-call | flops 10000000000 | bytes 1024 | tf_op jit(solution)/shard_map/activate/pallas_call | solution.py:108
  5.9 0.5 collective-permute-start.1
  6.4 0.1 collective-permute-start
  6.5 2.9 %collective-permute-start.4 = (bf16[80,5120]{1,0:T(8,128)(2,1)S(1)}, bf16[80,5120]{1,0:T(8,128)(2,1)S(1)}, u32[]{:S(2)}, u32[]{:S(2)}) collective-permute-start(bf16[80,5120]{1,0:T(8,128)(2,1)S(1)} %get-tuple-element.92), channel_id=1, source_target_pairs={{0,2},{1,3},{2,0},{3,1},{4,6},{5,7},{6,4},{7,5},{8,10},{9,11},{10,... | collective-permute-start | bytes 2457608 | tf_op jit(solution)/shard_map/ppermute | solution.py:375
  9.4 9.0 %multiply.7 = (f32[256,2048]{1,0:T(8,128)S(1)}, f32[8,128]{1,0:T(8,128)S(1)}) custom-call(bf16[128,5120]{1,0:T(8,128)(2,1)S(1)} %get-tuple-element.82.refs_0_, bf16[128,5120]{1,0:T(8,128)(2,1)S(1)} %collective-permute-done.1.refs_1_, bf16[13312,2048]{1,0:T(8,128)(2,1)} %refs_2_.13, f32[8,128]{1,0:T(8,128)S(1)} %get-tuple-element.83.refs_3_), custom_call_target="tpu_custom_call" | custom-call | flops 10000000000 | bytes 1024 | tf_op jit(solution)/shard_map/multiply/pallas_call | solution.py:108
  18.5 2.6 %collective-permute-start.3 = (bf16[80,4096]{1,0:T(8,128)(2,1)S(1)}, bf16[80,4096]{1,0:T(8,128)(2,1)S(1)}, u32[]{:S(2)}, u32[]{:S(2)}) collective-permute-start(bf16[80,4096]{1,0:T(8,128)(2,1)S(1)} %get-tuple-element.91), channel_id=1, source_target_pairs={{0,2},{1,3},{2,0},{3,1},{4,6},{5,7},{6,4},{7,5},{8,10},{9,11},{10,... | collective-permute-start | bytes 1966088 | tf_op jit(solution)/shard_map/ppermute | solution.py:375
  21.0 13.3 %multiply.8 = (bf16[2,256,512]{2,1,0:T(8,128)(2,1)S(1)}, bf16[2,256,512]{2,1,0:T(8,128)(2,1)S(1)}, f32[8,128]{1,0:T(8,128)S(1)}) custom-call(bf16[128,8192]{1,0:T(8,128)(2,1)S(1)} %get-tuple-element.81.refs_0_, bf16[128,8192]{1,0:T(8,128)(2,1)S(1)} %collective-permute-done.refs_1_, bf16[13312,2048]{1,0:T(8,128)(2,1)} %refs_2_.13, ...), custom_call_target="tpu_custom_call" | custom-call | flops 10000000000 | bytes 1024 | tf_op jit(solution)/shard_map/multiply/pallas_call | solution.py:108
  34.4 1.6 %collective-permute-start.2 = (bf16[2,256,512]{2,1,0:T(8,128)(2,1)S(1)}, bf16[2,256,512]{2,1,0:T(8,128)(2,1)S(1)}, u32[]{:S(2)}, u32[]{:S(2)}) collective-permute-start(bf16[2,256,512]{2,1,0:T(8,128)(2,1)S(1)} %get-tuple-element.89), channel_id=1, source_target_pairs={{0,4},{4,0},{8,12},{12,8},{1,5},{5,1},{9,13},{13,9},{2,6},{6,2},{1... | collective-permute-start | bytes 1572872 | tf_op jit(solution)/shard_map/ppermute | solution.py:378
  36.0 0.6 collective-permute-start.7
  36.6 1.7 %collective-permute-done.5.refs_1_ = bf16[80,5120]{1,0:T(8,128)(2,1)S(1)} collective-permute-done((bf16[80,5120]{1,0:T(8,128)(2,1)S(1)}, bf16[80,5120]{1,0:T(8,128)(2,1)S(1)}, u32[]{:S(2)}, u32[]{:S(2)}) %collective-permute-start.5) | collective-permute-done | bytes 819232 | tf_op jit(solution)/shard_map/ppermute | solution.py:375
  38.3 7.9 %multiply.9 = (f32[160,2048]{1,0:T(8,128)S(1)}, f32[8,128]{1,0:T(8,128)S(1)}) custom-call(bf16[80,5120]{1,0:T(8,128)(2,1)S(1)} %get-tuple-element.94.refs_0_, bf16[80,5120]{1,0:T(8,128)(2,1)S(1)} %collective-permute-done.5.refs_1_, bf16[13312,2048]{1,0:T(8,128)(2,1)} %refs_2_.13, f32[8,128]{1,0:T(8,128)S(1)} %get-tuple-element.97.refs_3_), custom_call_target="tpu_custom_call" | custom-call | flops 10000000000 | bytes 1024 | tf_op jit(solution)/shard_map/multiply/pallas_call | solution.py:108
  46.2 0.2 collective-permute-start.8
  46.4 1.7 %collective-permute-done.2.refs_1_ = bf16[2,256,512]{2,1,0:T(8,128)(2,1)S(1)} collective-permute-done((bf16[2,256,512]{2,1,0:T(8,128)(2,1)S(1)}, bf16[2,256,512]{2,1,0:T(8,128)(2,1)S(1)}, u32[]{:S(2)}, u32[]{:S(2)}) %collective-permute-start.2) | collective-permute-done | bytes 524320 | tf_op jit(solution)/shard_map/ppermute | solution.py:378
  48.1 0.1 add.6
  48.2 2.7 %collective-permute-start.6 = (bf16[1,256,512]{2,1,0:T(8,128)(2,1)S(1)}, bf16[1,256,512]{2,1,0:T(8,128)(2,1)S(1)}, u32[]{:S(2)}, u32[]{:S(2)}) collective-permute-start(bf16[1,256,512]{2,1,0:T(8,128)(2,1)S(1)} %get-tuple-element.102), channel_id=1, source_target_pairs={{0,8},{4,12},{8,0},{12,4},{1,9},{5,13},{9,1},{13,5},{2,10},{6,14},... | collective-permute-start | bytes 786440 | tf_op jit(solution)/shard_map/ppermute | solution.py:378
  50.9 0.5 collective-permute-start.11
  51.4 6.7 %multiply.10 = (f32[160,2048]{1,0:T(8,128)S(1)}, f32[8,128]{1,0:T(8,128)S(1)}) custom-call(bf16[80,4096]{1,0:T(8,128)(2,1)S(1)} %get-tuple-element.104.refs_0_, bf16[80,4096]{1,0:T(8,128)(2,1)S(1)} %collective-permute-done.8.refs_1_, bf16[13312,2048]{1,0:T(8,128)(2,1)} %refs_2_.13, f32[160,2048]{1,0:T(8,128)S(1)} %get-tuple-element.105.refs_3_, ...), custom_call_target="tpu_custom_call" | custom-call | flops 10000000000 | bytes 1024 | tf_op jit(solution)/shard_map/multiply/pallas_call | solution.py:108
  58.2 2.1 %collective-permute-done.9.refs_1_ = bf16[80,4096]{1,0:T(8,128)(2,1)S(1)} collective-permute-done((bf16[80,4096]{1,0:T(8,128)(2,1)S(1)}, bf16[80,4096]{1,0:T(8,128)(2,1)S(1)}, u32[]{:S(2)}, u32[]{:S(2)}) %collective-permute-start.9) | collective-permute-done | bytes 655392 | tf_op jit(solution)/shard_map/ppermute | solution.py:375
  60.3 6.8 %multiply.11 = (bf16[2,160,512]{2,1,0:T(8,128)(2,1)S(1)}, bf16[2,160,512]{2,1,0:T(8,128)(2,1)S(1)}, f32[8,128]{1,0:T(8,128)S(1)}) custom-call(bf16[80,4096]{1,0:T(8,128)(2,1)S(1)} %get-tuple-element.108.refs_0_, bf16[80,4096]{1,0:T(8,128)(2,1)S(1)} %collective-permute-done.9.refs_1_, bf16[13312,2048]{1,0:T(8,128)(2,1)} %refs_2_.13, ...), custom_call_target="tpu_custom_call" | custom-call | flops 10000000000 | bytes 1024 | tf_op jit(solution)/shard_map/multiply/pallas_call | solution.py:108
  67.2 1.5 %collective-permute-done.11.refs_0_ = bf16[48,6144]{1,0:T(8,128)(2,1)S(1)} collective-permute-done((bf16[48,6144]{1,0:T(8,128)(2,1)S(1)}, bf16[48,6144]{1,0:T(8,128)(2,1)S(1)}, u32[]{:S(2)}, u32[]{:S(2)}) %collective-permute-start.11) | collective-permute-done | bytes 589856 | tf_op jit(solution)/shard_map/ppermute | solution.py:375
  68.6 0.5 collective-permute-start.10
  69.2 1.7 %collective-permute-start.16 = (bf16[48,7168]{1,0:T(8,128)(2,1)S(1)}, bf16[48,7168]{1,0:T(8,128)(2,1)S(1)}, u32[]{:S(2)}, u32[]{:S(2)}) collective-permute-start(bf16[48,7168]{1,0:T(8,128)(2,1)S(1)} %get-tuple-element.127), channel_id=1, source_target_pairs={{0,2},{1,3},{2,0},{3,1},{4,6},{5,7},{6,4},{7,5},{8,10},{9,11},{10,... | collective-permute-start | bytes 2064392 | tf_op jit(solution)/shard_map/ppermute | solution.py:375
  70.9 1.6 %collective-permute-start.13 = (bf16[2,160,512]{2,1,0:T(8,128)(2,1)S(1)}, bf16[2,160,512]{2,1,0:T(8,128)(2,1)S(1)}, u32[]{:S(2)}, u32[]{:S(2)}) collective-permute-start(bf16[2,160,512]{2,1,0:T(8,128)(2,1)S(1)} %get-tuple-element.121), channel_id=1, source_target_pairs={{0,4},{4,0},{8,12},{12,8},{1,5},{5,1},{9,13},{13,9},{2,6},{6,2},{1... | collective-permute-start | bytes 983048 | tf_op jit(solution)/shard_map/ppermute | solution.py:378
  72.5 2.7 %collective-permute-start.12 = (bf16[2,128,512]{2,1,0:T(8,128)(2,1)S(1)}, bf16[2,128,512]{2,1,0:T(8,128)(2,1)S(1)}, u32[]{:S(2)}, u32[]{:S(2)}) collective-permute-start(bf16[2,128,512]{2,1,0:T(8,128)(2,1)S(1)} %get-tuple-element.119.refs_0_), channel_id=1, source_target_pairs={{0,8},{4,12},{8,0},{12,4},{1,9},{5,13},{9,1},{13,5},{2,10},{6,14},... | collective-permute-start | bytes 786440 | tf_op jit(solution)/shard_map/ppermute | solution.py:378
  75.2 9.0 %multiply.12 = (f32[96,2048]{1,0:T(8,128)S(1)}, f32[8,128]{1,0:T(8,128)S(1)}) custom-call(bf16[48,6144]{1,0:T(8,128)(2,1)S(1)} %get-tuple-element.122.refs_0_, bf16[48,6144]{1,0:T(8,128)(2,1)S(1)} %collective-permute-done.14.refs_1_, bf16[13312,2048]{1,0:T(8,128)(2,1)} %refs_2_.13, f32[8,128]{1,0:T(8,128)S(1)} %get-tuple-element.123.refs_3_), custom_call_target="tpu_custom_call" | custom-call | flops 10000000000 | bytes 1024 | tf_op jit(solution)/shard_map/multiply/pallas_call | solution.py:108
  84.2 1.7 %collective-permute-done.13.refs_1_ = bf16[2,160,512]{2,1,0:T(8,128)(2,1)S(1)} collective-permute-done((bf16[2,160,512]{2,1,0:T(8,128)(2,1)S(1)}, bf16[2,160,512]{2,1,0:T(8,128)(2,1)S(1)}, u32[]{:S(2)}, u32[]{:S(2)}) %collective-permute-start.13) | collective-permute-done | bytes 327712 | tf_op jit(solution)/shard_map/ppermute | solution.py:378
  86.0 0.5 collective-permute-done.16.refs_0_
  86.5 2.8 %collective-permute-start.19 = (bf16[1,160,512]{2,1,0:T(8,128)(2,1)S(1)}, bf16[1,160,512]{2,1,0:T(8,128)(2,1)S(1)}, u32[]{:S(2)}, u32[]{:S(2)}) collective-permute-start(bf16[1,160,512]{2,1,0:T(8,128)(2,1)S(1)} %get-tuple-element.135), channel_id=1, source_target_pairs={{0,8},{4,12},{8,0},{12,4},{1,9},{5,13},{9,1},{13,5},{2,10},{6,14},... | collective-permute-start | bytes 491528 | tf_op jit(solution)/shard_map/ppermute | solution.py:378
  89.3 1.6 %collective-permute-start.15 = (bf16[4,128,512]{2,1,0:T(8,128)(2,1)S(1)}, bf16[4,128,512]{2,1,0:T(8,128)(2,1)S(1)}, u32[]{:S(2)}, u32[]{:S(2)}) collective-permute-start(bf16[4,128,512]{2,1,0:T(8,128)(2,1)S(1)} %get-tuple-element.126), channel_id=1, source_target_pairs={{0,4},{4,0},{8,12},{12,8},{1,5},{5,1},{9,13},{13,9},{2,6},{6,2},{1... | collective-permute-start | bytes 1572872 | tf_op jit(solution)/shard_map/ppermute | solution.py:378
  90.9 10.3 %multiply.13 = (bf16[2,96,512]{2,1,0:T(8,128)(2,1)S(1)}, bf16[2,96,512]{2,1,0:T(8,128)(2,1)S(1)}, f32[8,128]{1,0:T(8,128)S(1)}) custom-call(bf16[48,7168]{1,0:T(8,128)(2,1)S(1)} %get-tuple-element.129.refs_0_, bf16[48,7168]{1,0:T(8,128)(2,1)S(1)} %collective-permute-done.17.refs_1_, bf16[13312,2048]{1,0:T(8,128)(2,1)} %refs_2_.13, ...), custom_call_target="tpu_custom_call" | custom-call | flops 10000000000 | bytes 1024 | tf_op jit(solution)/shard_map/multiply/pallas_call | solution.py:108
  101.2 0.5 collective-permute-start.18
  101.8 1.6 %collective-permute-start.20 = (bf16[1,80,512]{2,1,0:T(8,128)(2,1)S(1)}, bf16[1,80,512]{2,1,0:T(8,128)(2,1)S(1)}, u32[]{:S(2)}, u32[]{:S(2)}) collective-permute-start(bf16[1,80,512]{2,1,0:T(8,128)(2,1)S(1)} %get-tuple-element.141), channel_id=1, source_target_pairs={{0,2},{1,3},{2,0},{3,1},{4,6},{5,7},{6,4},{7,5},{8,10},{9,11},{10,... | collective-permute-start | bytes 245768 | tf_op jit(solution)/shard_map/ppermute | solution.py:375
  103.3 6.4 %collective-permute-done.18.refs_1_ = bf16[2,96,512]{2,1,0:T(8,128)(2,1)S(1)} collective-permute-done((bf16[2,96,512]{2,1,0:T(8,128)(2,1)S(1)}, bf16[2,96,512]{2,1,0:T(8,128)(2,1)S(1)}, u32[]{:S(2)}, u32[]{:S(2)}) %collective-permute-start.18) | collective-permute-done | bytes 196640 | tf_op jit(solution)/shard_map/ppermute | solution.py:378
  109.8 1.5 %encode.3 = (bf16[128,8192]{1,0:T(8,128)(2,1)}, f32[128,128]{1,0:T(8,128)S(1)}, f32[8,128]{1,0:T(8,128)S(1)}) custom-call(bf16[2,128,512]{2,1,0:T(8,128)(2,1)S(1)} %get-tuple-element.119.refs_0_, bf16[4,128,512]{2,1,0:T(8,128)(2,1)S(1)} %collective-permute-done.15.refs_1_.refs_3_, bf16[2,128,512]{2,1,0:T(8,128)(2,1)S(1)} %collective-permute-done.12.refs_1_.refs_2_, ...), custom_call_target="tpu_custom_call" | custom-call | flops 10000000000 | bytes 1024 | tf_op jit(solution)/shard_map/encode/pallas_call | solution.py:108
  111.3 2.0 %collective-permute-start.22 = (bf16[2,80,512]{2,1,0:T(8,128)(2,1)S(1)}, bf16[2,80,512]{2,1,0:T(8,128)(2,1)S(1)}, u32[]{:S(2)}, u32[]{:S(2)}) collective-permute-start(bf16[2,80,512]{2,1,0:T(8,128)(2,1)S(1)} %get-tuple-element.144.refs_0_.refs_2_), channel_id=1, source_target_pairs={{0,8},{4,12},{8,0},{12,4},{1,9},{5,13},{9,1},{13,5},{2,10},{6,14},... | collective-permute-start | bytes 491528 | tf_op jit(solution)/shard_map/ppermute | solution.py:378
  113.3 1.0 collective-permute-start.23
  114.3 11.2 %collective-permute-done.23.refs_1_ = bf16[1,96,512]{2,1,0:T(8,128)(2,1)S(1)} collective-permute-done((bf16[1,96,512]{2,1,0:T(8,128)(2,1)S(1)}, bf16[1,96,512]{2,1,0:T(8,128)(2,1)S(1)}, u32[]{:S(2)}, u32[]{:S(2)}) %collective-permute-start.23) | collective-permute-done | bytes 98336 | tf_op jit(solution)/shard_map/ppermute | solution.py:378
  125.6 0.2 collective-permute-start.24
  125.8 1.7 %collective-permute-start.25 = (bf16[1,48,512]{2,1,0:T(8,128)(2,1)S(1)}, bf16[1,48,512]{2,1,0:T(8,128)(2,1)S(1)}, u32[]{:S(2)}, u32[]{:S(2)}) collective-permute-start(bf16[1,48,512]{2,1,0:T(8,128)(2,1)S(1)} %get-tuple-element.150), channel_id=1, source_target_pairs={{0,2},{1,3},{2,0},{3,1},{4,6},{5,7},{6,4},{7,5},{8,10},{9,11},{10,... | collective-permute-start | bytes 147464 | tf_op jit(solution)/shard_map/ppermute | solution.py:375
  127.6 2.4 %collective-permute-done.25.refs_0_ = bf16[1,48,512]{2,1,0:T(8,128)(2,1)S(1)} collective-permute-done((bf16[1,48,512]{2,1,0:T(8,128)(2,1)S(1)}, bf16[1,48,512]{2,1,0:T(8,128)(2,1)S(1)}, u32[]{:S(2)}, u32[]{:S(2)}) %collective-permute-start.25) | collective-permute-done | bytes 49184 | tf_op jit(solution)/shard_map/ppermute | solution.py:375
  129.9 1.1 collective-permute-done.26.refs_1_
  131.1 2.9 %collective-permute-start.29 = (bf16[2,48,512]{2,1,0:T(8,128)(2,1)S(1)}, bf16[2,48,512]{2,1,0:T(8,128)(2,1)S(1)}, u32[]{:S(2)}, u32[]{:S(2)}) collective-permute-start(bf16[2,48,512]{2,1,0:T(8,128)(2,1)S(1)} %get-tuple-element.156.refs_2_), channel_id=1, source_target_pairs={{0,12},{4,8},{8,4},{12,0},{1,13},{5,9},{9,5},{13,1},{2,14},{6,10},... | collective-permute-start | bytes 294920 | tf_op jit(solution)/shard_map/ppermute | solution.py:378
  134.0 0.6 collective-permute-start.28
  134.6 1.0 collective-permute-start.27
  135.5 1.2 encode.4
  136.8 2.6 %collective-permute-done.29.refs_5_ = bf16[2,48,512]{2,1,0:T(8,128)(2,1)S(1)} collective-permute-done((bf16[2,48,512]{2,1,0:T(8,128)(2,1)S(1)}, bf16[2,48,512]{2,1,0:T(8,128)(2,1)S(1)}, u32[]{:S(2)}, u32[]{:S(2)}) %collective-permute-start.29) | collective-permute-done | bytes 98336 | tf_op jit(solution)/shard_map/ppermute | solution.py:378
  139.4 4.3 %collective-permute-done.28.refs_4_ = bf16[2,48,512]{2,1,0:T(8,128)(2,1)S(1)} collective-permute-done((bf16[2,48,512]{2,1,0:T(8,128)(2,1)S(1)}, bf16[2,48,512]{2,1,0:T(8,128)(2,1)S(1)}, u32[]{:S(2)}, u32[]{:S(2)}) %collective-permute-start.28) | collective-permute-done | bytes 98336 | tf_op jit(solution)/shard_map/ppermute | solution.py:378
  143.7 1.6 %encode.5 = (bf16[128,8192]{1,0:T(8,128)(2,1)}, bf16[64,128]{1,0:T(8,128)(2,1)}, f32[8,128]{1,0:T(8,128)}) custom-call(bf16[128,8192]{1,0:T(8,128)(2,1)} %get-tuple-element.154.refs_0_, f32[128,128]{1,0:T(8,128)S(1)} %get-tuple-element.155.refs_1_, bf16[2,48,512]{2,1,0:T(8,128)(2,1)S(1)} %get-tuple-element.156.refs_2_, ...), custom_call_target="tpu_custom_call", output_to_operand_aliasing={{0}: (0, {})} | custom-call | bytes 1024 | tf_op jit(solution)/shard_map/encode/pallas_call | solution.py:108
  (43 shorter events, 0.5 us)
Async XLA Ops:
  5.9 3.5 %collective-permute-start.1 = (bf16[128,5120]{1,0:T(8,128)(2,1)S(1)}, bf16[128,5120]{1,0:T(8,128)(2,1)S(1)}, u32[]{:S(2)}, u32[]{:S(2)}) collective-permute-start(bf16[128,5120]{1,0:T(8,128)(2,1)S(1)} %get-tuple-element.82.refs_0_), channel_id=1, source_target_pairs={{0,1},{1,0},{2,3},{3,2},{4,5},{5,4},{6,7},{7,6},{8,9},{9,8},{10,11... | collective-permute-start | bytes 3932168 | tf_op jit(solution)/shard_map/ppermute | solution.py:375
  6.4 14.6 %collective-permute-start = (bf16[128,8192]{1,0:T(8,128)(2,1)S(1)}, bf16[128,8192]{1,0:T(8,128)(2,1)S(1)}, u32[]{:S(2)}, u32[]{:S(2)}) collective-permute-start(bf16[128,8192]{1,0:T(8,128)(2,1)S(1)} %get-tuple-element.81.refs_0_), channel_id=1, source_target_pairs={{0,1},{1,0},{2,3},{3,2},{4,5},{5,4},{6,7},{7,6},{8,9},{9,8},{10,11... | collective-permute-start | bytes 6291464 | tf_op jit(solution)/shard_map/ppermute | solution.py:375
  6.5 29.5 %collective-permute-start.4 = (bf16[80,5120]{1,0:T(8,128)(2,1)S(1)}, bf16[80,5120]{1,0:T(8,128)(2,1)S(1)}, u32[]{:S(2)}, u32[]{:S(2)}) collective-permute-start(bf16[80,5120]{1,0:T(8,128)(2,1)S(1)} %get-tuple-element.92), channel_id=1, source_target_pairs={{0,2},{1,3},{2,0},{3,1},{4,6},{5,7},{6,4},{7,5},{8,10},{9,11},{10,... | collective-permute-start | bytes 2457608 | tf_op jit(solution)/shard_map/ppermute | solution.py:375
  18.5 27.8 %collective-permute-start.3 = (bf16[80,4096]{1,0:T(8,128)(2,1)S(1)}, bf16[80,4096]{1,0:T(8,128)(2,1)S(1)}, u32[]{:S(2)}, u32[]{:S(2)}) collective-permute-start(bf16[80,4096]{1,0:T(8,128)(2,1)S(1)} %get-tuple-element.91), channel_id=1, source_target_pairs={{0,2},{1,3},{2,0},{3,1},{4,6},{5,7},{6,4},{7,5},{8,10},{9,11},{10,... | collective-permute-start | bytes 1966088 | tf_op jit(solution)/shard_map/ppermute | solution.py:375
  34.4 13.7 %collective-permute-start.2 = (bf16[2,256,512]{2,1,0:T(8,128)(2,1)S(1)}, bf16[2,256,512]{2,1,0:T(8,128)(2,1)S(1)}, u32[]{:S(2)}, u32[]{:S(2)}) collective-permute-start(bf16[2,256,512]{2,1,0:T(8,128)(2,1)S(1)} %get-tuple-element.89), channel_id=1, source_target_pairs={{0,4},{4,0},{8,12},{12,8},{1,5},{5,1},{9,13},{13,9},{2,6},{6,2},{1... | collective-permute-start | bytes 1572872 | tf_op jit(solution)/shard_map/ppermute | solution.py:378
  36.0 2.3 %collective-permute-start.5 = (bf16[80,5120]{1,0:T(8,128)(2,1)S(1)}, bf16[80,5120]{1,0:T(8,128)(2,1)S(1)}, u32[]{:S(2)}, u32[]{:S(2)}) collective-permute-start(bf16[80,5120]{1,0:T(8,128)(2,1)S(1)} %get-tuple-element.94.refs_0_), channel_id=1, source_target_pairs={{0,1},{1,0},{2,3},{3,2},{4,5},{5,4},{6,7},{7,6},{8,9},{9,8},{10,11... | collective-permute-start | bytes 2457608 | tf_op jit(solution)/shard_map/ppermute | solution.py:375
  36.0 22.1 %collective-permute-start.7 = (bf16[80,4096]{1,0:T(8,128)(2,1)S(1)}, bf16[80,4096]{1,0:T(8,128)(2,1)S(1)}, u32[]{:S(2)}, u32[]{:S(2)}) collective-permute-start(bf16[80,4096]{1,0:T(8,128)(2,1)S(1)} %get-tuple-element.103), channel_id=1, source_target_pairs={{0,2},{1,3},{2,0},{3,1},{4,6},{5,7},{6,4},{7,5},{8,10},{9,11},{10,... | collective-permute-start | bytes 1966088 | tf_op jit(solution)/shard_map/ppermute | solution.py:375
  46.2 5.2 %collective-permute-start.8 = (bf16[80,4096]{1,0:T(8,128)(2,1)S(1)}, bf16[80,4096]{1,0:T(8,128)(2,1)S(1)}, u32[]{:S(2)}, u32[]{:S(2)}) collective-permute-start(bf16[80,4096]{1,0:T(8,128)(2,1)S(1)} %get-tuple-element.104.refs_0_), channel_id=1, source_target_pairs={{0,1},{1,0},{2,3},{3,2},{4,5},{5,4},{6,7},{7,6},{8,9},{9,8},{10,11... | collective-permute-start | bytes 1966088 | tf_op jit(solution)/shard_map/ppermute | solution.py:375
  48.2 18.9 %collective-permute-start.6 = (bf16[1,256,512]{2,1,0:T(8,128)(2,1)S(1)}, bf16[1,256,512]{2,1,0:T(8,128)(2,1)S(1)}, u32[]{:S(2)}, u32[]{:S(2)}) collective-permute-start(bf16[1,256,512]{2,1,0:T(8,128)(2,1)S(1)} %get-tuple-element.102), channel_id=1, source_target_pairs={{0,8},{4,12},{8,0},{12,4},{1,9},{5,13},{9,1},{13,5},{2,10},{6,14},... | collective-permute-start | bytes 786440 | tf_op jit(solution)/shard_map/ppermute | solution.py:378
  50.9 17.8 %collective-permute-start.11 = (bf16[48,6144]{1,0:T(8,128)(2,1)S(1)}, bf16[48,6144]{1,0:T(8,128)(2,1)S(1)}, u32[]{:S(2)}, u32[]{:S(2)}) collective-permute-start(bf16[48,6144]{1,0:T(8,128)(2,1)S(1)} %get-tuple-element.116), channel_id=1, source_target_pairs={{0,2},{1,3},{2,0},{3,1},{4,6},{5,7},{6,4},{7,5},{8,10},{9,11},{10,... | collective-permute-start | bytes 1769480 | tf_op jit(solution)/shard_map/ppermute | solution.py:375
  58.1 2.2 %collective-permute-start.9 = (bf16[80,4096]{1,0:T(8,128)(2,1)S(1)}, bf16[80,4096]{1,0:T(8,128)(2,1)S(1)}, u32[]{:S(2)}, u32[]{:S(2)}) collective-permute-start(bf16[80,4096]{1,0:T(8,128)(2,1)S(1)} %get-tuple-element.108.refs_0_), channel_id=1, source_target_pairs={{0,1},{1,0},{2,3},{3,2},{4,5},{5,4},{6,7},{7,6},{8,9},{9,8},{10,11... | collective-permute-start | bytes 1966088 | tf_op jit(solution)/shard_map/ppermute | solution.py:375
  68.6 6.5 %collective-permute-start.14 = (bf16[48,6144]{1,0:T(8,128)(2,1)S(1)}, bf16[48,6144]{1,0:T(8,128)(2,1)S(1)}, u32[]{:S(2)}, u32[]{:S(2)}) collective-permute-start(bf16[48,6144]{1,0:T(8,128)(2,1)S(1)} %get-tuple-element.122.refs_0_), channel_id=1, source_target_pairs={{0,1},{1,0},{2,3},{3,2},{4,5},{5,4},{6,7},{7,6},{8,9},{9,8},{10,11... | collective-permute-start | bytes 1769480 | tf_op jit(solution)/shard_map/ppermute | solution.py:375
  68.6 3.8 %collective-permute-start.10 = (bf16[1,128,512]{2,1,0:T(8,128)(2,1)S(1)}, bf16[1,128,512]{2,1,0:T(8,128)(2,1)S(1)}, u32[]{:S(2)}, u32[]{:S(2)}) collective-permute-start(bf16[1,128,512]{2,1,0:T(8,128)(2,1)S(1)} %get-tuple-element.115), channel_id=1, source_target_pairs={{0,1},{1,0},{2,3},{3,2},{4,5},{5,4},{6,7},{7,6},{8,9},{9,8},{10,11... | collective-permute-start | bytes 393224 | tf_op jit(solution)/shard_map/ppermute | solution.py:375
  69.2 17.3 %collective-permute-start.16 = (bf16[48,7168]{1,0:T(8,128)(2,1)S(1)}, bf16[48,7168]{1,0:T(8,128)(2,1)S(1)}, u32[]{:S(2)}, u32[]{:S(2)}) collective-permute-start(bf16[48,7168]{1,0:T(8,128)(2,1)S(1)} %get-tuple-element.127), channel_id=1, source_target_pairs={{0,2},{1,3},{2,0},{3,1},{4,6},{5,7},{6,4},{7,5},{8,10},{9,11},{10,... | collective-permute-start | bytes 2064392 | tf_op jit(solution)/shard_map/ppermute | solution.py:375
  70.9 15.0 %collective-permute-start.13 = (bf16[2,160,512]{2,1,0:T(8,128)(2,1)S(1)}, bf16[2,160,512]{2,1,0:T(8,128)(2,1)S(1)}, u32[]{:S(2)}, u32[]{:S(2)}) collective-permute-start(bf16[2,160,512]{2,1,0:T(8,128)(2,1)S(1)} %get-tuple-element.121), channel_id=1, source_target_pairs={{0,4},{4,0},{8,12},{12,8},{1,5},{5,1},{9,13},{13,9},{2,6},{6,2},{1... | collective-permute-start | bytes 983048 | tf_op jit(solution)/shard_map/ppermute | solution.py:378
  72.5 13.4 %collective-permute-start.12 = (bf16[2,128,512]{2,1,0:T(8,128)(2,1)S(1)}, bf16[2,128,512]{2,1,0:T(8,128)(2,1)S(1)}, u32[]{:S(2)}, u32[]{:S(2)}) collective-permute-start(bf16[2,128,512]{2,1,0:T(8,128)(2,1)S(1)} %get-tuple-element.119.refs_0_), channel_id=1, source_target_pairs={{0,8},{4,12},{8,0},{12,4},{1,9},{5,13},{9,1},{13,5},{2,10},{6,14},... | collective-permute-start | bytes 786440 | tf_op jit(solution)/shard_map/ppermute | solution.py:378
  86.5 4.4 %collective-permute-start.17 = (bf16[48,7168]{1,0:T(8,128)(2,1)S(1)}, bf16[48,7168]{1,0:T(8,128)(2,1)S(1)}, u32[]{:S(2)}, u32[]{:S(2)}) collective-permute-start(bf16[48,7168]{1,0:T(8,128)(2,1)S(1)} %get-tuple-element.129.refs_0_), channel_id=1, source_target_pairs={{0,1},{1,0},{2,3},{3,2},{4,5},{5,4},{6,7},{7,6},{8,9},{9,8},{10,11... | collective-permute-start | bytes 2064392 | tf_op jit(solution)/shard_map/ppermute | solution.py:375
  86.5 15.2 %collective-permute-start.19 = (bf16[1,160,512]{2,1,0:T(8,128)(2,1)S(1)}, bf16[1,160,512]{2,1,0:T(8,128)(2,1)S(1)}, u32[]{:S(2)}, u32[]{:S(2)}) collective-permute-start(bf16[1,160,512]{2,1,0:T(8,128)(2,1)S(1)} %get-tuple-element.135), channel_id=1, source_target_pairs={{0,8},{4,12},{8,0},{12,4},{1,9},{5,13},{9,1},{13,5},{2,10},{6,14},... | collective-permute-start | bytes 491528 | tf_op jit(solution)/shard_map/ppermute | solution.py:378
  89.3 20.4 %collective-permute-start.15 = (bf16[4,128,512]{2,1,0:T(8,128)(2,1)S(1)}, bf16[4,128,512]{2,1,0:T(8,128)(2,1)S(1)}, u32[]{:S(2)}, u32[]{:S(2)}) collective-permute-start(bf16[4,128,512]{2,1,0:T(8,128)(2,1)S(1)} %get-tuple-element.126), channel_id=1, source_target_pairs={{0,4},{4,0},{8,12},{12,8},{1,5},{5,1},{9,13},{13,9},{2,6},{6,2},{1... | collective-permute-start | bytes 1572872 | tf_op jit(solution)/shard_map/ppermute | solution.py:378
  101.2 8.5 %collective-permute-start.18 = (bf16[2,96,512]{2,1,0:T(8,128)(2,1)S(1)}, bf16[2,96,512]{2,1,0:T(8,128)(2,1)S(1)}, u32[]{:S(2)}, u32[]{:S(2)}) collective-permute-start(bf16[2,96,512]{2,1,0:T(8,128)(2,1)S(1)} %get-tuple-element.133), channel_id=1, source_target_pairs={{0,4},{4,0},{8,12},{12,8},{1,5},{5,1},{9,13},{13,9},{2,6},{6,2},{1... | collective-permute-start | bytes 589832 | tf_op jit(solution)/shard_map/ppermute | solution.py:378
  101.8 9.5 %collective-permute-start.20 = (bf16[1,80,512]{2,1,0:T(8,128)(2,1)S(1)}, bf16[1,80,512]{2,1,0:T(8,128)(2,1)S(1)}, u32[]{:S(2)}, u32[]{:S(2)}) collective-permute-start(bf16[1,80,512]{2,1,0:T(8,128)(2,1)S(1)} %get-tuple-element.141), channel_id=1, source_target_pairs={{0,2},{1,3},{2,0},{3,1},{4,6},{5,7},{6,4},{7,5},{8,10},{9,11},{10,... | collective-permute-start | bytes 245768 | tf_op jit(solution)/shard_map/ppermute | solution.py:375
  103.3 8.0 %collective-permute-start.21 = (bf16[1,80,512]{2,1,0:T(8,128)(2,1)S(1)}, bf16[1,80,512]{2,1,0:T(8,128)(2,1)S(1)}, u32[]{:S(2)}, u32[]{:S(2)}) collective-permute-start(bf16[1,80,512]{2,1,0:T(8,128)(2,1)S(1)} %get-tuple-element.142), channel_id=1, source_target_pairs={{0,3},{1,2},{2,1},{3,0},{4,7},{5,6},{6,5},{7,4},{8,11},{9,10},{10,... | collective-permute-start | bytes 245768 | tf_op jit(solution)/shard_map/ppermute | solution.py:375
  111.3 14.2 %collective-permute-start.22 = (bf16[2,80,512]{2,1,0:T(8,128)(2,1)S(1)}, bf16[2,80,512]{2,1,0:T(8,128)(2,1)S(1)}, u32[]{:S(2)}, u32[]{:S(2)}) collective-permute-start(bf16[2,80,512]{2,1,0:T(8,128)(2,1)S(1)} %get-tuple-element.144.refs_0_.refs_2_), channel_id=1, source_target_pairs={{0,8},{4,12},{8,0},{12,4},{1,9},{5,13},{9,1},{13,5},{2,10},{6,14},... | collective-permute-start | bytes 491528 | tf_op jit(solution)/shard_map/ppermute | solution.py:378
  113.3 12.2 %collective-permute-start.23 = (bf16[1,96,512]{2,1,0:T(8,128)(2,1)S(1)}, bf16[1,96,512]{2,1,0:T(8,128)(2,1)S(1)}, u32[]{:S(2)}, u32[]{:S(2)}) collective-permute-start(bf16[1,96,512]{2,1,0:T(8,128)(2,1)S(1)} %get-tuple-element.146), channel_id=1, source_target_pairs={{0,8},{4,12},{8,0},{12,4},{1,9},{5,13},{9,1},{13,5},{2,10},{6,14},... | collective-permute-start | bytes 294920 | tf_op jit(solution)/shard_map/ppermute | solution.py:378
  125.6 9.9 %collective-permute-start.24 = (bf16[4,80,512]{2,1,0:T(8,128)(2,1)S(1)}, bf16[4,80,512]{2,1,0:T(8,128)(2,1)S(1)}, u32[]{:S(2)}, u32[]{:S(2)}) collective-permute-start(bf16[4,80,512]{2,1,0:T(8,128)(2,1)S(1)} %get-tuple-element.149), channel_id=1, source_target_pairs={{0,4},{4,0},{8,12},{12,8},{1,5},{5,1},{9,13},{13,9},{2,6},{6,2},{1... | collective-permute-start | bytes 983048 | tf_op jit(solution)/shard_map/ppermute | solution.py:378
  125.8 4.1 %collective-permute-start.25 = (bf16[1,48,512]{2,1,0:T(8,128)(2,1)S(1)}, bf16[1,48,512]{2,1,0:T(8,128)(2,1)S(1)}, u32[]{:S(2)}, u32[]{:S(2)}) collective-permute-start(bf16[1,48,512]{2,1,0:T(8,128)(2,1)S(1)} %get-tuple-element.150), channel_id=1, source_target_pairs={{0,2},{1,3},{2,0},{3,1},{4,6},{5,7},{6,4},{7,5},{8,10},{9,11},{10,... | collective-permute-start | bytes 147464 | tf_op jit(solution)/shard_map/ppermute | solution.py:375
  127.6 3.5 %collective-permute-start.26 = (bf16[1,48,512]{2,1,0:T(8,128)(2,1)S(1)}, bf16[1,48,512]{2,1,0:T(8,128)(2,1)S(1)}, u32[]{:S(2)}, u32[]{:S(2)}) collective-permute-start(bf16[1,48,512]{2,1,0:T(8,128)(2,1)S(1)} %get-tuple-element.151), channel_id=1, source_target_pairs={{0,3},{1,2},{2,1},{3,0},{4,7},{5,6},{6,5},{7,4},{8,11},{9,10},{10,... | collective-permute-start | bytes 147464 | tf_op jit(solution)/shard_map/ppermute | solution.py:375
  131.1 8.3 %collective-permute-start.29 = (bf16[2,48,512]{2,1,0:T(8,128)(2,1)S(1)}, bf16[2,48,512]{2,1,0:T(8,128)(2,1)S(1)}, u32[]{:S(2)}, u32[]{:S(2)}) collective-permute-start(bf16[2,48,512]{2,1,0:T(8,128)(2,1)S(1)} %get-tuple-element.156.refs_2_), channel_id=1, source_target_pairs={{0,12},{4,8},{8,4},{12,0},{1,13},{5,9},{9,5},{13,1},{2,14},{6,10},... | collective-permute-start | bytes 294920 | tf_op jit(solution)/shard_map/ppermute | solution.py:378
  134.0 9.7 %collective-permute-start.28 = (bf16[2,48,512]{2,1,0:T(8,128)(2,1)S(1)}, bf16[2,48,512]{2,1,0:T(8,128)(2,1)S(1)}, u32[]{:S(2)}, u32[]{:S(2)}) collective-permute-start(bf16[2,48,512]{2,1,0:T(8,128)(2,1)S(1)} %get-tuple-element.156.refs_2_), channel_id=1, source_target_pairs={{0,8},{4,12},{8,0},{12,4},{1,9},{5,13},{9,1},{13,5},{2,10},{6,14},... | collective-permute-start | bytes 294920 | tf_op jit(solution)/shard_map/ppermute | solution.py:378
  134.6 9.1 %collective-permute-start.27 = (bf16[2,48,512]{2,1,0:T(8,128)(2,1)S(1)}, bf16[2,48,512]{2,1,0:T(8,128)(2,1)S(1)}, u32[]{:S(2)}, u32[]{:S(2)}) collective-permute-start(bf16[2,48,512]{2,1,0:T(8,128)(2,1)S(1)} %get-tuple-element.156.refs_2_), channel_id=1, source_target_pairs={{0,4},{4,0},{8,12},{12,8},{1,5},{5,1},{9,13},{13,9},{2,6},{6,2},{1... | collective-permute-start | bytes 294920 | tf_op jit(solution)/shard_map/ppermute | solution.py:378

commit v9 on v8

--- a/solution.py
+++ b/solution.py
@@ -437,11 +437,11 @@
     last = product([late_1], half, total, HALVES)
     last = [last[0], shift(last[1], 1)]
     far = sum_home(far, 2, 10**10)
+    far = join(chain, *far)
+    far = [far, shift(far, 2)]
     last = sum_pair(last)
     near = [(near[0], 0), (near[2], 0), (near[1], 0), (near[2], 2)]
     codes, scales = encode_columns(chain, None, None, near, 0, 0, rows, out_width, cost=10**10)
-    far = join(chain, *far)
-    far = [far, shift(far, 2)]
     last = sum_home(last, 2)
     far.append(join(chain, *far))
     far[2] = shift(far[2], 1)

time: 145 us -> 142 us (0.979)
  waiting for transfers between devices: 37.2 us -> 33.9 us
    ppermute x13, waiting for transfers between devices: 27.8 us -> 19.4 us  [shift(): return lax.ppermute(value, 'tp', [(t, t ^ flip) for t in range(tp)])]
    ppermute x17, waiting for transfers between devices: 9.32 us -> 14.5 us  [swap(): lax.ppermute(value, 'batch', [(b, b ^ flip) for b in range(batch)])]
  transfers between devices with their start and end apart: 30 -> 30, of which waited for: 12 -> 13; matrix products, arithmetic and copies ran while one was open for 0% -> 0% of each run, Pallas kernels for 46% -> 46%
where the time goes in v9:
time: 142 us
  Pallas kernels  73.1 us (51%)
  starting transfers between devices  34.4 us (24%)
  waiting for transfers between devices  33.9 us (24%)
    pallas_call x31, Pallas kernels, call(): pl.pallas_call(with_tokens, grid=grid, in_specs=list(in_specs) + [ANY] *...  73.1 us
    ppermute x13, starting transfers between devices, shift(): return lax.ppermute(value, 'tp', [(t, t ^ flip) for t in range(tp)])  21.6 us
    ppermute x13, waiting for transfers between devices, shift(): return lax.ppermute(value, 'tp', [(t, t ^ flip) for t in range(tp)])  19.4 us
    ppermute x17, waiting for transfers between devices, swap(): lax.ppermute(value, 'batch', [(b, b ^ flip) for b in range(batch)])  14.5 us
    ppermute x17, starting transfers between devices, swap(): lax.ppermute(value, 'batch', [(b, b ^ flip) for b in range(batch)])  12.8 us
  transfers between devices with their start and end apart: 30, of which 13 were waited for; matrix products, arithmetic and copies ran while one was open for 0% of the time, Pallas kernels for 46%

profile of v9, /device:TPU:0, one launch (start us, length us, event | category | flops | bytes accessed | tf_op | source)
XLA Modules:
  0.0 142.3 jit_solution(6901422691535276851)
XLA Ops:
  0.6 5.3 %activate.1 = (bf16[128,5120]{1,0:T(8,128)(2,1)S(1)}, bf16[128,8192]{1,0:T(8,128)(2,1)S(1)}, bf16[80,5120]{1,0:T(8,128)(2,1)S(1)}, bf16[80,4096]{1,0:T(8,128)(2,...) custom-call(bf16[128,13312]{1,0:T(8,128)(2,1)} %refs_0_.1, ...), custom_call_target="tpu_custom_call" | custom-call | flops 10000000000 | bytes 1024 | tf_op jit(solution)/shard_map/activate/pallas_call | solution.py:108
  5.9 0.5 collective-permute-start.1
  6.4 0.1 collective-permute-start
  6.5 2.9 %collective-permute-start.4 = (bf16[80,5120]{1,0:T(8,128)(2,1)S(1)}, bf16[80,5120]{1,0:T(8,128)(2,1)S(1)}, u32[]{:S(2)}, u32[]{:S(2)}) collective-permute-start(bf16[80,5120]{1,0:T(8,128)(2,1)S(1)} %get-tuple-element.92), channel_id=1, source_target_pairs={{0,2},{1,3},{2,0},{3,1},{4,6},{5,7},{6,4},{7,5},{8,10},{9,11},{10,... | collective-permute-start | bytes 2457608 | tf_op jit(solution)/shard_map/ppermute | solution.py:375
  9.4 9.0 %multiply.7 = (f32[256,2048]{1,0:T(8,128)S(1)}, f32[8,128]{1,0:T(8,128)S(1)}) custom-call(bf16[128,5120]{1,0:T(8,128)(2,1)S(1)} %get-tuple-element.82.refs_0_, bf16[128,5120]{1,0:T(8,128)(2,1)S(1)} %collective-permute-done.1.refs_1_, bf16[13312,2048]{1,0:T(8,128)(2,1)} %refs_2_.13, f32[8,128]{1,0:T(8,128)S(1)} %get-tuple-element.83.refs_3_), custom_call_target="tpu_custom_call" | custom-call | flops 10000000000 | bytes 1024 | tf_op jit(solution)/shard_map/multiply/pallas_call | solution.py:108
  18.5 2.6 %collective-permute-start.3 = (bf16[80,4096]{1,0:T(8,128)(2,1)S(1)}, bf16[80,4096]{1,0:T(8,128)(2,1)S(1)}, u32[]{:S(2)}, u32[]{:S(2)}) collective-permute-start(bf16[80,4096]{1,0:T(8,128)(2,1)S(1)} %get-tuple-element.91), channel_id=1, source_target_pairs={{0,2},{1,3},{2,0},{3,1},{4,6},{5,7},{6,4},{7,5},{8,10},{9,11},{10,... | collective-permute-start | bytes 1966088 | tf_op jit(solution)/shard_map/ppermute | solution.py:375
  21.0 13.3 %multiply.8 = (bf16[2,256,512]{2,1,0:T(8,128)(2,1)S(1)}, bf16[2,256,512]{2,1,0:T(8,128)(2,1)S(1)}, f32[8,128]{1,0:T(8,128)S(1)}) custom-call(bf16[128,8192]{1,0:T(8,128)(2,1)S(1)} %get-tuple-element.81.refs_0_, bf16[128,8192]{1,0:T(8,128)(2,1)S(1)} %collective-permute-done.refs_1_, bf16[13312,2048]{1,0:T(8,128)(2,1)} %refs_2_.13, ...), custom_call_target="tpu_custom_call" | custom-call | flops 10000000000 | bytes 1024 | tf_op jit(solution)/shard_map/multiply/pallas_call | solution.py:108
  34.4 1.6 %collective-permute-start.2 = (bf16[2,256,512]{2,1,0:T(8,128)(2,1)S(1)}, bf16[2,256,512]{2,1,0:T(8,128)(2,1)S(1)}, u32[]{:S(2)}, u32[]{:S(2)}) collective-permute-start(bf16[2,256,512]{2,1,0:T(8,128)(2,1)S(1)} %get-tuple-element.89), channel_id=1, source_target_pairs={{0,4},{4,0},{8,12},{12,8},{1,5},{5,1},{9,13},{13,9},{2,6},{6,2},{1... | collective-permute-start | bytes 1572872 | tf_op jit(solution)/shard_map/ppermute | solution.py:378
  36.0 0.6 collective-permute-start.7
  36.6 1.7 %collective-permute-done.5.refs_1_ = bf16[80,5120]{1,0:T(8,128)(2,1)S(1)} collective-permute-done((bf16[80,5120]{1,0:T(8,128)(2,1)S(1)}, bf16[80,5120]{1,0:T(8,128)(2,1)S(1)}, u32[]{:S(2)}, u32[]{:S(2)}) %collective-permute-start.5) | collective-permute-done | bytes 819232 | tf_op jit(solution)/shard_map/ppermute | solution.py:375
  38.3 7.9 %multiply.9 = (f32[160,2048]{1,0:T(8,128)S(1)}, f32[8,128]{1,0:T(8,128)S(1)}) custom-call(bf16[80,5120]{1,0:T(8,128)(2,1)S(1)} %get-tuple-element.94.refs_0_, bf16[80,5120]{1,0:T(8,128)(2,1)S(1)} %collective-permute-done.5.refs_1_, bf16[13312,2048]{1,0:T(8,128)(2,1)} %refs_2_.13, f32[8,128]{1,0:T(8,128)S(1)} %get-tuple-element.97.refs_3_), custom_call_target="tpu_custom_call" | custom-call | flops 10000000000 | bytes 1024 | tf_op jit(solution)/shard_map/multiply/pallas_call | solution.py:108
  46.2 0.2 collective-permute-start.8
  46.4 1.7 %collective-permute-done.2.refs_1_ = bf16[2,256,512]{2,1,0:T(8,128)(2,1)S(1)} collective-permute-done((bf16[2,256,512]{2,1,0:T(8,128)(2,1)S(1)}, bf16[2,256,512]{2,1,0:T(8,128)(2,1)S(1)}, u32[]{:S(2)}, u32[]{:S(2)}) %collective-permute-start.2) | collective-permute-done | bytes 524320 | tf_op jit(solution)/shard_map/ppermute | solution.py:378
  48.1 0.1 add.6
  48.2 2.7 %collective-permute-start.6 = (bf16[1,256,512]{2,1,0:T(8,128)(2,1)S(1)}, bf16[1,256,512]{2,1,0:T(8,128)(2,1)S(1)}, u32[]{:S(2)}, u32[]{:S(2)}) collective-permute-start(bf16[1,256,512]{2,1,0:T(8,128)(2,1)S(1)} %get-tuple-element.102), channel_id=1, source_target_pairs={{0,8},{4,12},{8,0},{12,4},{1,9},{5,13},{9,1},{13,5},{2,10},{6,14},... | collective-permute-start | bytes 786440 | tf_op jit(solution)/shard_map/ppermute | solution.py:378
  50.9 0.5 collective-permute-start.11
  51.4 6.7 %multiply.10 = (f32[160,2048]{1,0:T(8,128)S(1)}, f32[8,128]{1,0:T(8,128)S(1)}) custom-call(bf16[80,4096]{1,0:T(8,128)(2,1)S(1)} %get-tuple-element.104.refs_0_, bf16[80,4096]{1,0:T(8,128)(2,1)S(1)} %collective-permute-done.8.refs_1_, bf16[13312,2048]{1,0:T(8,128)(2,1)} %refs_2_.13, f32[160,2048]{1,0:T(8,128)S(1)} %get-tuple-element.105.refs_3_, ...), custom_call_target="tpu_custom_call" | custom-call | flops 10000000000 | bytes 1024 | tf_op jit(solution)/shard_map/multiply/pallas_call | solution.py:108
  58.2 2.1 %collective-permute-done.9.refs_1_ = bf16[80,4096]{1,0:T(8,128)(2,1)S(1)} collective-permute-done((bf16[80,4096]{1,0:T(8,128)(2,1)S(1)}, bf16[80,4096]{1,0:T(8,128)(2,1)S(1)}, u32[]{:S(2)}, u32[]{:S(2)}) %collective-permute-start.9) | collective-permute-done | bytes 655392 | tf_op jit(solution)/shard_map/ppermute | solution.py:375
  60.3 6.8 %multiply.11 = (bf16[2,160,512]{2,1,0:T(8,128)(2,1)S(1)}, bf16[2,160,512]{2,1,0:T(8,128)(2,1)S(1)}, f32[8,128]{1,0:T(8,128)S(1)}) custom-call(bf16[80,4096]{1,0:T(8,128)(2,1)S(1)} %get-tuple-element.108.refs_0_, bf16[80,4096]{1,0:T(8,128)(2,1)S(1)} %collective-permute-done.9.refs_1_, bf16[13312,2048]{1,0:T(8,128)(2,1)} %refs_2_.13, ...), custom_call_target="tpu_custom_call" | custom-call | flops 10000000000 | bytes 1024 | tf_op jit(solution)/shard_map/multiply/pallas_call | solution.py:108
  67.2 1.5 %collective-permute-done.11.refs_0_ = bf16[48,6144]{1,0:T(8,128)(2,1)S(1)} collective-permute-done((bf16[48,6144]{1,0:T(8,128)(2,1)S(1)}, bf16[48,6144]{1,0:T(8,128)(2,1)S(1)}, u32[]{:S(2)}, u32[]{:S(2)}) %collective-permute-start.11) | collective-permute-done | bytes 589856 | tf_op jit(solution)/shard_map/ppermute | solution.py:375
  68.6 0.5 collective-permute-start.10
  69.2 1.7 %collective-permute-start.16 = (bf16[48,7168]{1,0:T(8,128)(2,1)S(1)}, bf16[48,7168]{1,0:T(8,128)(2,1)S(1)}, u32[]{:S(2)}, u32[]{:S(2)}) collective-permute-start(bf16[48,7168]{1,0:T(8,128)(2,1)S(1)} %get-tuple-element.127), channel_id=1, source_target_pairs={{0,2},{1,3},{2,0},{3,1},{4,6},{5,7},{6,4},{7,5},{8,10},{9,11},{10,... | collective-permute-start | bytes 2064392 | tf_op jit(solution)/shard_map/ppermute | solution.py:375
  70.9 1.6 %collective-permute-start.13 = (bf16[2,160,512]{2,1,0:T(8,128)(2,1)S(1)}, bf16[2,160,512]{2,1,0:T(8,128)(2,1)S(1)}, u32[]{:S(2)}, u32[]{:S(2)}) collective-permute-start(bf16[2,160,512]{2,1,0:T(8,128)(2,1)S(1)} %get-tuple-element.121), channel_id=1, source_target_pairs={{0,4},{4,0},{8,12},{12,8},{1,5},{5,1},{9,13},{13,9},{2,6},{6,2},{1... | collective-permute-start | bytes 983048 | tf_op jit(solution)/shard_map/ppermute | solution.py:378
  72.5 2.7 %collective-permute-start.12 = (bf16[2,128,512]{2,1,0:T(8,128)(2,1)S(1)}, bf16[2,128,512]{2,1,0:T(8,128)(2,1)S(1)}, u32[]{:S(2)}, u32[]{:S(2)}) collective-permute-start(bf16[2,128,512]{2,1,0:T(8,128)(2,1)S(1)} %get-tuple-element.119.refs_0_), channel_id=1, source_target_pairs={{0,8},{4,12},{8,0},{12,4},{1,9},{5,13},{9,1},{13,5},{2,10},{6,14},... | collective-permute-start | bytes 786440 | tf_op jit(solution)/shard_map/ppermute | solution.py:378
  75.2 9.0 %multiply.12 = (f32[96,2048]{1,0:T(8,128)S(1)}, f32[8,128]{1,0:T(8,128)S(1)}) custom-call(bf16[48,6144]{1,0:T(8,128)(2,1)S(1)} %get-tuple-element.122.refs_0_, bf16[48,6144]{1,0:T(8,128)(2,1)S(1)} %collective-permute-done.14.refs_1_, bf16[13312,2048]{1,0:T(8,128)(2,1)} %refs_2_.13, f32[8,128]{1,0:T(8,128)S(1)} %get-tuple-element.123.refs_3_), custom_call_target="tpu_custom_call" | custom-call | flops 10000000000 | bytes 1024 | tf_op jit(solution)/shard_map/multiply/pallas_call | solution.py:108
  84.2 1.7 %collective-permute-done.13.refs_1_ = bf16[2,160,512]{2,1,0:T(8,128)(2,1)S(1)} collective-permute-done((bf16[2,160,512]{2,1,0:T(8,128)(2,1)S(1)}, bf16[2,160,512]{2,1,0:T(8,128)(2,1)S(1)}, u32[]{:S(2)}, u32[]{:S(2)}) %collective-permute-start.13) | collective-permute-done | bytes 327712 | tf_op jit(solution)/shard_map/ppermute | solution.py:378
  86.0 0.5 collective-permute-done.16.refs_0_
  86.5 2.8 %collective-permute-start.19 = (bf16[1,160,512]{2,1,0:T(8,128)(2,1)S(1)}, bf16[1,160,512]{2,1,0:T(8,128)(2,1)S(1)}, u32[]{:S(2)}, u32[]{:S(2)}) collective-permute-start(bf16[1,160,512]{2,1,0:T(8,128)(2,1)S(1)} %get-tuple-element.135), channel_id=1, source_target_pairs={{0,8},{4,12},{8,0},{12,4},{1,9},{5,13},{9,1},{13,5},{2,10},{6,14},... | collective-permute-start | bytes 491528 | tf_op jit(solution)/shard_map/ppermute | solution.py:378
  89.3 1.6 %collective-permute-start.15 = (bf16[4,128,512]{2,1,0:T(8,128)(2,1)S(1)}, bf16[4,128,512]{2,1,0:T(8,128)(2,1)S(1)}, u32[]{:S(2)}, u32[]{:S(2)}) collective-permute-start(bf16[4,128,512]{2,1,0:T(8,128)(2,1)S(1)} %get-tuple-element.126), channel_id=1, source_target_pairs={{0,4},{4,0},{8,12},{12,8},{1,5},{5,1},{9,13},{13,9},{2,6},{6,2},{1... | collective-permute-start | bytes 1572872 | tf_op jit(solution)/shard_map/ppermute | solution.py:378
  90.9 10.3 %multiply.13 = (bf16[2,96,512]{2,1,0:T(8,128)(2,1)S(1)}, bf16[2,96,512]{2,1,0:T(8,128)(2,1)S(1)}, f32[8,128]{1,0:T(8,128)S(1)}) custom-call(bf16[48,7168]{1,0:T(8,128)(2,1)S(1)} %get-tuple-element.129.refs_0_, bf16[48,7168]{1,0:T(8,128)(2,1)S(1)} %collective-permute-done.17.refs_1_, bf16[13312,2048]{1,0:T(8,128)(2,1)} %refs_2_.13, ...), custom_call_target="tpu_custom_call" | custom-call | flops 10000000000 | bytes 1024 | tf_op jit(solution)/shard_map/multiply/pallas_call | solution.py:108
  101.2 0.5 collective-permute-start.18
  101.8 1.6 %collective-permute-start.20 = (bf16[1,80,512]{2,1,0:T(8,128)(2,1)S(1)}, bf16[1,80,512]{2,1,0:T(8,128)(2,1)S(1)}, u32[]{:S(2)}, u32[]{:S(2)}) collective-permute-start(bf16[1,80,512]{2,1,0:T(8,128)(2,1)S(1)} %get-tuple-element.137), channel_id=1, source_target_pairs={{0,2},{1,3},{2,0},{3,1},{4,6},{5,7},{6,4},{7,5},{8,10},{9,11},{10,... | collective-permute-start | bytes 245768 | tf_op jit(solution)/shard_map/ppermute | solution.py:375
  103.3 2.9 %collective-permute-done.20.refs_0_ = bf16[1,80,512]{2,1,0:T(8,128)(2,1)S(1)} collective-permute-done((bf16[1,80,512]{2,1,0:T(8,128)(2,1)S(1)}, bf16[1,80,512]{2,1,0:T(8,128)(2,1)S(1)}, u32[]{:S(2)}, u32[]{:S(2)}) %collective-permute-start.20) | collective-permute-done | bytes 81952 | tf_op jit(solution)/shard_map/ppermute | solution.py:375
  106.3 1.8 %collective-permute-done.21.refs_1_ = bf16[1,80,512]{2,1,0:T(8,128)(2,1)S(1)} collective-permute-done((bf16[1,80,512]{2,1,0:T(8,128)(2,1)S(1)}, bf16[1,80,512]{2,1,0:T(8,128)(2,1)S(1)}, u32[]{:S(2)}, u32[]{:S(2)}) %collective-permute-start.21) | collective-permute-done | bytes 81952 | tf_op jit(solution)/shard_map/ppermute | solution.py:375
  108.0 1.7 %collective-permute-start.22 = (bf16[2,80,512]{2,1,0:T(8,128)(2,1)S(1)}, bf16[2,80,512]{2,1,0:T(8,128)(2,1)S(1)}, u32[]{:S(2)}, u32[]{:S(2)}) collective-permute-start(bf16[2,80,512]{2,1,0:T(8,128)(2,1)S(1)} %get-tuple-element.144.refs_0_.refs_2_), channel_id=1, source_target_pairs={{0,8},{4,12},{8,0},{12,4},{1,9},{5,13},{9,1},{13,5},{2,10},{6,14},... | collective-permute-start | bytes 491528 | tf_op jit(solution)/shard_map/ppermute | solution.py:378
  109.8 1.9 %collective-permute-start.23 = (bf16[1,96,512]{2,1,0:T(8,128)(2,1)S(1)}, bf16[1,96,512]{2,1,0:T(8,128)(2,1)S(1)}, u32[]{:S(2)}, u32[]{:S(2)}) collective-permute-start(bf16[1,96,512]{2,1,0:T(8,128)(2,1)S(1)} %get-tuple-element.146), channel_id=1, source_target_pairs={{0,8},{4,12},{8,0},{12,4},{1,9},{5,13},{9,1},{13,5},{2,10},{6,14},... | collective-permute-start | bytes 294920 | tf_op jit(solution)/shard_map/ppermute | solution.py:378
  111.7 1.5 %encode.3 = (bf16[128,8192]{1,0:T(8,128)(2,1)}, f32[128,128]{1,0:T(8,128)S(1)}, f32[8,128]{1,0:T(8,128)S(1)}) custom-call(bf16[2,128,512]{2,1,0:T(8,128)(2,1)S(1)} %get-tuple-element.119.refs_0_, bf16[4,128,512]{2,1,0:T(8,128)(2,1)S(1)} %collective-permute-done.15.refs_1_.refs_3_, bf16[2,128,512]{2,1,0:T(8,128)(2,1)S(1)} %collective-permute-done.12.refs_1_.refs_2_, ...), custom_call_target="tpu_custom_call" | custom-call | flops 10000000000 | bytes 1024 | tf_op jit(solution)/shard_map/encode/pallas_call | solution.py:108
  113.2 9.7 %collective-permute-done.23.refs_1_ = bf16[1,96,512]{2,1,0:T(8,128)(2,1)S(1)} collective-permute-done((bf16[1,96,512]{2,1,0:T(8,128)(2,1)S(1)}, bf16[1,96,512]{2,1,0:T(8,128)(2,1)S(1)}, u32[]{:S(2)}, u32[]{:S(2)}) %collective-permute-start.23) | collective-permute-done | bytes 98336 | tf_op jit(solution)/shard_map/ppermute | solution.py:378
  123.1 1.5 %collective-permute-start.25 = (bf16[1,48,512]{2,1,0:T(8,128)(2,1)S(1)}, bf16[1,48,512]{2,1,0:T(8,128)(2,1)S(1)}, u32[]{:S(2)}, u32[]{:S(2)}) collective-permute-start(bf16[1,48,512]{2,1,0:T(8,128)(2,1)S(1)} %get-tuple-element.150), channel_id=1, source_target_pairs={{0,2},{1,3},{2,0},{3,1},{4,6},{5,7},{6,4},{7,5},{8,10},{9,11},{10,... | collective-permute-start | bytes 147464 | tf_op jit(solution)/shard_map/ppermute | solution.py:375
  124.6 2.6 %collective-permute-done.25.refs_0_ = bf16[1,48,512]{2,1,0:T(8,128)(2,1)S(1)} collective-permute-done((bf16[1,48,512]{2,1,0:T(8,128)(2,1)S(1)}, bf16[1,48,512]{2,1,0:T(8,128)(2,1)S(1)}, u32[]{:S(2)}, u32[]{:S(2)}) %collective-permute-start.25) | collective-permute-done | bytes 49184 | tf_op jit(solution)/shard_map/ppermute | solution.py:375
  127.2 1.4 collective-permute-done.26.refs_1_
  128.6 1.7 %collective-permute-start.29 = (bf16[2,48,512]{2,1,0:T(8,128)(2,1)S(1)}, bf16[2,48,512]{2,1,0:T(8,128)(2,1)S(1)}, u32[]{:S(2)}, u32[]{:S(2)}) collective-permute-start(bf16[2,48,512]{2,1,0:T(8,128)(2,1)S(1)} %get-tuple-element.156.refs_2_), channel_id=1, source_target_pairs={{0,12},{4,8},{8,4},{12,0},{1,13},{5,9},{9,5},{13,1},{2,14},{6,10},... | collective-permute-start | bytes 294920 | tf_op jit(solution)/shard_map/ppermute | solution.py:378
  130.3 1.5 %collective-permute-start.28 = (bf16[2,48,512]{2,1,0:T(8,128)(2,1)S(1)}, bf16[2,48,512]{2,1,0:T(8,128)(2,1)S(1)}, u32[]{:S(2)}, u32[]{:S(2)}) collective-permute-start(bf16[2,48,512]{2,1,0:T(8,128)(2,1)S(1)} %get-tuple-element.156.refs_2_), channel_id=1, source_target_pairs={{0,8},{4,12},{8,0},{12,4},{1,9},{5,13},{9,1},{13,5},{2,10},{6,14},... | collective-permute-start | bytes 294920 | tf_op jit(solution)/shard_map/ppermute | solution.py:378
  131.8 1.2 collective-permute-start.27
  133.1 1.2 encode.4
  134.3 1.9 %collective-permute-done.29.refs_5_ = bf16[2,48,512]{2,1,0:T(8,128)(2,1)S(1)} collective-permute-done((bf16[2,48,512]{2,1,0:T(8,128)(2,1)S(1)}, bf16[2,48,512]{2,1,0:T(8,128)(2,1)S(1)}, u32[]{:S(2)}, u32[]{:S(2)}) %collective-permute-start.29) | collective-permute-done | bytes 98336 | tf_op jit(solution)/shard_map/ppermute | solution.py:378
  136.2 4.5 %collective-permute-done.28.refs_4_ = bf16[2,48,512]{2,1,0:T(8,128)(2,1)S(1)} collective-permute-done((bf16[2,48,512]{2,1,0:T(8,128)(2,1)S(1)}, bf16[2,48,512]{2,1,0:T(8,128)(2,1)S(1)}, u32[]{:S(2)}, u32[]{:S(2)}) %collective-permute-start.28) | collective-permute-done | bytes 98336 | tf_op jit(solution)/shard_map/ppermute | solution.py:378
  140.7 1.6 %encode.5 = (bf16[128,8192]{1,0:T(8,128)(2,1)}, bf16[64,128]{1,0:T(8,128)(2,1)}, f32[8,128]{1,0:T(8,128)}) custom-call(bf16[128,8192]{1,0:T(8,128)(2,1)} %get-tuple-element.154.refs_0_, f32[128,128]{1,0:T(8,128)S(1)} %get-tuple-element.155.refs_1_, bf16[2,48,512]{2,1,0:T(8,128)(2,1)S(1)} %get-tuple-element.156.refs_2_, ...), custom_call_target="tpu_custom_call", output_to_operand_aliasing={{0}: (0, {})} | custom-call | bytes 1024 | tf_op jit(solution)/shard_map/encode/pallas_call | solution.py:108
  (43 shorter events, 0.6 us)
Async XLA Ops:
  5.9 3.5 %collective-permute-start.1 = (bf16[128,5120]{1,0:T(8,128)(2,1)S(1)}, bf16[128,5120]{1,0:T(8,128)(2,1)S(1)}, u32[]{:S(2)}, u32[]{:S(2)}) collective-permute-start(bf16[128,5120]{1,0:T(8,128)(2,1)S(1)} %get-tuple-element.82.refs_0_), channel_id=1, source_target_pairs={{0,1},{1,0},{2,3},{3,2},{4,5},{5,4},{6,7},{7,6},{8,9},{9,8},{10,11... | collective-permute-start | bytes 3932168 | tf_op jit(solution)/shard_map/ppermute | solution.py:375
  6.4 14.6 %collective-permute-start = (bf16[128,8192]{1,0:T(8,128)(2,1)S(1)}, bf16[128,8192]{1,0:T(8,128)(2,1)S(1)}, u32[]{:S(2)}, u32[]{:S(2)}) collective-permute-start(bf16[128,8192]{1,0:T(8,128)(2,1)S(1)} %get-tuple-element.81.refs_0_), channel_id=1, source_target_pairs={{0,1},{1,0},{2,3},{3,2},{4,5},{5,4},{6,7},{7,6},{8,9},{9,8},{10,11... | collective-permute-start | bytes 6291464 | tf_op jit(solution)/shard_map/ppermute | solution.py:375
  6.5 29.5 %collective-permute-start.4 = (bf16[80,5120]{1,0:T(8,128)(2,1)S(1)}, bf16[80,5120]{1,0:T(8,128)(2,1)S(1)}, u32[]{:S(2)}, u32[]{:S(2)}) collective-permute-start(bf16[80,5120]{1,0:T(8,128)(2,1)S(1)} %get-tuple-element.92), channel_id=1, source_target_pairs={{0,2},{1,3},{2,0},{3,1},{4,6},{5,7},{6,4},{7,5},{8,10},{9,11},{10,... | collective-permute-start | bytes 2457608 | tf_op jit(solution)/shard_map/ppermute | solution.py:375
  18.5 27.8 %collective-permute-start.3 = (bf16[80,4096]{1,0:T(8,128)(2,1)S(1)}, bf16[80,4096]{1,0:T(8,128)(2,1)S(1)}, u32[]{:S(2)}, u32[]{:S(2)}) collective-permute-start(bf16[80,4096]{1,0:T(8,128)(2,1)S(1)} %get-tuple-element.91), channel_id=1, source_target_pairs={{0,2},{1,3},{2,0},{3,1},{4,6},{5,7},{6,4},{7,5},{8,10},{9,11},{10,... | collective-permute-start | bytes 1966088 | tf_op jit(solution)/shard_map/ppermute | solution.py:375
  34.4 13.7 %collective-permute-start.2 = (bf16[2,256,512]{2,1,0:T(8,128)(2,1)S(1)}, bf16[2,256,512]{2,1,0:T(8,128)(2,1)S(1)}, u32[]{:S(2)}, u32[]{:S(2)}) collective-permute-start(bf16[2,256,512]{2,1,0:T(8,128)(2,1)S(1)} %get-tuple-element.89), channel_id=1, source_target_pairs={{0,4},{4,0},{8,12},{12,8},{1,5},{5,1},{9,13},{13,9},{2,6},{6,2},{1... | collective-permute-start | bytes 1572872 | tf_op jit(solution)/shard_map/ppermute | solution.py:378
  36.0 2.3 %collective-permute-start.5 = (bf16[80,5120]{1,0:T(8,128)(2,1)S(1)}, bf16[80,5120]{1,0:T(8,128)(2,1)S(1)}, u32[]{:S(2)}, u32[]{:S(2)}) collective-permute-start(bf16[80,5120]{1,0:T(8,128)(2,1)S(1)} %get-tuple-element.94.refs_0_), channel_id=1, source_target_pairs={{0,1},{1,0},{2,3},{3,2},{4,5},{5,4},{6,7},{7,6},{8,9},{9,8},{10,11... | collective-permute-start | bytes 2457608 | tf_op jit(solution)/shard_map/ppermute | solution.py:375
  36.0 22.1 %collective-permute-start.7 = (bf16[80,4096]{1,0:T(8,128)(2,1)S(1)}, bf16[80,4096]{1,0:T(8,128)(2,1)S(1)}, u32[]{:S(2)}, u32[]{:S(2)}) collective-permute-start(bf16[80,4096]{1,0:T(8,128)(2,1)S(1)} %get-tuple-element.103), channel_id=1, source_target_pairs={{0,2},{1,3},{2,0},{3,1},{4,6},{5,7},{6,4},{7,5},{8,10},{9,11},{10,... | collective-permute-start | bytes 1966088 | tf_op jit(solution)/shard_map/ppermute | solution.py:375
  46.2 5.2 %collective-permute-start.8 = (bf16[80,4096]{1,0:T(8,128)(2,1)S(1)}, bf16[80,4096]{1,0:T(8,128)(2,1)S(1)}, u32[]{:S(2)}, u32[]{:S(2)}) collective-permute-start(bf16[80,4096]{1,0:T(8,128)(2,1)S(1)} %get-tuple-element.104.refs_0_), channel_id=1, source_target_pairs={{0,1},{1,0},{2,3},{3,2},{4,5},{5,4},{6,7},{7,6},{8,9},{9,8},{10,11... | collective-permute-start | bytes 1966088 | tf_op jit(solution)/shard_map/ppermute | solution.py:375
  48.2 18.9 %collective-permute-start.6 = (bf16[1,256,512]{2,1,0:T(8,128)(2,1)S(1)}, bf16[1,256,512]{2,1,0:T(8,128)(2,1)S(1)}, u32[]{:S(2)}, u32[]{:S(2)}) collective-permute-start(bf16[1,256,512]{2,1,0:T(8,128)(2,1)S(1)} %get-tuple-element.102), channel_id=1, source_target_pairs={{0,8},{4,12},{8,0},{12,4},{1,9},{5,13},{9,1},{13,5},{2,10},{6,14},... | collective-permute-start | bytes 786440 | tf_op jit(solution)/shard_map/ppermute | solution.py:378
  50.9 17.8 %collective-permute-start.11 = (bf16[48,6144]{1,0:T(8,128)(2,1)S(1)}, bf16[48,6144]{1,0:T(8,128)(2,1)S(1)}, u32[]{:S(2)}, u32[]{:S(2)}) collective-permute-start(bf16[48,6144]{1,0:T(8,128)(2,1)S(1)} %get-tuple-element.116), channel_id=1, source_target_pairs={{0,2},{1,3},{2,0},{3,1},{4,6},{5,7},{6,4},{7,5},{8,10},{9,11},{10,... | collective-permute-start | bytes 1769480 | tf_op jit(solution)/shard_map/ppermute | solution.py:375
  58.1 2.2 %collective-permute-start.9 = (bf16[80,4096]{1,0:T(8,128)(2,1)S(1)}, bf16[80,4096]{1,0:T(8,128)(2,1)S(1)}, u32[]{:S(2)}, u32[]{:S(2)}) collective-permute-start(bf16[80,4096]{1,0:T(8,128)(2,1)S(1)} %get-tuple-element.108.refs_0_), channel_id=1, source_target_pairs={{0,1},{1,0},{2,3},{3,2},{4,5},{5,4},{6,7},{7,6},{8,9},{9,8},{10,11... | collective-permute-start | bytes 1966088 | tf_op jit(solution)/shard_map/ppermute | solution.py:375
  68.6 6.5 %collective-permute-start.14 = (bf16[48,6144]{1,0:T(8,128)(2,1)S(1)}, bf16[48,6144]{1,0:T(8,128)(2,1)S(1)}, u32[]{:S(2)}, u32[]{:S(2)}) collective-permute-start(bf16[48,6144]{1,0:T(8,128)(2,1)S(1)} %get-tuple-element.122.refs_0_), channel_id=1, source_target_pairs={{0,1},{1,0},{2,3},{3,2},{4,5},{5,4},{6,7},{7,6},{8,9},{9,8},{10,11... | collective-permute-start | bytes 1769480 | tf_op jit(solution)/shard_map/ppermute | solution.py:375
  68.6 3.8 %collective-permute-start.10 = (bf16[1,128,512]{2,1,0:T(8,128)(2,1)S(1)}, bf16[1,128,512]{2,1,0:T(8,128)(2,1)S(1)}, u32[]{:S(2)}, u32[]{:S(2)}) collective-permute-start(bf16[1,128,512]{2,1,0:T(8,128)(2,1)S(1)} %get-tuple-element.115), channel_id=1, source_target_pairs={{0,1},{1,0},{2,3},{3,2},{4,5},{5,4},{6,7},{7,6},{8,9},{9,8},{10,11... | collective-permute-start | bytes 393224 | tf_op jit(solution)/shard_map/ppermute | solution.py:375
  69.2 17.3 %collective-permute-start.16 = (bf16[48,7168]{1,0:T(8,128)(2,1)S(1)}, bf16[48,7168]{1,0:T(8,128)(2,1)S(1)}, u32[]{:S(2)}, u32[]{:S(2)}) collective-permute-start(bf16[48,7168]{1,0:T(8,128)(2,1)S(1)} %get-tuple-element.127), channel_id=1, source_target_pairs={{0,2},{1,3},{2,0},{3,1},{4,6},{5,7},{6,4},{7,5},{8,10},{9,11},{10,... | collective-permute-start | bytes 2064392 | tf_op jit(solution)/shard_map/ppermute | solution.py:375
  70.9 15.0 %collective-permute-start.13 = (bf16[2,160,512]{2,1,0:T(8,128)(2,1)S(1)}, bf16[2,160,512]{2,1,0:T(8,128)(2,1)S(1)}, u32[]{:S(2)}, u32[]{:S(2)}) collective-permute-start(bf16[2,160,512]{2,1,0:T(8,128)(2,1)S(1)} %get-tuple-element.121), channel_id=1, source_target_pairs={{0,4},{4,0},{8,12},{12,8},{1,5},{5,1},{9,13},{13,9},{2,6},{6,2},{1... | collective-permute-start | bytes 983048 | tf_op jit(solution)/shard_map/ppermute | solution.py:378
  72.5 13.4 %collective-permute-start.12 = (bf16[2,128,512]{2,1,0:T(8,128)(2,1)S(1)}, bf16[2,128,512]{2,1,0:T(8,128)(2,1)S(1)}, u32[]{:S(2)}, u32[]{:S(2)}) collective-permute-start(bf16[2,128,512]{2,1,0:T(8,128)(2,1)S(1)} %get-tuple-element.119.refs_0_), channel_id=1, source_target_pairs={{0,8},{4,12},{8,0},{12,4},{1,9},{5,13},{9,1},{13,5},{2,10},{6,14},... | collective-permute-start | bytes 786440 | tf_op jit(solution)/shard_map/ppermute | solution.py:378
  86.5 4.4 %collective-permute-start.17 = (bf16[48,7168]{1,0:T(8,128)(2,1)S(1)}, bf16[48,7168]{1,0:T(8,128)(2,1)S(1)}, u32[]{:S(2)}, u32[]{:S(2)}) collective-permute-start(bf16[48,7168]{1,0:T(8,128)(2,1)S(1)} %get-tuple-element.129.refs_0_), channel_id=1, source_target_pairs={{0,1},{1,0},{2,3},{3,2},{4,5},{5,4},{6,7},{7,6},{8,9},{9,8},{10,11... | collective-permute-start | bytes 2064392 | tf_op jit(solution)/shard_map/ppermute | solution.py:375
  86.5 15.2 %collective-permute-start.19 = (bf16[1,160,512]{2,1,0:T(8,128)(2,1)S(1)}, bf16[1,160,512]{2,1,0:T(8,128)(2,1)S(1)}, u32[]{:S(2)}, u32[]{:S(2)}) collective-permute-start(bf16[1,160,512]{2,1,0:T(8,128)(2,1)S(1)} %get-tuple-element.135), channel_id=1, source_target_pairs={{0,8},{4,12},{8,0},{12,4},{1,9},{5,13},{9,1},{13,5},{2,10},{6,14},... | collective-permute-start | bytes 491528 | tf_op jit(solution)/shard_map/ppermute | solution.py:378
  89.3 22.4 %collective-permute-start.15 = (bf16[4,128,512]{2,1,0:T(8,128)(2,1)S(1)}, bf16[4,128,512]{2,1,0:T(8,128)(2,1)S(1)}, u32[]{:S(2)}, u32[]{:S(2)}) collective-permute-start(bf16[4,128,512]{2,1,0:T(8,128)(2,1)S(1)} %get-tuple-element.126), channel_id=1, source_target_pairs={{0,4},{4,0},{8,12},{12,8},{1,5},{5,1},{9,13},{13,9},{2,6},{6,2},{1... | collective-permute-start | bytes 1572872 | tf_op jit(solution)/shard_map/ppermute | solution.py:378
  101.2 8.6 %collective-permute-start.18 = (bf16[2,96,512]{2,1,0:T(8,128)(2,1)S(1)}, bf16[2,96,512]{2,1,0:T(8,128)(2,1)S(1)}, u32[]{:S(2)}, u32[]{:S(2)}) collective-permute-start(bf16[2,96,512]{2,1,0:T(8,128)(2,1)S(1)} %get-tuple-element.133), channel_id=1, source_target_pairs={{0,4},{4,0},{8,12},{12,8},{1,5},{5,1},{9,13},{13,9},{2,6},{6,2},{1... | collective-permute-start | bytes 589832 | tf_op jit(solution)/shard_map/ppermute | solution.py:378
  101.8 4.5 %collective-permute-start.20 = (bf16[1,80,512]{2,1,0:T(8,128)(2,1)S(1)}, bf16[1,80,512]{2,1,0:T(8,128)(2,1)S(1)}, u32[]{:S(2)}, u32[]{:S(2)}) collective-permute-start(bf16[1,80,512]{2,1,0:T(8,128)(2,1)S(1)} %get-tuple-element.137), channel_id=1, source_target_pairs={{0,2},{1,3},{2,0},{3,1},{4,6},{5,7},{6,4},{7,5},{8,10},{9,11},{10,... | collective-permute-start | bytes 245768 | tf_op jit(solution)/shard_map/ppermute | solution.py:375
  103.3 4.7 %collective-permute-start.21 = (bf16[1,80,512]{2,1,0:T(8,128)(2,1)S(1)}, bf16[1,80,512]{2,1,0:T(8,128)(2,1)S(1)}, u32[]{:S(2)}, u32[]{:S(2)}) collective-permute-start(bf16[1,80,512]{2,1,0:T(8,128)(2,1)S(1)} %get-tuple-element.138), channel_id=1, source_target_pairs={{0,3},{1,2},{2,1},{3,0},{4,7},{5,6},{6,5},{7,4},{8,11},{9,10},{10,... | collective-permute-start | bytes 245768 | tf_op jit(solution)/shard_map/ppermute | solution.py:375
  108.0 14.9 %collective-permute-start.22 = (bf16[2,80,512]{2,1,0:T(8,128)(2,1)S(1)}, bf16[2,80,512]{2,1,0:T(8,128)(2,1)S(1)}, u32[]{:S(2)}, u32[]{:S(2)}) collective-permute-start(bf16[2,80,512]{2,1,0:T(8,128)(2,1)S(1)} %get-tuple-element.144.refs_0_.refs_2_), channel_id=1, source_target_pairs={{0,8},{4,12},{8,0},{12,4},{1,9},{5,13},{9,1},{13,5},{2,10},{6,14},... | collective-permute-start | bytes 491528 | tf_op jit(solution)/shard_map/ppermute | solution.py:378
  109.8 13.1 %collective-permute-start.23 = (bf16[1,96,512]{2,1,0:T(8,128)(2,1)S(1)}, bf16[1,96,512]{2,1,0:T(8,128)(2,1)S(1)}, u32[]{:S(2)}, u32[]{:S(2)}) collective-permute-start(bf16[1,96,512]{2,1,0:T(8,128)(2,1)S(1)} %get-tuple-element.146), channel_id=1, source_target_pairs={{0,8},{4,12},{8,0},{12,4},{1,9},{5,13},{9,1},{13,5},{2,10},{6,14},... | collective-permute-start | bytes 294920 | tf_op jit(solution)/shard_map/ppermute | solution.py:378
  123.0 10.1 %collective-permute-start.24 = (bf16[4,80,512]{2,1,0:T(8,128)(2,1)S(1)}, bf16[4,80,512]{2,1,0:T(8,128)(2,1)S(1)}, u32[]{:S(2)}, u32[]{:S(2)}) collective-permute-start(bf16[4,80,512]{2,1,0:T(8,128)(2,1)S(1)} %get-tuple-element.149), channel_id=1, source_target_pairs={{0,4},{4,0},{8,12},{12,8},{1,5},{5,1},{9,13},{13,9},{2,6},{6,2},{1... | collective-permute-start | bytes 983048 | tf_op jit(solution)/shard_map/ppermute | solution.py:378
  123.1 4.2 %collective-permute-start.25 = (bf16[1,48,512]{2,1,0:T(8,128)(2,1)S(1)}, bf16[1,48,512]{2,1,0:T(8,128)(2,1)S(1)}, u32[]{:S(2)}, u32[]{:S(2)}) collective-permute-start(bf16[1,48,512]{2,1,0:T(8,128)(2,1)S(1)} %get-tuple-element.150), channel_id=1, source_target_pairs={{0,2},{1,3},{2,0},{3,1},{4,6},{5,7},{6,4},{7,5},{8,10},{9,11},{10,... | collective-permute-start | bytes 147464 | tf_op jit(solution)/shard_map/ppermute | solution.py:375
  124.6 4.0 %collective-permute-start.26 = (bf16[1,48,512]{2,1,0:T(8,128)(2,1)S(1)}, bf16[1,48,512]{2,1,0:T(8,128)(2,1)S(1)}, u32[]{:S(2)}, u32[]{:S(2)}) collective-permute-start(bf16[1,48,512]{2,1,0:T(8,128)(2,1)S(1)} %get-tuple-element.151), channel_id=1, source_target_pairs={{0,3},{1,2},{2,1},{3,0},{4,7},{5,6},{6,5},{7,4},{8,11},{9,10},{10,... | collective-permute-start | bytes 147464 | tf_op jit(solution)/shard_map/ppermute | solution.py:375
  128.6 7.6 %collective-permute-start.29 = (bf16[2,48,512]{2,1,0:T(8,128)(2,1)S(1)}, bf16[2,48,512]{2,1,0:T(8,128)(2,1)S(1)}, u32[]{:S(2)}, u32[]{:S(2)}) collective-permute-start(bf16[2,48,512]{2,1,0:T(8,128)(2,1)S(1)} %get-tuple-element.156.refs_2_), channel_id=1, source_target_pairs={{0,12},{4,8},{8,4},{12,0},{1,13},{5,9},{9,5},{13,1},{2,14},{6,10},... | collective-permute-start | bytes 294920 | tf_op jit(solution)/shard_map/ppermute | solution.py:378
  130.3 10.3 %collective-permute-start.28 = (bf16[2,48,512]{2,1,0:T(8,128)(2,1)S(1)}, bf16[2,48,512]{2,1,0:T(8,128)(2,1)S(1)}, u32[]{:S(2)}, u32[]{:S(2)}) collective-permute-start(bf16[2,48,512]{2,1,0:T(8,128)(2,1)S(1)} %get-tuple-element.156.refs_2_), channel_id=1, source_target_pairs={{0,8},{4,12},{8,0},{12,4},{1,9},{5,13},{9,1},{13,5},{2,10},{6,14},... | collective-permute-start | bytes 294920 | tf_op jit(solution)/shard_map/ppermute | solution.py:378
  131.8 8.8 %collective-permute-start.27 = (bf16[2,48,512]{2,1,0:T(8,128)(2,1)S(1)}, bf16[2,48,512]{2,1,0:T(8,128)(2,1)S(1)}, u32[]{:S(2)}, u32[]{:S(2)}) collective-permute-start(bf16[2,48,512]{2,1,0:T(8,128)(2,1)S(1)} %get-tuple-element.156.refs_2_), channel_id=1, source_target_pairs={{0,4},{4,0},{8,12},{12,8},{1,5},{5,1},{9,13},{13,9},{2,6},{6,2},{1... | collective-permute-start | bytes 294920 | tf_op jit(solution)/shard_map/ppermute | solution.py:378

commit v10 on v8

--- a/solution.py
+++ b/solution.py
@@ -440,13 +440,13 @@
     last = sum_pair(last)
     near = [(near[0], 0), (near[2], 0), (near[1], 0), (near[2], 2)]
     codes, scales = encode_columns(chain, None, None, near, 0, 0, rows, out_width, cost=10**10)
+    last = sum_home(last, 2)
     far = join(chain, *far)
     far = [far, shift(far, 2)]
-    last = sum_home(last, 2)
+    last = join(chain, *last)
+    last = [last] + [shift(last, flip) for flip in range(1, tp)]
     far.append(join(chain, *far))
     far[2] = shift(far[2], 1)
-    last = join(chain, *last)
-    last = [last] + [shift(last, flip) for flip in range(1, tp)]
     far = [(far[0], 0), (far[2], 0), (far[1], 0), (far[2], 2)]
     codes, scales = encode_columns(chain, codes, scales, far, 2, 0, rows, out_width)
     last = [(array, 0) for array in last]

time: 145 us -> 142 us (0.979)
  waiting for transfers between devices: 37.2 us -> 35.1 us
    ppermute x13, waiting for transfers between devices: 27.8 us -> 25.5 us  [shift(): return lax.ppermute(value, 'tp', [(t, t ^ flip) for t in range(tp)])]
  transfers between devices with their start and end apart: 30 -> 30, of which waited for: 12 -> 12; matrix products, arithmetic and copies ran while one was open for 0% -> 0% of each run, Pallas kernels for 46% -> 47%
where the time goes in v10:
time: 142 us
  Pallas kernels  73.1 us (51%)
  waiting for transfers between devices  35.1 us (25%)
  starting transfers between devices  32.8 us (23%)
    pallas_call x31, Pallas kernels, call(): pl.pallas_call(with_tokens, grid=grid, in_specs=list(in_specs) + [ANY] *...  73.1 us
    ppermute x13, waiting for transfers between devices, shift(): return lax.ppermute(value, 'tp', [(t, t ^ flip) for t in range(tp)])  25.5 us
    ppermute x13, starting transfers between devices, shift(): return lax.ppermute(value, 'tp', [(t, t ^ flip) for t in range(tp)])  20 us
    ppermute x17, starting transfers between devices, swap(): lax.ppermute(value, 'batch', [(b, b ^ flip) for b in range(batch)])  12.8 us
    ppermute x17, waiting for transfers between devices, swap(): lax.ppermute(value, 'batch', [(b, b ^ flip) for b in range(batch)])  9.54 us
  transfers between devices with their start and end apart: 30, of which 12 were waited for; matrix products, arithmetic and copies ran while one was open for 0% of the time, Pallas kernels for 47%

profile of v10, /device:TPU:0, one launch (start us, length us, event | category | flops | bytes accessed | tf_op | source)
XLA Modules:
  0.0 141.9 jit_solution(7094897950336552347)
XLA Ops:
  0.6 5.3 %activate.1 = (bf16[128,5120]{1,0:T(8,128)(2,1)S(1)}, bf16[128,8192]{1,0:T(8,128)(2,1)S(1)}, bf16[80,5120]{1,0:T(8,128)(2,1)S(1)}, bf16[80,4096]{1,0:T(8,128)(2,...) custom-call(bf16[128,13312]{1,0:T(8,128)(2,1)} %refs_0_.1, ...), custom_call_target="tpu_custom_call" | custom-call | flops 10000000000 | bytes 1024 | tf_op jit(solution)/shard_map/activate/pallas_call | solution.py:108
  5.9 0.5 collective-permute-start.1
  6.4 0.1 collective-permute-start
  6.5 2.9 %collective-permute-start.4 = (bf16[80,5120]{1,0:T(8,128)(2,1)S(1)}, bf16[80,5120]{1,0:T(8,128)(2,1)S(1)}, u32[]{:S(2)}, u32[]{:S(2)}) collective-permute-start(bf16[80,5120]{1,0:T(8,128)(2,1)S(1)} %get-tuple-element.92), channel_id=1, source_target_pairs={{0,2},{1,3},{2,0},{3,1},{4,6},{5,7},{6,4},{7,5},{8,10},{9,11},{10,... | collective-permute-start | bytes 2457608 | tf_op jit(solution)/shard_map/ppermute | solution.py:375
  9.4 9.0 %multiply.7 = (f32[256,2048]{1,0:T(8,128)S(1)}, f32[8,128]{1,0:T(8,128)S(1)}) custom-call(bf16[128,5120]{1,0:T(8,128)(2,1)S(1)} %get-tuple-element.82.refs_0_, bf16[128,5120]{1,0:T(8,128)(2,1)S(1)} %collective-permute-done.1.refs_1_, bf16[13312,2048]{1,0:T(8,128)(2,1)} %refs_2_.13, f32[8,128]{1,0:T(8,128)S(1)} %get-tuple-element.83.refs_3_), custom_call_target="tpu_custom_call" | custom-call | flops 10000000000 | bytes 1024 | tf_op jit(solution)/shard_map/multiply/pallas_call | solution.py:108
  18.5 2.6 %collective-permute-start.3 = (bf16[80,4096]{1,0:T(8,128)(2,1)S(1)}, bf16[80,4096]{1,0:T(8,128)(2,1)S(1)}, u32[]{:S(2)}, u32[]{:S(2)}) collective-permute-start(bf16[80,4096]{1,0:T(8,128)(2,1)S(1)} %get-tuple-element.91), channel_id=1, source_target_pairs={{0,2},{1,3},{2,0},{3,1},{4,6},{5,7},{6,4},{7,5},{8,10},{9,11},{10,... | collective-permute-start | bytes 1966088 | tf_op jit(solution)/shard_map/ppermute | solution.py:375
  21.0 13.3 %multiply.8 = (bf16[2,256,512]{2,1,0:T(8,128)(2,1)S(1)}, bf16[2,256,512]{2,1,0:T(8,128)(2,1)S(1)}, f32[8,128]{1,0:T(8,128)S(1)}) custom-call(bf16[128,8192]{1,0:T(8,128)(2,1)S(1)} %get-tuple-element.81.refs_0_, bf16[128,8192]{1,0:T(8,128)(2,1)S(1)} %collective-permute-done.refs_1_, bf16[13312,2048]{1,0:T(8,128)(2,1)} %refs_2_.13, ...), custom_call_target="tpu_custom_call" | custom-call | flops 10000000000 | bytes 1024 | tf_op jit(solution)/shard_map/multiply/pallas_call | solution.py:108
  34.4 1.6 %collective-permute-start.2 = (bf16[2,256,512]{2,1,0:T(8,128)(2,1)S(1)}, bf16[2,256,512]{2,1,0:T(8,128)(2,1)S(1)}, u32[]{:S(2)}, u32[]{:S(2)}) collective-permute-start(bf16[2,256,512]{2,1,0:T(8,128)(2,1)S(1)} %get-tuple-element.89), channel_id=1, source_target_pairs={{0,4},{4,0},{8,12},{12,8},{1,5},{5,1},{9,13},{13,9},{2,6},{6,2},{1... | collective-permute-start | bytes 1572872 | tf_op jit(solution)/shard_map/ppermute | solution.py:378
  36.0 0.6 collective-permute-start.7
  36.6 1.7 %collective-permute-done.5.refs_1_ = bf16[80,5120]{1,0:T(8,128)(2,1)S(1)} collective-permute-done((bf16[80,5120]{1,0:T(8,128)(2,1)S(1)}, bf16[80,5120]{1,0:T(8,128)(2,1)S(1)}, u32[]{:S(2)}, u32[]{:S(2)}) %collective-permute-start.5) | collective-permute-done | bytes 819232 | tf_op jit(solution)/shard_map/ppermute | solution.py:375
  38.3 7.9 %multiply.9 = (f32[160,2048]{1,0:T(8,128)S(1)}, f32[8,128]{1,0:T(8,128)S(1)}) custom-call(bf16[80,5120]{1,0:T(8,128)(2,1)S(1)} %get-tuple-element.94.refs_0_, bf16[80,5120]{1,0:T(8,128)(2,1)S(1)} %collective-permute-done.5.refs_1_, bf16[13312,2048]{1,0:T(8,128)(2,1)} %refs_2_.13, f32[8,128]{1,0:T(8,128)S(1)} %get-tuple-element.97.refs_3_), custom_call_target="tpu_custom_call" | custom-call | flops 10000000000 | bytes 1024 | tf_op jit(solution)/shard_map/multiply/pallas_call | solution.py:108
  46.2 0.2 collective-permute-start.8
  46.4 1.7 %collective-permute-done.2.refs_1_ = bf16[2,256,512]{2,1,0:T(8,128)(2,1)S(1)} collective-permute-done((bf16[2,256,512]{2,1,0:T(8,128)(2,1)S(1)}, bf16[2,256,512]{2,1,0:T(8,128)(2,1)S(1)}, u32[]{:S(2)}, u32[]{:S(2)}) %collective-permute-start.2) | collective-permute-done | bytes 524320 | tf_op jit(solution)/shard_map/ppermute | solution.py:378
  48.1 0.1 add.6
  48.2 2.7 %collective-permute-start.6 = (bf16[1,256,512]{2,1,0:T(8,128)(2,1)S(1)}, bf16[1,256,512]{2,1,0:T(8,128)(2,1)S(1)}, u32[]{:S(2)}, u32[]{:S(2)}) collective-permute-start(bf16[1,256,512]{2,1,0:T(8,128)(2,1)S(1)} %get-tuple-element.102), channel_id=1, source_target_pairs={{0,8},{4,12},{8,0},{12,4},{1,9},{5,13},{9,1},{13,5},{2,10},{6,14},... | collective-permute-start | bytes 786440 | tf_op jit(solution)/shard_map/ppermute | solution.py:378
  50.9 0.5 collective-permute-start.11
  51.4 6.7 %multiply.10 = (f32[160,2048]{1,0:T(8,128)S(1)}, f32[8,128]{1,0:T(8,128)S(1)}) custom-call(bf16[80,4096]{1,0:T(8,128)(2,1)S(1)} %get-tuple-element.104.refs_0_, bf16[80,4096]{1,0:T(8,128)(2,1)S(1)} %collective-permute-done.8.refs_1_, bf16[13312,2048]{1,0:T(8,128)(2,1)} %refs_2_.13, f32[160,2048]{1,0:T(8,128)S(1)} %get-tuple-element.105.refs_3_, ...), custom_call_target="tpu_custom_call" | custom-call | flops 10000000000 | bytes 1024 | tf_op jit(solution)/shard_map/multiply/pallas_call | solution.py:108
  58.1 0.1 collective-permute-start.9
  58.2 2.1 %collective-permute-done.9.refs_1_ = bf16[80,4096]{1,0:T(8,128)(2,1)S(1)} collective-permute-done((bf16[80,4096]{1,0:T(8,128)(2,1)S(1)}, bf16[80,4096]{1,0:T(8,128)(2,1)S(1)}, u32[]{:S(2)}, u32[]{:S(2)}) %collective-permute-start.9) | collective-permute-done | bytes 655392 | tf_op jit(solution)/shard_map/ppermute | solution.py:375
  60.3 6.8 %multiply.11 = (bf16[2,160,512]{2,1,0:T(8,128)(2,1)S(1)}, bf16[2,160,512]{2,1,0:T(8,128)(2,1)S(1)}, f32[8,128]{1,0:T(8,128)S(1)}) custom-call(bf16[80,4096]{1,0:T(8,128)(2,1)S(1)} %get-tuple-element.108.refs_0_, bf16[80,4096]{1,0:T(8,128)(2,1)S(1)} %collective-permute-done.9.refs_1_, bf16[13312,2048]{1,0:T(8,128)(2,1)} %refs_2_.13, ...), custom_call_target="tpu_custom_call" | custom-call | flops 10000000000 | bytes 1024 | tf_op jit(solution)/shard_map/multiply/pallas_call | solution.py:108
  67.2 1.5 %collective-permute-done.11.refs_0_ = bf16[48,6144]{1,0:T(8,128)(2,1)S(1)} collective-permute-done((bf16[48,6144]{1,0:T(8,128)(2,1)S(1)}, bf16[48,6144]{1,0:T(8,128)(2,1)S(1)}, u32[]{:S(2)}, u32[]{:S(2)}) %collective-permute-start.11) | collective-permute-done | bytes 589856 | tf_op jit(solution)/shard_map/ppermute | solution.py:375
  68.6 0.5 collective-permute-start.10
  69.2 1.7 %collective-permute-start.16 = (bf16[48,7168]{1,0:T(8,128)(2,1)S(1)}, bf16[48,7168]{1,0:T(8,128)(2,1)S(1)}, u32[]{:S(2)}, u32[]{:S(2)}) collective-permute-start(bf16[48,7168]{1,0:T(8,128)(2,1)S(1)} %get-tuple-element.127), channel_id=1, source_target_pairs={{0,2},{1,3},{2,0},{3,1},{4,6},{5,7},{6,4},{7,5},{8,10},{9,11},{10,... | collective-permute-start | bytes 2064392 | tf_op jit(solution)/shard_map/ppermute | solution.py:375
  70.9 1.6 %collective-permute-start.13 = (bf16[2,160,512]{2,1,0:T(8,128)(2,1)S(1)}, bf16[2,160,512]{2,1,0:T(8,128)(2,1)S(1)}, u32[]{:S(2)}, u32[]{:S(2)}) collective-permute-start(bf16[2,160,512]{2,1,0:T(8,128)(2,1)S(1)} %get-tuple-element.121), channel_id=1, source_target_pairs={{0,4},{4,0},{8,12},{12,8},{1,5},{5,1},{9,13},{13,9},{2,6},{6,2},{1... | collective-permute-start | bytes 983048 | tf_op jit(solution)/shard_map/ppermute | solution.py:378
  72.5 2.7 %collective-permute-start.12 = (bf16[2,128,512]{2,1,0:T(8,128)(2,1)S(1)}, bf16[2,128,512]{2,1,0:T(8,128)(2,1)S(1)}, u32[]{:S(2)}, u32[]{:S(2)}) collective-permute-start(bf16[2,128,512]{2,1,0:T(8,128)(2,1)S(1)} %get-tuple-element.119.refs_0_), channel_id=1, source_target_pairs={{0,8},{4,12},{8,0},{12,4},{1,9},{5,13},{9,1},{13,5},{2,10},{6,14},... | collective-permute-start | bytes 786440 | tf_op jit(solution)/shard_map/ppermute | solution.py:378
  75.2 9.0 %multiply.12 = (f32[96,2048]{1,0:T(8,128)S(1)}, f32[8,128]{1,0:T(8,128)S(1)}) custom-call(bf16[48,6144]{1,0:T(8,128)(2,1)S(1)} %get-tuple-element.122.refs_0_, bf16[48,6144]{1,0:T(8,128)(2,1)S(1)} %collective-permute-done.14.refs_1_, bf16[13312,2048]{1,0:T(8,128)(2,1)} %refs_2_.13, f32[8,128]{1,0:T(8,128)S(1)} %get-tuple-element.123.refs_3_), custom_call_target="tpu_custom_call" | custom-call | flops 10000000000 | bytes 1024 | tf_op jit(solution)/shard_map/multiply/pallas_call | solution.py:108
  84.2 1.7 %collective-permute-done.13.refs_1_ = bf16[2,160,512]{2,1,0:T(8,128)(2,1)S(1)} collective-permute-done((bf16[2,160,512]{2,1,0:T(8,128)(2,1)S(1)}, bf16[2,160,512]{2,1,0:T(8,128)(2,1)S(1)}, u32[]{:S(2)}, u32[]{:S(2)}) %collective-permute-start.13) | collective-permute-done | bytes 327712 | tf_op jit(solution)/shard_map/ppermute | solution.py:378
  85.9 0.1 add.8
  86.0 0.5 collective-permute-done.16.refs_0_
  86.5 2.8 %collective-permute-start.19 = (bf16[1,160,512]{2,1,0:T(8,128)(2,1)S(1)}, bf16[1,160,512]{2,1,0:T(8,128)(2,1)S(1)}, u32[]{:S(2)}, u32[]{:S(2)}) collective-permute-start(bf16[1,160,512]{2,1,0:T(8,128)(2,1)S(1)} %get-tuple-element.135), channel_id=1, source_target_pairs={{0,8},{4,12},{8,0},{12,4},{1,9},{5,13},{9,1},{13,5},{2,10},{6,14},... | collective-permute-start | bytes 491528 | tf_op jit(solution)/shard_map/ppermute | solution.py:378
  89.3 1.6 %collective-permute-start.15 = (bf16[4,128,512]{2,1,0:T(8,128)(2,1)S(1)}, bf16[4,128,512]{2,1,0:T(8,128)(2,1)S(1)}, u32[]{:S(2)}, u32[]{:S(2)}) collective-permute-start(bf16[4,128,512]{2,1,0:T(8,128)(2,1)S(1)} %get-tuple-element.126), channel_id=1, source_target_pairs={{0,4},{4,0},{8,12},{12,8},{1,5},{5,1},{9,13},{13,9},{2,6},{6,2},{1... | collective-permute-start | bytes 1572872 | tf_op jit(solution)/shard_map/ppermute | solution.py:378
  90.9 10.3 %multiply.13 = (bf16[2,96,512]{2,1,0:T(8,128)(2,1)S(1)}, bf16[2,96,512]{2,1,0:T(8,128)(2,1)S(1)}, f32[8,128]{1,0:T(8,128)S(1)}) custom-call(bf16[48,7168]{1,0:T(8,128)(2,1)S(1)} %get-tuple-element.129.refs_0_, bf16[48,7168]{1,0:T(8,128)(2,1)S(1)} %collective-permute-done.17.refs_1_, bf16[13312,2048]{1,0:T(8,128)(2,1)} %refs_2_.13, ...), custom_call_target="tpu_custom_call" | custom-call | flops 10000000000 | bytes 1024 | tf_op jit(solution)/shard_map/multiply/pallas_call | solution.py:108
  101.2 0.5 collective-permute-start.18
  101.8 1.6 %collective-permute-start.20 = (bf16[1,80,512]{2,1,0:T(8,128)(2,1)S(1)}, bf16[1,80,512]{2,1,0:T(8,128)(2,1)S(1)}, u32[]{:S(2)}, u32[]{:S(2)}) collective-permute-start(bf16[1,80,512]{2,1,0:T(8,128)(2,1)S(1)} %get-tuple-element.141), channel_id=1, source_target_pairs={{0,2},{1,3},{2,0},{3,1},{4,6},{5,7},{6,4},{7,5},{8,10},{9,11},{10,... | collective-permute-start | bytes 245768 | tf_op jit(solution)/shard_map/ppermute | solution.py:375
  103.3 6.4 %collective-permute-done.18.refs_1_ = bf16[2,96,512]{2,1,0:T(8,128)(2,1)S(1)} collective-permute-done((bf16[2,96,512]{2,1,0:T(8,128)(2,1)S(1)}, bf16[2,96,512]{2,1,0:T(8,128)(2,1)S(1)}, u32[]{:S(2)}, u32[]{:S(2)}) %collective-permute-start.18) | collective-permute-done | bytes 196640 | tf_op jit(solution)/shard_map/ppermute | solution.py:378
  109.8 2.0 %collective-permute-start.22 = (bf16[1,96,512]{2,1,0:T(8,128)(2,1)S(1)}, bf16[1,96,512]{2,1,0:T(8,128)(2,1)S(1)}, u32[]{:S(2)}, u32[]{:S(2)}) collective-permute-start(bf16[1,96,512]{2,1,0:T(8,128)(2,1)S(1)} %get-tuple-element.144), channel_id=1, source_target_pairs={{0,8},{4,12},{8,0},{12,4},{1,9},{5,13},{9,1},{13,5},{2,10},{6,14},... | collective-permute-start | bytes 294920 | tf_op jit(solution)/shard_map/ppermute | solution.py:378
  111.7 1.5 %encode.3 = (bf16[128,8192]{1,0:T(8,128)(2,1)}, f32[128,128]{1,0:T(8,128)S(1)}, f32[8,128]{1,0:T(8,128)S(1)}) custom-call(bf16[2,128,512]{2,1,0:T(8,128)(2,1)S(1)} %get-tuple-element.119.refs_0_, bf16[4,128,512]{2,1,0:T(8,128)(2,1)S(1)} %collective-permute-done.15.refs_1_.refs_3_, bf16[2,128,512]{2,1,0:T(8,128)(2,1)S(1)} %collective-permute-done.12.refs_1_.refs_2_, ...), custom_call_target="tpu_custom_call" | custom-call | flops 10000000000 | bytes 1024 | tf_op jit(solution)/shard_map/encode/pallas_call | solution.py:108
  113.2 4.2 %collective-permute-done.22.refs_1_ = bf16[1,96,512]{2,1,0:T(8,128)(2,1)S(1)} collective-permute-done((bf16[1,96,512]{2,1,0:T(8,128)(2,1)S(1)}, bf16[1,96,512]{2,1,0:T(8,128)(2,1)S(1)}, u32[]{:S(2)}, u32[]{:S(2)}) %collective-permute-start.22) | collective-permute-done | bytes 98336 | tf_op jit(solution)/shard_map/ppermute | solution.py:378
  117.6 1.5 %collective-permute-start.24 = (bf16[1,48,512]{2,1,0:T(8,128)(2,1)S(1)}, bf16[1,48,512]{2,1,0:T(8,128)(2,1)S(1)}, u32[]{:S(2)}, u32[]{:S(2)}) collective-permute-start(bf16[1,48,512]{2,1,0:T(8,128)(2,1)S(1)} %get-tuple-element.148), channel_id=1, source_target_pairs={{0,2},{1,3},{2,0},{3,1},{4,6},{5,7},{6,4},{7,5},{8,10},{9,11},{10,... | collective-permute-start | bytes 147464 | tf_op jit(solution)/shard_map/ppermute | solution.py:375
  119.1 2.7 %collective-permute-done.24.refs_0_ = bf16[1,48,512]{2,1,0:T(8,128)(2,1)S(1)} collective-permute-done((bf16[1,48,512]{2,1,0:T(8,128)(2,1)S(1)}, bf16[1,48,512]{2,1,0:T(8,128)(2,1)S(1)}, u32[]{:S(2)}, u32[]{:S(2)}) %collective-permute-start.24) | collective-permute-done | bytes 49184 | tf_op jit(solution)/shard_map/ppermute | solution.py:375
  121.8 1.1 collective-permute-done.25.refs_1_
  122.8 3.1 %collective-permute-done.23.refs_1_.refs_4_ = bf16[2,80,512]{2,1,0:T(8,128)(2,1)S(1)} collective-permute-done((bf16[2,80,512]{2,1,0:T(8,128)(2,1)S(1)}, bf16[2,80,512]{2,1,0:T(8,128)(2,1)S(1)}, u32[]{:S(2)}, u32[]{:S(2)}) %collective-permute-start.23) | collective-permute-done | bytes 163872 | tf_op jit(solution)/shard_map/ppermute | solution.py:378
  126.0 2.4 %collective-permute-start.29 = (bf16[2,48,512]{2,1,0:T(8,128)(2,1)S(1)}, bf16[2,48,512]{2,1,0:T(8,128)(2,1)S(1)}, u32[]{:S(2)}, u32[]{:S(2)}) collective-permute-start(bf16[2,48,512]{2,1,0:T(8,128)(2,1)S(1)} %get-tuple-element.156.refs_2_), channel_id=1, source_target_pairs={{0,12},{4,8},{8,4},{12,0},{1,13},{5,9},{9,5},{13,1},{2,14},{6,10},... | collective-permute-start | bytes 294920 | tf_op jit(solution)/shard_map/ppermute | solution.py:378
  128.4 1.1 collective-permute-start.28
  129.5 1.0 collective-permute-start.27
  130.5 8.5 %collective-permute-done.26.refs_3_.refs_5_ = bf16[4,80,512]{2,1,0:T(8,128)(2,1)S(1)} collective-permute-done((bf16[4,80,512]{2,1,0:T(8,128)(2,1)S(1)}, bf16[4,80,512]{2,1,0:T(8,128)(2,1)S(1)}, u32[]{:S(2)}, u32[]{:S(2)}) %collective-permute-start.26) | collective-permute-done | bytes 327712 | tf_op jit(solution)/shard_map/ppermute | solution.py:378
  139.0 1.2 encode.4
  140.2 1.6 %encode.5 = (bf16[128,8192]{1,0:T(8,128)(2,1)}, bf16[64,128]{1,0:T(8,128)(2,1)}, f32[8,128]{1,0:T(8,128)}) custom-call(bf16[128,8192]{1,0:T(8,128)(2,1)} %get-tuple-element.154.refs_0_, f32[128,128]{1,0:T(8,128)S(1)} %get-tuple-element.155.refs_1_, bf16[2,48,512]{2,1,0:T(8,128)(2,1)S(1)} %get-tuple-element.156.refs_2_, ...), custom_call_target="tpu_custom_call", output_to_operand_aliasing={{0}: (0, {})} | custom-call | bytes 1024 | tf_op jit(solution)/shard_map/encode/pallas_call | solution.py:108
  (43 shorter events, 0.5 us)
Async XLA Ops:
  5.9 3.5 %collective-permute-start.1 = (bf16[128,5120]{1,0:T(8,128)(2,1)S(1)}, bf16[128,5120]{1,0:T(8,128)(2,1)S(1)}, u32[]{:S(2)}, u32[]{:S(2)}) collective-permute-start(bf16[128,5120]{1,0:T(8,128)(2,1)S(1)} %get-tuple-element.82.refs_0_), channel_id=1, source_target_pairs={{0,1},{1,0},{2,3},{3,2},{4,5},{5,4},{6,7},{7,6},{8,9},{9,8},{10,11... | collective-permute-start | bytes 3932168 | tf_op jit(solution)/shard_map/ppermute | solution.py:375
  6.4 14.6 %collective-permute-start = (bf16[128,8192]{1,0:T(8,128)(2,1)S(1)}, bf16[128,8192]{1,0:T(8,128)(2,1)S(1)}, u32[]{:S(2)}, u32[]{:S(2)}) collective-permute-start(bf16[128,8192]{1,0:T(8,128)(2,1)S(1)} %get-tuple-element.81.refs_0_), channel_id=1, source_target_pairs={{0,1},{1,0},{2,3},{3,2},{4,5},{5,4},{6,7},{7,6},{8,9},{9,8},{10,11... | collective-permute-start | bytes 6291464 | tf_op jit(solution)/shard_map/ppermute | solution.py:375
  6.5 29.5 %collective-permute-start.4 = (bf16[80,5120]{1,0:T(8,128)(2,1)S(1)}, bf16[80,5120]{1,0:T(8,128)(2,1)S(1)}, u32[]{:S(2)}, u32[]{:S(2)}) collective-permute-start(bf16[80,5120]{1,0:T(8,128)(2,1)S(1)} %get-tuple-element.92), channel_id=1, source_target_pairs={{0,2},{1,3},{2,0},{3,1},{4,6},{5,7},{6,4},{7,5},{8,10},{9,11},{10,... | collective-permute-start | bytes 2457608 | tf_op jit(solution)/shard_map/ppermute | solution.py:375
  18.5 27.8 %collective-permute-start.3 = (bf16[80,4096]{1,0:T(8,128)(2,1)S(1)}, bf16[80,4096]{1,0:T(8,128)(2,1)S(1)}, u32[]{:S(2)}, u32[]{:S(2)}) collective-permute-start(bf16[80,4096]{1,0:T(8,128)(2,1)S(1)} %get-tuple-element.91), channel_id=1, source_target_pairs={{0,2},{1,3},{2,0},{3,1},{4,6},{5,7},{6,4},{7,5},{8,10},{9,11},{10,... | collective-permute-start | bytes 1966088 | tf_op jit(solution)/shard_map/ppermute | solution.py:375
  34.4 13.7 %collective-permute-start.2 = (bf16[2,256,512]{2,1,0:T(8,128)(2,1)S(1)}, bf16[2,256,512]{2,1,0:T(8,128)(2,1)S(1)}, u32[]{:S(2)}, u32[]{:S(2)}) collective-permute-start(bf16[2,256,512]{2,1,0:T(8,128)(2,1)S(1)} %get-tuple-element.89), channel_id=1, source_target_pairs={{0,4},{4,0},{8,12},{12,8},{1,5},{5,1},{9,13},{13,9},{2,6},{6,2},{1... | collective-permute-start | bytes 1572872 | tf_op jit(solution)/shard_map/ppermute | solution.py:378
  36.0 2.3 %collective-permute-start.5 = (bf16[80,5120]{1,0:T(8,128)(2,1)S(1)}, bf16[80,5120]{1,0:T(8,128)(2,1)S(1)}, u32[]{:S(2)}, u32[]{:S(2)}) collective-permute-start(bf16[80,5120]{1,0:T(8,128)(2,1)S(1)} %get-tuple-element.94.refs_0_), channel_id=1, source_target_pairs={{0,1},{1,0},{2,3},{3,2},{4,5},{5,4},{6,7},{7,6},{8,9},{9,8},{10,11... | collective-permute-start | bytes 2457608 | tf_op jit(solution)/shard_map/ppermute | solution.py:375
  36.0 22.1 %collective-permute-start.7 = (bf16[80,4096]{1,0:T(8,128)(2,1)S(1)}, bf16[80,4096]{1,0:T(8,128)(2,1)S(1)}, u32[]{:S(2)}, u32[]{:S(2)}) collective-permute-start(bf16[80,4096]{1,0:T(8,128)(2,1)S(1)} %get-tuple-element.103), channel_id=1, source_target_pairs={{0,2},{1,3},{2,0},{3,1},{4,6},{5,7},{6,4},{7,5},{8,10},{9,11},{10,... | collective-permute-start | bytes 1966088 | tf_op jit(solution)/shard_map/ppermute | solution.py:375
  46.2 5.2 %collective-permute-start.8 = (bf16[80,4096]{1,0:T(8,128)(2,1)S(1)}, bf16[80,4096]{1,0:T(8,128)(2,1)S(1)}, u32[]{:S(2)}, u32[]{:S(2)}) collective-permute-start(bf16[80,4096]{1,0:T(8,128)(2,1)S(1)} %get-tuple-element.104.refs_0_), channel_id=1, source_target_pairs={{0,1},{1,0},{2,3},{3,2},{4,5},{5,4},{6,7},{7,6},{8,9},{9,8},{10,11... | collective-permute-start | bytes 1966088 | tf_op jit(solution)/shard_map/ppermute | solution.py:375
  48.2 18.9 %collective-permute-start.6 = (bf16[1,256,512]{2,1,0:T(8,128)(2,1)S(1)}, bf16[1,256,512]{2,1,0:T(8,128)(2,1)S(1)}, u32[]{:S(2)}, u32[]{:S(2)}) collective-permute-start(bf16[1,256,512]{2,1,0:T(8,128)(2,1)S(1)} %get-tuple-element.102), channel_id=1, source_target_pairs={{0,8},{4,12},{8,0},{12,4},{1,9},{5,13},{9,1},{13,5},{2,10},{6,14},... | collective-permute-start | bytes 786440 | tf_op jit(solution)/shard_map/ppermute | solution.py:378
  50.9 17.8 %collective-permute-start.11 = (bf16[48,6144]{1,0:T(8,128)(2,1)S(1)}, bf16[48,6144]{1,0:T(8,128)(2,1)S(1)}, u32[]{:S(2)}, u32[]{:S(2)}) collective-permute-start(bf16[48,6144]{1,0:T(8,128)(2,1)S(1)} %get-tuple-element.116), channel_id=1, source_target_pairs={{0,2},{1,3},{2,0},{3,1},{4,6},{5,7},{6,4},{7,5},{8,10},{9,11},{10,... | collective-permute-start | bytes 1769480 | tf_op jit(solution)/shard_map/ppermute | solution.py:375
  58.1 2.2 %collective-permute-start.9 = (bf16[80,4096]{1,0:T(8,128)(2,1)S(1)}, bf16[80,4096]{1,0:T(8,128)(2,1)S(1)}, u32[]{:S(2)}, u32[]{:S(2)}) collective-permute-start(bf16[80,4096]{1,0:T(8,128)(2,1)S(1)} %get-tuple-element.108.refs_0_), channel_id=1, source_target_pairs={{0,1},{1,0},{2,3},{3,2},{4,5},{5,4},{6,7},{7,6},{8,9},{9,8},{10,11... | collective-permute-start | bytes 1966088 | tf_op jit(solution)/shard_map/ppermute | solution.py:375
  68.6 6.5 %collective-permute-start.14 = (bf16[48,6144]{1,0:T(8,128)(2,1)S(1)}, bf16[48,6144]{1,0:T(8,128)(2,1)S(1)}, u32[]{:S(2)}, u32[]{:S(2)}) collective-permute-start(bf16[48,6144]{1,0:T(8,128)(2,1)S(1)} %get-tuple-element.122.refs_0_), channel_id=1, source_target_pairs={{0,1},{1,0},{2,3},{3,2},{4,5},{5,4},{6,7},{7,6},{8,9},{9,8},{10,11... | collective-permute-start | bytes 1769480 | tf_op jit(solution)/shard_map/ppermute | solution.py:375
  68.6 3.8 %collective-permute-start.10 = (bf16[1,128,512]{2,1,0:T(8,128)(2,1)S(1)}, bf16[1,128,512]{2,1,0:T(8,128)(2,1)S(1)}, u32[]{:S(2)}, u32[]{:S(2)}) collective-permute-start(bf16[1,128,512]{2,1,0:T(8,128)(2,1)S(1)} %get-tuple-element.115), channel_id=1, source_target_pairs={{0,1},{1,0},{2,3},{3,2},{4,5},{5,4},{6,7},{7,6},{8,9},{9,8},{10,11... | collective-permute-start | bytes 393224 | tf_op jit(solution)/shard_map/ppermute | solution.py:375
  69.2 17.3 %collective-permute-start.16 = (bf16[48,7168]{1,0:T(8,128)(2,1)S(1)}, bf16[48,7168]{1,0:T(8,128)(2,1)S(1)}, u32[]{:S(2)}, u32[]{:S(2)}) collective-permute-start(bf16[48,7168]{1,0:T(8,128)(2,1)S(1)} %get-tuple-element.127), channel_id=1, source_target_pairs={{0,2},{1,3},{2,0},{3,1},{4,6},{5,7},{6,4},{7,5},{8,10},{9,11},{10,... | collective-permute-start | bytes 2064392 | tf_op jit(solution)/shard_map/ppermute | solution.py:375
  70.9 15.0 %collective-permute-start.13 = (bf16[2,160,512]{2,1,0:T(8,128)(2,1)S(1)}, bf16[2,160,512]{2,1,0:T(8,128)(2,1)S(1)}, u32[]{:S(2)}, u32[]{:S(2)}) collective-permute-start(bf16[2,160,512]{2,1,0:T(8,128)(2,1)S(1)} %get-tuple-element.121), channel_id=1, source_target_pairs={{0,4},{4,0},{8,12},{12,8},{1,5},{5,1},{9,13},{13,9},{2,6},{6,2},{1... | collective-permute-start | bytes 983048 | tf_op jit(solution)/shard_map/ppermute | solution.py:378
  72.5 13.4 %collective-permute-start.12 = (bf16[2,128,512]{2,1,0:T(8,128)(2,1)S(1)}, bf16[2,128,512]{2,1,0:T(8,128)(2,1)S(1)}, u32[]{:S(2)}, u32[]{:S(2)}) collective-permute-start(bf16[2,128,512]{2,1,0:T(8,128)(2,1)S(1)} %get-tuple-element.119.refs_0_), channel_id=1, source_target_pairs={{0,8},{4,12},{8,0},{12,4},{1,9},{5,13},{9,1},{13,5},{2,10},{6,14},... | collective-permute-start | bytes 786440 | tf_op jit(solution)/shard_map/ppermute | solution.py:378
  86.5 4.4 %collective-permute-start.17 = (bf16[48,7168]{1,0:T(8,128)(2,1)S(1)}, bf16[48,7168]{1,0:T(8,128)(2,1)S(1)}, u32[]{:S(2)}, u32[]{:S(2)}) collective-permute-start(bf16[48,7168]{1,0:T(8,128)(2,1)S(1)} %get-tuple-element.129.refs_0_), channel_id=1, source_target_pairs={{0,1},{1,0},{2,3},{3,2},{4,5},{5,4},{6,7},{7,6},{8,9},{9,8},{10,11... | collective-permute-start | bytes 2064392 | tf_op jit(solution)/shard_map/ppermute | solution.py:375
  86.5 15.2 %collective-permute-start.19 = (bf16[1,160,512]{2,1,0:T(8,128)(2,1)S(1)}, bf16[1,160,512]{2,1,0:T(8,128)(2,1)S(1)}, u32[]{:S(2)}, u32[]{:S(2)}) collective-permute-start(bf16[1,160,512]{2,1,0:T(8,128)(2,1)S(1)} %get-tuple-element.135), channel_id=1, source_target_pairs={{0,8},{4,12},{8,0},{12,4},{1,9},{5,13},{9,1},{13,5},{2,10},{6,14},... | collective-permute-start | bytes 491528 | tf_op jit(solution)/shard_map/ppermute | solution.py:378
  89.3 22.4 %collective-permute-start.15 = (bf16[4,128,512]{2,1,0:T(8,128)(2,1)S(1)}, bf16[4,128,512]{2,1,0:T(8,128)(2,1)S(1)}, u32[]{:S(2)}, u32[]{:S(2)}) collective-permute-start(bf16[4,128,512]{2,1,0:T(8,128)(2,1)S(1)} %get-tuple-element.126), channel_id=1, source_target_pairs={{0,4},{4,0},{8,12},{12,8},{1,5},{5,1},{9,13},{13,9},{2,6},{6,2},{1... | collective-permute-start | bytes 1572872 | tf_op jit(solution)/shard_map/ppermute | solution.py:378
  101.2 8.5 %collective-permute-start.18 = (bf16[2,96,512]{2,1,0:T(8,128)(2,1)S(1)}, bf16[2,96,512]{2,1,0:T(8,128)(2,1)S(1)}, u32[]{:S(2)}, u32[]{:S(2)}) collective-permute-start(bf16[2,96,512]{2,1,0:T(8,128)(2,1)S(1)} %get-tuple-element.133), channel_id=1, source_target_pairs={{0,4},{4,0},{8,12},{12,8},{1,5},{5,1},{9,13},{13,9},{2,6},{6,2},{1... | collective-permute-start | bytes 589832 | tf_op jit(solution)/shard_map/ppermute | solution.py:378
  101.8 15.7 %collective-permute-start.20 = (bf16[1,80,512]{2,1,0:T(8,128)(2,1)S(1)}, bf16[1,80,512]{2,1,0:T(8,128)(2,1)S(1)}, u32[]{:S(2)}, u32[]{:S(2)}) collective-permute-start(bf16[1,80,512]{2,1,0:T(8,128)(2,1)S(1)} %get-tuple-element.141), channel_id=1, source_target_pairs={{0,2},{1,3},{2,0},{3,1},{4,6},{5,7},{6,4},{7,5},{8,10},{9,11},{10,... | collective-permute-start | bytes 245768 | tf_op jit(solution)/shard_map/ppermute | solution.py:375
  103.3 14.2 %collective-permute-start.21 = (bf16[1,80,512]{2,1,0:T(8,128)(2,1)S(1)}, bf16[1,80,512]{2,1,0:T(8,128)(2,1)S(1)}, u32[]{:S(2)}, u32[]{:S(2)}) collective-permute-start(bf16[1,80,512]{2,1,0:T(8,128)(2,1)S(1)} %get-tuple-element.142), channel_id=1, source_target_pairs={{0,3},{1,2},{2,1},{3,0},{4,7},{5,6},{6,5},{7,4},{8,11},{9,10},{10,... | collective-permute-start | bytes 245768 | tf_op jit(solution)/shard_map/ppermute | solution.py:375
  109.8 7.7 %collective-permute-start.22 = (bf16[1,96,512]{2,1,0:T(8,128)(2,1)S(1)}, bf16[1,96,512]{2,1,0:T(8,128)(2,1)S(1)}, u32[]{:S(2)}, u32[]{:S(2)}) collective-permute-start(bf16[1,96,512]{2,1,0:T(8,128)(2,1)S(1)} %get-tuple-element.144), channel_id=1, source_target_pairs={{0,8},{4,12},{8,0},{12,4},{1,9},{5,13},{9,1},{13,5},{2,10},{6,14},... | collective-permute-start | bytes 294920 | tf_op jit(solution)/shard_map/ppermute | solution.py:378
  117.5 8.4 %collective-permute-start.23 = (bf16[2,80,512]{2,1,0:T(8,128)(2,1)S(1)}, bf16[2,80,512]{2,1,0:T(8,128)(2,1)S(1)}, u32[]{:S(2)}, u32[]{:S(2)}) collective-permute-start(bf16[2,80,512]{2,1,0:T(8,128)(2,1)S(1)} %get-tuple-element.147.refs_0_.refs_2_), channel_id=1, source_target_pairs={{0,8},{4,12},{8,0},{12,4},{1,9},{5,13},{9,1},{13,5},{2,10},{6,14},... | collective-permute-start | bytes 491528 | tf_op jit(solution)/shard_map/ppermute | solution.py:378
  117.6 4.2 %collective-permute-start.24 = (bf16[1,48,512]{2,1,0:T(8,128)(2,1)S(1)}, bf16[1,48,512]{2,1,0:T(8,128)(2,1)S(1)}, u32[]{:S(2)}, u32[]{:S(2)}) collective-permute-start(bf16[1,48,512]{2,1,0:T(8,128)(2,1)S(1)} %get-tuple-element.148), channel_id=1, source_target_pairs={{0,2},{1,3},{2,0},{3,1},{4,6},{5,7},{6,4},{7,5},{8,10},{9,11},{10,... | collective-permute-start | bytes 147464 | tf_op jit(solution)/shard_map/ppermute | solution.py:375
  119.1 3.7 %collective-permute-start.25 = (bf16[1,48,512]{2,1,0:T(8,128)(2,1)S(1)}, bf16[1,48,512]{2,1,0:T(8,128)(2,1)S(1)}, u32[]{:S(2)}, u32[]{:S(2)}) collective-permute-start(bf16[1,48,512]{2,1,0:T(8,128)(2,1)S(1)} %get-tuple-element.149), channel_id=1, source_target_pairs={{0,3},{1,2},{2,1},{3,0},{4,7},{5,6},{6,5},{7,4},{8,11},{9,10},{10,... | collective-permute-start | bytes 147464 | tf_op jit(solution)/shard_map/ppermute | solution.py:375
  126.0 13.0 %collective-permute-start.26 = (bf16[4,80,512]{2,1,0:T(8,128)(2,1)S(1)}, bf16[4,80,512]{2,1,0:T(8,128)(2,1)S(1)}, u32[]{:S(2)}, u32[]{:S(2)}) collective-permute-start(bf16[4,80,512]{2,1,0:T(8,128)(2,1)S(1)} %get-tuple-element.152), channel_id=1, source_target_pairs={{0,4},{4,0},{8,12},{12,8},{1,5},{5,1},{9,13},{13,9},{2,6},{6,2},{1... | collective-permute-start | bytes 983048 | tf_op jit(solution)/shard_map/ppermute | solution.py:378
  126.0 14.2 %collective-permute-start.29 = (bf16[2,48,512]{2,1,0:T(8,128)(2,1)S(1)}, bf16[2,48,512]{2,1,0:T(8,128)(2,1)S(1)}, u32[]{:S(2)}, u32[]{:S(2)}) collective-permute-start(bf16[2,48,512]{2,1,0:T(8,128)(2,1)S(1)} %get-tuple-element.156.refs_2_), channel_id=1, source_target_pairs={{0,12},{4,8},{8,4},{12,0},{1,13},{5,9},{9,5},{13,1},{2,14},{6,10},... | collective-permute-start | bytes 294920 | tf_op jit(solution)/shard_map/ppermute | solution.py:378
  128.4 11.8 %collective-permute-start.28 = (bf16[2,48,512]{2,1,0:T(8,128)(2,1)S(1)}, bf16[2,48,512]{2,1,0:T(8,128)(2,1)S(1)}, u32[]{:S(2)}, u32[]{:S(2)}) collective-permute-start(bf16[2,48,512]{2,1,0:T(8,128)(2,1)S(1)} %get-tuple-element.156.refs_2_), channel_id=1, source_target_pairs={{0,8},{4,12},{8,0},{12,4},{1,9},{5,13},{9,1},{13,5},{2,10},{6,14},... | collective-permute-start | bytes 294920 | tf_op jit(solution)/shard_map/ppermute | solution.py:378
  129.5 10.7 %collective-permute-start.27 = (bf16[2,48,512]{2,1,0:T(8,128)(2,1)S(1)}, bf16[2,48,512]{2,1,0:T(8,128)(2,1)S(1)}, u32[]{:S(2)}, u32[]{:S(2)}) collective-permute-start(bf16[2,48,512]{2,1,0:T(8,128)(2,1)S(1)} %get-tuple-element.156.refs_2_), channel_id=1, source_target_pairs={{0,4},{4,0},{8,12},{12,8},{1,5},{5,1},{9,13},{13,9},{2,6},{6,2},{1... | collective-permute-start | bytes 294920 | tf_op jit(solution)/shard_map/ppermute | solution.py:378

commit v11 on v10

--- a/solution.py
+++ b/solution.py
@@ -368,7 +368,7 @@
     cut = rows * EARLY // 8
     steps = width // STEP
     first, middle = steps - 2 * PIECE, steps - PIECE
-    half = steps // 2
+    half = steps - steps // 2
     chain = Chain()
 
     def swap(value, flip):

time: 142 us -> 146 us (1.028)
  waiting for transfers between devices: 35.1 us -> 39.1 us
    ppermute x13, waiting for transfers between devices: 25.5 us -> 27.7 us  [shift(): return lax.ppermute(value, 'tp', [(t, t ^ flip) for t in range(tp)])]
    ppermute x17, waiting for transfers between devices: 9.54 us -> 11.4 us  [swap(): lax.ppermute(value, 'batch', [(b, b ^ flip) for b in range(batch)])]
  transfers between devices with their start and end apart: 30 -> 30, of which waited for: 12 -> 11; matrix products, arithmetic and copies ran while one was open for 0% -> 0% of each run, Pallas kernels for 47% -> 45%
where the time goes in v11:
time: 146 us
  Pallas kernels  73.1 us (50%)
  waiting for transfers between devices  39.1 us (27%)
  starting transfers between devices  32.8 us (22%)
    pallas_call x31, Pallas kernels, call(): pl.pallas_call(with_tokens, grid=grid, in_specs=list(in_specs) + [ANY] *...  73.1 us
    ppermute x13, waiting for transfers between devices, shift(): return lax.ppermute(value, 'tp', [(t, t ^ flip) for t in range(tp)])  27.7 us
    ppermute x13, starting transfers between devices, shift(): return lax.ppermute(value, 'tp', [(t, t ^ flip) for t in range(tp)])  20.7 us
    ppermute x17, starting transfers between devices, swap(): lax.ppermute(value, 'batch', [(b, b ^ flip) for b in range(batch)])  12.1 us
    ppermute x17, waiting for transfers between devices, swap(): lax.ppermute(value, 'batch', [(b, b ^ flip) for b in range(batch)])  11.4 us
  transfers between devices with their start and end apart: 30, of which 11 were waited for; matrix products, arithmetic and copies ran while one was open for 0% of the time, Pallas kernels for 45%

profile of v11, /device:TPU:0, one launch (start us, length us, event | category | flops | bytes accessed | tf_op | source)
XLA Modules:
  0.0 145.9 jit_solution(6298324263209377517)
XLA Ops:
  0.6 5.3 %activate.1 = (bf16[128,5120]{1,0:T(8,128)(2,1)S(1)}, bf16[128,8192]{1,0:T(8,128)(2,1)S(1)}, bf16[80,5120]{1,0:T(8,128)(2,1)S(1)}, bf16[80,4096]{1,0:T(8,128)(2,...) custom-call(bf16[128,13312]{1,0:T(8,128)(2,1)} %refs_0_.1, ...), custom_call_target="tpu_custom_call" | custom-call | flops 10000000000 | bytes 1024 | tf_op jit(solution)/shard_map/activate/pallas_call | solution.py:108
  5.9 0.5 collective-permute-start.1
  6.4 0.1 collective-permute-start
  6.5 2.9 %collective-permute-start.4 = (bf16[80,5120]{1,0:T(8,128)(2,1)S(1)}, bf16[80,5120]{1,0:T(8,128)(2,1)S(1)}, u32[]{:S(2)}, u32[]{:S(2)}) collective-permute-start(bf16[80,5120]{1,0:T(8,128)(2,1)S(1)} %get-tuple-element.92), channel_id=1, source_target_pairs={{0,2},{1,3},{2,0},{3,1},{4,6},{5,7},{6,4},{7,5},{8,10},{9,11},{10,... | collective-permute-start | bytes 2457608 | tf_op jit(solution)/shard_map/ppermute | solution.py:375
  9.4 9.0 %multiply.7 = (f32[256,2048]{1,0:T(8,128)S(1)}, f32[8,128]{1,0:T(8,128)S(1)}) custom-call(bf16[128,5120]{1,0:T(8,128)(2,1)S(1)} %get-tuple-element.82.refs_0_, bf16[128,5120]{1,0:T(8,128)(2,1)S(1)} %collective-permute-done.1.refs_1_, bf16[13312,2048]{1,0:T(8,128)(2,1)} %refs_2_.13, f32[8,128]{1,0:T(8,128)S(1)} %get-tuple-element.83.refs_3_), custom_call_target="tpu_custom_call" | custom-call | flops 10000000000 | bytes 1024 | tf_op jit(solution)/shard_map/multiply/pallas_call | solution.py:108
  18.5 2.6 %collective-permute-start.3 = (bf16[80,4096]{1,0:T(8,128)(2,1)S(1)}, bf16[80,4096]{1,0:T(8,128)(2,1)S(1)}, u32[]{:S(2)}, u32[]{:S(2)}) collective-permute-start(bf16[80,4096]{1,0:T(8,128)(2,1)S(1)} %get-tuple-element.91), channel_id=1, source_target_pairs={{0,2},{1,3},{2,0},{3,1},{4,6},{5,7},{6,4},{7,5},{8,10},{9,11},{10,... | collective-permute-start | bytes 1966088 | tf_op jit(solution)/shard_map/ppermute | solution.py:375
  21.0 13.3 %multiply.8 = (bf16[2,256,512]{2,1,0:T(8,128)(2,1)S(1)}, bf16[2,256,512]{2,1,0:T(8,128)(2,1)S(1)}, f32[8,128]{1,0:T(8,128)S(1)}) custom-call(bf16[128,8192]{1,0:T(8,128)(2,1)S(1)} %get-tuple-element.81.refs_0_, bf16[128,8192]{1,0:T(8,128)(2,1)S(1)} %collective-permute-done.refs_1_, bf16[13312,2048]{1,0:T(8,128)(2,1)} %refs_2_.13, ...), custom_call_target="tpu_custom_call" | custom-call | flops 10000000000 | bytes 1024 | tf_op jit(solution)/shard_map/multiply/pallas_call | solution.py:108
  34.4 1.6 %collective-permute-start.2 = (bf16[2,256,512]{2,1,0:T(8,128)(2,1)S(1)}, bf16[2,256,512]{2,1,0:T(8,128)(2,1)S(1)}, u32[]{:S(2)}, u32[]{:S(2)}) collective-permute-start(bf16[2,256,512]{2,1,0:T(8,128)(2,1)S(1)} %get-tuple-element.89), channel_id=1, source_target_pairs={{0,4},{4,0},{8,12},{12,8},{1,5},{5,1},{9,13},{13,9},{2,6},{6,2},{1... | collective-permute-start | bytes 1572872 | tf_op jit(solution)/shard_map/ppermute | solution.py:378
  36.0 0.6 collective-permute-start.7
  36.6 1.7 %collective-permute-done.5.refs_1_ = bf16[80,5120]{1,0:T(8,128)(2,1)S(1)} collective-permute-done((bf16[80,5120]{1,0:T(8,128)(2,1)S(1)}, bf16[80,5120]{1,0:T(8,128)(2,1)S(1)}, u32[]{:S(2)}, u32[]{:S(2)}) %collective-permute-start.5) | collective-permute-done | bytes 819232 | tf_op jit(solution)/shard_map/ppermute | solution.py:375
  38.3 7.9 %multiply.9 = (f32[160,2048]{1,0:T(8,128)S(1)}, f32[8,128]{1,0:T(8,128)S(1)}) custom-call(bf16[80,5120]{1,0:T(8,128)(2,1)S(1)} %get-tuple-element.94.refs_0_, bf16[80,5120]{1,0:T(8,128)(2,1)S(1)} %collective-permute-done.5.refs_1_, bf16[13312,2048]{1,0:T(8,128)(2,1)} %refs_2_.13, f32[8,128]{1,0:T(8,128)S(1)} %get-tuple-element.97.refs_3_), custom_call_target="tpu_custom_call" | custom-call | flops 10000000000 | bytes 1024 | tf_op jit(solution)/shard_map/multiply/pallas_call | solution.py:108
  46.2 0.2 collective-permute-start.8
  46.4 1.7 %collective-permute-done.2.refs_1_ = bf16[2,256,512]{2,1,0:T(8,128)(2,1)S(1)} collective-permute-done((bf16[2,256,512]{2,1,0:T(8,128)(2,1)S(1)}, bf16[2,256,512]{2,1,0:T(8,128)(2,1)S(1)}, u32[]{:S(2)}, u32[]{:S(2)}) %collective-permute-start.2) | collective-permute-done | bytes 524320 | tf_op jit(solution)/shard_map/ppermute | solution.py:378
  48.1 0.1 add.6
  48.2 2.7 %collective-permute-start.6 = (bf16[1,256,512]{2,1,0:T(8,128)(2,1)S(1)}, bf16[1,256,512]{2,1,0:T(8,128)(2,1)S(1)}, u32[]{:S(2)}, u32[]{:S(2)}) collective-permute-start(bf16[1,256,512]{2,1,0:T(8,128)(2,1)S(1)} %get-tuple-element.102), channel_id=1, source_target_pairs={{0,8},{4,12},{8,0},{12,4},{1,9},{5,13},{9,1},{13,5},{2,10},{6,14},... | collective-permute-start | bytes 786440 | tf_op jit(solution)/shard_map/ppermute | solution.py:378
  50.9 0.5 collective-permute-start.11
  51.4 6.7 %multiply.10 = (f32[160,2048]{1,0:T(8,128)S(1)}, f32[8,128]{1,0:T(8,128)S(1)}) custom-call(bf16[80,4096]{1,0:T(8,128)(2,1)S(1)} %get-tuple-element.104.refs_0_, bf16[80,4096]{1,0:T(8,128)(2,1)S(1)} %collective-permute-done.8.refs_1_, bf16[13312,2048]{1,0:T(8,128)(2,1)} %refs_2_.13, f32[160,2048]{1,0:T(8,128)S(1)} %get-tuple-element.105.refs_3_, ...), custom_call_target="tpu_custom_call" | custom-call | flops 10000000000 | bytes 1024 | tf_op jit(solution)/shard_map/multiply/pallas_call | solution.py:108
  58.1 0.1 collective-permute-start.9
  58.2 2.1 %collective-permute-done.9.refs_1_ = bf16[80,4096]{1,0:T(8,128)(2,1)S(1)} collective-permute-done((bf16[80,4096]{1,0:T(8,128)(2,1)S(1)}, bf16[80,4096]{1,0:T(8,128)(2,1)S(1)}, u32[]{:S(2)}, u32[]{:S(2)}) %collective-permute-start.9) | collective-permute-done | bytes 655392 | tf_op jit(solution)/shard_map/ppermute | solution.py:375
  60.3 6.8 %multiply.11 = (bf16[2,160,512]{2,1,0:T(8,128)(2,1)S(1)}, bf16[2,160,512]{2,1,0:T(8,128)(2,1)S(1)}, f32[8,128]{1,0:T(8,128)S(1)}) custom-call(bf16[80,4096]{1,0:T(8,128)(2,1)S(1)} %get-tuple-element.108.refs_0_, bf16[80,4096]{1,0:T(8,128)(2,1)S(1)} %collective-permute-done.9.refs_1_, bf16[13312,2048]{1,0:T(8,128)(2,1)} %refs_2_.13, ...), custom_call_target="tpu_custom_call" | custom-call | flops 10000000000 | bytes 1024 | tf_op jit(solution)/shard_map/multiply/pallas_call | solution.py:108
  67.2 3.6 %collective-permute-done.11.refs_0_ = bf16[48,7168]{1,0:T(8,128)(2,1)S(1)} collective-permute-done((bf16[48,7168]{1,0:T(8,128)(2,1)S(1)}, bf16[48,7168]{1,0:T(8,128)(2,1)S(1)}, u32[]{:S(2)}, u32[]{:S(2)}) %collective-permute-start.11) | collective-permute-done | bytes 688160 | tf_op jit(solution)/shard_map/ppermute | solution.py:375
  70.8 0.5 collective-permute-start.10
  71.3 1.7 %collective-permute-start.16 = (bf16[48,6144]{1,0:T(8,128)(2,1)S(1)}, bf16[48,6144]{1,0:T(8,128)(2,1)S(1)}, u32[]{:S(2)}, u32[]{:S(2)}) collective-permute-start(bf16[48,6144]{1,0:T(8,128)(2,1)S(1)} %get-tuple-element.127), channel_id=1, source_target_pairs={{0,2},{1,3},{2,0},{3,1},{4,6},{5,7},{6,4},{7,5},{8,10},{9,11},{10,... | collective-permute-start | bytes 1769480 | tf_op jit(solution)/shard_map/ppermute | solution.py:375
  73.0 1.6 %collective-permute-start.13 = (bf16[2,160,512]{2,1,0:T(8,128)(2,1)S(1)}, bf16[2,160,512]{2,1,0:T(8,128)(2,1)S(1)}, u32[]{:S(2)}, u32[]{:S(2)}) collective-permute-start(bf16[2,160,512]{2,1,0:T(8,128)(2,1)S(1)} %get-tuple-element.121), channel_id=1, source_target_pairs={{0,4},{4,0},{8,12},{12,8},{1,5},{5,1},{9,13},{13,9},{2,6},{6,2},{1... | collective-permute-start | bytes 983048 | tf_op jit(solution)/shard_map/ppermute | solution.py:378
  74.6 2.7 %collective-permute-start.12 = (bf16[2,128,512]{2,1,0:T(8,128)(2,1)S(1)}, bf16[2,128,512]{2,1,0:T(8,128)(2,1)S(1)}, u32[]{:S(2)}, u32[]{:S(2)}) collective-permute-start(bf16[2,128,512]{2,1,0:T(8,128)(2,1)S(1)} %get-tuple-element.119.refs_0_), channel_id=1, source_target_pairs={{0,8},{4,12},{8,0},{12,4},{1,9},{5,13},{9,1},{13,5},{2,10},{6,14},... | collective-permute-start | bytes 786440 | tf_op jit(solution)/shard_map/ppermute | solution.py:378
  77.3 10.2 %multiply.12 = (f32[96,2048]{1,0:T(8,128)S(1)}, f32[8,128]{1,0:T(8,128)S(1)}) custom-call(bf16[48,7168]{1,0:T(8,128)(2,1)S(1)} %get-tuple-element.122.refs_0_, bf16[48,7168]{1,0:T(8,128)(2,1)S(1)} %collective-permute-done.14.refs_1_, bf16[13312,2048]{1,0:T(8,128)(2,1)} %refs_2_.13, f32[8,128]{1,0:T(8,128)S(1)} %get-tuple-element.123.refs_3_), custom_call_target="tpu_custom_call" | custom-call | flops 10000000000 | bytes 1024 | tf_op jit(solution)/shard_map/multiply/pallas_call | solution.py:108
  87.5 0.5 collective-permute-done.13.refs_1_
  88.0 0.1 add.8
  88.2 2.5 %collective-permute-start.19 = (bf16[1,160,512]{2,1,0:T(8,128)(2,1)S(1)}, bf16[1,160,512]{2,1,0:T(8,128)(2,1)S(1)}, u32[]{:S(2)}, u32[]{:S(2)}) collective-permute-start(bf16[1,160,512]{2,1,0:T(8,128)(2,1)S(1)} %get-tuple-element.135), channel_id=1, source_target_pairs={{0,8},{4,12},{8,0},{12,4},{1,9},{5,13},{9,1},{13,5},{2,10},{6,14},... | collective-permute-start | bytes 491528 | tf_op jit(solution)/shard_map/ppermute | solution.py:378
  90.7 2.0 %collective-permute-start.15 = (bf16[4,128,512]{2,1,0:T(8,128)(2,1)S(1)}, bf16[4,128,512]{2,1,0:T(8,128)(2,1)S(1)}, u32[]{:S(2)}, u32[]{:S(2)}) collective-permute-start(bf16[4,128,512]{2,1,0:T(8,128)(2,1)S(1)} %get-tuple-element.126), channel_id=1, source_target_pairs={{0,4},{4,0},{8,12},{12,8},{1,5},{5,1},{9,13},{13,9},{2,6},{6,2},{1... | collective-permute-start | bytes 1572872 | tf_op jit(solution)/shard_map/ppermute | solution.py:378
  92.7 9.1 %multiply.13 = (bf16[2,96,512]{2,1,0:T(8,128)(2,1)S(1)}, bf16[2,96,512]{2,1,0:T(8,128)(2,1)S(1)}, f32[8,128]{1,0:T(8,128)S(1)}) custom-call(bf16[48,6144]{1,0:T(8,128)(2,1)S(1)} %get-tuple-element.129.refs_0_, bf16[48,6144]{1,0:T(8,128)(2,1)S(1)} %collective-permute-done.17.refs_1_, bf16[13312,2048]{1,0:T(8,128)(2,1)} %refs_2_.13, ...), custom_call_target="tpu_custom_call" | custom-call | flops 10000000000 | bytes 1024 | tf_op jit(solution)/shard_map/multiply/pallas_call | solution.py:108
  101.8 0.1 collective-permute-start.18
  102.0 1.5 %collective-permute-start.20 = (bf16[1,80,512]{2,1,0:T(8,128)(2,1)S(1)}, bf16[1,80,512]{2,1,0:T(8,128)(2,1)S(1)}, u32[]{:S(2)}, u32[]{:S(2)}) collective-permute-start(bf16[1,80,512]{2,1,0:T(8,128)(2,1)S(1)} %get-tuple-element.141), channel_id=1, source_target_pairs={{0,2},{1,3},{2,0},{3,1},{4,6},{5,7},{6,4},{7,5},{8,10},{9,11},{10,... | collective-permute-start | bytes 245768 | tf_op jit(solution)/shard_map/ppermute | solution.py:375
  103.5 7.7 %collective-permute-done.18.refs_1_ = bf16[2,96,512]{2,1,0:T(8,128)(2,1)S(1)} collective-permute-done((bf16[2,96,512]{2,1,0:T(8,128)(2,1)S(1)}, bf16[2,96,512]{2,1,0:T(8,128)(2,1)S(1)}, u32[]{:S(2)}, u32[]{:S(2)}) %collective-permute-start.18) | collective-permute-done | bytes 196640 | tf_op jit(solution)/shard_map/ppermute | solution.py:378
  111.2 2.6 %collective-permute-start.22 = (bf16[1,96,512]{2,1,0:T(8,128)(2,1)S(1)}, bf16[1,96,512]{2,1,0:T(8,128)(2,1)S(1)}, u32[]{:S(2)}, u32[]{:S(2)}) collective-permute-start(bf16[1,96,512]{2,1,0:T(8,128)(2,1)S(1)} %get-tuple-element.144), channel_id=1, source_target_pairs={{0,8},{4,12},{8,0},{12,4},{1,9},{5,13},{9,1},{13,5},{2,10},{6,14},... | collective-permute-start | bytes 294920 | tf_op jit(solution)/shard_map/ppermute | solution.py:378
  113.8 1.5 %encode.3 = (bf16[128,8192]{1,0:T(8,128)(2,1)}, f32[128,128]{1,0:T(8,128)S(1)}, f32[8,128]{1,0:T(8,128)S(1)}) custom-call(bf16[2,128,512]{2,1,0:T(8,128)(2,1)S(1)} %get-tuple-element.119.refs_0_, bf16[4,128,512]{2,1,0:T(8,128)(2,1)S(1)} %collective-permute-done.15.refs_1_.refs_3_, bf16[2,128,512]{2,1,0:T(8,128)(2,1)S(1)} %collective-permute-done.12.refs_1_.refs_2_, ...), custom_call_target="tpu_custom_call" | custom-call | flops 10000000000 | bytes 1024 | tf_op jit(solution)/shard_map/encode/pallas_call | solution.py:108
  115.4 3.7 %collective-permute-done.22.refs_1_ = bf16[1,96,512]{2,1,0:T(8,128)(2,1)S(1)} collective-permute-done((bf16[1,96,512]{2,1,0:T(8,128)(2,1)S(1)}, bf16[1,96,512]{2,1,0:T(8,128)(2,1)S(1)}, u32[]{:S(2)}, u32[]{:S(2)}) %collective-permute-start.22) | collective-permute-done | bytes 98336 | tf_op jit(solution)/shard_map/ppermute | solution.py:378
  119.1 0.4 collective-permute-start.23
  119.5 0.8 collective-permute-start.24
  120.3 3.6 %collective-permute-done.24.refs_0_ = bf16[1,48,512]{2,1,0:T(8,128)(2,1)S(1)} collective-permute-done((bf16[1,48,512]{2,1,0:T(8,128)(2,1)S(1)}, bf16[1,48,512]{2,1,0:T(8,128)(2,1)S(1)}, u32[]{:S(2)}, u32[]{:S(2)}) %collective-permute-start.24) | collective-permute-done | bytes 49184 | tf_op jit(solution)/shard_map/ppermute | solution.py:375
  123.9 0.4 collective-permute-done.25.refs_1_
  124.3 4.7 %collective-permute-done.23.refs_1_.refs_4_ = bf16[2,80,512]{2,1,0:T(8,128)(2,1)S(1)} collective-permute-done((bf16[2,80,512]{2,1,0:T(8,128)(2,1)S(1)}, bf16[2,80,512]{2,1,0:T(8,128)(2,1)S(1)}, u32[]{:S(2)}, u32[]{:S(2)}) %collective-permute-start.23) | collective-permute-done | bytes 163872 | tf_op jit(solution)/shard_map/ppermute | solution.py:378
  129.1 1.2 collective-permute-start.29
  130.4 2.2 %collective-permute-start.28 = (bf16[2,48,512]{2,1,0:T(8,128)(2,1)S(1)}, bf16[2,48,512]{2,1,0:T(8,128)(2,1)S(1)}, u32[]{:S(2)}, u32[]{:S(2)}) collective-permute-start(bf16[2,48,512]{2,1,0:T(8,128)(2,1)S(1)} %get-tuple-element.156.refs_2_), channel_id=1, source_target_pairs={{0,8},{4,12},{8,0},{12,4},{1,9},{5,13},{9,1},{13,5},{2,10},{6,14},... | collective-permute-start | bytes 294920 | tf_op jit(solution)/shard_map/ppermute | solution.py:378
  132.6 1.0 collective-permute-start.27
  133.6 9.5 %collective-permute-done.26.refs_3_.refs_5_ = bf16[4,80,512]{2,1,0:T(8,128)(2,1)S(1)} collective-permute-done((bf16[4,80,512]{2,1,0:T(8,128)(2,1)S(1)}, bf16[4,80,512]{2,1,0:T(8,128)(2,1)S(1)}, u32[]{:S(2)}, u32[]{:S(2)}) %collective-permute-start.26) | collective-permute-done | bytes 327712 | tf_op jit(solution)/shard_map/ppermute | solution.py:378
  143.1 1.2 encode.4
  144.3 1.6 %encode.5 = (bf16[128,8192]{1,0:T(8,128)(2,1)}, bf16[64,128]{1,0:T(8,128)(2,1)}, f32[8,128]{1,0:T(8,128)}) custom-call(bf16[128,8192]{1,0:T(8,128)(2,1)} %get-tuple-element.154.refs_0_, f32[128,128]{1,0:T(8,128)S(1)} %get-tuple-element.155.refs_1_, bf16[2,48,512]{2,1,0:T(8,128)(2,1)S(1)} %get-tuple-element.156.refs_2_, ...), custom_call_target="tpu_custom_call", output_to_operand_aliasing={{0}: (0, {})} | custom-call | bytes 1024 | tf_op jit(solution)/shard_map/encode/pallas_call | solution.py:108
  (43 shorter events, 0.5 us)
Async XLA Ops:
  5.9 3.5 %collective-permute-start.1 = (bf16[128,5120]{1,0:T(8,128)(2,1)S(1)}, bf16[128,5120]{1,0:T(8,128)(2,1)S(1)}, u32[]{:S(2)}, u32[]{:S(2)}) collective-permute-start(bf16[128,5120]{1,0:T(8,128)(2,1)S(1)} %get-tuple-element.82.refs_0_), channel_id=1, source_target_pairs={{0,1},{1,0},{2,3},{3,2},{4,5},{5,4},{6,7},{7,6},{8,9},{9,8},{10,11... | collective-permute-start | bytes 3932168 | tf_op jit(solution)/shard_map/ppermute | solution.py:375
  6.4 14.6 %collective-permute-start = (bf16[128,8192]{1,0:T(8,128)(2,1)S(1)}, bf16[128,8192]{1,0:T(8,128)(2,1)S(1)}, u32[]{:S(2)}, u32[]{:S(2)}) collective-permute-start(bf16[128,8192]{1,0:T(8,128)(2,1)S(1)} %get-tuple-element.81.refs_0_), channel_id=1, source_target_pairs={{0,1},{1,0},{2,3},{3,2},{4,5},{5,4},{6,7},{7,6},{8,9},{9,8},{10,11... | collective-permute-start | bytes 6291464 | tf_op jit(solution)/shard_map/ppermute | solution.py:375
  6.5 29.5 %collective-permute-start.4 = (bf16[80,5120]{1,0:T(8,128)(2,1)S(1)}, bf16[80,5120]{1,0:T(8,128)(2,1)S(1)}, u32[]{:S(2)}, u32[]{:S(2)}) collective-permute-start(bf16[80,5120]{1,0:T(8,128)(2,1)S(1)} %get-tuple-element.92), channel_id=1, source_target_pairs={{0,2},{1,3},{2,0},{3,1},{4,6},{5,7},{6,4},{7,5},{8,10},{9,11},{10,... | collective-permute-start | bytes 2457608 | tf_op jit(solution)/shard_map/ppermute | solution.py:375
  18.5 27.8 %collective-permute-start.3 = (bf16[80,4096]{1,0:T(8,128)(2,1)S(1)}, bf16[80,4096]{1,0:T(8,128)(2,1)S(1)}, u32[]{:S(2)}, u32[]{:S(2)}) collective-permute-start(bf16[80,4096]{1,0:T(8,128)(2,1)S(1)} %get-tuple-element.91), channel_id=1, source_target_pairs={{0,2},{1,3},{2,0},{3,1},{4,6},{5,7},{6,4},{7,5},{8,10},{9,11},{10,... | collective-permute-start | bytes 1966088 | tf_op jit(solution)/shard_map/ppermute | solution.py:375
  34.4 13.7 %collective-permute-start.2 = (bf16[2,256,512]{2,1,0:T(8,128)(2,1)S(1)}, bf16[2,256,512]{2,1,0:T(8,128)(2,1)S(1)}, u32[]{:S(2)}, u32[]{:S(2)}) collective-permute-start(bf16[2,256,512]{2,1,0:T(8,128)(2,1)S(1)} %get-tuple-element.89), channel_id=1, source_target_pairs={{0,4},{4,0},{8,12},{12,8},{1,5},{5,1},{9,13},{13,9},{2,6},{6,2},{1... | collective-permute-start | bytes 1572872 | tf_op jit(solution)/shard_map/ppermute | solution.py:378
  36.0 2.3 %collective-permute-start.5 = (bf16[80,5120]{1,0:T(8,128)(2,1)S(1)}, bf16[80,5120]{1,0:T(8,128)(2,1)S(1)}, u32[]{:S(2)}, u32[]{:S(2)}) collective-permute-start(bf16[80,5120]{1,0:T(8,128)(2,1)S(1)} %get-tuple-element.94.refs_0_), channel_id=1, source_target_pairs={{0,1},{1,0},{2,3},{3,2},{4,5},{5,4},{6,7},{7,6},{8,9},{9,8},{10,11... | collective-permute-start | bytes 2457608 | tf_op jit(solution)/shard_map/ppermute | solution.py:375
  36.0 22.1 %collective-permute-start.7 = (bf16[80,4096]{1,0:T(8,128)(2,1)S(1)}, bf16[80,4096]{1,0:T(8,128)(2,1)S(1)}, u32[]{:S(2)}, u32[]{:S(2)}) collective-permute-start(bf16[80,4096]{1,0:T(8,128)(2,1)S(1)} %get-tuple-element.103), channel_id=1, source_target_pairs={{0,2},{1,3},{2,0},{3,1},{4,6},{5,7},{6,4},{7,5},{8,10},{9,11},{10,... | collective-permute-start | bytes 1966088 | tf_op jit(solution)/shard_map/ppermute | solution.py:375
  46.2 5.2 %collective-permute-start.8 = (bf16[80,4096]{1,0:T(8,128)(2,1)S(1)}, bf16[80,4096]{1,0:T(8,128)(2,1)S(1)}, u32[]{:S(2)}, u32[]{:S(2)}) collective-permute-start(bf16[80,4096]{1,0:T(8,128)(2,1)S(1)} %get-tuple-element.104.refs_0_), channel_id=1, source_target_pairs={{0,1},{1,0},{2,3},{3,2},{4,5},{5,4},{6,7},{7,6},{8,9},{9,8},{10,11... | collective-permute-start | bytes 1966088 | tf_op jit(solution)/shard_map/ppermute | solution.py:375
  48.2 18.9 %collective-permute-start.6 = (bf16[1,256,512]{2,1,0:T(8,128)(2,1)S(1)}, bf16[1,256,512]{2,1,0:T(8,128)(2,1)S(1)}, u32[]{:S(2)}, u32[]{:S(2)}) collective-permute-start(bf16[1,256,512]{2,1,0:T(8,128)(2,1)S(1)} %get-tuple-element.102), channel_id=1, source_target_pairs={{0,8},{4,12},{8,0},{12,4},{1,9},{5,13},{9,1},{13,5},{2,10},{6,14},... | collective-permute-start | bytes 786440 | tf_op jit(solution)/shard_map/ppermute | solution.py:378
  50.9 19.9 %collective-permute-start.11 = (bf16[48,7168]{1,0:T(8,128)(2,1)S(1)}, bf16[48,7168]{1,0:T(8,128)(2,1)S(1)}, u32[]{:S(2)}, u32[]{:S(2)}) collective-permute-start(bf16[48,7168]{1,0:T(8,128)(2,1)S(1)} %get-tuple-element.116), channel_id=1, source_target_pairs={{0,2},{1,3},{2,0},{3,1},{4,6},{5,7},{6,4},{7,5},{8,10},{9,11},{10,... | collective-permute-start | bytes 2064392 | tf_op jit(solution)/shard_map/ppermute | solution.py:375
  58.1 2.2 %collective-permute-start.9 = (bf16[80,4096]{1,0:T(8,128)(2,1)S(1)}, bf16[80,4096]{1,0:T(8,128)(2,1)S(1)}, u32[]{:S(2)}, u32[]{:S(2)}) collective-permute-start(bf16[80,4096]{1,0:T(8,128)(2,1)S(1)} %get-tuple-element.108.refs_0_), channel_id=1, source_target_pairs={{0,1},{1,0},{2,3},{3,2},{4,5},{5,4},{6,7},{7,6},{8,9},{9,8},{10,11... | collective-permute-start | bytes 1966088 | tf_op jit(solution)/shard_map/ppermute | solution.py:375
  70.7 6.5 %collective-permute-start.14 = (bf16[48,7168]{1,0:T(8,128)(2,1)S(1)}, bf16[48,7168]{1,0:T(8,128)(2,1)S(1)}, u32[]{:S(2)}, u32[]{:S(2)}) collective-permute-start(bf16[48,7168]{1,0:T(8,128)(2,1)S(1)} %get-tuple-element.122.refs_0_), channel_id=1, source_target_pairs={{0,1},{1,0},{2,3},{3,2},{4,5},{5,4},{6,7},{7,6},{8,9},{9,8},{10,11... | collective-permute-start | bytes 2064392 | tf_op jit(solution)/shard_map/ppermute | solution.py:375
  70.8 3.8 %collective-permute-start.10 = (bf16[1,128,512]{2,1,0:T(8,128)(2,1)S(1)}, bf16[1,128,512]{2,1,0:T(8,128)(2,1)S(1)}, u32[]{:S(2)}, u32[]{:S(2)}) collective-permute-start(bf16[1,128,512]{2,1,0:T(8,128)(2,1)S(1)} %get-tuple-element.115), channel_id=1, source_target_pairs={{0,1},{1,0},{2,3},{3,2},{4,5},{5,4},{6,7},{7,6},{8,9},{9,8},{10,11... | collective-permute-start | bytes 393224 | tf_op jit(solution)/shard_map/ppermute | solution.py:375
  71.3 16.8 %collective-permute-start.16 = (bf16[48,6144]{1,0:T(8,128)(2,1)S(1)}, bf16[48,6144]{1,0:T(8,128)(2,1)S(1)}, u32[]{:S(2)}, u32[]{:S(2)}) collective-permute-start(bf16[48,6144]{1,0:T(8,128)(2,1)S(1)} %get-tuple-element.127), channel_id=1, source_target_pairs={{0,2},{1,3},{2,0},{3,1},{4,6},{5,7},{6,4},{7,5},{8,10},{9,11},{10,... | collective-permute-start | bytes 1769480 | tf_op jit(solution)/shard_map/ppermute | solution.py:375
  73.0 15.0 %collective-permute-start.13 = (bf16[2,160,512]{2,1,0:T(8,128)(2,1)S(1)}, bf16[2,160,512]{2,1,0:T(8,128)(2,1)S(1)}, u32[]{:S(2)}, u32[]{:S(2)}) collective-permute-start(bf16[2,160,512]{2,1,0:T(8,128)(2,1)S(1)} %get-tuple-element.121), channel_id=1, source_target_pairs={{0,4},{4,0},{8,12},{12,8},{1,5},{5,1},{9,13},{13,9},{2,6},{6,2},{1... | collective-permute-start | bytes 983048 | tf_op jit(solution)/shard_map/ppermute | solution.py:378
  74.6 13.4 %collective-permute-start.12 = (bf16[2,128,512]{2,1,0:T(8,128)(2,1)S(1)}, bf16[2,128,512]{2,1,0:T(8,128)(2,1)S(1)}, u32[]{:S(2)}, u32[]{:S(2)}) collective-permute-start(bf16[2,128,512]{2,1,0:T(8,128)(2,1)S(1)} %get-tuple-element.119.refs_0_), channel_id=1, source_target_pairs={{0,8},{4,12},{8,0},{12,4},{1,9},{5,13},{9,1},{13,5},{2,10},{6,14},... | collective-permute-start | bytes 786440 | tf_op jit(solution)/shard_map/ppermute | solution.py:378
  88.1 4.6 %collective-permute-start.17 = (bf16[48,6144]{1,0:T(8,128)(2,1)S(1)}, bf16[48,6144]{1,0:T(8,128)(2,1)S(1)}, u32[]{:S(2)}, u32[]{:S(2)}) collective-permute-start(bf16[48,6144]{1,0:T(8,128)(2,1)S(1)} %get-tuple-element.129.refs_0_), channel_id=1, source_target_pairs={{0,1},{1,0},{2,3},{3,2},{4,5},{5,4},{6,7},{7,6},{8,9},{9,8},{10,11... | collective-permute-start | bytes 1769480 | tf_op jit(solution)/shard_map/ppermute | solution.py:375
  88.2 13.7 %collective-permute-start.19 = (bf16[1,160,512]{2,1,0:T(8,128)(2,1)S(1)}, bf16[1,160,512]{2,1,0:T(8,128)(2,1)S(1)}, u32[]{:S(2)}, u32[]{:S(2)}) collective-permute-start(bf16[1,160,512]{2,1,0:T(8,128)(2,1)S(1)} %get-tuple-element.135), channel_id=1, source_target_pairs={{0,8},{4,12},{8,0},{12,4},{1,9},{5,13},{9,1},{13,5},{2,10},{6,14},... | collective-permute-start | bytes 491528 | tf_op jit(solution)/shard_map/ppermute | solution.py:378
  90.7 23.1 %collective-permute-start.15 = (bf16[4,128,512]{2,1,0:T(8,128)(2,1)S(1)}, bf16[4,128,512]{2,1,0:T(8,128)(2,1)S(1)}, u32[]{:S(2)}, u32[]{:S(2)}) collective-permute-start(bf16[4,128,512]{2,1,0:T(8,128)(2,1)S(1)} %get-tuple-element.126), channel_id=1, source_target_pairs={{0,4},{4,0},{8,12},{12,8},{1,5},{5,1},{9,13},{13,9},{2,6},{6,2},{1... | collective-permute-start | bytes 1572872 | tf_op jit(solution)/shard_map/ppermute | solution.py:378
  101.8 9.4 %collective-permute-start.18 = (bf16[2,96,512]{2,1,0:T(8,128)(2,1)S(1)}, bf16[2,96,512]{2,1,0:T(8,128)(2,1)S(1)}, u32[]{:S(2)}, u32[]{:S(2)}) collective-permute-start(bf16[2,96,512]{2,1,0:T(8,128)(2,1)S(1)} %get-tuple-element.133), channel_id=1, source_target_pairs={{0,4},{4,0},{8,12},{12,8},{1,5},{5,1},{9,13},{13,9},{2,6},{6,2},{1... | collective-permute-start | bytes 589832 | tf_op jit(solution)/shard_map/ppermute | solution.py:378
  102.0 17.1 %collective-permute-start.20 = (bf16[1,80,512]{2,1,0:T(8,128)(2,1)S(1)}, bf16[1,80,512]{2,1,0:T(8,128)(2,1)S(1)}, u32[]{:S(2)}, u32[]{:S(2)}) collective-permute-start(bf16[1,80,512]{2,1,0:T(8,128)(2,1)S(1)} %get-tuple-element.141), channel_id=1, source_target_pairs={{0,2},{1,3},{2,0},{3,1},{4,6},{5,7},{6,4},{7,5},{8,10},{9,11},{10,... | collective-permute-start | bytes 245768 | tf_op jit(solution)/shard_map/ppermute | solution.py:375
  103.5 15.6 %collective-permute-start.21 = (bf16[1,80,512]{2,1,0:T(8,128)(2,1)S(1)}, bf16[1,80,512]{2,1,0:T(8,128)(2,1)S(1)}, u32[]{:S(2)}, u32[]{:S(2)}) collective-permute-start(bf16[1,80,512]{2,1,0:T(8,128)(2,1)S(1)} %get-tuple-element.142), channel_id=1, source_target_pairs={{0,3},{1,2},{2,1},{3,0},{4,7},{5,6},{6,5},{7,4},{8,11},{9,10},{10,... | collective-permute-start | bytes 245768 | tf_op jit(solution)/shard_map/ppermute | solution.py:375
  111.2 7.8 %collective-permute-start.22 = (bf16[1,96,512]{2,1,0:T(8,128)(2,1)S(1)}, bf16[1,96,512]{2,1,0:T(8,128)(2,1)S(1)}, u32[]{:S(2)}, u32[]{:S(2)}) collective-permute-start(bf16[1,96,512]{2,1,0:T(8,128)(2,1)S(1)} %get-tuple-element.144), channel_id=1, source_target_pairs={{0,8},{4,12},{8,0},{12,4},{1,9},{5,13},{9,1},{13,5},{2,10},{6,14},... | collective-permute-start | bytes 294920 | tf_op jit(solution)/shard_map/ppermute | solution.py:378
  119.1 9.9 %collective-permute-start.23 = (bf16[2,80,512]{2,1,0:T(8,128)(2,1)S(1)}, bf16[2,80,512]{2,1,0:T(8,128)(2,1)S(1)}, u32[]{:S(2)}, u32[]{:S(2)}) collective-permute-start(bf16[2,80,512]{2,1,0:T(8,128)(2,1)S(1)} %get-tuple-element.147.refs_0_.refs_2_), channel_id=1, source_target_pairs={{0,8},{4,12},{8,0},{12,4},{1,9},{5,13},{9,1},{13,5},{2,10},{6,14},... | collective-permute-start | bytes 491528 | tf_op jit(solution)/shard_map/ppermute | solution.py:378
  119.5 4.4 %collective-permute-start.24 = (bf16[1,48,512]{2,1,0:T(8,128)(2,1)S(1)}, bf16[1,48,512]{2,1,0:T(8,128)(2,1)S(1)}, u32[]{:S(2)}, u32[]{:S(2)}) collective-permute-start(bf16[1,48,512]{2,1,0:T(8,128)(2,1)S(1)} %get-tuple-element.148), channel_id=1, source_target_pairs={{0,2},{1,3},{2,0},{3,1},{4,6},{5,7},{6,4},{7,5},{8,10},{9,11},{10,... | collective-permute-start | bytes 147464 | tf_op jit(solution)/shard_map/ppermute | solution.py:375
  120.3 4.0 %collective-permute-start.25 = (bf16[1,48,512]{2,1,0:T(8,128)(2,1)S(1)}, bf16[1,48,512]{2,1,0:T(8,128)(2,1)S(1)}, u32[]{:S(2)}, u32[]{:S(2)}) collective-permute-start(bf16[1,48,512]{2,1,0:T(8,128)(2,1)S(1)} %get-tuple-element.149), channel_id=1, source_target_pairs={{0,3},{1,2},{2,1},{3,0},{4,7},{5,6},{6,5},{7,4},{8,11},{9,10},{10,... | collective-permute-start | bytes 147464 | tf_op jit(solution)/shard_map/ppermute | solution.py:375
  129.0 14.0 %collective-permute-start.26 = (bf16[4,80,512]{2,1,0:T(8,128)(2,1)S(1)}, bf16[4,80,512]{2,1,0:T(8,128)(2,1)S(1)}, u32[]{:S(2)}, u32[]{:S(2)}) collective-permute-start(bf16[4,80,512]{2,1,0:T(8,128)(2,1)S(1)} %get-tuple-element.152), channel_id=1, source_target_pairs={{0,4},{4,0},{8,12},{12,8},{1,5},{5,1},{9,13},{13,9},{2,6},{6,2},{1... | collective-permute-start | bytes 983048 | tf_op jit(solution)/shard_map/ppermute | solution.py:378
  129.1 15.2 %collective-permute-start.29 = (bf16[2,48,512]{2,1,0:T(8,128)(2,1)S(1)}, bf16[2,48,512]{2,1,0:T(8,128)(2,1)S(1)}, u32[]{:S(2)}, u32[]{:S(2)}) collective-permute-start(bf16[2,48,512]{2,1,0:T(8,128)(2,1)S(1)} %get-tuple-element.156.refs_2_), channel_id=1, source_target_pairs={{0,12},{4,8},{8,4},{12,0},{1,13},{5,9},{9,5},{13,1},{2,14},{6,10},... | collective-permute-start | bytes 294920 | tf_op jit(solution)/shard_map/ppermute | solution.py:378
  130.4 13.9 %collective-permute-start.28 = (bf16[2,48,512]{2,1,0:T(8,128)(2,1)S(1)}, bf16[2,48,512]{2,1,0:T(8,128)(2,1)S(1)}, u32[]{:S(2)}, u32[]{:S(2)}) collective-permute-start(bf16[2,48,512]{2,1,0:T(8,128)(2,1)S(1)} %get-tuple-element.156.refs_2_), channel_id=1, source_target_pairs={{0,8},{4,12},{8,0},{12,4},{1,9},{5,13},{9,1},{13,5},{2,10},{6,14},... | collective-permute-start | bytes 294920 | tf_op jit(solution)/shard_map/ppermute | solution.py:378
  132.6 11.7 %collective-permute-start.27 = (bf16[2,48,512]{2,1,0:T(8,128)(2,1)S(1)}, bf16[2,48,512]{2,1,0:T(8,128)(2,1)S(1)}, u32[]{:S(2)}, u32[]{:S(2)}) collective-permute-start(bf16[2,48,512]{2,1,0:T(8,128)(2,1)S(1)} %get-tuple-element.156.refs_2_), channel_id=1, source_target_pairs={{0,4},{4,0},{8,12},{12,8},{1,5},{5,1},{9,13},{13,9},{2,6},{6,2},{1... | collective-permute-start | bytes 294920 | tf_op jit(solution)/shard_map/ppermute | solution.py:378
